TPU v7x, 32 devices: a whole 2x2x4 slice. The times are simulated.
32 devices in a mesh: dp: 8 (over z, core), mp: 4 (over y, x).
Axes of the slice: x: 2, y: 2, z: 4, core: 2. Of those that a mesh axis runs over, the one named last changes fastest.
Arguments:
- context: bfloat16 [2048, 4096], P('dp', 'mp'), parts along dimension 0, may hold values from -150 to 150
- w_out: bfloat16 [4096, 4096], P('mp'), may hold values from -0.09375 to 0.09375
- residual: bfloat16 [2048, 4096], P('dp', 'mp'), parts along dimension 0, may hold values from -150 to 150
- gain_temporal: float32 [4096], replicated, may hold values from 0.1 to 1.9
- w_in: bfloat16 [4096, 1024], P('mp'), may hold values from -0.09375 to 0.09375
- gain_depth: float32 [4, 1024], P('mp'), may hold values from 0.1 to 1.9
- w_depth: bfloat16 [4, 1024, 512], P('mp'), may hold values from -0.1875 to 0.1875
- cotangent: bfloat16 [4, 2048, 512], P('mp', 'dp'), parts along dimension 1, may hold values from -6 to 6
Outputs:
- depth_act: bfloat16 [4, 2048, 512], P('mp', 'dp'), parts along dimension 1
- grad_residual: bfloat16 [2048, 4096], P('dp', 'mp'), parts along dimension 0
- grad_context: bfloat16 [2048, 4096], P('dp', 'mp'), parts along dimension 0
There are 8 independent parts, one for each index of `dp`. A program takes and returns all parts, laid end to end along the dimension named above; an argument that names none is the same for every part. Nothing has to cross between parts.
All inputs are finite; a program needn't handle non-finite values.
Results may differ from a plain program's by a relative error of at most 0.0058.
Values may be sent and summed in bfloat16 or wider, within the bound.
No kernel may reach another device: no remote copies, remote signals or barrier semaphores. Data moves between devices by JAX's collectives and lax.ppermute only.
A program may use at most 64 MiB of HBM per device.

v0:
```python
import jax
import jax.numpy as jnp
from jax import lax
from jax.sharding import PartitionSpec as P

D = 4096


def norm_back(values, recip, gain, upstream):
    scaled = gain * upstream
    inner = jnp.mean(values * scaled, axis=-1, keepdims=True)
    return recip * scaled - values * recip * recip * recip * inner


def contract_last(left, right):
    return lax.dot_general(
        left, right, (((1,), (1,)), ((), ())), preferred_element_type=jnp.float32
    )


def local(context, w_out, residual, gain_temporal, w_in, gain_depth, w_depth, cotangent):
    feat_width = residual.shape[1]
    gain_cols = lax.dynamic_slice_in_dim(
        gain_temporal, lax.axis_index("mp") * feat_width, feat_width, 0
    )
    full_term = jnp.dot(context, w_out, preferred_element_type=jnp.float32)
    head_total = lax.psum_scatter(full_term, "mp", scatter_dimension=1, tiled=True)
    state = residual.astype(jnp.float32) + head_total
    squares = lax.psum(jnp.sum(state * state, axis=1, keepdims=True), "mp")
    recip = lax.rsqrt(squares / D + 1e-05)
    normed = (state * recip * gain_cols).astype(jnp.bfloat16)
    partial_value = jnp.dot(normed, w_in, preferred_element_type=jnp.float32)
    depth_in = lax.psum(partial_value, "mp")
    urecip = lax.rsqrt(jnp.mean(depth_in * depth_in, axis=-1, keepdims=True) + 1e-05)
    gain_code = gain_depth[0]
    latent = (depth_in * urecip * gain_code).astype(jnp.bfloat16)
    depth_act = jnp.dot(latent, w_depth[0], preferred_element_type=jnp.float32).astype(jnp.bfloat16)
    dlatent = contract_last(cotangent[0], w_depth[0])
    dinput = norm_back(depth_in, urecip, gain_code, dlatent)
    du_total = lax.psum(dinput, "mp").astype(jnp.bfloat16)
    dnormed = contract_last(du_total, w_in)
    scaled = gain_cols * dnormed
    inner = lax.psum(jnp.sum(state * scaled, axis=1, keepdims=True), "mp")
    grad_residual = (recip * scaled - state * recip * recip * recip * (inner / D)).astype(
        jnp.bfloat16
    )
    grad_context = contract_last(
        lax.all_gather(grad_residual, "mp", axis=1, tiled=True), w_out
    ).astype(jnp.bfloat16)
    return (depth_act[None], grad_residual, grad_context)


def solution(mesh):
    in_specs = (
        P("dp", "mp"),
        P("mp", None),
        P("dp", "mp"),
        P(),
        P("mp", None),
        P("mp", None),
        P("mp", None, None),
        P("mp", "dp", None),
    )
    out_specs = (P("mp", "dp", None), P("dp", "mp"), P("dp", "mp"))
    return jax.shard_map(local, mesh=mesh, in_specs=in_specs, out_specs=out_specs, check_vma=False)
```

profile of v0, /device:TPU:0, one launch (start us, length us, event | category | flops | bytes accessed | tf_op | source)
XLA Modules:
  0.0 245.5 jit_solution(16052231701991800400)
XLA Ops:
  7.2 0.0 copy-start
  7.2 0.0 reduce-scatter.2.cloned.1.call-start
  7.2 7.9 %fusion.10 = f32[256,4096]{1,0:T(8,128)} fusion(bf16[256,1024]{1,0:T(8,128)(2,1)} %param.8, bf16[1024,4096]{1,0:T(8,128)(2,1)} %param.9), kind=kOutput, calls=%fused_computation.27 | convolution fusion | flops 2147483648 | bytes 13107200 | tf_op jit(solution)/shard_map/dot_general | solution.py:26
  15.2 0.0 reduce-scatter.2.cloned.1.call-update
  15.2 0.0 all-reduce.3.cloned.1.call-start
  15.2 0.7 dynamic_slice.3
  15.9 54.8 %reduce-scatter.2.cloned.1.call-done = f32[256,1024]{1,0:T(8,128)} async-done(((f32[256,4096]{1,0:T(8,128)}), f32[256,1024]{1,0:T(8,128)}) %reduce-scatter.2.cloned.1.call-update) | async-done | bytes 1048592 | tf_op jit(solution)/shard_map/reduce_scatter | solution.py:27
  70.7 0.0 copy-start.1
  70.7 1.7 multiply_reduce_fusion.3
  72.4 8.9 %psum.28 = f32[256,1]{0,1:T(1,128)S(1)} all-reduce(f32[256,1]{0,1:T(1,128)S(1)} %bitcast.32), channel_id=1, replica_groups=mesh['dp'=8,'mp'=4] {'mp'}, use_global_device_ids=true, to_apply=%region_2.0 | all-reduce | flops 256 | bytes 2048 | tf_op jit(solution)/shard_map/psum | solution.py:29
  81.3 0.0 copy-done
  81.3 0.0 copy-done.1
  81.4 0.0 copy-start.3
  81.4 0.0 copy-start.4
  81.4 2.8 %fusion.3 = f32[256,1024]{1,0:T(8,128)} fusion(bf16[1024,1024]{1,0:T(8,128)(2,1)S(1)} %copy-done, f32[1024]{0:T(1024)S(1)} %dynamic_slice.3, f32[256]{0:T(256)S(1)} %bitcast.26, f32[256,1024]{1,0:T(8,128)S(1)} %copy-done.1, bf16[256,1024]{1,0:T(8,128)(2,1)} %param.10), kind=kOutput, calls=%fused_computation.16 | convolution fusion | flops 538181632 | bytes 4723712 | tf_op jit(solution)/shard_map/dot_general | solution.py:32
  84.2 0.0 all-reduce.3.cloned.1.call-update
  84.2 0.0 all-gather.2.cloned.1.call-start
  84.3 52.6 %all-reduce.3.cloned.1.call-done = f32[256,1024]{1,0:T(8,128)} async-done(((f32[256,1024]{1,0:T(8,128)}), f32[256,1024]{1,0:T(8,128)}) %all-reduce.3.cloned.1.call-update) | async-done | bytes 1048592 | tf_op jit(solution)/shard_map/psum | solution.py:33
  136.8 0.0 copy-start.2
  136.8 0.0 copy-done.3
  136.8 0.0 copy-done.4
  136.9 2.2 multiply_reduce_fusion.1
  139.1 0.0 copy-done.2
  139.1 1.3 multiply_subtract_fusion
  140.4 41.7 %all-reduce.4 = bf16[256,1024]{1,0:T(8,128)(2,1)} all-reduce(f32[256,1024]{1,0:T(8,128)} %multiply_subtract_fusion), channel_id=1, replica_groups=mesh['dp'=8,'mp'=4] {'mp'}, use_global_device_ids=true, to_apply=%region_6.0 | all-reduce | flops 262144 | bytes 1572864 | tf_op jit(solution)/shard_map/psum | solution.py:40
  182.1 3.0 %multiply_reduce_fusion = (f32[256]{0:T(256)S(1)}, f32[256,1024]{1,0:T(8,128)}) fusion(f32[256,1024]{1,0:T(8,128)S(1)} %copy-done.1, bf16[256,1024]{1,0:T(8,128)(2,1)} %param.10, bf16[256,1024]{1,0:T(8,128)(2,1)} %all-reduce.4, bf16[1024,1024]{1,0:T(8,128)(2,1)S(1)} %copy-done, f32[1024]{0:T(1024)S(1)} %dynamic_slice.3), kind=kOutput, calls=%fused_computation.8 | convolution fusion | flops 538181376 | bytes 5248000 | tf_op jit(solution)/shard_map/dot_general | solution.py:16
  185.1 9.4 %psum.31 = f32[256,1]{0,1:T(1,128)S(1)} all-reduce(f32[256,1]{0,1:T(1,128)S(1)} %bitcast.31), channel_id=1, replica_groups=mesh['dp'=8,'mp'=4] {'mp'}, use_global_device_ids=true, to_apply=%region_8.0 | all-reduce | flops 256 | bytes 2048 | tf_op jit(solution)/shard_map/psum | solution.py:43
  194.5 2.5 %subtract_convert_fusion = bf16[256,1024]{1,0:T(8,128)(2,1)} fusion(f32[256,1024]{1,0:T(8,128)} %get-tuple-element.7, f32[256]{0:T(256)S(1)} %bitcast.30, f32[256]{0:T(256)S(1)} %bitcast.27, f32[256,1024]{1,0:T(8,128)S(1)} %copy-done.1, bf16[256,1024]{1,0:T(8,128)(2,1)} %param.10), kind=kLoop, calls=%fused_computation.7 | loop fusion | flops 2359296 | bytes 3147776 | tf_op jit(solution)/shard_map/convert_element_type | solution.py:44
  197.0 0.0 all-gather.2.cloned.1.call-update
  197.0 2.7 %fusion = bf16[1,256,512]{2,1,0:T(8,128)(2,1)} fusion(bf16[1,1024,512]{2,1,0:T(8,128)(2,1)} %param.14, f32[256,1024]{1,0:T(8,128)} %all-reduce.3.cloned.1.call-done, f32[1024]{0:T(1024)S(1)} %bitcast.29, f32[256]{0:T(256)S(1)} %get-tuple-element.8), kind=kOutput, calls=%fused_computation.4 | convolution fusion | flops 269352960 | bytes 2364416 | tf_op jit(solution)/shard_map/dot_general | solution.py:37
  199.8 32.1 %all-gather.2.cloned.1.call-done = bf16[256,4096]{1,0:T(8,128)(2,1)} async-done(((bf16[256,1024]{1,0:T(8,128)(2,1)}), bf16[256,4096]{1,0:T(8,128)(2,1)}) %all-gather.2.cloned.1.call-update) | async-done | bytes 2097168 | tf_op jit(solution)/shard_map/all_gather | solution.py:48
  231.8 7.2 %convolution_convert_fusion = bf16[256,1024]{1,0:T(8,128)(2,1)} fusion(bf16[256,4096]{1,0:T(8,128)(2,1)} %all-gather.2.cloned.1.call-done, bf16[1024,4096]{1,0:T(8,128)(2,1)} %param.9), kind=kOutput, calls=%fused_computation.2 | convolution fusion | flops 2147745792 | bytes 11010048 | tf_op jit(solution)/shard_map/dot_general | solution.py:16
  (3 shorter events, 0.0 us)
Async XLA Ops:
  7.2 74.2 %copy-start = (bf16[1024,1024]{1,0:T(8,128)(2,1)S(1)}, bf16[1024,1024]{1,0:T(8,128)(2,1)}, u32[]{:S(2)}) copy-start(bf16[1024,1024]{1,0:T(8,128)(2,1)} %param.12) | copy-start | bytes 6291460
  7.2 63.6 %reduce-scatter.2.cloned.1.call-start = ((), (), s32[]{:S(2)}) async-start(), calls=%async_computation.1 | async-start | bytes 5242880 | tf_op jit(solution)/shard_map/reduce_scatter | solution.py:27
  15.2 121.7 %all-reduce.3.cloned.1.call-start = ((), (), s32[]{:S(2)}) async-start(), calls=%async_computation.2 | async-start | bytes 2097152 | tf_op jit(solution)/shard_map/psum | solution.py:33
  70.7 10.6 %copy-start.1 = (f32[256,1024]{1,0:T(8,128)S(1)}, f32[256,1024]{1,0:T(8,128)}, u32[]{:S(2)}) copy-start(f32[256,1024]{1,0:T(8,128)} %reduce-scatter.2.cloned.1.call-done) | copy-start | bytes 3145732
  81.4 55.5 %copy-start.3 = (bf16[1,256,512]{2,1,0:T(8,128)(2,1)S(1)}, bf16[1,256,512]{2,1,0:T(8,128)(2,1)}, u32[]{:S(2)}) copy-start(bf16[1,256,512]{2,1,0:T(8,128)(2,1)} %param.15) | copy-start | bytes 786436
  81.4 55.5 %copy-start.4 = (f32[1,1024]{1,0:T(1,128)S(1)}, f32[1,1024]{1,0:T(1,128)}, u32[]{:S(2)}) copy-start(f32[1,1024]{1,0:T(1,128)} %param.13) | copy-start | bytes 12292
  84.2 147.6 %all-gather.2.cloned.1.call-start = ((), (), s32[]{:S(2)}) async-start(), calls=%async_computation.3 | async-start | bytes 2621440 | tf_op jit(solution)/shard_map/all_gather | solution.py:48
  136.8 2.2 copy-start.2
Sparse Core Ops, SparseCore 0:
  15.3 55.3 reduce-scatter.1
  84.4 52.4 all-reduce.2
  197.2 34.6 all-gather.1
where the time goes:
time: 246 us
  waiting for transfers between devices  139 us (57%)
  blocking collectives  60.1 us (24%)
  matrix products  25.9 us (11%)
  between operations  13.8 us (6%)
  other arithmetic  5.44 us (2%)
    reduce_scatter x1, waiting for transfers between devices, local(): lax.psum_scatter(full_term, 'mp', scatter_dimension=1, tiled=True)  54.8 us
    psum x1, waiting for transfers between devices, local(): depth_in = lax.psum(partial_value, 'mp')  52.6 us
    psum x1, blocking collectives, local(): du_total = lax.psum(dinput, 'mp').astype(jnp.bfloat16)  41.7 us
    all_gather x1, waiting for transfers between devices, local(): lax.all_gather(grad_residual, 'mp', axis=1, tiled=True)  32.1 us
    dot_general x3, matrix products, contract_last(): lax.dot_general(left, right, (((1,), (1,)), ((), ())), preferred_element_...  12.4 us
    psum x1, blocking collectives, local(): inner = lax.psum(jnp.sum(state * scaled, axis=1, keepdims=True), 'mp')  9.44 us
    psum x1, blocking collectives, local(): squares = lax.psum(jnp.sum(state * state, axis=1, keepdims=True), 'mp')  8.92 us
    dot_general x1, matrix products, local(): full_term = jnp.dot(context, w_out, preferred_element_type=jnp.float32)  7.94 us
  transfers between devices with their start and end apart: 3, of which 3 were waited for; matrix products, arithmetic and copies ran while one was open for 1% of the time, Pallas kernels for 0%

commit v1 on v0

v1 whole, which is shorter than its diff:
```python
import jax
import jax.numpy as jnp
from jax import lax
from jax.sharding import PartitionSpec as P

EPS = 1e-05


def contract_last(left, right):
    return lax.dot_general(
        left, right, (((1,), (1,)), ((), ())), preferred_element_type=jnp.float32
    )


def local(n, context, w_out, residual, gain_temporal, w_in, gain_depth, w_depth, cotangent):
    bf16, f32 = jnp.bfloat16, jnp.float32
    me = lax.axis_index("mp")
    frames, width = residual.shape
    half = width // 2
    share = frames // n
    features = width * n
    depth = w_in.shape[1]
    bits = [1 << i for i in range(n.bit_length() - 1)]
    orders = (bits, bits[::-1])

    def swap(value, mask):
        return lax.ppermute(value, "mp", [(i, i ^ mask) for i in range(n)])

    def block_of(mask, side):
        return ((me ^ mask) * 2 + side) * half

    def w_out_cols(mask, side):
        return lax.dynamic_slice_in_dim(w_out, block_of(mask, side), half, 1)

    def rows_of(value, mask):
        return lax.dynamic_slice_in_dim(value, (me ^ mask) * share, share, 0)

    def sum_rows(value, kept):
        total = rows_of(kept, 0).astype(f32)
        for mask in range(n - 1, 0, -1):
            total = total + swap(rows_of(value, mask), mask).astype(f32)
        return total

    def gather_rows(own):
        whole = jnp.zeros((frames,) + own.shape[1:], own.dtype)
        parts = [(0, own)] + [(mask, swap(own, mask)) for mask in range(n - 1, 0, -1)]
        for mask, part in parts:
            whole = lax.dynamic_update_slice_in_dim(whole, part, (me ^ mask) * share, 0)
        return whole

    upstream = gain_depth[0] * contract_last(cotangent[0], w_depth[0])
    up_own = sum_rows(upstream.astype(bf16), upstream).astype(bf16)
    up_full = gather_rows(up_own).astype(f32)

    gains, state = [], []
    for side, order in enumerate(orders):
        total = {
            mask: jnp.dot(context, w_out_cols(mask, side), preferred_element_type=f32)
            for mask in range(n - 1, -1, -1)
        }
        left = list(total)
        for bit in order:
            for mask in [k for k in left if k & bit]:
                total[mask ^ bit] = total[mask ^ bit] + swap(
                    total[mask].astype(bf16), bit
                ).astype(f32)
            left = [k for k in left if not k & bit]
        state.append(residual[:, side * half : (side + 1) * half].astype(f32) + total[0])
        gains.append(lax.dynamic_slice_in_dim(gain_temporal, block_of(0, side), half, 0))

    squares = sum(jnp.sum(s * s, axis=1, keepdims=True) for s in state)
    high = squares.astype(bf16)
    low = (squares - high.astype(f32)).astype(bf16)
    raw = sum(
        jnp.dot((s * g).astype(bf16), w_in[i * half : (i + 1) * half], preferred_element_type=f32)
        for i, (s, g) in enumerate(zip(state, gains))
    )
    tail = jnp.concatenate([high, low, jnp.zeros((frames, 126), bf16)], axis=1)
    sent = jnp.concatenate([raw.astype(bf16), tail], axis=1)
    own = sum_rows(sent, sent)
    sq = own[:, depth : depth + 1] + own[:, depth + 1 : depth + 2]
    high = sq.astype(bf16)
    low = (sq - high.astype(f32)).astype(bf16)
    own = jnp.concatenate(
        [own[:, :depth].astype(bf16), high, low, jnp.zeros((share, 126), bf16)], axis=1
    )
    got = gather_rows(own)
    raw = got[:, :depth].astype(f32)
    squares = got[:, depth : depth + 1].astype(f32) + got[:, depth + 1 : depth + 2].astype(f32)

    recip = lax.rsqrt(squares / features + EPS)
    depth_in = raw * recip
    urecip = lax.rsqrt(jnp.mean(depth_in * depth_in, axis=-1, keepdims=True) + EPS)
    inner = jnp.mean(depth_in * up_full, axis=-1, keepdims=True)
    du = (urecip * up_full - depth_in * (urecip * urecip * urecip * inner)).astype(bf16)
    dot_du = jnp.sum(du.astype(f32) * depth_in, axis=1, keepdims=True) / recip
    back = recip * recip * recip * (dot_du / features)

    grad = []
    for side in range(2):
        dnormed = contract_last(du, w_in[side * half : (side + 1) * half])
        grad.append((recip * gains[side] * dnormed - state[side] * back).astype(bf16))

    grad_context = jnp.zeros((frames, w_out.shape[0]), f32)
    for side, order in enumerate(orders):
        have = {0: grad[side]}
        for bit in order:
            for mask in list(have):
                have[mask ^ bit] = swap(have[mask], bit)
        for mask, block in have.items():
            grad_context = grad_context + contract_last(block, w_out_cols(mask, side))

    latent = (depth_in * urecip * gain_depth[0]).astype(bf16)
    depth_act = jnp.dot(latent, w_depth[0], preferred_element_type=f32).astype(bf16)
    return (depth_act[None], jnp.concatenate(grad, axis=1), grad_context.astype(bf16))


def solution(mesh):
    in_specs = (
        P("dp", "mp"),
        P("mp", None),
        P("dp", "mp"),
        P(),
        P("mp", None),
        P("mp", None),
        P("mp", None, None),
        P("mp", "dp", None),
    )
    out_specs = (P("mp", "dp", None), P("dp", "mp"), P("dp", "mp"))
    n = mesh.shape["mp"]

    def run(*args):
        return local(n, *args)

    return jax.shard_map(run, mesh=mesh, in_specs=in_specs, out_specs=out_specs, check_vma=False)
```

time: 246 us -> 139 us (0.57)
  waiting for transfers between devices: 139 us -> 34.9 us
  blocking collectives: 60.1 us -> 0 us
  local copies, waits for them, and re-layouts: 0.72 us -> 27.8 us
  starting transfers between devices: 0.12 us -> 27 us
  matrix products: 25.9 us -> 42.8 us
  between operations: 13.8 us -> 1.12 us
    psum x3 -> x0, blocking collectives: 60.1 us -> none  [the longest x1 41.7 us: local(): du_total = lax.psum(dinput, 'mp').astype(jnp.bfloat16)]
    reduce_scatter x1 -> x0, waiting for transfers between devices: 54.8 us -> none  [local(): lax.psum_scatter(full_term, 'mp', scatter_dimension=1, tiled=True)]
    psum x1 -> x0, waiting for transfers between devices: 52.6 us -> none  [local(): depth_in = lax.psum(partial_value, 'mp')]
    ppermute x0 -> x24, waiting for transfers between devices: none -> 34.9 us  [swap(): return lax.ppermute(value, 'mp', [(i, i ^ mask) for i in range(n)])]
    all_gather x1 -> x0, waiting for transfers between devices: 32.1 us -> none  [local(): lax.all_gather(grad_residual, 'mp', axis=1, tiled=True)]
    ppermute x0 -> x24, starting transfers between devices: none -> 27 us  [swap(): return lax.ppermute(value, 'mp', [(i, i ^ mask) for i in range(n)])]
    dynamic_update_slice x0 -> x8, local copies, waits for them, and re-layouts: none -> 18.9 us  [gather_rows(): whole = lax.dynamic_update_slice_in_dim(whole, part, (me ^ mask) * share, 0)]
    dot_general x3 -> x11, matrix products: 13.5 us -> 23 us  [the longest x8 18.8 us: local(): jnp.dot(context, w_out_cols(mask, side), preferred_element_type=f32)]
  transfers between devices with their start and end apart: 3 -> 24, of which waited for: 3 -> 6; matrix products, arithmetic and copies ran while one was open for 1% -> 45% of each run, Pallas kernels for 0% -> 0%
where the time goes in v1:
time: 139 us; the launch traced here: 138 us
  matrix products  42.8 us (31%)
  waiting for transfers between devices  34.9 us (25%)
  local copies, waits for them, and re-layouts  27.8 us (20%)
  starting transfers between devices  27 us (19%)
  other arithmetic  4.7 us (3%)
    ppermute x24, waiting for transfers between devices, swap(): return lax.ppermute(value, 'mp', [(i, i ^ mask) for i in range(n)])  34.9 us
    ppermute x24, starting transfers between devices, swap(): return lax.ppermute(value, 'mp', [(i, i ^ mask) for i in range(n)])  27 us
    dot_general x11, matrix products, contract_last(): lax.dot_general(left, right, (((1,), (1,)), ((), ())), preferred_element_...  19.8 us
    dynamic_update_slice x8, local copies, waits for them, and re-layouts, gather_rows(): whole = lax.dynamic_update_slice_in_dim(whole, part, (me ^ mask) * share, 0)  18.9 us
    dot_general x8, matrix products, local(): jnp.dot(context, w_out_cols(mask, side), preferred_element_type=f32)  18.8 us
    unnamed x17, local copies, waits for them, and re-layouts  3.68 us
  transfers between devices with their start and end apart: 24, of which 6 were waited for; matrix products, arithmetic and copies ran while one was open for 45% of the time, Pallas kernels for 0%

profile of v1, /device:TPU:0, one launch (start us, length us, event | category | flops | bytes accessed | tf_op | source)
XLA Modules:
  0.0 138.3 jit_solution(10989325104425441897)
XLA Ops:
  0.7 2.7 %fusion.9 = bf16[256,512]{0,1:T(8,128)(2,1)} fusion(bf16[256,1024]{1,0:T(8,128)(2,1)} %param.8, bf16[1024,4096]{1,0:T(8,128)(2,1)} %param.9, s32[]{:T(128)S(6)} %select_n.27), kind=kOutput, calls=%fused_computation.29 | convolution fusion | flops 268566528 | bytes 1835012 | tf_op jit(solution)/shard_map/dot_general | solution.py:58
  3.3 2.9 %collective-permute-start.1 = (bf16[256,512]{0,1:T(8,128)(2,1)}, bf16[256,512]{0,1:T(8,128)(2,1)}, u32[]{:S(2)}, u32[]{:S(2)}) collective-permute-start(bf16[256,512]{0,1:T(8,128)(2,1)} %fusion.9), channel_id=1, source_target_pairs={{0,1},{1,0},{2,3},{3,2},{4,5},{5,4},{6,7},{7,6},{8,9},{9,8},{10,11... | collective-permute-start | bytes 786440 | tf_op jit(solution)/shard_map/ppermute | solution.py:27
  6.3 2.6 %fusion.8 = bf16[256,512]{0,1:T(8,128)(2,1)} fusion(bf16[256,1024]{1,0:T(8,128)(2,1)} %param.8, bf16[1024,4096]{1,0:T(8,128)(2,1)} %param.9, s32[]{:T(128)S(6)} %select_n.25), kind=kOutput, calls=%fused_computation.28 | convolution fusion | flops 268566528 | bytes 1835012 | tf_op jit(solution)/shard_map/dot_general | solution.py:58
  8.9 2.5 %fusion.11 = bf16[256,512]{0,1:T(8,128)(2,1)} fusion(bf16[256,1024]{1,0:T(8,128)(2,1)} %param.8, bf16[1024,4096]{1,0:T(8,128)(2,1)} %param.9, s32[]{:T(128)S(6)} %select_n.31), kind=kOutput, calls=%fused_computation.31 | convolution fusion | flops 268566528 | bytes 1835012 | tf_op jit(solution)/shard_map/dot_general | solution.py:58
  11.4 2.0 %collective-permute-start.4 = (bf16[256,512]{0,1:T(8,128)(2,1)}, bf16[256,512]{0,1:T(8,128)(2,1)}, u32[]{:S(2)}, u32[]{:S(2)}) collective-permute-start(bf16[256,512]{0,1:T(8,128)(2,1)} %fusion.11), channel_id=1, source_target_pairs={{0,2},{1,3},{2,0},{3,1},{4,6},{5,7},{6,4},{7,5},{8,10},{9,11},{10,... | collective-permute-start | bytes 786440 | tf_op jit(solution)/shard_map/ppermute | solution.py:27
  13.5 2.5 %fusion.10 = bf16[256,512]{0,1:T(8,128)(2,1)} fusion(bf16[256,1024]{1,0:T(8,128)(2,1)} %param.8, bf16[1024,4096]{1,0:T(8,128)(2,1)} %param.9, s32[]{:T(128)S(6)} %select_n.29), kind=kOutput, calls=%fused_computation.30 | convolution fusion | flops 268566528 | bytes 1835012 | tf_op jit(solution)/shard_map/dot_general | solution.py:58
  16.0 1.4 %fusion.77 = (bf16[256,1024]{0,1:T(8,128)(2,1)S(1)}, f32[256,1024]{0,1:T(8,128)S(1)}) fusion(bf16[1,1024,512]{2,1,0:T(8,128)(2,1)S(1)} %copy-done, bf16[1,256,512]{2,1,0:T(8,128)(2,1)} %param.15, f32[1024]{0:T(1024)} %bitcast.64), kind=kOutput, calls=%fused_computation.123 | convolution fusion | flops 268959744 | bytes 2887680 | tf_op jit(solution)/shard_map/dot_general | solution.py:10
  18.6 3.0 %collective-permute-start.12 = (bf16[64,1024]{0,1:T(8,128)(2,1)}, bf16[64,1024]{0,1:T(8,128)(2,1)}, u32[]{:S(2)}, u32[]{:S(2)}) collective-permute-start(bf16[64,1024]{0,1:T(8,128)(2,1)} %get-tuple-element.27), channel_id=1, source_target_pairs={{0,3},{1,2},{2,1},{3,0},{4,7},{5,6},{6,5},{7,4},{8,11},{9,10},{10,... | collective-permute-start | bytes 393224 | tf_op jit(solution)/shard_map/ppermute | solution.py:27
  21.6 1.7 %convolution_bitcast_fusion.3 = f32[256,512]{0,1:T(8,128)S(1)} fusion(bf16[256,1024]{1,0:T(8,128)(2,1)S(1)} %copy-done.1, bf16[1024,4096]{1,0:T(8,128)(2,1)} %param.9, s32[]{:T(128)S(6)} %select_n.24), kind=kOutput, calls=%fused_computation.20 | convolution fusion | flops 268435456 | bytes 2097156 | tf_op jit(solution)/shard_map/dot_general | solution.py:58
  23.3 1.8 %fusion.75 = (bf16[256,512]{1,0:T(8,128)(2,1)}, bf16[256,512]{1,0:T(8,128)(2,1)S(1)}) fusion(bf16[256,1024]{1,0:T(8,128)(2,1)} %param.10), kind=kLoop, calls=%fused_computation.121 | loop fusion | bytes 1048576 | tf_op jit(solution)/shard_map/slice | solution.py:68
  25.0 2.5 %convolution_bitcast_fusion.1 = f32[256,512]{0,1:T(8,128)} fusion(bf16[256,1024]{1,0:T(8,128)(2,1)S(1)} %copy-done.1, bf16[1024,4096]{1,0:T(8,128)(2,1)} %param.9, s32[]{:T(128)S(6)} %select_n.28), kind=kOutput, calls=%fused_computation.18 | convolution fusion | flops 268435456 | bytes 2097156 | tf_op jit(solution)/shard_map/dot_general | solution.py:58
  27.5 2.5 %add_convert_fusion.2 = bf16[256,512]{0,1:T(8,128)(2,1)} fusion(bf16[256,512]{0,1:T(8,128)(2,1)} %collective-permute-done.1, bf16[256,1024]{1,0:T(8,128)(2,1)S(1)} %copy-done.1, bf16[1024,4096]{1,0:T(8,128)(2,1)} %param.9, s32[]{:T(128)S(6)} %select_n.26), kind=kOutput, calls=%fused_computation.80 | convolution fusion | flops 268828672 | bytes 2097156 | tf_op jit(solution)/shard_map/dot_general | solution.py:58
  33.3 1.6 %collective-permute-start.13 = (bf16[64,1024]{0,1:T(8,128)(2,1)}, bf16[64,1024]{0,1:T(8,128)(2,1)}, u32[]{:S(2)}, u32[]{:S(2)}) collective-permute-start(bf16[64,1024]{0,1:T(8,128)(2,1)} %get-tuple-element.29), channel_id=1, source_target_pairs={{0,2},{1,3},{2,0},{3,1},{4,6},{5,7},{6,4},{7,5},{8,10},{9,11},{10,... | collective-permute-start | bytes 393224 | tf_op jit(solution)/shard_map/ppermute | solution.py:27
  34.9 1.8 %add_convert_fusion.1 = bf16[256,512]{0,1:T(8,128)(2,1)S(1)} fusion(bf16[256,512]{0,1:T(8,128)(2,1)} %collective-permute-done.4, bf16[256,1024]{1,0:T(8,128)(2,1)S(1)} %copy-done.1, bf16[1024,4096]{1,0:T(8,128)(2,1)} %param.9, s32[]{:T(128)S(6)} %select_n.30), kind=kOutput, calls=%fused_computation.77 | convolution fusion | flops 268828672 | bytes 2097156 | tf_op jit(solution)/shard_map/dot_general | solution.py:58
  37.3 2.2 %collective-permute-done.2 = bf16[256,512]{0,1:T(8,128)(2,1)} collective-permute-done((bf16[256,512]{0,1:T(8,128)(2,1)}, bf16[256,512]{0,1:T(8,128)(2,1)}, u32[]{:S(2)}, u32[]{:S(2)}) %collective-permute-start.2) | collective-permute-done | bytes 262176 | tf_op jit(solution)/shard_map/ppermute | solution.py:27
  40.1 1.3 multiply_reduce_fusion.3
  41.4 7.3 %collective-permute-done.5 = bf16[256,512]{0,1:T(8,128)(2,1)S(1)} collective-permute-done((bf16[256,512]{0,1:T(8,128)(2,1)S(1)}, bf16[256,512]{0,1:T(8,128)(2,1)S(1)}, u32[]{:S(2)}, u32[]{:S(2)}) %collective-permute-start.5) | collective-permute-done | bytes 262176 | tf_op jit(solution)/shard_map/ppermute | solution.py:27
  48.7 1.3 multiply_reduce_fusion.2
  50.0 2.0 %fusion.21 = f32[256,1024]{0,1:T(8,128)S(1)} fusion(bf16[1024,1024]{1,0:T(8,128)(2,1)} %param.12, f32[256,512]{0,1:T(8,128)S(1)} %get-tuple-element.19, f32[512]{0:T(512)S(1)} %get-tuple-element.31), kind=kOutput, calls=%fused_computation.45 | convolution fusion | flops 268697600 | bytes 2623488 | tf_op jit(solution)/shard_map/dot_general | solution.py:75
  54.2 1.6 %collective-permute-start.7 = (bf16[64,1152]{0,1:T(8,128)(2,1)S(1)}, bf16[64,1152]{0,1:T(8,128)(2,1)S(1)}, u32[]{:S(2)}, u32[]{:S(2)}) collective-permute-start(bf16[64,1152]{0,1:T(8,128)(2,1)S(1)} %get-tuple-element.24), channel_id=1, source_target_pairs={{0,2},{1,3},{2,0},{3,1},{4,6},{5,7},{6,4},{7,5},{8,10},{9,11},{10,... | collective-permute-start | bytes 442376 | tf_op jit(solution)/shard_map/ppermute | solution.py:27
  55.8 1.5 %collective-permute-start.8 = (bf16[64,1152]{0,1:T(8,128)(2,1)S(1)}, bf16[64,1152]{0,1:T(8,128)(2,1)S(1)}, u32[]{:S(2)}, u32[]{:S(2)}) collective-permute-start(bf16[64,1152]{0,1:T(8,128)(2,1)S(1)} %get-tuple-element.23), channel_id=1, source_target_pairs={{0,1},{1,0},{2,3},{3,2},{4,5},{5,4},{6,7},{7,6},{8,9},{9,8},{10,11... | collective-permute-start | bytes 442376 | tf_op jit(solution)/shard_map/ppermute | solution.py:27
  57.3 1.3 add_convert_fusion
  59.1 5.6 %collective-permute-done.6 = bf16[64,1152]{0,1:T(8,128)(2,1)S(1)} collective-permute-done((bf16[64,1152]{0,1:T(8,128)(2,1)S(1)}, bf16[64,1152]{0,1:T(8,128)(2,1)S(1)}, u32[]{:S(2)}, u32[]{:S(2)}) %collective-permute-start.6) | collective-permute-done | bytes 147488 | tf_op jit(solution)/shard_map/ppermute | solution.py:27
  64.7 4.6 %collective-permute-done.7 = bf16[64,1152]{0,1:T(8,128)(2,1)S(1)} collective-permute-done((bf16[64,1152]{0,1:T(8,128)(2,1)S(1)}, bf16[64,1152]{0,1:T(8,128)(2,1)S(1)}, u32[]{:S(2)}, u32[]{:S(2)}) %collective-permute-start.7) | collective-permute-done | bytes 147488 | tf_op jit(solution)/shard_map/ppermute | solution.py:27
  70.0 1.2 collective-permute-start.9
  71.2 1.3 collective-permute-start.10
  73.5 1.3 collective-permute-start.16
  76.0 1.2 dynamic_update_slice.28
  77.2 3.1 %dynamic_update_slice.29 = bf16[256,1024]{0,1:T(8,128)(2,1)S(1)} dynamic-update-slice(bf16[256,1024]{0,1:T(8,128)(2,1)S(1)} %dynamic_update_slice.28, bf16[64,1024]{0,1:T(8,128)(2,1)} %copy-done.5, s32[]{:T(128)S(6)} %select_n.33, s32[]{:T(128)} %constant.16.clone.1) | dynamic-update-slice | bytes 262148 | tf_op jit(solution)/shard_map/dynamic_update_slice | solution.py:48
  80.3 10.6 %collective-permute-done.16 = bf16[64,1024]{0,1:T(8,128)(2,1)S(1)} collective-permute-done((bf16[64,1024]{0,1:T(8,128)(2,1)S(1)}, bf16[64,1024]{0,1:T(8,128)(2,1)S(1)}, u32[]{:S(2)}, u32[]{:S(2)}) %collective-permute-start.16) | collective-permute-done | bytes 131104 | tf_op jit(solution)/shard_map/ppermute | solution.py:27
  91.9 3.2 %dynamic_update_slice.31 = bf16[256,1024]{0,1:T(8,128)(2,1)S(1)} dynamic-update-slice(bf16[256,1024]{0,1:T(8,128)(2,1)S(1)} %dynamic_update_slice.30, bf16[64,1024]{0,1:T(8,128)(2,1)} %collective-permute-done.17, s32[]{:T(128)S(6)} %select_n.69, s32[]{:T(128)} %constant.16.clone.1) | dynamic-update-slice | bytes 262148 | tf_op jit(solution)/shard_map/dynamic_update_slice | solution.py:48
  95.2 2.1 %dynamic_update_slice.24 = bf16[256,1152]{0,1:T(8,128)(2,1)S(1)} dynamic-update-slice(bf16[256,1152]{0,1:T(8,128)(2,1)S(1)} %broadcast_in_dim.12, bf16[64,1152]{0,1:T(8,128)(2,1)S(1)} %concatenate.10, s32[]{:T(128)S(6)} %select_n.32, s32[]{:T(128)} %constant.16.clone.1) | dynamic-update-slice | bytes 294916 | tf_op jit(solution)/shard_map/dynamic_update_slice | solution.py:48
  97.3 3.0 %dynamic_update_slice.25 = bf16[256,1152]{0,1:T(8,128)(2,1)S(1)} dynamic-update-slice(bf16[256,1152]{0,1:T(8,128)(2,1)S(1)} %dynamic_update_slice.24, bf16[64,1152]{0,1:T(8,128)(2,1)S(1)} %collective-permute-done.9, s32[]{:T(128)S(6)} %select_n.33, s32[]{:T(128)} %constant.16.clone.1) | dynamic-update-slice | bytes 294916 | tf_op jit(solution)/shard_map/dynamic_update_slice | solution.py:48
  100.3 1.7 %dynamic_update_slice.26 = bf16[256,1152]{0,1:T(8,128)(2,1)S(1)} dynamic-update-slice(bf16[256,1152]{0,1:T(8,128)(2,1)S(1)} %dynamic_update_slice.25, bf16[64,1152]{0,1:T(8,128)(2,1)S(1)} %collective-permute-done.10, s32[]{:T(128)S(6)} %select_n.68, s32[]{:T(128)} %constant.16.clone.1) | dynamic-update-slice | bytes 294916 | tf_op jit(solution)/shard_map/dynamic_update_slice | solution.py:48
  102.1 3.6 %dynamic_update_slice.27 = bf16[256,1152]{0,1:T(8,128)(2,1)S(1)} dynamic-update-slice(bf16[256,1152]{0,1:T(8,128)(2,1)S(1)} %dynamic_update_slice.26, bf16[64,1152]{0,1:T(8,128)(2,1)S(1)} %collective-permute-done.11, s32[]{:T(128)S(6)} %select_n.69, s32[]{:T(128)} %constant.16.clone.1) | dynamic-update-slice | bytes 294916 | tf_op jit(solution)/shard_map/dynamic_update_slice | solution.py:48
  106.3 1.8 %fusion.7 = bf16[256,512]{0,1:T(8,128)(2,1)S(1)} fusion(bf16[256,1024]{0,1:T(8,128)(2,1)S(1)} %get-tuple-element.15, bf16[1024,1024]{1,0:T(8,128)(2,1)} %param.12, f32[256,512]{0,1:T(8,128)} %copy-done.2, f32[256]{0:T(256)S(1)} %bitcast.67, f32[256]{0:T(256)S(1)} %bitcast.59, f32[512]{0:T(512)S(1)} %get-tuple-element.31), kind=kOutput, calls=%fused_computation.22 | convolution fusion | flops 269090816 | bytes 2363392 | tf_op jit(solution)/shard_map/dot_general | solution.py:10
  108.1 1.7 %fusion.39 = f32[256,1024]{1,0:T(8,128)S(1)} fusion(bf16[256,512]{0,1:T(8,128)(2,1)S(1)} %fusion.7, bf16[1024,4096]{1,0:T(8,128)(2,1)} %param.9, s32[]{:T(128)S(6)} %select_n.24), kind=kOutput, calls=%fused_computation.63 | convolution fusion | flops 268435456 | bytes 2359300 | tf_op jit(solution)/shard_map/dot_general | solution.py:10
  111.4 1.8 %fusion.6 = bf16[256,512]{0,1:T(8,128)(2,1)S(1)} fusion(bf16[256,1024]{0,1:T(8,128)(2,1)S(1)} %get-tuple-element.15, bf16[1024,1024]{1,0:T(8,128)(2,1)} %param.12, f32[256,512]{0,1:T(8,128)} %copy-done.3, f32[256]{0:T(256)S(1)} %bitcast.68, f32[256]{0:T(256)S(1)} %bitcast.60, f32[512]{0:T(512)S(1)} %get-tuple-element.30), kind=kOutput, calls=%fused_computation.21 | convolution fusion | flops 269090816 | bytes 2363392 | tf_op jit(solution)/shard_map/dot_general | solution.py:10
  113.2 1.6 %collective-permute-start.22 = (bf16[256,512]{0,1:T(8,128)(2,1)S(1)}, bf16[256,512]{0,1:T(8,128)(2,1)}, u32[]{:S(2)}, u32[]{:S(2)}) collective-permute-start(bf16[256,512]{0,1:T(8,128)(2,1)S(1)} %fusion.6), channel_id=1, source_target_pairs={{0,1},{1,0},{2,3},{3,2},{4,5},{5,4},{6,7},{7,6},{8,9},{9,8},{10,11... | collective-permute-start | bytes 786440 | tf_op jit(solution)/shard_map/ppermute | solution.py:27
  115.8 1.5 %fusion.12 = bf16[1,256,512]{2,1,0:T(8,128)(2,1)} fusion(bf16[1,1024,512]{2,1,0:T(8,128)(2,1)S(1)} %copy-done, f32[1024]{0:T(1024)S(1)} %bitcast.65, f32[256]{0:T(256)S(1)} %get-tuple-element.33, f32[256]{0:T(256)S(1)} %bitcast.61, bf16[256,1152]{0,1:T(8,128)(2,1)S(1)} %dynamic_update_slice.27), kind=kOutput, calls=%fused_computation.32 | convolution fusion | flops 269877248 | bytes 1841152 | tf_op jit(solution)/shard_map/dot_general | solution.py:114
  118.3 1.7 %fusion.30 = f32[256,1024]{1,0:T(8,128)S(1)} fusion(bf16[256,512]{0,1:T(8,128)(2,1)S(1)} %fusion.6, bf16[1024,4096]{1,0:T(8,128)(2,1)} %param.9, s32[]{:T(128)S(6)} %select_n.28), kind=kOutput, calls=%fused_computation.54 | convolution fusion | flops 268435456 | bytes 2359300 | tf_op jit(solution)/shard_map/dot_general | solution.py:10
  121.1 4.6 %collective-permute-done.21 = bf16[256,512]{0,1:T(8,128)(2,1)} collective-permute-done((bf16[256,512]{0,1:T(8,128)(2,1)S(1)}, bf16[256,512]{0,1:T(8,128)(2,1)}, u32[]{:S(2)}, u32[]{:S(2)}) %collective-permute-start.21) | collective-permute-done | bytes 262176 | tf_op jit(solution)/shard_map/ppermute | solution.py:27
  126.8 1.7 %convolution_add_fusion.4 = f32[256,1024]{1,0:T(8,128)S(1)} fusion(f32[256,1024]{1,0:T(8,128)S(1)} %fusion.39, bf16[256,512]{0,1:T(8,128)(2,1)S(1)} %collective-permute-done.18, bf16[1024,4096]{1,0:T(8,128)(2,1)} %param.9, s32[]{:T(128)S(6)} %select_n.25), kind=kOutput, calls=%fused_computation.6 | convolution fusion | flops 268697600 | bytes 3407876 | tf_op jit(solution)/shard_map/dot_general | solution.py:10
  128.6 1.8 %convolution_add_fusion.3 = f32[256,1024]{1,0:T(8,128)S(1)} fusion(f32[256,1024]{1,0:T(8,128)S(1)} %convolution_add_fusion.4, bf16[256,512]{0,1:T(8,128)(2,1)} %collective-permute-done.19, bf16[1024,4096]{1,0:T(8,128)(2,1)} %param.9, s32[]{:T(128)S(6)} %select_n.26), kind=kOutput, calls=%fused_computation.5 | convolution fusion | flops 268697600 | bytes 3407876 | tf_op jit(solution)/shard_map/dot_general | solution.py:10
  130.4 1.8 %fusion.25 = f32[256,1024]{1,0:T(8,128)S(1)} fusion(bf16[256,512]{0,1:T(8,128)(2,1)} %collective-permute-done.22, bf16[1024,4096]{1,0:T(8,128)(2,1)} %param.9, s32[]{:T(128)S(6)} %select_n.30), kind=kOutput, calls=%fused_computation.49 | convolution fusion | flops 268435456 | bytes 2359300 | tf_op jit(solution)/shard_map/dot_general | solution.py:10
  132.2 1.7 %fusion.1 = f32[256,1024]{1,0:T(8,128)S(1)} fusion(f32[256,1024]{1,0:T(8,128)S(1)} %fusion.30, f32[256,1024]{1,0:T(8,128)S(1)} %convolution_add_fusion.3, bf16[256,512]{0,1:T(8,128)(2,1)S(1)} %collective-permute-done.20, bf16[1024,4096]{1,0:T(8,128)(2,1)} %param.9, s32[]{:T(128)S(6)} %select_n.27), kind=kOutput, calls=%fused_computation.4 | convolution fusion | flops 268959744 | bytes 4456452 | tf_op jit(solution)/shard_map/dot_general | solution.py:10
  133.9 1.8 %fusion = f32[256,1024]{1,0:T(8,128)S(1)} fusion(f32[256,1024]{1,0:T(8,128)S(1)} %fusion.25, f32[256,1024]{1,0:T(8,128)S(1)} %fusion.1, bf16[256,512]{0,1:T(8,128)(2,1)} %collective-permute-done.21, bf16[1024,4096]{1,0:T(8,128)(2,1)} %param.9, s32[]{:T(128)S(6)} %select_n.29), kind=kOutput, calls=%fused_computation.2 | convolution fusion | flops 268959744 | bytes 4456452 | tf_op jit(solution)/shard_map/dot_general | solution.py:10
  135.8 2.5 %fusion.3 = bf16[256,1024]{1,0:T(8,128)(2,1)} fusion(f32[256,1024]{1,0:T(8,128)S(1)} %fusion, bf16[256,512]{0,1:T(8,128)(2,1)S(1)} %collective-permute-done.23, bf16[1024,4096]{1,0:T(8,128)(2,1)} %param.9, s32[]{:T(128)S(6)} %select_n.31), kind=kOutput, calls=%fused_computation.12 | convolution fusion | flops 268959744 | bytes 2883588 | tf_op jit(solution)/shard_map/dot_general | solution.py:10
  (72 shorter events, 18.7 us)
Async XLA Ops:
  0.6 15.4 %copy-start = (bf16[1,1024,512]{2,1,0:T(8,128)(2,1)S(1)}, bf16[1,1024,512]{2,1,0:T(8,128)(2,1)}, u32[]{:S(2)}) copy-start(bf16[1,1024,512]{2,1,0:T(8,128)(2,1)} %param.14) | copy-start | bytes 3145732
  0.6 20.9 %copy-start.1 = (bf16[256,1024]{1,0:T(8,128)(2,1)S(1)}, bf16[256,1024]{1,0:T(8,128)(2,1)}, u32[]{:S(2)}) copy-start(bf16[256,1024]{1,0:T(8,128)(2,1)} %param.8) | copy-start | bytes 1572868
  3.3 24.2 %collective-permute-start.1 = (bf16[256,512]{0,1:T(8,128)(2,1)}, bf16[256,512]{0,1:T(8,128)(2,1)}, u32[]{:S(2)}, u32[]{:S(2)}) collective-permute-start(bf16[256,512]{0,1:T(8,128)(2,1)} %fusion.9), channel_id=1, source_target_pairs={{0,1},{1,0},{2,3},{3,2},{4,5},{5,4},{6,7},{7,6},{8,9},{9,8},{10,11... | collective-permute-start | bytes 786440 | tf_op jit(solution)/shard_map/ppermute | solution.py:27
  8.9 27.8 %collective-permute-start = (bf16[256,512]{0,1:T(8,128)(2,1)}, bf16[256,512]{0,1:T(8,128)(2,1)}, u32[]{:S(2)}, u32[]{:S(2)}) collective-permute-start(bf16[256,512]{0,1:T(8,128)(2,1)} %fusion.8), channel_id=1, source_target_pairs={{0,1},{1,0},{2,3},{3,2},{4,5},{5,4},{6,7},{7,6},{8,9},{9,8},{10,11... | collective-permute-start | bytes 786440 | tf_op jit(solution)/shard_map/ppermute | solution.py:27
  11.4 21.9 %collective-permute-start.4 = (bf16[256,512]{0,1:T(8,128)(2,1)}, bf16[256,512]{0,1:T(8,128)(2,1)}, u32[]{:S(2)}, u32[]{:S(2)}) collective-permute-start(bf16[256,512]{0,1:T(8,128)(2,1)} %fusion.11), channel_id=1, source_target_pairs={{0,2},{1,3},{2,0},{3,1},{4,6},{5,7},{6,4},{7,5},{8,10},{9,11},{10,... | collective-permute-start | bytes 786440 | tf_op jit(solution)/shard_map/ppermute | solution.py:27
  16.0 25.4 %collective-permute-start.3 = (bf16[256,512]{0,1:T(8,128)(2,1)}, bf16[256,512]{0,1:T(8,128)(2,1)}, u32[]{:S(2)}, u32[]{:S(2)}) collective-permute-start(bf16[256,512]{0,1:T(8,128)(2,1)} %fusion.10), channel_id=1, source_target_pairs={{0,2},{1,3},{2,0},{3,1},{4,6},{5,7},{6,4},{7,5},{8,10},{9,11},{10,... | collective-permute-start | bytes 786440 | tf_op jit(solution)/shard_map/ppermute | solution.py:27
  18.6 37.2 %collective-permute-start.12 = (bf16[64,1024]{0,1:T(8,128)(2,1)}, bf16[64,1024]{0,1:T(8,128)(2,1)}, u32[]{:S(2)}, u32[]{:S(2)}) collective-permute-start(bf16[64,1024]{0,1:T(8,128)(2,1)} %get-tuple-element.27), channel_id=1, source_target_pairs={{0,3},{1,2},{2,1},{3,0},{4,7},{5,6},{6,5},{7,4},{8,11},{9,10},{10,... | collective-permute-start | bytes 393224 | tf_op jit(solution)/shard_map/ppermute | solution.py:27
  30.0 9.5 %collective-permute-start.2 = (bf16[256,512]{0,1:T(8,128)(2,1)}, bf16[256,512]{0,1:T(8,128)(2,1)}, u32[]{:S(2)}, u32[]{:S(2)}) collective-permute-start(bf16[256,512]{0,1:T(8,128)(2,1)} %add_convert_fusion.2), channel_id=1, source_target_pairs={{0,2},{1,3},{2,0},{3,1},{4,6},{5,7},{6,4},{7,5},{8,10},{9,11},{10,... | collective-permute-start | bytes 786440 | tf_op jit(solution)/shard_map/ppermute | solution.py:27
  33.3 18.7 %copy-start.4 = (bf16[1024,1024]{1,0:T(8,128)(2,1)S(1)}, bf16[1024,1024]{1,0:T(8,128)(2,1)}, u32[]{:S(2)}) copy-start(bf16[1024,1024]{1,0:T(8,128)(2,1)} %param.12) | copy-start | bytes 6291460
  33.3 23.9 %collective-permute-start.13 = (bf16[64,1024]{0,1:T(8,128)(2,1)}, bf16[64,1024]{0,1:T(8,128)(2,1)}, u32[]{:S(2)}, u32[]{:S(2)}) collective-permute-start(bf16[64,1024]{0,1:T(8,128)(2,1)} %get-tuple-element.29), channel_id=1, source_target_pairs={{0,2},{1,3},{2,0},{3,1},{4,6},{5,7},{6,4},{7,5},{8,10},{9,11},{10,... | collective-permute-start | bytes 393224 | tf_op jit(solution)/shard_map/ppermute | solution.py:27
  36.7 20.6 %collective-permute-start.14 = (bf16[64,1024]{0,1:T(8,128)(2,1)}, bf16[64,1024]{0,1:T(8,128)(2,1)}, u32[]{:S(2)}, u32[]{:S(2)}) collective-permute-start(bf16[64,1024]{0,1:T(8,128)(2,1)} %get-tuple-element.28), channel_id=1, source_target_pairs={{0,1},{1,0},{2,3},{3,2},{4,5},{5,4},{6,7},{7,6},{8,9},{9,8},{10,11... | collective-permute-start | bytes 393224 | tf_op jit(solution)/shard_map/ppermute | solution.py:27
  39.5 9.2 %collective-permute-start.5 = (bf16[256,512]{0,1:T(8,128)(2,1)S(1)}, bf16[256,512]{0,1:T(8,128)(2,1)S(1)}, u32[]{:S(2)}, u32[]{:S(2)}) collective-permute-start(bf16[256,512]{0,1:T(8,128)(2,1)S(1)} %add_convert_fusion.1), channel_id=1, source_target_pairs={{0,1},{1,0},{2,3},{3,2},{4,5},{5,4},{6,7},{7,6},{8,9},{9,8},{10,11... | collective-permute-start | bytes 786440 | tf_op jit(solution)/shard_map/ppermute | solution.py:27
  41.4 8.6 %copy-start.2 = (f32[256,512]{0,1:T(8,128)}, f32[256,512]{0,1:T(8,128)S(1)}, u32[]{:S(2)}) copy-start(f32[256,512]{0,1:T(8,128)S(1)} %get-tuple-element.19) | copy-start | bytes 1572868
  49.9 2.8 %copy-start.3 = (f32[256,512]{0,1:T(8,128)}, f32[256,512]{0,1:T(8,128)S(1)}, u32[]{:S(2)}) copy-start(f32[256,512]{0,1:T(8,128)S(1)} %get-tuple-element.17) | copy-start | bytes 1572868
  53.7 11.0 %collective-permute-start.6 = (bf16[64,1152]{0,1:T(8,128)(2,1)S(1)}, bf16[64,1152]{0,1:T(8,128)(2,1)S(1)}, u32[]{:S(2)}, u32[]{:S(2)}) collective-permute-start(bf16[64,1152]{0,1:T(8,128)(2,1)S(1)} %get-tuple-element.22), channel_id=1, source_target_pairs={{0,3},{1,2},{2,1},{3,0},{4,7},{5,6},{6,5},{7,4},{8,11},{9,10},{10,... | collective-permute-start | bytes 442376 | tf_op jit(solution)/shard_map/ppermute | solution.py:27
  54.2 15.1 %collective-permute-start.7 = (bf16[64,1152]{0,1:T(8,128)(2,1)S(1)}, bf16[64,1152]{0,1:T(8,128)(2,1)S(1)}, u32[]{:S(2)}, u32[]{:S(2)}) collective-permute-start(bf16[64,1152]{0,1:T(8,128)(2,1)S(1)} %get-tuple-element.24), channel_id=1, source_target_pairs={{0,2},{1,3},{2,0},{3,1},{4,6},{5,7},{6,4},{7,5},{8,10},{9,11},{10,... | collective-permute-start | bytes 442376 | tf_op jit(solution)/shard_map/ppermute | solution.py:27
  55.8 13.5 %collective-permute-start.8 = (bf16[64,1152]{0,1:T(8,128)(2,1)S(1)}, bf16[64,1152]{0,1:T(8,128)(2,1)S(1)}, u32[]{:S(2)}, u32[]{:S(2)}) collective-permute-start(bf16[64,1152]{0,1:T(8,128)(2,1)S(1)} %get-tuple-element.23), channel_id=1, source_target_pairs={{0,1},{1,0},{2,3},{3,2},{4,5},{5,4},{6,7},{7,6},{8,9},{9,8},{10,11... | collective-permute-start | bytes 442376 | tf_op jit(solution)/shard_map/ppermute | solution.py:27
  58.6 16.2 %collective-permute-start.15 = (bf16[64,1024]{0,1:T(8,128)(2,1)S(1)}, bf16[64,1024]{0,1:T(8,128)(2,1)S(1)}, u32[]{:S(2)}, u32[]{:S(2)}) collective-permute-start(bf16[64,1024]{0,1:T(8,128)(2,1)S(1)} %add_convert_fusion), channel_id=1, source_target_pairs={{0,3},{1,2},{2,1},{3,0},{4,7},{5,6},{6,5},{7,4},{8,11},{9,10},{10,... | collective-permute-start | bytes 393224 | tf_op jit(solution)/shard_map/ppermute | solution.py:27
  69.5 46.3 %copy-start.6 = (f32[1,1024]{1,0:T(1,128)S(1)}, f32[1,1024]{1,0:T(1,128)}, u32[]{:S(2)}) copy-start(f32[1,1024]{1,0:T(1,128)} %param.13) | copy-start | bytes 12292
  70.0 27.3 %collective-permute-start.9 = (bf16[64,1152]{0,1:T(8,128)(2,1)S(1)}, bf16[64,1152]{0,1:T(8,128)(2,1)S(1)}, u32[]{:S(2)}, u32[]{:S(2)}) collective-permute-start(bf16[64,1152]{0,1:T(8,128)(2,1)S(1)} %concatenate.10), channel_id=1, source_target_pairs={{0,3},{1,2},{2,1},{3,0},{4,7},{5,6},{6,5},{7,4},{8,11},{9,10},{10,... | collective-permute-start | bytes 442376 | tf_op jit(solution)/shard_map/ppermute | solution.py:27
  71.2 29.1 %collective-permute-start.10 = (bf16[64,1152]{0,1:T(8,128)(2,1)S(1)}, bf16[64,1152]{0,1:T(8,128)(2,1)S(1)}, u32[]{:S(2)}, u32[]{:S(2)}) collective-permute-start(bf16[64,1152]{0,1:T(8,128)(2,1)S(1)} %concatenate.10), channel_id=1, source_target_pairs={{0,2},{1,3},{2,0},{3,1},{4,6},{5,7},{6,4},{7,5},{8,10},{9,11},{10,... | collective-permute-start | bytes 442376 | tf_op jit(solution)/shard_map/ppermute | solution.py:27
  72.5 29.5 %collective-permute-start.11 = (bf16[64,1152]{0,1:T(8,128)(2,1)S(1)}, bf16[64,1152]{0,1:T(8,128)(2,1)S(1)}, u32[]{:S(2)}, u32[]{:S(2)}) collective-permute-start(bf16[64,1152]{0,1:T(8,128)(2,1)S(1)} %concatenate.10), channel_id=1, source_target_pairs={{0,1},{1,0},{2,3},{3,2},{4,5},{5,4},{6,7},{7,6},{8,9},{9,8},{10,11... | collective-permute-start | bytes 442376 | tf_op jit(solution)/shard_map/ppermute | solution.py:27
  73.5 17.4 %collective-permute-start.16 = (bf16[64,1024]{0,1:T(8,128)(2,1)S(1)}, bf16[64,1024]{0,1:T(8,128)(2,1)S(1)}, u32[]{:S(2)}, u32[]{:S(2)}) collective-permute-start(bf16[64,1024]{0,1:T(8,128)(2,1)S(1)} %add_convert_fusion), channel_id=1, source_target_pairs={{0,2},{1,3},{2,0},{3,1},{4,6},{5,7},{6,4},{7,5},{8,10},{9,11},{10,... | collective-permute-start | bytes 393224 | tf_op jit(solution)/shard_map/ppermute | solution.py:27
  74.8 0.7 copy-start.5
  75.5 16.4 %collective-permute-start.17 = (bf16[64,1024]{0,1:T(8,128)(2,1)S(1)}, bf16[64,1024]{0,1:T(8,128)(2,1)}, u32[]{:S(2)}, u32[]{:S(2)}) collective-permute-start(bf16[64,1024]{0,1:T(8,128)(2,1)S(1)} %add_convert_fusion), channel_id=1, source_target_pairs={{0,1},{1,0},{2,3},{3,2},{4,5},{5,4},{6,7},{7,6},{8,9},{9,8},{10,11... | collective-permute-start | bytes 393224 | tf_op jit(solution)/shard_map/ppermute | solution.py:27
  109.8 10.2 %collective-permute-start.18 = (bf16[256,512]{0,1:T(8,128)(2,1)S(1)}, bf16[256,512]{0,1:T(8,128)(2,1)S(1)}, u32[]{:S(2)}, u32[]{:S(2)}) collective-permute-start(bf16[256,512]{0,1:T(8,128)(2,1)S(1)} %fusion.7), channel_id=1, source_target_pairs={{0,1},{1,0},{2,3},{3,2},{4,5},{5,4},{6,7},{7,6},{8,9},{9,8},{10,11... | collective-permute-start | bytes 786440 | tf_op jit(solution)/shard_map/ppermute | solution.py:27
  110.7 17.8 %collective-permute-start.19 = (bf16[256,512]{0,1:T(8,128)(2,1)S(1)}, bf16[256,512]{0,1:T(8,128)(2,1)}, u32[]{:S(2)}, u32[]{:S(2)}) collective-permute-start(bf16[256,512]{0,1:T(8,128)(2,1)S(1)} %fusion.7), channel_id=1, source_target_pairs={{0,2},{1,3},{2,0},{3,1},{4,6},{5,7},{6,4},{7,5},{8,10},{9,11},{10,... | collective-permute-start | bytes 786440 | tf_op jit(solution)/shard_map/ppermute | solution.py:27
  113.2 17.2 %collective-permute-start.22 = (bf16[256,512]{0,1:T(8,128)(2,1)S(1)}, bf16[256,512]{0,1:T(8,128)(2,1)}, u32[]{:S(2)}, u32[]{:S(2)}) collective-permute-start(bf16[256,512]{0,1:T(8,128)(2,1)S(1)} %fusion.6), channel_id=1, source_target_pairs={{0,1},{1,0},{2,3},{3,2},{4,5},{5,4},{6,7},{7,6},{8,9},{9,8},{10,11... | collective-permute-start | bytes 786440 | tf_op jit(solution)/shard_map/ppermute | solution.py:27
  114.8 10.9 %collective-permute-start.21 = (bf16[256,512]{0,1:T(8,128)(2,1)S(1)}, bf16[256,512]{0,1:T(8,128)(2,1)}, u32[]{:S(2)}, u32[]{:S(2)}) collective-permute-start(bf16[256,512]{0,1:T(8,128)(2,1)S(1)} %fusion.6), channel_id=1, source_target_pairs={{0,2},{1,3},{2,0},{3,1},{4,6},{5,7},{6,4},{7,5},{8,10},{9,11},{10,... | collective-permute-start | bytes 786440 | tf_op jit(solution)/shard_map/ppermute | solution.py:27
  120.0 12.1 %collective-permute-start.20 = (bf16[256,512]{0,1:T(8,128)(2,1)S(1)}, bf16[256,512]{0,1:T(8,128)(2,1)S(1)}, u32[]{:S(2)}, u32[]{:S(2)}) collective-permute-start(bf16[256,512]{0,1:T(8,128)(2,1)S(1)} %collective-permute-done.18), channel_id=1, source_target_pairs={{0,2},{1,3},{2,0},{3,1},{4,6},{5,7},{6,4},{7,5},{8,10},{9,11},{10,... | collective-permute-start | bytes 786440 | tf_op jit(solution)/shard_map/ppermute | solution.py:27
  125.7 10.1 %collective-permute-start.23 = (bf16[256,512]{0,1:T(8,128)(2,1)}, bf16[256,512]{0,1:T(8,128)(2,1)S(1)}, u32[]{:S(2)}, u32[]{:S(2)}) collective-permute-start(bf16[256,512]{0,1:T(8,128)(2,1)} %collective-permute-done.21), channel_id=1, source_target_pairs={{0,1},{1,0},{2,3},{3,2},{4,5},{5,4},{6,7},{7,6},{8,9},{9,8},{10,11... | collective-permute-start | bytes 786440 | tf_op jit(solution)/shard_map/ppermute | solution.py:27

commit v2 on v0

v2 whole, which is shorter than its diff:
```python
import functools

import jax
import jax.numpy as jnp
from jax import lax
from jax.experimental import pallas as pl
from jax.experimental.pallas import tpu as pltpu
from jax.sharding import PartitionSpec as P

EPS = 1e-05
LANES = 128
bf16, f32 = jnp.bfloat16, jnp.float32
VMEM = pl.BlockSpec(memory_space=pltpu.VMEM)
ANY = pl.BlockSpec(memory_space=pl.ANY)


def contract_last(left, right):
    return lax.dot_general(
        left, right, (((1,), (1,)), ((), ())), preferred_element_type=f32
    )


def call(body, outs, ins, in_specs, scratch=(), flops=0, name=None):
    moved = sum(a.size * a.dtype.itemsize for a in ins) // 4
    return pl.pallas_call(
        body,
        out_shape=[jax.ShapeDtypeStruct(s, d) for s, d in outs],
        in_specs=in_specs,
        out_specs=[VMEM] * len(outs),
        scratch_shapes=list(scratch),
        compiler_params=pltpu.CompilerParams(vmem_limit_bytes=16 * 2**20),
        cost_estimate=pl.CostEstimate(flops=flops, bytes_accessed=moved, transcendentals=0),
        name=name,
    )(*ins)


def high_low(total):
    high = total.astype(bf16)
    low = (total - high.astype(f32)).astype(bf16)
    lane = lax.broadcasted_iota(jnp.int32, (total.shape[0], LANES), 1)
    return jnp.where(lane < LANES // 2, high.astype(f32), low.astype(f32)).astype(bf16)


def from_high_low(block):
    return block[:, :1] + block[:, LANES // 2 : LANES // 2 + 1]


def upstream_kernel(n, share, cot, w_depth, gain_depth, *refs):
    outs, whole = refs[:n], refs[n]
    me = lax.axis_index("mp")
    whole[...] = gain_depth[...] * contract_last(cot[...], w_depth[...])
    for mask, out in enumerate(outs):
        rows = pl.ds(pl.multiple_of((me ^ mask) * share, share), share)
        out[...] = whole[rows, :].astype(out.dtype)


def project_kernel(items, half, context, w_out, *refs):
    count = sum(k for _, _, k in items)
    adds, outs = refs[:count], refs[count : count + len(items)]
    buf, sems = refs[count + len(items) :]
    me = lax.axis_index("mp")
    copies = []
    for i, (mask, side, _) in enumerate(items):
        start = pl.multiple_of(((me ^ mask) * 2 + side) * half, half)
        copies.append(
            pltpu.make_async_copy(w_out.at[:, pl.ds(start, half)], buf.at[i], sems.at[i])
        )
        copies[-1].start()
    at = 0
    for i, (_, _, k) in enumerate(items):
        copies[i].wait()
        total = jnp.dot(context[...], buf[i], preferred_element_type=f32)
        for add in adds[at : at + k]:
            total = total + add[...].astype(f32)
        at += k
        outs[i][...] = total.astype(outs[i].dtype)


def state_kernel(n, share, adds_per_side, gain, w_in, *refs):
    count = 2 * adds_per_side
    adds, (state, *outs), raw = refs[:count], refs[count : count + 1 + n], refs[count + 1 + n]
    me = lax.axis_index("mp")
    frames, width = state.shape
    half = width // 2
    depth = w_in.shape[1]
    for side in range(2):
        mine = adds[side * adds_per_side : (side + 1) * adds_per_side]
        total = mine[0][...]
        for add in mine[1:]:
            total = total + add[...].astype(f32)
        state[:, side * half : (side + 1) * half] = total
    value = state[...]
    gains = gain[:, pl.ds(pl.multiple_of(me * width, width), width)]
    raw[:, :depth] = jnp.dot((value * gains).astype(bf16), w_in[...], preferred_element_type=f32)
    raw[:, depth:] = jnp.broadcast_to(
        jnp.sum(value * value, axis=1, keepdims=True), (frames, LANES)
    )
    for mask, out in enumerate(outs):
        rows = pl.ds(pl.multiple_of((me ^ mask) * share, share), share)
        if mask == 0:
            out[...] = raw[rows, :]
        else:
            out[:, :depth] = raw[rows, :depth].astype(bf16)
            out[:, depth:] = high_low(raw[rows, depth:][:, :1])


def sum_kernel(n, own, *refs):
    out = refs[-1]
    total = own[...]
    for ref in refs[:-1]:
        total = total + ref[...].astype(f32)
    out[...] = total.astype(bf16)


def sum_state_kernel(n, depth, own, *refs):
    out = refs[-1]
    total = own[:, :depth]
    squares = own[:, depth : depth + 1]
    for ref in refs[:-1]:
        total = total + ref[:, :depth].astype(f32)
        squares = squares + from_high_low(ref[:, depth:].astype(f32))
    out[:, :depth] = total.astype(bf16)
    out[:, depth:] = high_low(squares)


def back_kernel(n, share, features, gain, gain_depth, w_in, state, *refs):
    raws, ups = refs[:n], refs[n : 2 * n]
    latent, grad, *halves = refs[2 * n : 2 * n + 4]
    du, recips, backs = refs[2 * n + 4 :]
    me = lax.axis_index("mp")
    width = state.shape[1]
    depth = w_in.shape[1]
    half = width // 2
    for mask in range(n):
        rows = pl.ds(pl.multiple_of((me ^ mask) * share, share), share)
        raw = raws[mask][:, :depth].astype(f32)
        squares = from_high_low(raws[mask][:, depth:].astype(f32))
        up = ups[mask][...].astype(f32)
        recip = lax.rsqrt(squares / features + EPS)
        depth_in = raw * recip
        urecip = lax.rsqrt(jnp.mean(depth_in * depth_in, axis=1, keepdims=True) + EPS)
        inner = jnp.mean(depth_in * up, axis=1, keepdims=True)
        part = (urecip * up - depth_in * (urecip * urecip * urecip * inner)).astype(bf16)
        du[rows, :] = part
        dot_du = jnp.sum(part.astype(f32) * depth_in, axis=1, keepdims=True) / recip
        recips[rows, :] = jnp.broadcast_to(recip, (share, LANES))
        backs[rows, :] = jnp.broadcast_to(
            recip * recip * recip * (dot_du / features), (share, LANES)
        )
        latent[rows, :] = (depth_in * urecip * gain_depth[...]).astype(bf16)
    gains = gain[:, pl.ds(pl.multiple_of(me * width, width), width)]
    for side in range(2):
        cols = slice(side * half, (side + 1) * half)
        dnormed = contract_last(du[...], w_in[cols, :])
        value = (
            recips[:, :1] * (gains[:, cols] * dnormed) - state[:, cols] * backs[:, :1]
        ).astype(bf16)
        halves[side][...] = value
        grad[:, cols] = value


def act_kernel(latent, w_depth, out):
    out[...] = jnp.dot(latent[...], w_depth[...], preferred_element_type=f32).astype(bf16)


def context_kernel(items, half, first, w_out, *refs):
    blocks = refs[: len(items)]
    before = None if first else refs[len(items)]
    out, buf, sems = refs[-3:]
    me = lax.axis_index("mp")
    copies = []
    for i, (mask, side) in enumerate(items):
        start = pl.multiple_of(((me ^ mask) * 2 + side) * half, half)
        copies.append(
            pltpu.make_async_copy(w_out.at[:, pl.ds(start, half)], buf.at[i], sems.at[i])
        )
        copies[-1].start()
    total = None if first else before[...]
    for i in range(len(items)):
        copies[i].wait()
        part = contract_last(blocks[i][...], buf[i])
        total = part if total is None else total + part
    out[...] = total.astype(out.dtype)


def local(n, context, w_out, residual, gain_temporal, w_in, gain_depth, w_depth, cotangent):
    frames, width = residual.shape
    half = width // 2
    share = frames // n
    features = width * n
    heads = w_out.shape[0]
    depth, act = w_depth.shape[1:]
    log = n.bit_length() - 1
    bits = [1 << i for i in range(log)]
    orders = (bits, bits[::-1])
    gain = gain_temporal[None, :]

    def mirror(mask):
        return sum(1 << (log - 1 - i) for i in range(log) if mask >> i & 1)

    pairs = sorted(range(n), key=lambda k: (-k.bit_count(), k))
    pairs = [((k, 0), (mirror(k), 1)) for k in pairs]

    def swap(value, mask):
        return lax.ppermute(value, "mp", [(i, i ^ mask) for i in range(n)])

    def exchange(values):
        return [swap(values[mask], mask) for mask in range(n - 1, 0, -1)]

    def gather(own):
        got = {mask: swap(own, mask) for mask in range(n - 1, 0, -1)}
        return [own] + [got[mask] for mask in range(1, n)]

    ups = call(
        functools.partial(upstream_kernel, n, share),
        [((share, depth), f32 if mask == 0 else bf16) for mask in range(n)],
        [cotangent[0], w_depth[0], gain_depth],
        [VMEM] * 3,
        [pltpu.VMEM((frames, depth), f32)],
        flops=2 * frames * depth * act,
        name="upstream",
    )

    def project(items, addends, dtype):
        listed = [a for adds in addends for a in adds]
        return call(
            functools.partial(
                project_kernel, [(m, s, len(a)) for (m, s), a in zip(items, addends)], half
            ),
            [((frames, half), dtype)] * len(items),
            [context, w_out] + listed,
            [VMEM, ANY] + [VMEM] * len(listed),
            [
                pltpu.VMEM((len(items), heads, half), bf16),
                pltpu.SemaphoreType.DMA((len(items),)),
            ],
            flops=2 * frames * heads * half * len(items),
            name="project",
        )

    arrived = {}
    for pair in pairs[:-1]:
        addends = []
        for mask, side in pair:
            order = orders[side]
            phase = min(i for i, bit in enumerate(order) if mask & bit)
            addends.append([arrived[mask ^ order[i], side] for i in range(phase)])
        sent = project(pair, addends, bf16)
        for (mask, side), value in zip(pair, sent):
            bit = next(bit for bit in orders[side] if mask & bit)
            arrived[mask, side] = swap(value, bit)
    kept = project(
        pairs[-1], [[residual[:, s * half : (s + 1) * half]] for s in range(2)], f32
    )

    up_own = call(
        functools.partial(sum_kernel, n),
        [((share, depth), bf16)],
        [ups[0]] + exchange(ups),
        [VMEM] * n,
        name="sum_upstream",
    )[0]
    up_parts = gather(up_own)

    adds = [[kept[side]] + [arrived[bit, side] for bit in orders[side]] for side in range(2)]
    state, *raws = call(
        functools.partial(state_kernel, n, share, 1 + log),
        [((frames, width), f32)]
        + [((share, depth + LANES), f32 if mask == 0 else bf16) for mask in range(n)],
        [gain, w_in] + adds[0] + adds[1],
        [VMEM] * (4 + 2 * log),
        [pltpu.VMEM((frames, depth + LANES), f32)],
        flops=2 * frames * width * depth,
        name="state",
    )
    raw_own = call(
        functools.partial(sum_state_kernel, n, depth),
        [((share, depth + LANES), bf16)],
        [raws[0]] + exchange(raws),
        [VMEM] * n,
        name="sum_state",
    )[0]
    raw_parts = gather(raw_own)

    latent, grad_residual, *grads = call(
        functools.partial(back_kernel, n, share, features),
        [((frames, depth), bf16), ((frames, width), bf16)] + [((frames, half), bf16)] * 2,
        [gain, gain_depth, w_in, state] + raw_parts + up_parts,
        [VMEM] * (4 + 2 * n),
        [
            pltpu.VMEM((frames, depth), bf16),
            pltpu.VMEM((frames, LANES), f32),
            pltpu.VMEM((frames, LANES), f32),
        ],
        flops=2 * frames * width * depth,
        name="back",
    )

    blocks = {}
    for side, order in enumerate(orders):
        blocks[0, side] = grads[side]
        have = [0]
        for bit in order:
            for mask in list(have):
                blocks[mask ^ bit, side] = swap(blocks[mask, side], bit)
                have.append(mask ^ bit)

    depth_act = call(
        act_kernel,
        [((frames, act), bf16)],
        [latent, w_depth[0]],
        [VMEM] * 2,
        flops=2 * frames * depth * act,
        name="act",
    )[0]

    total = None
    for i, pair in enumerate(pairs[::-1]):
        ins = [w_out] + [blocks[key] for key in pair] + ([] if total is None else [total])
        total = call(
            functools.partial(context_kernel, pair, half, total is None),
            [((frames, heads), bf16 if i == n - 1 else f32)],
            ins,
            [ANY] + [VMEM] * (len(ins) - 1),
            [
                pltpu.VMEM((len(pair), heads, half), bf16),
                pltpu.SemaphoreType.DMA((len(pair),)),
            ],
            flops=2 * frames * heads * half * len(pair),
            name="grad_context",
        )[0]
    return (depth_act[None], grad_residual, total)


def solution(mesh):
    in_specs = (
        P("dp", "mp"),
        P("mp", None),
        P("dp", "mp"),
        P(),
        P("mp", None),
        P("mp", None),
        P("mp", None, None),
        P("mp", "dp", None),
    )
    out_specs = (P("mp", "dp", None), P("dp", "mp"), P("dp", "mp"))
    n = mesh.shape["mp"]

    def run(*args):
        return local(n, *args)

    return jax.shard_map(run, mesh=mesh, in_specs=in_specs, out_specs=out_specs, check_vma=False)
```

time: 246 us -> 74.6 us (0.30)
  waiting for transfers between devices: 139 us -> 27 us
  blocking collectives: 60.1 us -> 0 us
  starting transfers between devices: 0.12 us -> 26.2 us
  matrix products: 25.9 us -> 0 us
  Pallas kernels: 0 us -> 15.8 us
  between operations: 13.8 us -> 0.81 us
  other arithmetic: 5.44 us -> 0.01 us
  local copies, waits for them, and re-layouts: 0.72 us -> 4.49 us
    psum x3 -> x0, blocking collectives: 60.1 us -> none  [the longest x1 41.7 us: local(): du_total = lax.psum(dinput, 'mp').astype(jnp.bfloat16)]
    reduce_scatter x1 -> x0, waiting for transfers between devices: 54.8 us -> none  [local(): lax.psum_scatter(full_term, 'mp', scatter_dimension=1, tiled=True)]
    psum x1 -> x0, waiting for transfers between devices: 52.6 us -> none  [local(): depth_in = lax.psum(partial_value, 'mp')]
    all_gather x1 -> x0, waiting for transfers between devices: 32.1 us -> none  [local(): lax.all_gather(grad_residual, 'mp', axis=1, tiled=True)]
    ppermute x0 -> x24, waiting for transfers between devices: none -> 27 us  [swap(): return lax.ppermute(value, 'mp', [(i, i ^ mask) for i in range(n)])]
    ppermute x0 -> x24, starting transfers between devices: none -> 26.2 us  [swap(): return lax.ppermute(value, 'mp', [(i, i ^ mask) for i in range(n)])]
    dot_general x6 -> x0, matrix products: 25.9 us -> none  [the longest x3 12.4 us: contract_last(): lax.dot_general(left, right, (((1,), (1,)), ((), ())), preferred_element_...]
    pallas_call x0 -> x14, Pallas kernels: none -> 15.8 us  [call(): pl.pallas_call(body, out_shape=[jax.ShapeDtypeStruct(s, d) for s, d in ou...]
  transfers between devices with their start and end apart: 3 -> 24, of which waited for: 3 -> 13; matrix products, arithmetic and copies ran while one was open for 1% -> 0% of each run, Pallas kernels for 0% -> 14%
where the time goes in v2:
time: 74.6 us; the launch traced here: 74.4 us
  waiting for transfers between devices  27 us (36%)
  starting transfers between devices  26.2 us (35%)
  Pallas kernels  15.8 us (21%)
  local copies, waits for them, and re-layouts  4.49 us (6%)
  between operations  0.81 us (1%)
    ppermute x24, waiting for transfers between devices, swap(): return lax.ppermute(value, 'mp', [(i, i ^ mask) for i in range(n)])  27 us
    ppermute x24, starting transfers between devices, swap(): return lax.ppermute(value, 'mp', [(i, i ^ mask) for i in range(n)])  26.2 us
    pallas_call x14, Pallas kernels, call(): pl.pallas_call(body, out_shape=[jax.ShapeDtypeStruct(s, d) for s, d in ou...  15.8 us
    unnamed x22, local copies, waits for them, and re-layouts  4.46 us
  transfers between devices with their start and end apart: 24, of which 13 were waited for; matrix products, arithmetic and copies ran while one was open for 0% of the time, Pallas kernels for 14%

profile of v2, /device:TPU:0, one launch (start us, length us, event | category | flops | bytes accessed | tf_op | source)
XLA Modules:
  0.0 74.4 jit_solution(12152359785859342526)
XLA Ops:
  0.6 3.4 %copy-done = bf16[1024,4096]{1,0:T(8,128)(2,1)S(1)} copy-done((bf16[1024,4096]{1,0:T(8,128)(2,1)S(1)}, bf16[1024,4096]{1,0:T(8,128)(2,1)}, u32[]{:S(2)}) %copy-start) | copy-done | bytes 8388632
  4.0 1.0 %copy-done.1 = bf16[256,1024]{1,0:T(8,128)(2,1)S(1)} copy-done((bf16[256,1024]{1,0:T(8,128)(2,1)S(1)}, bf16[256,1024]{1,0:T(8,128)(2,1)}, u32[]{:S(2)}) %copy-start.1) | copy-done | bytes 524312
  5.1 1.2 %project.6 = (bf16[256,512]{1,0:T(8,128)(2,1)S(1)}, bf16[256,512]{1,0:T(8,128)(2,1)S(1)}) custom-call(bf16[256,1024]{1,0:T(8,128)(2,1)S(1)} %copy-done.1, bf16[1024,4096]{1,0:T(8,128)(2,1)S(1)} %copy-done), custom_call_target="tpu_custom_call" | custom-call | flops 536870912 | bytes 2228224 | tf_op jit(solution)/shard_map/project/pallas_call | solution.py:25
  6.3 3.0 %collective-permute-start.1 = (bf16[256,512]{1,0:T(8,128)(2,1)S(1)}, bf16[256,512]{1,0:T(8,128)(2,1)S(1)}, u32[]{:S(2)}, u32[]{:S(2)}) collective-permute-start(bf16[256,512]{1,0:T(8,128)(2,1)S(1)} %get-tuple-element.26), channel_id=1, source_target_pairs={{0,1},{1,0},{2,3},{3,2},{4,5},{5,4},{6,7},{7,6},{8,9},{9,8},{10,11... | collective-permute-start | bytes 786440 | tf_op jit(solution)/shard_map/ppermute | solution.py:205
  9.3 1.5 %collective-permute-start.2 = (bf16[256,512]{1,0:T(8,128)(2,1)S(1)}, bf16[256,512]{1,0:T(8,128)(2,1)S(1)}, u32[]{:S(2)}, u32[]{:S(2)}) collective-permute-start(bf16[256,512]{1,0:T(8,128)(2,1)S(1)} %get-tuple-element.27), channel_id=1, source_target_pairs={{0,2},{1,3},{2,0},{3,1},{4,6},{5,7},{6,4},{7,5},{8,10},{9,11},{10,... | collective-permute-start | bytes 786440 | tf_op jit(solution)/shard_map/ppermute | solution.py:205
  10.9 1.2 %project.5 = (bf16[256,512]{1,0:T(8,128)(2,1)S(1)}, bf16[256,512]{1,0:T(8,128)(2,1)S(1)}) custom-call(bf16[256,1024]{1,0:T(8,128)(2,1)S(1)} %copy-done.1, bf16[1024,4096]{1,0:T(8,128)(2,1)S(1)} %copy-done), custom_call_target="tpu_custom_call" | custom-call | flops 536870912 | bytes 2228224 | tf_op jit(solution)/shard_map/project/pallas_call | solution.py:25
  12.1 0.6 collective-permute-start
  12.8 0.5 upstream.1
  13.3 3.0 %collective-permute-start.12 = (bf16[64,1024]{1,0:T(8,128)(2,1)S(1)}, bf16[64,1024]{1,0:T(8,128)(2,1)S(1)}, u32[]{:S(2)}, u32[]{:S(2)}) collective-permute-start(bf16[64,1024]{1,0:T(8,128)(2,1)S(1)} %get-tuple-element.38), channel_id=1, source_target_pairs={{0,3},{1,2},{2,1},{3,0},{4,7},{5,6},{6,5},{7,4},{8,11},{9,10},{10,... | collective-permute-start | bytes 393224 | tf_op jit(solution)/shard_map/ppermute | solution.py:205
  16.3 0.2 collective-permute-done.1.refs_0_
  16.5 2.1 %collective-permute-done.2.refs_1_ = bf16[256,512]{1,0:T(8,128)(2,1)S(1)} collective-permute-done((bf16[256,512]{1,0:T(8,128)(2,1)S(1)}, bf16[256,512]{1,0:T(8,128)(2,1)S(1)}, u32[]{:S(2)}, u32[]{:S(2)}) %collective-permute-start.2) | collective-permute-done | bytes 262176 | tf_op jit(solution)/shard_map/ppermute | solution.py:205
  18.6 1.2 %project.7 = (bf16[256,512]{1,0:T(8,128)(2,1)S(1)}, bf16[256,512]{1,0:T(8,128)(2,1)S(1)}) custom-call(bf16[256,1024]{1,0:T(8,128)(2,1)S(1)} %copy-done.2, bf16[1024,4096]{1,0:T(8,128)(2,1)S(1)} %bitcast.5, bf16[256,512]{1,0:T(8,128)(2,1)S(1)} %collective-permute-done.1.refs_0_, bf16[256,512]{1,0:T(8,128)(2,1)S(1)} %collective-permute-done.2.refs_1_), custom_call_target="tpu_custom_call" | custom-call | flops 536870912 | bytes 2359296 | tf_op jit(solution)/shard_map/project/pallas_call | solution.py:25
  19.8 1.6 %collective-permute-start.3 = (bf16[256,512]{1,0:T(8,128)(2,1)S(1)}, bf16[256,512]{1,0:T(8,128)(2,1)S(1)}, u32[]{:S(2)}, u32[]{:S(2)}) collective-permute-start(bf16[256,512]{1,0:T(8,128)(2,1)S(1)} %get-tuple-element.28), channel_id=1, source_target_pairs={{0,2},{1,3},{2,0},{3,1},{4,6},{5,7},{6,4},{7,5},{8,10},{9,11},{10,... | collective-permute-start | bytes 786440 | tf_op jit(solution)/shard_map/ppermute | solution.py:205
  21.4 0.5 collective-permute-start.5
  22.0 0.1 collective-permute-done.refs_1_
  22.1 2.1 %collective-permute-start.13 = (bf16[64,1024]{1,0:T(8,128)(2,1)S(1)}, bf16[64,1024]{1,0:T(8,128)(2,1)S(1)}, u32[]{:S(2)}, u32[]{:S(2)}) collective-permute-start(bf16[64,1024]{1,0:T(8,128)(2,1)S(1)} %get-tuple-element.39), channel_id=1, source_target_pairs={{0,2},{1,3},{2,0},{3,1},{4,6},{5,7},{6,4},{7,5},{8,10},{9,11},{10,... | collective-permute-start | bytes 393224 | tf_op jit(solution)/shard_map/ppermute | solution.py:205
  24.2 2.8 %collective-permute-done.4.refs_4_ = bf16[256,512]{1,0:T(8,128)(2,1)S(1)} collective-permute-done((bf16[256,512]{1,0:T(8,128)(2,1)S(1)}, bf16[256,512]{1,0:T(8,128)(2,1)S(1)}, u32[]{:S(2)}, u32[]{:S(2)}) %collective-permute-start.4) | collective-permute-done | bytes 262176 | tf_op jit(solution)/shard_map/ppermute | solution.py:205
  27.0 1.2 %project.4 = (f32[256,512]{1,0:T(8,128)S(1)}, f32[256,512]{1,0:T(8,128)S(1)}) custom-call(bf16[256,1024]{1,0:T(8,128)(2,1)S(1)} %copy-done.2, bf16[1024,4096]{1,0:T(8,128)(2,1)S(1)} %bitcast.5, bf16[256,512]{1,0:T(8,128)(2,1)S(1)} %get-tuple-element.46.refs_0_, bf16[256,512]{1,0:T(8,128)(2,1)S(1)} %get-tuple-element.45.refs_1_), custom_call_target="tpu_custom_call" | custom-call | flops 536870912 | bytes 2359296 | tf_op jit(solution)/shard_map/project/pallas_call | solution.py:25
  28.2 4.3 %collective-permute-done.3.refs_2_ = bf16[256,512]{1,0:T(8,128)(2,1)S(1)} collective-permute-done((bf16[256,512]{1,0:T(8,128)(2,1)S(1)}, bf16[256,512]{1,0:T(8,128)(2,1)S(1)}, u32[]{:S(2)}, u32[]{:S(2)}) %collective-permute-start.3) | collective-permute-done | bytes 262176 | tf_op jit(solution)/shard_map/ppermute | solution.py:205
  32.6 0.9 %state.1 = (f32[256,1024]{1,0:T(8,128)S(1)}, f32[64,1152]{1,0:T(8,128)S(1)}, bf16[64,1152]{1,0:T(8,128)(2,1)S(1)}, bf16[64,1152]{1,0:T(8,128)(2,1)S(1)}, bf16[64,1152]{1,0:T(8,128)(2,1)S(1)}) custom-call(f32[1,4096]{1,0:T(1,128)S(1)} %bitcast.9, bf16[1024,1024]{1,0:T(8,128)(2,1)S(1)} %copy-done.3, f32[256,512]{1,0:T(8,128)S(1)} %get-tuple-element.24.refs_0_, ...), custom_call_target="tpu_custom_call" | custom-call | flops 536870912 | bytes 1052672 | tf_op jit(solution)/shard_map/state/pallas_call | solution.py:25
  33.5 1.6 %collective-permute-start.6 = (bf16[64,1152]{1,0:T(8,128)(2,1)S(1)}, bf16[64,1152]{1,0:T(8,128)(2,1)S(1)}, u32[]{:S(2)}, u32[]{:S(2)}) collective-permute-start(bf16[64,1152]{1,0:T(8,128)(2,1)S(1)} %get-tuple-element.34), channel_id=1, source_target_pairs={{0,3},{1,2},{2,1},{3,0},{4,7},{5,6},{6,5},{7,4},{8,11},{9,10},{10,... | collective-permute-start | bytes 442376 | tf_op jit(solution)/shard_map/ppermute | solution.py:205
  35.0 0.1 collective-permute-start.7
  35.1 1.9 %collective-permute-start.8 = (bf16[64,1152]{1,0:T(8,128)(2,1)S(1)}, bf16[64,1152]{1,0:T(8,128)(2,1)S(1)}, u32[]{:S(2)}, u32[]{:S(2)}) collective-permute-start(bf16[64,1152]{1,0:T(8,128)(2,1)S(1)} %get-tuple-element.36), channel_id=1, source_target_pairs={{0,1},{1,0},{2,3},{3,2},{4,5},{5,4},{6,7},{7,6},{8,9},{9,8},{10,11... | collective-permute-start | bytes 442376 | tf_op jit(solution)/shard_map/ppermute | solution.py:205
  37.1 0.2 collective-permute-start.15
  37.3 3.2 %collective-permute-done.6.refs_0_ = bf16[64,1152]{1,0:T(8,128)(2,1)S(1)} collective-permute-done((bf16[64,1152]{1,0:T(8,128)(2,1)S(1)}, bf16[64,1152]{1,0:T(8,128)(2,1)S(1)}, u32[]{:S(2)}, u32[]{:S(2)}) %collective-permute-start.6) | collective-permute-done | bytes 147488 | tf_op jit(solution)/shard_map/ppermute | solution.py:205
  40.5 2.3 %collective-permute-done.7.refs_1_ = bf16[64,1152]{1,0:T(8,128)(2,1)S(1)} collective-permute-done((bf16[64,1152]{1,0:T(8,128)(2,1)S(1)}, bf16[64,1152]{1,0:T(8,128)(2,1)S(1)}, u32[]{:S(2)}, u32[]{:S(2)}) %collective-permute-start.7) | collective-permute-done | bytes 147488 | tf_op jit(solution)/shard_map/ppermute | solution.py:205
  42.8 0.2 sum_state.1.refs_0_
  43.1 1.6 %collective-permute-start.11 = (bf16[64,1152]{1,0:T(8,128)(2,1)S(1)}, bf16[64,1152]{1,0:T(8,128)(2,1)S(1)}, u32[]{:S(2)}, u32[]{:S(2)}) collective-permute-start(bf16[64,1152]{1,0:T(8,128)(2,1)S(1)} %sum_state.1.refs_0_), channel_id=1, source_target_pairs={{0,3},{1,2},{2,1},{3,0},{4,7},{5,6},{6,5},{7,4},{8,11},{9,10},{10,... | collective-permute-start | bytes 442376 | tf_op jit(solution)/shard_map/ppermute | solution.py:205
  44.6 1.9 %collective-permute-start.9 = (bf16[64,1152]{1,0:T(8,128)(2,1)S(1)}, bf16[64,1152]{1,0:T(8,128)(2,1)S(1)}, u32[]{:S(2)}, u32[]{:S(2)}) collective-permute-start(bf16[64,1152]{1,0:T(8,128)(2,1)S(1)} %sum_state.1.refs_0_), channel_id=1, source_target_pairs={{0,1},{1,0},{2,3},{3,2},{4,5},{5,4},{6,7},{7,6},{8,9},{9,8},{10,11... | collective-permute-start | bytes 442376 | tf_op jit(solution)/shard_map/ppermute | solution.py:205
  46.6 1.5 %collective-permute-start.17 = (bf16[64,1024]{1,0:T(8,128)(2,1)S(1)}, bf16[64,1024]{1,0:T(8,128)(2,1)S(1)}, u32[]{:S(2)}, u32[]{:S(2)}) collective-permute-start(bf16[64,1024]{1,0:T(8,128)(2,1)S(1)} %sum_upstream.1.refs_4_), channel_id=1, source_target_pairs={{0,3},{1,2},{2,1},{3,0},{4,7},{5,6},{6,5},{7,4},{8,11},{9,10},{10,... | collective-permute-start | bytes 393224 | tf_op jit(solution)/shard_map/ppermute | solution.py:205
  48.1 5.8 %collective-permute-done.16.refs_6_ = bf16[64,1024]{1,0:T(8,128)(2,1)S(1)} collective-permute-done((bf16[64,1024]{1,0:T(8,128)(2,1)S(1)}, bf16[64,1024]{1,0:T(8,128)(2,1)S(1)}, u32[]{:S(2)}, u32[]{:S(2)}) %collective-permute-start.16) | collective-permute-done | bytes 131104 | tf_op jit(solution)/shard_map/ppermute | solution.py:205
  54.0 2.3 %back.1 = (bf16[256,1024]{1,0:T(8,128)(2,1)S(1)}, bf16[256,1024]{1,0:T(8,128)(2,1)}, bf16[256,512]{1,0:T(8,128)(2,1)S(1)}, bf16[256,512]{1,0:T(8,128)(2,1)S(1)}) custom-call(f32[1,4096]{1,0:T(1,128)S(1)} %bitcast.10, f32[1,1024]{1,0:T(1,128)S(1)} %copy-done.7, bf16[1024,1024]{1,0:T(8,128)(2,1)S(1)} %copy-done.3, f32[256,1024]{1,0:T(8,128)S(1)} %get-tuple-element.32.state, ...), custom_call_target="tpu_custom_call" | custom-call | flops 536870912 | bytes 1070080 | tf_op jit(solution)/shard_map/back/pallas_call | solution.py:25
  56.3 0.4 collective-permute-start.18
  56.7 1.1 %collective-permute-start.20 = (bf16[256,512]{1,0:T(8,128)(2,1)S(1)}, bf16[256,512]{1,0:T(8,128)(2,1)S(1)}, u32[]{:S(2)}, u32[]{:S(2)}) collective-permute-start(bf16[256,512]{1,0:T(8,128)(2,1)S(1)} %get-tuple-element.44.refs_1_), channel_id=1, source_target_pairs={{0,2},{1,3},{2,0},{3,1},{4,6},{5,7},{6,4},{7,5},{8,10},{9,11},{10,... | collective-permute-start | bytes 786440 | tf_op jit(solution)/shard_map/ppermute | solution.py:205
  57.8 0.9 %collective-permute-start.22 = (bf16[256,512]{1,0:T(8,128)(2,1)S(1)}, bf16[256,512]{1,0:T(8,128)(2,1)S(1)}, u32[]{:S(2)}, u32[]{:S(2)}) collective-permute-start(bf16[256,512]{1,0:T(8,128)(2,1)S(1)} %get-tuple-element.43.refs_0_), channel_id=1, source_target_pairs={{0,2},{1,3},{2,0},{3,1},{4,6},{5,7},{6,4},{7,5},{8,10},{9,11},{10,... | collective-permute-start | bytes 786440 | tf_op jit(solution)/shard_map/ppermute | solution.py:205
  58.7 1.6 %collective-permute-start.23 = (bf16[256,512]{1,0:T(8,128)(2,1)S(1)}, bf16[256,512]{1,0:T(8,128)(2,1)S(1)}, u32[]{:S(2)}, u32[]{:S(2)}) collective-permute-start(bf16[256,512]{1,0:T(8,128)(2,1)S(1)} %get-tuple-element.44.refs_1_), channel_id=1, source_target_pairs={{0,1},{1,0},{2,3},{3,2},{4,5},{5,4},{6,7},{7,6},{8,9},{9,8},{10,11... | collective-permute-start | bytes 786440 | tf_op jit(solution)/shard_map/ppermute | solution.py:205
  60.3 4.9 %collective-permute-done.18.refs_0_ = bf16[256,512]{1,0:T(8,128)(2,1)S(1)} collective-permute-done((bf16[256,512]{1,0:T(8,128)(2,1)S(1)}, bf16[256,512]{1,0:T(8,128)(2,1)S(1)}, u32[]{:S(2)}, u32[]{:S(2)}) %collective-permute-start.18) | collective-permute-done | bytes 262176 | tf_op jit(solution)/shard_map/ppermute | solution.py:205
  65.3 0.6 collective-permute-start.19
  65.8 0.1 collective-permute-done.20.refs_1_
  66.0 0.4 collective-permute-start.21
  66.3 1.2 %act.1 = bf16[256,512]{1,0:T(8,128)(2,1)} custom-call(bf16[256,1024]{1,0:T(8,128)(2,1)S(1)} %get-tuple-element.41.latent, bf16[1024,512]{1,0:T(8,128)(2,1)S(1)} %bitcast.7), custom_call_target="tpu_custom_call" | custom-call | flops 268435456 | bytes 393216 | tf_op jit(solution)/shard_map/act/pallas_call | solution.py:25
  67.5 1.2 %grad_context.4.refs_2_ = f32[256,1024]{1,0:T(8,128)S(1)} custom-call(bf16[1024,4096]{1,0:T(8,128)(2,1)S(1)} %bitcast.5, bf16[256,512]{1,0:T(8,128)(2,1)S(1)} %get-tuple-element.43.refs_0_, bf16[256,512]{1,0:T(8,128)(2,1)S(1)} %get-tuple-element.44.refs_1_), custom_call_target="tpu_custom_call" | custom-call | flops 536870912 | bytes 2228224 | tf_op jit(solution)/shard_map/grad_context/pallas_call | solution.py:25
  68.7 0.2 collective-permute-done.22.refs_0_
  68.9 1.2 %grad_context.5.refs_2_ = f32[256,1024]{1,0:T(8,128)S(1)} custom-call(bf16[1024,4096]{1,0:T(8,128)(2,1)S(1)} %bitcast.5, bf16[256,512]{1,0:T(8,128)(2,1)S(1)} %collective-permute-done.22.refs_0_, bf16[256,512]{1,0:T(8,128)(2,1)S(1)} %collective-permute-done.23.refs_1_, f32[256,1024]{1,0:T(8,128)S(1)} %grad_context.4.refs_2_), custom_call_target="tpu_custom_call" | custom-call | flops 536870912 | bytes 2490368 | tf_op jit(solution)/shard_map/grad_context/pallas_call | solution.py:25
  70.1 1.3 %grad_context.6.refs_2_ = f32[256,1024]{1,0:T(8,128)S(1)} custom-call(bf16[1024,4096]{1,0:T(8,128)(2,1)S(1)} %bitcast.5, bf16[256,512]{1,0:T(8,128)(2,1)S(1)} %collective-permute-done.18.refs_0_, bf16[256,512]{1,0:T(8,128)(2,1)S(1)} %collective-permute-done.20.refs_1_, f32[256,1024]{1,0:T(8,128)S(1)} %grad_context.5.refs_2_), custom_call_target="tpu_custom_call" | custom-call | flops 536870912 | bytes 2490368 | tf_op jit(solution)/shard_map/grad_context/pallas_call | solution.py:25
  71.4 0.3 collective-permute-done.19.refs_0_
  71.7 0.7 collective-permute-done.21.refs_1_
  72.3 2.0 %grad_context.7 = bf16[256,1024]{1,0:T(8,128)(2,1)} custom-call(bf16[1024,4096]{1,0:T(8,128)(2,1)S(1)} %bitcast.5, bf16[256,512]{1,0:T(8,128)(2,1)S(1)} %collective-permute-done.19.refs_0_, bf16[256,512]{1,0:T(8,128)(2,1)S(1)} %collective-permute-done.21.refs_1_, f32[256,1024]{1,0:T(8,128)S(1)} %grad_context.6.refs_2_), custom_call_target="tpu_custom_call" | custom-call | flops 536870912 | bytes 2490368 | tf_op jit(solution)/shard_map/grad_context/pallas_call | solution.py:25
  (38 shorter events, 0.4 us)
Async XLA Ops:
  0.6 3.4 %copy-start = (bf16[1024,4096]{1,0:T(8,128)(2,1)S(1)}, bf16[1024,4096]{1,0:T(8,128)(2,1)}, u32[]{:S(2)}) copy-start(bf16[1024,4096]{1,0:T(8,128)(2,1)} %w_out.15) | copy-start | bytes 25165828
  4.0 1.0 %copy-start.1 = (bf16[256,1024]{1,0:T(8,128)(2,1)S(1)}, bf16[256,1024]{1,0:T(8,128)(2,1)}, u32[]{:S(2)}) copy-start(bf16[256,1024]{1,0:T(8,128)(2,1)} %context.7) | copy-start | bytes 1572868
  5.1 7.7 %copy-start.4 = (bf16[1,1024,512]{2,1,0:T(8,128)(2,1)S(1)}, bf16[1,1024,512]{2,1,0:T(8,128)(2,1)}, u32[]{:S(2)}) copy-start(bf16[1,1024,512]{2,1,0:T(8,128)(2,1)} %param.14) | copy-start | bytes 3145732
  5.1 7.7 %copy-start.5 = (bf16[1,256,512]{2,1,0:T(8,128)(2,1)S(1)}, bf16[1,256,512]{2,1,0:T(8,128)(2,1)}, u32[]{:S(2)}) copy-start(bf16[1,256,512]{2,1,0:T(8,128)(2,1)} %param.15) | copy-start | bytes 786436
  5.1 7.7 %copy-start.7 = (f32[1,1024]{1,0:T(1,128)S(1)}, f32[1,1024]{1,0:T(1,128)}, u32[]{:S(2)}) copy-start(f32[1,1024]{1,0:T(1,128)} %gain_depth.3) | copy-start | bytes 12292
  5.1 13.5 %slice-start = ((s8[8388608]{0:T(1024)(128)(4,1)}), s8[4194304]{0:T(1024)(128)(4,1)S(1)}, s32[]{:S(2)}) async-start(s8[8388608]{0:T(1024)(128)(4,1)} %bitcast.4), calls=%async_computation | async-start | bytes 8388608
  5.1 13.5 %copy-start.2 = (bf16[256,1024]{1,0:T(8,128)(2,1)S(1)}, bf16[256,1024]{1,0:T(8,128)(2,1)}, u32[]{:S(2)}) copy-start(bf16[256,1024]{1,0:T(8,128)(2,1)} %context.7) | copy-start | bytes 1572868
  6.3 10.1 %collective-permute-start.1 = (bf16[256,512]{1,0:T(8,128)(2,1)S(1)}, bf16[256,512]{1,0:T(8,128)(2,1)S(1)}, u32[]{:S(2)}, u32[]{:S(2)}) collective-permute-start(bf16[256,512]{1,0:T(8,128)(2,1)S(1)} %get-tuple-element.26), channel_id=1, source_target_pairs={{0,1},{1,0},{2,3},{3,2},{4,5},{5,4},{6,7},{7,6},{8,9},{9,8},{10,11... | collective-permute-start | bytes 786440 | tf_op jit(solution)/shard_map/ppermute | solution.py:205
  9.3 9.2 %slice-start.1 = ((s8[8388608]{0:T(1024)(128)(4,1)}), s8[4194304]{0:T(1024)(128)(4,1)S(1)}, s32[]{:S(2)}) async-start(s8[8388608]{0:T(1024)(128)(4,1)} %bitcast.4), calls=%async_computation.1 | async-start | bytes 8388608
  9.3 12.6 %copy-start.8 = (bf16[256,1024]{1,0:T(8,128)(2,1)S(1)}, bf16[256,1024]{1,0:T(8,128)(2,1)}, u32[]{:S(2)}) copy-start(bf16[256,1024]{1,0:T(8,128)(2,1)} %param.10) | copy-start | bytes 1572868
  9.3 9.2 %collective-permute-start.2 = (bf16[256,512]{1,0:T(8,128)(2,1)S(1)}, bf16[256,512]{1,0:T(8,128)(2,1)S(1)}, u32[]{:S(2)}, u32[]{:S(2)}) collective-permute-start(bf16[256,512]{1,0:T(8,128)(2,1)S(1)} %get-tuple-element.27), channel_id=1, source_target_pairs={{0,2},{1,3},{2,0},{3,1},{4,6},{5,7},{6,4},{7,5},{8,10},{9,11},{10,... | collective-permute-start | bytes 786440 | tf_op jit(solution)/shard_map/ppermute | solution.py:205
  12.1 10.0 %collective-permute-start = (bf16[256,512]{1,0:T(8,128)(2,1)S(1)}, bf16[256,512]{1,0:T(8,128)(2,1)S(1)}, u32[]{:S(2)}, u32[]{:S(2)}) collective-permute-start(bf16[256,512]{1,0:T(8,128)(2,1)S(1)} %get-tuple-element.25), channel_id=1, source_target_pairs={{0,1},{1,0},{2,3},{3,2},{4,5},{5,4},{6,7},{7,6},{8,9},{9,8},{10,11... | collective-permute-start | bytes 786440 | tf_op jit(solution)/shard_map/ppermute | solution.py:205
  12.7 14.3 %collective-permute-start.4 = (bf16[256,512]{1,0:T(8,128)(2,1)S(1)}, bf16[256,512]{1,0:T(8,128)(2,1)S(1)}, u32[]{:S(2)}, u32[]{:S(2)}) collective-permute-start(bf16[256,512]{1,0:T(8,128)(2,1)S(1)} %get-tuple-element.30), channel_id=1, source_target_pairs={{0,2},{1,3},{2,0},{3,1},{4,6},{5,7},{6,4},{7,5},{8,10},{9,11},{10,... | collective-permute-start | bytes 786440 | tf_op jit(solution)/shard_map/ppermute | solution.py:205
  13.3 19.3 %copy-start.3 = (bf16[1024,1024]{1,0:T(8,128)(2,1)S(1)}, bf16[1024,1024]{1,0:T(8,128)(2,1)}, u32[]{:S(2)}) copy-start(bf16[1024,1024]{1,0:T(8,128)(2,1)} %w_in.3) | copy-start | bytes 6291460
  13.3 19.2 %copy-start.6 = (f32[4096]{0:T(1024)S(1)}, f32[4096]{0:T(1024)}, u32[]{:S(2)}) copy-start(f32[4096]{0:T(1024)} %param.11) | copy-start | bytes 49156
  13.3 21.8 %collective-permute-start.12 = (bf16[64,1024]{1,0:T(8,128)(2,1)S(1)}, bf16[64,1024]{1,0:T(8,128)(2,1)S(1)}, u32[]{:S(2)}, u32[]{:S(2)}) collective-permute-start(bf16[64,1024]{1,0:T(8,128)(2,1)S(1)} %get-tuple-element.38), channel_id=1, source_target_pairs={{0,3},{1,2},{2,1},{3,0},{4,7},{5,6},{6,5},{7,4},{8,11},{9,10},{10,... | collective-permute-start | bytes 393224 | tf_op jit(solution)/shard_map/ppermute | solution.py:205
  19.8 12.7 %collective-permute-start.3 = (bf16[256,512]{1,0:T(8,128)(2,1)S(1)}, bf16[256,512]{1,0:T(8,128)(2,1)S(1)}, u32[]{:S(2)}, u32[]{:S(2)}) collective-permute-start(bf16[256,512]{1,0:T(8,128)(2,1)S(1)} %get-tuple-element.28), channel_id=1, source_target_pairs={{0,2},{1,3},{2,0},{3,1},{4,6},{5,7},{6,4},{7,5},{8,10},{9,11},{10,... | collective-permute-start | bytes 786440 | tf_op jit(solution)/shard_map/ppermute | solution.py:205
  21.4 11.1 %collective-permute-start.5 = (bf16[256,512]{1,0:T(8,128)(2,1)S(1)}, bf16[256,512]{1,0:T(8,128)(2,1)S(1)}, u32[]{:S(2)}, u32[]{:S(2)}) collective-permute-start(bf16[256,512]{1,0:T(8,128)(2,1)S(1)} %get-tuple-element.31), channel_id=1, source_target_pairs={{0,1},{1,0},{2,3},{3,2},{4,5},{5,4},{6,7},{7,6},{8,9},{9,8},{10,11... | collective-permute-start | bytes 786440 | tf_op jit(solution)/shard_map/ppermute | solution.py:205
  22.1 15.0 %collective-permute-start.13 = (bf16[64,1024]{1,0:T(8,128)(2,1)S(1)}, bf16[64,1024]{1,0:T(8,128)(2,1)S(1)}, u32[]{:S(2)}, u32[]{:S(2)}) collective-permute-start(bf16[64,1024]{1,0:T(8,128)(2,1)S(1)} %get-tuple-element.39), channel_id=1, source_target_pairs={{0,2},{1,3},{2,0},{3,1},{4,6},{5,7},{6,4},{7,5},{8,10},{9,11},{10,... | collective-permute-start | bytes 393224 | tf_op jit(solution)/shard_map/ppermute | solution.py:205
  27.0 10.0 %collective-permute-start.14 = (bf16[64,1024]{1,0:T(8,128)(2,1)S(1)}, bf16[64,1024]{1,0:T(8,128)(2,1)S(1)}, u32[]{:S(2)}, u32[]{:S(2)}) collective-permute-start(bf16[64,1024]{1,0:T(8,128)(2,1)S(1)} %get-tuple-element.40), channel_id=1, source_target_pairs={{0,1},{1,0},{2,3},{3,2},{4,5},{5,4},{6,7},{7,6},{8,9},{9,8},{10,11... | collective-permute-start | bytes 393224 | tf_op jit(solution)/shard_map/ppermute | solution.py:205
  33.5 7.1 %collective-permute-start.6 = (bf16[64,1152]{1,0:T(8,128)(2,1)S(1)}, bf16[64,1152]{1,0:T(8,128)(2,1)S(1)}, u32[]{:S(2)}, u32[]{:S(2)}) collective-permute-start(bf16[64,1152]{1,0:T(8,128)(2,1)S(1)} %get-tuple-element.34), channel_id=1, source_target_pairs={{0,3},{1,2},{2,1},{3,0},{4,7},{5,6},{6,5},{7,4},{8,11},{9,10},{10,... | collective-permute-start | bytes 442376 | tf_op jit(solution)/shard_map/ppermute | solution.py:205
  35.0 7.8 %collective-permute-start.7 = (bf16[64,1152]{1,0:T(8,128)(2,1)S(1)}, bf16[64,1152]{1,0:T(8,128)(2,1)S(1)}, u32[]{:S(2)}, u32[]{:S(2)}) collective-permute-start(bf16[64,1152]{1,0:T(8,128)(2,1)S(1)} %get-tuple-element.35), channel_id=1, source_target_pairs={{0,2},{1,3},{2,0},{3,1},{4,6},{5,7},{6,4},{7,5},{8,10},{9,11},{10,... | collective-permute-start | bytes 442376 | tf_op jit(solution)/shard_map/ppermute | solution.py:205
  35.1 7.7 %collective-permute-start.8 = (bf16[64,1152]{1,0:T(8,128)(2,1)S(1)}, bf16[64,1152]{1,0:T(8,128)(2,1)S(1)}, u32[]{:S(2)}, u32[]{:S(2)}) collective-permute-start(bf16[64,1152]{1,0:T(8,128)(2,1)S(1)} %get-tuple-element.36), channel_id=1, source_target_pairs={{0,1},{1,0},{2,3},{3,2},{4,5},{5,4},{6,7},{7,6},{8,9},{9,8},{10,11... | collective-permute-start | bytes 442376 | tf_op jit(solution)/shard_map/ppermute | solution.py:205
  37.1 9.5 %collective-permute-start.15 = (bf16[64,1024]{1,0:T(8,128)(2,1)S(1)}, bf16[64,1024]{1,0:T(8,128)(2,1)S(1)}, u32[]{:S(2)}, u32[]{:S(2)}) collective-permute-start(bf16[64,1024]{1,0:T(8,128)(2,1)S(1)} %sum_upstream.1.refs_4_), channel_id=1, source_target_pairs={{0,1},{1,0},{2,3},{3,2},{4,5},{5,4},{6,7},{7,6},{8,9},{9,8},{10,11... | collective-permute-start | bytes 393224 | tf_op jit(solution)/shard_map/ppermute | solution.py:205
  43.0 10.9 %collective-permute-start.10 = (bf16[64,1152]{1,0:T(8,128)(2,1)S(1)}, bf16[64,1152]{1,0:T(8,128)(2,1)S(1)}, u32[]{:S(2)}, u32[]{:S(2)}) collective-permute-start(bf16[64,1152]{1,0:T(8,128)(2,1)S(1)} %sum_state.1.refs_0_), channel_id=1, source_target_pairs={{0,2},{1,3},{2,0},{3,1},{4,6},{5,7},{6,4},{7,5},{8,10},{9,11},{10,... | collective-permute-start | bytes 442376 | tf_op jit(solution)/shard_map/ppermute | solution.py:205
  43.1 10.9 %collective-permute-start.11 = (bf16[64,1152]{1,0:T(8,128)(2,1)S(1)}, bf16[64,1152]{1,0:T(8,128)(2,1)S(1)}, u32[]{:S(2)}, u32[]{:S(2)}) collective-permute-start(bf16[64,1152]{1,0:T(8,128)(2,1)S(1)} %sum_state.1.refs_0_), channel_id=1, source_target_pairs={{0,3},{1,2},{2,1},{3,0},{4,7},{5,6},{6,5},{7,4},{8,11},{9,10},{10,... | collective-permute-start | bytes 442376 | tf_op jit(solution)/shard_map/ppermute | solution.py:205
  44.6 9.3 %collective-permute-start.9 = (bf16[64,1152]{1,0:T(8,128)(2,1)S(1)}, bf16[64,1152]{1,0:T(8,128)(2,1)S(1)}, u32[]{:S(2)}, u32[]{:S(2)}) collective-permute-start(bf16[64,1152]{1,0:T(8,128)(2,1)S(1)} %sum_state.1.refs_0_), channel_id=1, source_target_pairs={{0,1},{1,0},{2,3},{3,2},{4,5},{5,4},{6,7},{7,6},{8,9},{9,8},{10,11... | collective-permute-start | bytes 442376 | tf_op jit(solution)/shard_map/ppermute | solution.py:205
  46.6 7.4 %collective-permute-start.16 = (bf16[64,1024]{1,0:T(8,128)(2,1)S(1)}, bf16[64,1024]{1,0:T(8,128)(2,1)S(1)}, u32[]{:S(2)}, u32[]{:S(2)}) collective-permute-start(bf16[64,1024]{1,0:T(8,128)(2,1)S(1)} %sum_upstream.1.refs_4_), channel_id=1, source_target_pairs={{0,2},{1,3},{2,0},{3,1},{4,6},{5,7},{6,4},{7,5},{8,10},{9,11},{10,... | collective-permute-start | bytes 393224 | tf_op jit(solution)/shard_map/ppermute | solution.py:205
  46.6 7.3 %collective-permute-start.17 = (bf16[64,1024]{1,0:T(8,128)(2,1)S(1)}, bf16[64,1024]{1,0:T(8,128)(2,1)S(1)}, u32[]{:S(2)}, u32[]{:S(2)}) collective-permute-start(bf16[64,1024]{1,0:T(8,128)(2,1)S(1)} %sum_upstream.1.refs_4_), channel_id=1, source_target_pairs={{0,3},{1,2},{2,1},{3,0},{4,7},{5,6},{6,5},{7,4},{8,11},{9,10},{10,... | collective-permute-start | bytes 393224 | tf_op jit(solution)/shard_map/ppermute | solution.py:205
  56.3 9.0 %collective-permute-start.18 = (bf16[256,512]{1,0:T(8,128)(2,1)S(1)}, bf16[256,512]{1,0:T(8,128)(2,1)S(1)}, u32[]{:S(2)}, u32[]{:S(2)}) collective-permute-start(bf16[256,512]{1,0:T(8,128)(2,1)S(1)} %get-tuple-element.43.refs_0_), channel_id=1, source_target_pairs={{0,1},{1,0},{2,3},{3,2},{4,5},{5,4},{6,7},{7,6},{8,9},{9,8},{10,11... | collective-permute-start | bytes 786440 | tf_op jit(solution)/shard_map/ppermute | solution.py:205
  56.7 9.2 %collective-permute-start.20 = (bf16[256,512]{1,0:T(8,128)(2,1)S(1)}, bf16[256,512]{1,0:T(8,128)(2,1)S(1)}, u32[]{:S(2)}, u32[]{:S(2)}) collective-permute-start(bf16[256,512]{1,0:T(8,128)(2,1)S(1)} %get-tuple-element.44.refs_1_), channel_id=1, source_target_pairs={{0,2},{1,3},{2,0},{3,1},{4,6},{5,7},{6,4},{7,5},{8,10},{9,11},{10,... | collective-permute-start | bytes 786440 | tf_op jit(solution)/shard_map/ppermute | solution.py:205
  57.8 11.0 %collective-permute-start.22 = (bf16[256,512]{1,0:T(8,128)(2,1)S(1)}, bf16[256,512]{1,0:T(8,128)(2,1)S(1)}, u32[]{:S(2)}, u32[]{:S(2)}) collective-permute-start(bf16[256,512]{1,0:T(8,128)(2,1)S(1)} %get-tuple-element.43.refs_0_), channel_id=1, source_target_pairs={{0,2},{1,3},{2,0},{3,1},{4,6},{5,7},{6,4},{7,5},{8,10},{9,11},{10,... | collective-permute-start | bytes 786440 | tf_op jit(solution)/shard_map/ppermute | solution.py:205
  58.7 10.1 %collective-permute-start.23 = (bf16[256,512]{1,0:T(8,128)(2,1)S(1)}, bf16[256,512]{1,0:T(8,128)(2,1)S(1)}, u32[]{:S(2)}, u32[]{:S(2)}) collective-permute-start(bf16[256,512]{1,0:T(8,128)(2,1)S(1)} %get-tuple-element.44.refs_1_), channel_id=1, source_target_pairs={{0,1},{1,0},{2,3},{3,2},{4,5},{5,4},{6,7},{7,6},{8,9},{9,8},{10,11... | collective-permute-start | bytes 786440 | tf_op jit(solution)/shard_map/ppermute | solution.py:205
  65.3 6.4 %collective-permute-start.19 = (bf16[256,512]{1,0:T(8,128)(2,1)S(1)}, bf16[256,512]{1,0:T(8,128)(2,1)S(1)}, u32[]{:S(2)}, u32[]{:S(2)}) collective-permute-start(bf16[256,512]{1,0:T(8,128)(2,1)S(1)} %collective-permute-done.18.refs_0_), channel_id=1, source_target_pairs={{0,2},{1,3},{2,0},{3,1},{4,6},{5,7},{6,4},{7,5},{8,10},{9,11},{10,... | collective-permute-start | bytes 786440 | tf_op jit(solution)/shard_map/ppermute | solution.py:205
  66.0 6.4 %collective-permute-start.21 = (bf16[256,512]{1,0:T(8,128)(2,1)S(1)}, bf16[256,512]{1,0:T(8,128)(2,1)S(1)}, u32[]{:S(2)}, u32[]{:S(2)}) collective-permute-start(bf16[256,512]{1,0:T(8,128)(2,1)S(1)} %collective-permute-done.20.refs_1_), channel_id=1, source_target_pairs={{0,1},{1,0},{2,3},{3,2},{4,5},{5,4},{6,7},{7,6},{8,9},{9,8},{10,11... | collective-permute-start | bytes 786440 | tf_op jit(solution)/shard_map/ppermute | solution.py:205

commit v3 on v0

v3 whole, which is shorter than its diff:
```python
import functools

import jax
import jax.numpy as jnp
from jax import lax
from jax.experimental import pallas as pl
from jax.experimental.pallas import tpu as pltpu
from jax.sharding import PartitionSpec as P

EPS = 1e-05
LANES = 128
SQ = 16
EARLY = 16
bf16, f32 = jnp.bfloat16, jnp.float32
VMEM = pl.BlockSpec(memory_space=pltpu.VMEM)
HBM = pl.BlockSpec(memory_space=pltpu.HBM)


def contract_last(left, right):
    return lax.dot_general(
        left, right, (((1,), (1,)), ((), ())), preferred_element_type=f32
    )


def call(body, outs, ins, in_specs, scratch=(), flops=0, name=None, limit=16):
    ins = [
        pltpu.with_memory_space_constraint(a, pltpu.HBM) if spec is HBM else a
        for a, spec in zip(ins, in_specs)
    ]
    moved = sum(a.size * a.dtype.itemsize for a in ins) // 4
    return pl.pallas_call(
        body,
        out_shape=[jax.ShapeDtypeStruct(s, d) for s, d in outs],
        in_specs=in_specs,
        out_specs=[VMEM] * len(outs),
        scratch_shapes=list(scratch),
        compiler_params=pltpu.CompilerParams(vmem_limit_bytes=limit * 2**20),
        cost_estimate=pl.CostEstimate(flops=flops, bytes_accessed=moved, transcendentals=0),
        name=name,
    )(*ins)


def put_squares(out, at, squares):
    frames = squares.shape[1]
    high = squares.astype(bf16).astype(f32)
    both = jnp.concatenate([high, squares - high], axis=0).astype(bf16)
    out[at : at + SQ, :frames] = both
    if frames < out.shape[1]:
        out[at : at + SQ, frames:] = jnp.zeros((SQ, out.shape[1] - frames), bf16)


def get_squares(ref, at, frames):
    both = ref[at : at + SQ, :frames].astype(f32)
    return both[: SQ // 2] + both[SQ // 2 :]


def rows_of(mask, share):
    return pl.ds(pl.multiple_of((lax.axis_index("mp") ^ mask) * share, share), share)


def block_of(mask, side, half):
    start = ((lax.axis_index("mp") ^ mask) * 2 + side) * half
    return pl.ds(pl.multiple_of(start, half), half)


def put_block(out, product, up, adds, mask, side, share):
    frames, half = product.shape
    wide = up.shape[1] // 2
    for add in adds:
        product = product + add[:frames, :].astype(f32)
    out[:frames, :] = product.astype(bf16)
    for c in range(wide // half):
        rows = slice(frames + c * share, frames + (c + 1) * share)
        col = side * wide + c * half
        part = up[rows_of(mask, share), col : col + half]
        for add in adds:
            part = part + add[rows, :].astype(f32)
        out[rows, :] = part.astype(bf16)


def head_kernel(items, share, cot, w_depth, gain_hbm, context, w_out, *refs):
    outs, up = refs[: len(items)], refs[len(items)]
    cot_buf, depth_buf, gain_depth, context_buf, buf, sems = refs[len(items) + 1 :]
    half = buf.shape[2]
    pairs = [(cot, cot_buf), (w_depth, depth_buf), (gain_hbm, gain_depth)]
    pairs += [(context, context_buf)]
    pairs += [(w_out.at[:, block_of(m, s, half)], buf.at[i]) for i, (m, s) in enumerate(items)]
    copies = [pltpu.make_async_copy(a, b, sems.at[i]) for i, (a, b) in enumerate(pairs)]
    for copy in copies:
        copy.start()
    for copy in copies[:3]:
        copy.wait()
    up[...] = gain_depth[...] * contract_last(cot_buf[...], depth_buf[...])
    copies[3].wait()
    for i, (mask, side) in enumerate(items):
        copies[4 + i].wait()
        product = jnp.dot(context_buf[...], buf[i], preferred_element_type=f32)
        put_block(outs[i], product, up, [], mask, side, share)


def project_kernel(items, share, context, w_out, up, *refs):
    count = sum(k for _, _, k in items)
    adds, outs = refs[:count], refs[count:]
    half = outs[0].shape[1]
    at = 0
    for i, (mask, side, k) in enumerate(items):
        product = jnp.dot(
            context[...], w_out[:, block_of(mask, side, half)], preferred_element_type=f32
        )
        put_block(outs[i], product, up, adds[at : at + k], mask, side, share)
        at += k


def early_kernel(items, share, context, w_out, up, *refs):
    outs, (buf, sems) = refs[: len(items)], refs[len(items) :]
    half = buf.shape[2]
    copies = [
        pltpu.make_async_copy(w_out.at[:, block_of(m, s, half)], buf.at[i], sems.at[i])
        for i, (m, s) in enumerate(items)
    ]
    for copy in copies:
        copy.start()
    for i, (mask, side) in enumerate(items):
        copies[i].wait()
        product = jnp.dot(context[...], buf[i], preferred_element_type=f32)
        put_block(outs[i], product, up, [], mask, side, share)


def keep_kernel(context, w_out, residual, out):
    half = out.shape[1] // 2
    for side in range(2):
        cols = slice(side * half, (side + 1) * half)
        out[:, cols] = residual[:, cols].astype(f32) + jnp.dot(
            context[...], w_out[:, block_of(0, side, half)], preferred_element_type=f32
        )


def state_kernel(log, share, gain, w_in, up, kept, *refs):
    adds = refs[: 2 * log]
    state, raw, squares, *sends = refs[2 * log :]
    frames, width = state.shape
    half = width // 2
    wide = raw.shape[1] // 2
    for side in range(2):
        cols = slice(side * half, (side + 1) * half)
        total = kept[:, cols]
        for add in adds[side * log : (side + 1) * log]:
            total = total + add[:frames, :].astype(f32)
        state[:, cols] = total
    value = state[...]
    gains = gain[:, pl.ds(pl.multiple_of(lax.axis_index("mp") * width, width), width)]
    raw[...] = jnp.dot((value * gains).astype(bf16), w_in[...], preferred_element_type=f32)
    column = jnp.sum(value * value, axis=1, keepdims=True)
    row = jnp.transpose(jnp.broadcast_to(column, (frames, LANES)))[: SQ // 2]
    for side, send in enumerate(sends):
        squares[side] = row
        send[:frames, :] = raw[:, side * wide : (side + 1) * wide].astype(bf16)
        put_squares(send, frames, row)
        for c in range(wide // half):
            col = side * wide + c * half
            part = up[rows_of(0, share), col : col + half]
            for add in adds[side * log : (side + 1) * log]:
                part = part + add[frames + c * share : frames + (c + 1) * share, :].astype(f32)
            send[frames + SQ :, c * half : (c + 1) * half] = part.astype(bf16)


def reduce_kernel(raw, squares, *refs):
    sent, got = refs[:2], refs[2:4]
    raw_out, squares_out, *sends = refs[4:]
    frames, depth = raw.shape
    wide = depth // 2
    for side in range(2):
        cols = slice(side * wide, (side + 1) * wide)
        total = raw[:, cols] + got[side][:frames, :].astype(f32)
        raw_out[:, cols] = total
        sends[side][:frames, :] = total.astype(bf16)
        row = squares[side] + get_squares(got[side], frames, frames)
        squares_out[side] = row
        put_squares(sends[side], frames, row)
        first = frames + SQ
        held = sent[side].shape[0] - first
        sends[side][first : first + held, :] = sent[side][first:, :]
        sends[side][first + held :, :] = got[side][first:, :]


def back_kernel(haves, share, features, gain, gain_depth, w_in, state, raw, squares, *refs):
    sent, got = refs[:2], refs[2:4]
    latent, grad, *halves = refs[4:8]
    up, du = refs[8:]
    frames, width = state.shape
    depth = w_in.shape[1]
    half, wide = width // 2, depth // 2
    first = frames + SQ
    for side in range(2):
        held = sent[side].shape[0] - first
        for i, mask in enumerate(haves[side]):
            ref, at = (sent[side], i * share) if i * share < held else (got[side], i * share - held)
            up[rows_of(mask, share), side * wide : (side + 1) * wide] = ref[
                first + at : first + at + share, :
            ]
    row = squares[0] + get_squares(got[0], frames, frames)
    recip = jnp.transpose(
        jnp.broadcast_to(lax.rsqrt(row[:1] / features + EPS), (LANES, frames))
    )[:, :1]
    back = []
    step = 64 if frames % 64 == 0 else frames
    for at in range(0, frames, step):
        rows = slice(at, at + step)
        total = [
            raw[rows, side * wide : (side + 1) * wide] + got[side][rows, :].astype(f32)
            for side in range(2)
        ]
        depth_in = jnp.concatenate(total, axis=1) * recip[rows]
        grads = up[rows, :].astype(f32)
        urecip = lax.rsqrt(jnp.mean(depth_in * depth_in, axis=1, keepdims=True) + EPS)
        inner = jnp.mean(depth_in * grads, axis=1, keepdims=True)
        part = (urecip * grads - depth_in * (urecip * urecip * urecip * inner)).astype(bf16)
        du[rows, :] = part
        dot_du = jnp.sum(part.astype(f32) * depth_in, axis=1, keepdims=True) / recip[rows]
        back.append(recip[rows] * recip[rows] * recip[rows] * (dot_du / features))
        latent[rows, :] = (depth_in * urecip * gain_depth[...]).astype(bf16)
    back = jnp.concatenate(back, axis=0)
    gains = gain[:, pl.ds(pl.multiple_of(lax.axis_index("mp") * width, width), width)]
    for side in range(2):
        cols = slice(side * half, (side + 1) * half)
        dnormed = contract_last(du[...], w_in[cols, :])
        value = (recip * (gains[:, cols] * dnormed) - state[:, cols] * back).astype(bf16)
        halves[side][...] = value
        grad[:, cols] = value


def act_kernel(latent, w_depth, out):
    out[...] = jnp.dot(latent[...], w_depth[...], preferred_element_type=f32).astype(bf16)


def context_kernel(items, w_out, *refs):
    blocks, rest, out = refs[: len(items)], refs[len(items) : -1], refs[-1]
    total = rest[0][...] if rest else None
    for (mask, side), block in zip(items, blocks):
        half = block.shape[1]
        part = contract_last(block[...], w_out[:, block_of(mask, side, half)])
        total = part if total is None else total + part
    out[...] = total.astype(out.dtype)


def local(n, context, w_out, residual, gain_temporal, w_in, gain_depth, w_depth, cotangent):
    frames, width = residual.shape
    half = width // 2
    share = frames // n
    features = width * n
    heads = w_out.shape[0]
    depth, act = w_depth.shape[1:]
    wide = depth // 2
    log = n.bit_length() - 1
    bits = [1 << i for i in range(log)]
    orders = (bits, bits[::-1])
    gain = gain_temporal[None, :]
    block = (frames + share * (wide // half), half)

    def mirror(mask):
        return sum(1 << (log - 1 - i) for i in range(log) if mask >> i & 1)

    pairs = sorted(range(n), key=lambda k: (-k.bit_count(), k))
    pairs = [((k, 0), (mirror(k), 1)) for k in pairs]

    def swap(value, mask):
        return lax.ppermute(value, "mp", [(i, i ^ mask) for i in range(n)])

    first = pairs[0]
    *blocks, up = call(
        functools.partial(head_kernel, first, share),
        [(block, bf16)] * 2 + [((frames, depth), f32)],
        [cotangent[0], w_depth[0], gain_depth, context, w_out],
        [HBM] * 5,
        [
            pltpu.VMEM((frames, act), bf16),
            pltpu.VMEM((depth, act), bf16),
            pltpu.VMEM((1, depth), f32),
            pltpu.VMEM(context.shape, bf16),
            pltpu.VMEM((2, heads, half), bf16),
            pltpu.SemaphoreType.DMA((6,)),
        ],
        flops=2 * frames * (depth * act + heads * width),
        name="head",
        limit=EARLY,
    )
    arrived = {}
    for pair in pairs[:-1]:
        if pair is not first:
            addends = []
            for mask, side in pair:
                order = orders[side]
                phase = min(i for i, bit in enumerate(order) if mask & bit)
                addends.append([arrived[mask ^ order[i], side] for i in range(phase)])
            listed = [a for adds in addends for a in adds]
            if not listed:
                blocks = call(
                    functools.partial(early_kernel, pair, share),
                    [(block, bf16)] * 2,
                    [context, w_out, up],
                    [VMEM, HBM, VMEM],
                    [pltpu.VMEM((2, heads, half), bf16), pltpu.SemaphoreType.DMA((2,))],
                    flops=2 * frames * heads * width,
                    name="early",
                    limit=EARLY,
                )
            else:
                blocks = call(
                    functools.partial(
                        project_kernel, [(m, s, len(a)) for (m, s), a in zip(pair, addends)], share
                    ),
                    [(block, bf16)] * 2,
                    [context, w_out, up] + listed,
                    [VMEM] * (3 + len(listed)),
                    flops=2 * frames * heads * width,
                    name="project",
                )
        for (mask, side), value in zip(pair, blocks):
            bit = next(bit for bit in orders[side] if mask & bit)
            arrived[mask, side] = swap(value, bit)
    kept = call(
        keep_kernel,
        [((frames, width), f32)],
        [context, w_out, residual],
        [VMEM] * 3,
        flops=2 * frames * heads * width,
        name="keep",
    )[0]

    state, raw, squares, *sends = call(
        functools.partial(state_kernel, log, share),
        [((frames, width), f32), ((frames, depth), f32), ((2, SQ // 2, frames), f32)]
        + [((frames + SQ + share, wide), bf16)] * 2,
        [gain, w_in, up, kept]
        + [arrived[bit, side] for side in range(2) for bit in orders[side]],
        [VMEM] * (4 + 2 * log),
        flops=2 * frames * width * depth,
        name="state",
    )

    haves = [[0], [0]]
    for i in range(log):
        got = [swap(sends[side], orders[side][i]) for side in range(2)]
        haves = [have + [k ^ orders[s][i] for k in have] for s, have in enumerate(haves)]
        if i < log - 1:
            raw, squares, *sends = call(
                reduce_kernel,
                [(raw.shape, f32), (squares.shape, f32)]
                + [((frames + SQ + share * len(haves[0]), wide), bf16)] * 2,
                [raw, squares] + list(sends) + got,
                [VMEM] * 6,
                name="reduce",
            )

    latent, grad_residual, *grads = call(
        functools.partial(back_kernel, haves, share, features),
        [((frames, depth), bf16), ((frames, width), bf16)] + [((frames, half), bf16)] * 2,
        [gain, gain_depth, w_in, state, raw, squares] + list(sends) + got,
        [VMEM] * 10,
        [pltpu.VMEM((frames, depth), bf16)] * 2,
        flops=2 * frames * width * depth,
        name="back",
    )

    blocks = {}
    for side, order in enumerate(orders):
        blocks[0, side] = grads[side]
        have = [0]
        for bit in order:
            for mask in list(have):
                blocks[mask ^ bit, side] = swap(blocks[mask, side], bit)
                have.append(mask ^ bit)

    depth_act = call(
        act_kernel,
        [((frames, act), bf16)],
        [latent, w_depth[0]],
        [VMEM] * 2,
        flops=2 * frames * depth * act,
        name="act",
    )[0]

    total = None
    for i, pair in enumerate(pairs[::-1]):
        ins = [w_out] + [blocks[key] for key in pair] + ([] if total is None else [total])
        total = call(
            functools.partial(context_kernel, pair),
            [((frames, heads), bf16 if i == n - 1 else f32)],
            ins,
            [VMEM] * len(ins),
            flops=2 * frames * heads * width,
            name="grad_context",
        )[0]
    return (depth_act[None], grad_residual, total)


def solution(mesh):
    in_specs = (
        P("dp", "mp"),
        P("mp", None),
        P("dp", "mp"),
        P(),
        P("mp", None),
        P("mp", None),
        P("mp", None, None),
        P("mp", "dp", None),
    )
    out_specs = (P("mp", "dp", None), P("dp", "mp"), P("dp", "mp"))
    n = mesh.shape["mp"]

    def run(*args):
        return local(n, *args)

    return jax.shard_map(run, mesh=mesh, in_specs=in_specs, out_specs=out_specs, check_vma=False)
```

time: 246 us -> 70.9 us (0.29)
  waiting for transfers between devices: 139 us -> 37.2 us
  blocking collectives: 60.1 us -> 0 us
  matrix products: 25.9 us -> 0 us
  starting transfers between devices: 0.12 us -> 18.1 us
  Pallas kernels: 0 us -> 14.7 us
  between operations: 13.8 us -> 0.75 us
  other arithmetic: 5.44 us -> 0.01 us
    psum x3 -> x0, blocking collectives: 60.1 us -> none  [the longest x1 41.7 us: local(): du_total = lax.psum(dinput, 'mp').astype(jnp.bfloat16)]
    reduce_scatter x1 -> x0, waiting for transfers between devices: 54.8 us -> none  [local(): lax.psum_scatter(full_term, 'mp', scatter_dimension=1, tiled=True)]
    psum x1 -> x0, waiting for transfers between devices: 52.6 us -> none  [local(): depth_in = lax.psum(partial_value, 'mp')]
    ppermute x0 -> x16, waiting for transfers between devices: none -> 37.2 us  [swap(): return lax.ppermute(value, 'mp', [(i, i ^ mask) for i in range(n)])]
    all_gather x1 -> x0, waiting for transfers between devices: 32.1 us -> none  [local(): lax.all_gather(grad_residual, 'mp', axis=1, tiled=True)]
    dot_general x6 -> x0, matrix products: 25.9 us -> none  [the longest x3 12.4 us: contract_last(): lax.dot_general(left, right, (((1,), (1,)), ((), ())), preferred_element_...]
    ppermute x0 -> x16, starting transfers between devices: none -> 18.1 us  [swap(): return lax.ppermute(value, 'mp', [(i, i ^ mask) for i in range(n)])]
    pallas_call x0 -> x12, Pallas kernels: none -> 14.7 us  [call(): pl.pallas_call(body, out_shape=[jax.ShapeDtypeStruct(s, d) for s, d in ou...]
  transfers between devices with their start and end apart: 3 -> 16, of which waited for: 3 -> 14; matrix products, arithmetic and copies ran while one was open for 1% -> 0% of each run, Pallas kernels for 0% -> 10%
where the time goes in v3:
time: 70.9 us; the launch traced here: 70.7 us
  waiting for transfers between devices  37.2 us (52%)
  starting transfers between devices  18.1 us (26%)
  Pallas kernels  14.7 us (21%)
  between operations  0.75 us (1%)
    ppermute x16, waiting for transfers between devices, swap(): return lax.ppermute(value, 'mp', [(i, i ^ mask) for i in range(n)])  37.2 us
    ppermute x16, starting transfers between devices, swap(): return lax.ppermute(value, 'mp', [(i, i ^ mask) for i in range(n)])  18.1 us
    pallas_call x12, Pallas kernels, call(): pl.pallas_call(body, out_shape=[jax.ShapeDtypeStruct(s, d) for s, d in ou...  14.7 us
  transfers between devices with their start and end apart: 16, of which 14 were waited for; matrix products, arithmetic and copies ran while one was open for 0% of the time, Pallas kernels for 10%

profile of v3, /device:TPU:0, one launch (start us, length us, event | category | flops | bytes accessed | tf_op | source)
XLA Modules:
  0.0 70.7 jit_solution(2462946330596468956)
XLA Ops:
  0.6 0.0 slice-start
  0.7 0.0 slice-start.1
  0.7 2.9 %head.1 = (bf16[320,512]{1,0:T(8,128)(2,1)S(1)}, bf16[320,512]{1,0:T(8,128)(2,1)S(1)}, f32[256,1024]{1,0:T(8,128)S(1)}) custom-call(bf16[256,512]{1,0:T(8,128)(2,1)} %bitcast.10, bf16[1024,512]{1,0:T(8,128)(2,1)} %bitcast.6, f32[1,1024]{1,0:T(1,128)} %gain_depth.1, bf16[256,1024]{1,0:T(8,128)(2,1)} %context.7, bf16[1024,4096]{1,0:T(8,128)(2,1)} %w_out.15), custom_call_target="tpu_custom_call" | custom-call | flops 805306368 | bytes 2556928 | tf_op jit(solution)/shard_map/head/pallas_call | solution.py:31
  3.6 3.0 %collective-permute-start.1 = (bf16[320,512]{1,0:T(8,128)(2,1)S(1)}, bf16[320,512]{1,0:T(8,128)(2,1)S(1)}, u32[]{:S(2)}, u32[]{:S(2)}) collective-permute-start(bf16[320,512]{1,0:T(8,128)(2,1)S(1)} %get-tuple-element.25), channel_id=1, source_target_pairs={{0,1},{1,0},{2,3},{3,2},{4,5},{5,4},{6,7},{7,6},{8,9},{9,8},{10,11... | collective-permute-start | bytes 983048 | tf_op jit(solution)/shard_map/ppermute | solution.py:267
  6.6 1.5 %collective-permute-start.2 = (bf16[320,512]{1,0:T(8,128)(2,1)S(1)}, bf16[320,512]{1,0:T(8,128)(2,1)S(1)}, u32[]{:S(2)}, u32[]{:S(2)}) collective-permute-start(bf16[320,512]{1,0:T(8,128)(2,1)S(1)} %get-tuple-element.26), channel_id=1, source_target_pairs={{0,2},{1,3},{2,0},{3,1},{4,6},{5,7},{6,4},{7,5},{8,10},{9,11},{10,... | collective-permute-start | bytes 983048 | tf_op jit(solution)/shard_map/ppermute | solution.py:267
  8.1 0.0 copy-done.1
  8.1 2.2 %early.1 = (bf16[320,512]{1,0:T(8,128)(2,1)S(1)}, bf16[320,512]{1,0:T(8,128)(2,1)S(1)}) custom-call(bf16[256,1024]{1,0:T(8,128)(2,1)S(1)} %copy-done.1, bf16[1024,4096]{1,0:T(8,128)(2,1)} %w_out.15, f32[256,1024]{1,0:T(8,128)S(1)} %get-tuple-element.23.up), custom_call_target="tpu_custom_call" | custom-call | flops 536870912 | bytes 2490368 | tf_op jit(solution)/shard_map/early/pallas_call | solution.py:31
  10.3 0.6 collective-permute-start
  10.9 0.2 collective-permute-start.4
  11.1 4.0 %collective-permute-done.1.refs_0_ = bf16[320,512]{1,0:T(8,128)(2,1)S(1)} collective-permute-done((bf16[320,512]{1,0:T(8,128)(2,1)S(1)}, bf16[320,512]{1,0:T(8,128)(2,1)S(1)}, u32[]{:S(2)}, u32[]{:S(2)}) %collective-permute-start.1) | collective-permute-done | bytes 327712 | tf_op jit(solution)/shard_map/ppermute | solution.py:267
  15.1 2.1 %collective-permute-done.2.refs_1_ = bf16[320,512]{1,0:T(8,128)(2,1)S(1)} collective-permute-done((bf16[320,512]{1,0:T(8,128)(2,1)S(1)}, bf16[320,512]{1,0:T(8,128)(2,1)S(1)}, u32[]{:S(2)}, u32[]{:S(2)}) %collective-permute-start.2) | collective-permute-done | bytes 327712 | tf_op jit(solution)/shard_map/ppermute | solution.py:267
  17.2 0.8 %project.1 = (bf16[320,512]{1,0:T(8,128)(2,1)S(1)}, bf16[320,512]{1,0:T(8,128)(2,1)S(1)}) custom-call(bf16[256,1024]{1,0:T(8,128)(2,1)S(1)} %copy-done.1, bf16[1024,4096]{1,0:T(8,128)(2,1)S(1)} %bitcast.5, f32[256,1024]{1,0:T(8,128)S(1)} %get-tuple-element.23.up, bf16[320,512]{1,0:T(8,128)(2,1)S(1)} %collective-permute-done.1.refs_0_, ...), custom_call_target="tpu_custom_call" | custom-call | flops 536870912 | bytes 2654208 | tf_op jit(solution)/shard_map/project/pallas_call | solution.py:31
  18.0 1.6 %collective-permute-start.3 = (bf16[320,512]{1,0:T(8,128)(2,1)S(1)}, bf16[320,512]{1,0:T(8,128)(2,1)S(1)}, u32[]{:S(2)}, u32[]{:S(2)}) collective-permute-start(bf16[320,512]{1,0:T(8,128)(2,1)S(1)} %get-tuple-element.27), channel_id=1, source_target_pairs={{0,2},{1,3},{2,0},{3,1},{4,6},{5,7},{6,4},{7,5},{8,10},{9,11},{10,... | collective-permute-start | bytes 983048 | tf_op jit(solution)/shard_map/ppermute | solution.py:267
  19.6 0.5 collective-permute-start.5
  20.1 0.7 %keep.1.kept = f32[256,1024]{1,0:T(8,128)S(1)} custom-call(bf16[256,1024]{1,0:T(8,128)(2,1)S(1)} %copy-done.1, bf16[1024,4096]{1,0:T(8,128)(2,1)S(1)} %bitcast.5, bf16[256,1024]{1,0:T(8,128)(2,1)S(1)} %copy-done.3), custom_call_target="tpu_custom_call" | custom-call | flops 536870912 | bytes 2359296 | tf_op jit(solution)/shard_map/keep/pallas_call | solution.py:31
  20.8 0.0 copy-start.2
  20.8 1.3 %collective-permute-done.refs_0_ = bf16[320,512]{1,0:T(8,128)(2,1)S(1)} collective-permute-done((bf16[320,512]{1,0:T(8,128)(2,1)S(1)}, bf16[320,512]{1,0:T(8,128)(2,1)S(1)}, u32[]{:S(2)}, u32[]{:S(2)}) %collective-permute-start) | collective-permute-done | bytes 327712 | tf_op jit(solution)/shard_map/ppermute | solution.py:267
  22.1 2.1 %collective-permute-done.4.refs_2_ = bf16[320,512]{1,0:T(8,128)(2,1)S(1)} collective-permute-done((bf16[320,512]{1,0:T(8,128)(2,1)S(1)}, bf16[320,512]{1,0:T(8,128)(2,1)S(1)}, u32[]{:S(2)}, u32[]{:S(2)}) %collective-permute-start.4) | collective-permute-done | bytes 327712 | tf_op jit(solution)/shard_map/ppermute | solution.py:267
  24.2 5.6 %collective-permute-done.3.refs_1_ = bf16[320,512]{1,0:T(8,128)(2,1)S(1)} collective-permute-done((bf16[320,512]{1,0:T(8,128)(2,1)S(1)}, bf16[320,512]{1,0:T(8,128)(2,1)S(1)}, u32[]{:S(2)}, u32[]{:S(2)}) %collective-permute-start.3) | collective-permute-done | bytes 327712 | tf_op jit(solution)/shard_map/ppermute | solution.py:267
  29.8 0.0 collective-permute-done.5.refs_3_
  29.8 0.8 %state.1 = (f32[256,1024]{1,0:T(8,128)S(1)}, f32[256,1024]{1,0:T(8,128)S(1)}, f32[2,8,256]{2,1,0:T(8,128)S(1)}, bf16[336,512]{1,0:T(8,128)(2,1)S(1)}, bf16[336,512]{1,0:T(8,128)(2,1)S(1)}) custom-call(f32[1,4096]{1,0:T(1,128)S(1)} %bitcast.8, bf16[1024,1024]{1,0:T(8,128)(2,1)S(1)} %copy-done, f32[256,1024]{1,0:T(8,128)S(1)} %get-tuple-element.23.up, ...), custom_call_target="tpu_custom_call" | custom-call | flops 536870912 | bytes 1380352 | tf_op jit(solution)/shard_map/state/pallas_call | solution.py:31
  30.6 0.4 collective-permute-start.6
  31.0 1.7 %collective-permute-start.7 = (bf16[336,512]{1,0:T(8,128)(2,1)S(1)}, bf16[336,512]{1,0:T(8,128)(2,1)S(1)}, u32[]{:S(2)}, u32[]{:S(2)}) collective-permute-start(bf16[336,512]{1,0:T(8,128)(2,1)S(1)} %get-tuple-element.34.refs_1_), channel_id=1, source_target_pairs={{0,2},{1,3},{2,0},{3,1},{4,6},{5,7},{6,4},{7,5},{8,10},{9,11},{10,... | collective-permute-start | bytes 1032200 | tf_op jit(solution)/shard_map/ppermute | solution.py:267
  32.7 6.5 %collective-permute-done.6.refs_2_ = bf16[336,512]{1,0:T(8,128)(2,1)S(1)} collective-permute-done((bf16[336,512]{1,0:T(8,128)(2,1)S(1)}, bf16[336,512]{1,0:T(8,128)(2,1)S(1)}, u32[]{:S(2)}, u32[]{:S(2)}) %collective-permute-start.6) | collective-permute-done | bytes 344096 | tf_op jit(solution)/shard_map/ppermute | solution.py:267
  39.2 0.4 collective-permute-done.7.refs_3_
  39.7 0.2 reduce.1
  39.8 1.5 %collective-permute-start.8 = (bf16[400,512]{1,0:T(8,128)(2,1)S(1)}, bf16[400,512]{1,0:T(8,128)(2,1)S(1)}, u32[]{:S(2)}, u32[]{:S(2)}) collective-permute-start(bf16[400,512]{1,0:T(8,128)(2,1)S(1)} %get-tuple-element.37.refs_0_), channel_id=1, source_target_pairs={{0,2},{1,3},{2,0},{3,1},{4,6},{5,7},{6,4},{7,5},{8,10},{9,11},{10,... | collective-permute-start | bytes 1228808 | tf_op jit(solution)/shard_map/ppermute | solution.py:267
  41.3 1.4 %collective-permute-start.9 = (bf16[400,512]{1,0:T(8,128)(2,1)S(1)}, bf16[400,512]{1,0:T(8,128)(2,1)S(1)}, u32[]{:S(2)}, u32[]{:S(2)}) collective-permute-start(bf16[400,512]{1,0:T(8,128)(2,1)S(1)} %get-tuple-element.38.refs_1_), channel_id=1, source_target_pairs={{0,1},{1,0},{2,3},{3,2},{4,5},{5,4},{6,7},{7,6},{8,9},{9,8},{10,11... | collective-permute-start | bytes 1228808 | tf_op jit(solution)/shard_map/ppermute | solution.py:267
  42.8 6.2 %collective-permute-done.8.refs_2_ = bf16[400,512]{1,0:T(8,128)(2,1)S(1)} collective-permute-done((bf16[400,512]{1,0:T(8,128)(2,1)S(1)}, bf16[400,512]{1,0:T(8,128)(2,1)S(1)}, u32[]{:S(2)}, u32[]{:S(2)}) %collective-permute-start.8) | collective-permute-done | bytes 409632 | tf_op jit(solution)/shard_map/ppermute | solution.py:267
  49.0 0.9 %collective-permute-done.9.refs_3_ = bf16[400,512]{1,0:T(8,128)(2,1)S(1)} collective-permute-done((bf16[400,512]{1,0:T(8,128)(2,1)S(1)}, bf16[400,512]{1,0:T(8,128)(2,1)S(1)}, u32[]{:S(2)}, u32[]{:S(2)}) %collective-permute-start.9) | collective-permute-done | bytes 409632 | tf_op jit(solution)/shard_map/ppermute | solution.py:267
  49.9 2.2 %back.1 = (bf16[256,1024]{1,0:T(8,128)(2,1)S(1)}, bf16[256,1024]{1,0:T(8,128)(2,1)}, bf16[256,512]{1,0:T(8,128)(2,1)S(1)}, bf16[256,512]{1,0:T(8,128)(2,1)S(1)}) custom-call(f32[1,4096]{1,0:T(1,128)S(1)} %bitcast.9, f32[1,1024]{1,0:T(1,128)S(1)} %copy-done.5, bf16[1024,1024]{1,0:T(8,128)(2,1)S(1)} %copy-done, f32[256,1024]{1,0:T(8,128)S(1)} %get-tuple-element.30.state, ...), custom_call_target="tpu_custom_call" | custom-call | flops 536870912 | bytes 1467392 | tf_op jit(solution)/shard_map/back/pallas_call | solution.py:31
  52.2 1.4 %collective-permute-start.10 = (bf16[256,512]{1,0:T(8,128)(2,1)S(1)}, bf16[256,512]{1,0:T(8,128)(2,1)S(1)}, u32[]{:S(2)}, u32[]{:S(2)}) collective-permute-start(bf16[256,512]{1,0:T(8,128)(2,1)S(1)} %get-tuple-element.41.refs_0_), channel_id=1, source_target_pairs={{0,1},{1,0},{2,3},{3,2},{4,5},{5,4},{6,7},{7,6},{8,9},{9,8},{10,11... | collective-permute-start | bytes 786440 | tf_op jit(solution)/shard_map/ppermute | solution.py:267
  53.6 0.5 collective-permute-start.12
  54.0 1.5 %collective-permute-start.14 = (bf16[256,512]{1,0:T(8,128)(2,1)S(1)}, bf16[256,512]{1,0:T(8,128)(2,1)S(1)}, u32[]{:S(2)}, u32[]{:S(2)}) collective-permute-start(bf16[256,512]{1,0:T(8,128)(2,1)S(1)} %get-tuple-element.41.refs_0_), channel_id=1, source_target_pairs={{0,2},{1,3},{2,0},{3,1},{4,6},{5,7},{6,4},{7,5},{8,10},{9,11},{10,... | collective-permute-start | bytes 786440 | tf_op jit(solution)/shard_map/ppermute | solution.py:267
  55.6 0.6 collective-permute-start.15
  56.2 5.2 %collective-permute-done.10.refs_0_ = bf16[256,512]{1,0:T(8,128)(2,1)S(1)} collective-permute-done((bf16[256,512]{1,0:T(8,128)(2,1)S(1)}, bf16[256,512]{1,0:T(8,128)(2,1)S(1)}, u32[]{:S(2)}, u32[]{:S(2)}) %collective-permute-start.10) | collective-permute-done | bytes 262176 | tf_op jit(solution)/shard_map/ppermute | solution.py:267
  61.4 0.9 %collective-permute-start.11 = (bf16[256,512]{1,0:T(8,128)(2,1)S(1)}, bf16[256,512]{1,0:T(8,128)(2,1)S(1)}, u32[]{:S(2)}, u32[]{:S(2)}) collective-permute-start(bf16[256,512]{1,0:T(8,128)(2,1)S(1)} %collective-permute-done.10.refs_0_), channel_id=1, source_target_pairs={{0,2},{1,3},{2,0},{3,1},{4,6},{5,7},{6,4},{7,5},{8,10},{9,11},{10,... | collective-permute-start | bytes 786440 | tf_op jit(solution)/shard_map/ppermute | solution.py:267
  62.3 0.5 collective-permute-done.12.refs_1_
  62.8 0.6 collective-permute-start.13
  63.4 1.2 %act.1 = bf16[256,512]{1,0:T(8,128)(2,1)} custom-call(bf16[256,1024]{1,0:T(8,128)(2,1)S(1)} %get-tuple-element.39.latent, bf16[1024,512]{1,0:T(8,128)(2,1)S(1)} %bitcast.7), custom_call_target="tpu_custom_call" | custom-call | flops 268435456 | bytes 393216 | tf_op jit(solution)/shard_map/act/pallas_call | solution.py:31
  64.6 0.7 %grad_context.4.refs_2_ = f32[256,1024]{1,0:T(8,128)S(1)} custom-call(bf16[1024,4096]{1,0:T(8,128)(2,1)S(1)} %bitcast.5, bf16[256,512]{1,0:T(8,128)(2,1)S(1)} %get-tuple-element.41.refs_0_, bf16[256,512]{1,0:T(8,128)(2,1)S(1)} %get-tuple-element.42.refs_1_), custom_call_target="tpu_custom_call" | custom-call | flops 536870912 | bytes 2228224 | tf_op jit(solution)/shard_map/grad_context/pallas_call | solution.py:31
  65.3 0.8 %collective-permute-done.14.refs_0_ = bf16[256,512]{1,0:T(8,128)(2,1)S(1)} collective-permute-done((bf16[256,512]{1,0:T(8,128)(2,1)S(1)}, bf16[256,512]{1,0:T(8,128)(2,1)S(1)}, u32[]{:S(2)}, u32[]{:S(2)}) %collective-permute-start.14) | collective-permute-done | bytes 262176 | tf_op jit(solution)/shard_map/ppermute | solution.py:267
  66.2 0.0 collective-permute-done.15.refs_1_
  66.2 0.7 %grad_context.5.refs_2_ = f32[256,1024]{1,0:T(8,128)S(1)} custom-call(bf16[1024,4096]{1,0:T(8,128)(2,1)S(1)} %bitcast.5, bf16[256,512]{1,0:T(8,128)(2,1)S(1)} %collective-permute-done.14.refs_0_, bf16[256,512]{1,0:T(8,128)(2,1)S(1)} %collective-permute-done.15.refs_1_, f32[256,1024]{1,0:T(8,128)S(1)} %grad_context.4.refs_2_), custom_call_target="tpu_custom_call" | custom-call | flops 536870912 | bytes 2490368 | tf_op jit(solution)/shard_map/grad_context/pallas_call | solution.py:31
  66.9 0.8 %grad_context.6.refs_2_ = f32[256,1024]{1,0:T(8,128)S(1)} custom-call(bf16[1024,4096]{1,0:T(8,128)(2,1)S(1)} %bitcast.5, bf16[256,512]{1,0:T(8,128)(2,1)S(1)} %collective-permute-done.10.refs_0_, bf16[256,512]{1,0:T(8,128)(2,1)S(1)} %collective-permute-done.12.refs_1_, f32[256,1024]{1,0:T(8,128)S(1)} %grad_context.5.refs_2_), custom_call_target="tpu_custom_call" | custom-call | flops 536870912 | bytes 2490368 | tf_op jit(solution)/shard_map/grad_context/pallas_call | solution.py:31
  67.7 1.3 %collective-permute-done.11.refs_0_ = bf16[256,512]{1,0:T(8,128)(2,1)S(1)} collective-permute-done((bf16[256,512]{1,0:T(8,128)(2,1)S(1)}, bf16[256,512]{1,0:T(8,128)(2,1)S(1)}, u32[]{:S(2)}, u32[]{:S(2)}) %collective-permute-start.11) | collective-permute-done | bytes 262176 | tf_op jit(solution)/shard_map/ppermute | solution.py:267
  69.0 0.2 collective-permute-done.13.refs_1_
  69.2 1.5 %grad_context.7 = bf16[256,1024]{1,0:T(8,128)(2,1)} custom-call(bf16[1024,4096]{1,0:T(8,128)(2,1)S(1)} %bitcast.5, bf16[256,512]{1,0:T(8,128)(2,1)S(1)} %collective-permute-done.11.refs_0_, bf16[256,512]{1,0:T(8,128)(2,1)S(1)} %collective-permute-done.13.refs_1_, f32[256,1024]{1,0:T(8,128)S(1)} %grad_context.6.refs_2_), custom_call_target="tpu_custom_call" | custom-call | flops 536870912 | bytes 2490368 | tf_op jit(solution)/shard_map/grad_context/pallas_call | solution.py:31
  (13 shorter events, 0.0 us)
Async XLA Ops:
  0.6 7.5 %copy-start.1 = (bf16[256,1024]{1,0:T(8,128)(2,1)S(1)}, bf16[256,1024]{1,0:T(8,128)(2,1)}, u32[]{:S(2)}) copy-start(bf16[256,1024]{1,0:T(8,128)(2,1)} %context.7) | copy-start | bytes 1572868
  0.6 16.6 %slice-start = ((s8[8388608]{0:T(1024)(128)(4,1)}), s8[4194304]{0:T(1024)(128)(4,1)S(1)}, s32[]{:S(2)}) async-start(s8[8388608]{0:T(1024)(128)(4,1)} %bitcast.4), calls=%async_computation | async-start | bytes 8388608
  0.7 16.6 %slice-start.1 = ((s8[8388608]{0:T(1024)(128)(4,1)}), s8[4194304]{0:T(1024)(128)(4,1)S(1)}, s32[]{:S(2)}) async-start(s8[8388608]{0:T(1024)(128)(4,1)} %bitcast.4), calls=%async_computation.1 | async-start | bytes 8388608
  3.6 11.5 %collective-permute-start.1 = (bf16[320,512]{1,0:T(8,128)(2,1)S(1)}, bf16[320,512]{1,0:T(8,128)(2,1)S(1)}, u32[]{:S(2)}, u32[]{:S(2)}) collective-permute-start(bf16[320,512]{1,0:T(8,128)(2,1)S(1)} %get-tuple-element.25), channel_id=1, source_target_pairs={{0,1},{1,0},{2,3},{3,2},{4,5},{5,4},{6,7},{7,6},{8,9},{9,8},{10,11... | collective-permute-start | bytes 983048 | tf_op jit(solution)/shard_map/ppermute | solution.py:267
  6.6 10.6 %collective-permute-start.2 = (bf16[320,512]{1,0:T(8,128)(2,1)S(1)}, bf16[320,512]{1,0:T(8,128)(2,1)S(1)}, u32[]{:S(2)}, u32[]{:S(2)}) collective-permute-start(bf16[320,512]{1,0:T(8,128)(2,1)S(1)} %get-tuple-element.26), channel_id=1, source_target_pairs={{0,2},{1,3},{2,0},{3,1},{4,6},{5,7},{6,4},{7,5},{8,10},{9,11},{10,... | collective-permute-start | bytes 983048 | tf_op jit(solution)/shard_map/ppermute | solution.py:267
  8.1 12.0 %copy-start.3 = (bf16[256,1024]{1,0:T(8,128)(2,1)S(1)}, bf16[256,1024]{1,0:T(8,128)(2,1)}, u32[]{:S(2)}) copy-start(bf16[256,1024]{1,0:T(8,128)(2,1)} %residual.1) | copy-start | bytes 1572868
  10.3 11.8 %collective-permute-start = (bf16[320,512]{1,0:T(8,128)(2,1)S(1)}, bf16[320,512]{1,0:T(8,128)(2,1)S(1)}, u32[]{:S(2)}, u32[]{:S(2)}) collective-permute-start(bf16[320,512]{1,0:T(8,128)(2,1)S(1)} %get-tuple-element.24), channel_id=1, source_target_pairs={{0,1},{1,0},{2,3},{3,2},{4,5},{5,4},{6,7},{7,6},{8,9},{9,8},{10,11... | collective-permute-start | bytes 983048 | tf_op jit(solution)/shard_map/ppermute | solution.py:267
  10.9 18.9 %copy-start = (bf16[1024,1024]{1,0:T(8,128)(2,1)S(1)}, bf16[1024,1024]{1,0:T(8,128)(2,1)}, u32[]{:S(2)}) copy-start(bf16[1024,1024]{1,0:T(8,128)(2,1)} %w_in.3) | copy-start | bytes 6291460
  10.9 18.9 %copy-start.4 = (f32[4096]{0:T(1024)S(1)}, f32[4096]{0:T(1024)}, u32[]{:S(2)}) copy-start(f32[4096]{0:T(1024)} %param.11) | copy-start | bytes 49156
  10.9 13.3 %collective-permute-start.4 = (bf16[320,512]{1,0:T(8,128)(2,1)S(1)}, bf16[320,512]{1,0:T(8,128)(2,1)S(1)}, u32[]{:S(2)}, u32[]{:S(2)}) collective-permute-start(bf16[320,512]{1,0:T(8,128)(2,1)S(1)} %get-tuple-element.28), channel_id=1, source_target_pairs={{0,2},{1,3},{2,0},{3,1},{4,6},{5,7},{6,4},{7,5},{8,10},{9,11},{10,... | collective-permute-start | bytes 983048 | tf_op jit(solution)/shard_map/ppermute | solution.py:267
  18.0 11.8 %collective-permute-start.3 = (bf16[320,512]{1,0:T(8,128)(2,1)S(1)}, bf16[320,512]{1,0:T(8,128)(2,1)S(1)}, u32[]{:S(2)}, u32[]{:S(2)}) collective-permute-start(bf16[320,512]{1,0:T(8,128)(2,1)S(1)} %get-tuple-element.27), channel_id=1, source_target_pairs={{0,2},{1,3},{2,0},{3,1},{4,6},{5,7},{6,4},{7,5},{8,10},{9,11},{10,... | collective-permute-start | bytes 983048 | tf_op jit(solution)/shard_map/ppermute | solution.py:267
  19.5 30.4 %copy-start.5 = (f32[1,1024]{1,0:T(1,128)S(1)}, f32[1,1024]{1,0:T(1,128)}, u32[]{:S(2)}) copy-start(f32[1,1024]{1,0:T(1,128)} %gain_depth.1) | copy-start | bytes 12292
  19.6 10.2 %collective-permute-start.5 = (bf16[320,512]{1,0:T(8,128)(2,1)S(1)}, bf16[320,512]{1,0:T(8,128)(2,1)S(1)}, u32[]{:S(2)}, u32[]{:S(2)}) collective-permute-start(bf16[320,512]{1,0:T(8,128)(2,1)S(1)} %get-tuple-element.29), channel_id=1, source_target_pairs={{0,1},{1,0},{2,3},{3,2},{4,5},{5,4},{6,7},{7,6},{8,9},{9,8},{10,11... | collective-permute-start | bytes 983048 | tf_op jit(solution)/shard_map/ppermute | solution.py:267
  20.8 42.6 %copy-start.2 = (bf16[1,1024,512]{2,1,0:T(8,128)(2,1)S(1)}, bf16[1,1024,512]{2,1,0:T(8,128)(2,1)}, u32[]{:S(2)}) copy-start(bf16[1,1024,512]{2,1,0:T(8,128)(2,1)} %param.14) | copy-start | bytes 3145732
  30.6 8.7 %collective-permute-start.6 = (bf16[336,512]{1,0:T(8,128)(2,1)S(1)}, bf16[336,512]{1,0:T(8,128)(2,1)S(1)}, u32[]{:S(2)}, u32[]{:S(2)}) collective-permute-start(bf16[336,512]{1,0:T(8,128)(2,1)S(1)} %get-tuple-element.33.refs_0_), channel_id=1, source_target_pairs={{0,1},{1,0},{2,3},{3,2},{4,5},{5,4},{6,7},{7,6},{8,9},{9,8},{10,11... | collective-permute-start | bytes 1032200 | tf_op jit(solution)/shard_map/ppermute | solution.py:267
  31.0 8.6 %collective-permute-start.7 = (bf16[336,512]{1,0:T(8,128)(2,1)S(1)}, bf16[336,512]{1,0:T(8,128)(2,1)S(1)}, u32[]{:S(2)}, u32[]{:S(2)}) collective-permute-start(bf16[336,512]{1,0:T(8,128)(2,1)S(1)} %get-tuple-element.34.refs_1_), channel_id=1, source_target_pairs={{0,2},{1,3},{2,0},{3,1},{4,6},{5,7},{6,4},{7,5},{8,10},{9,11},{10,... | collective-permute-start | bytes 1032200 | tf_op jit(solution)/shard_map/ppermute | solution.py:267
  39.8 9.2 %collective-permute-start.8 = (bf16[400,512]{1,0:T(8,128)(2,1)S(1)}, bf16[400,512]{1,0:T(8,128)(2,1)S(1)}, u32[]{:S(2)}, u32[]{:S(2)}) collective-permute-start(bf16[400,512]{1,0:T(8,128)(2,1)S(1)} %get-tuple-element.37.refs_0_), channel_id=1, source_target_pairs={{0,2},{1,3},{2,0},{3,1},{4,6},{5,7},{6,4},{7,5},{8,10},{9,11},{10,... | collective-permute-start | bytes 1228808 | tf_op jit(solution)/shard_map/ppermute | solution.py:267
  41.3 8.6 %collective-permute-start.9 = (bf16[400,512]{1,0:T(8,128)(2,1)S(1)}, bf16[400,512]{1,0:T(8,128)(2,1)S(1)}, u32[]{:S(2)}, u32[]{:S(2)}) collective-permute-start(bf16[400,512]{1,0:T(8,128)(2,1)S(1)} %get-tuple-element.38.refs_1_), channel_id=1, source_target_pairs={{0,1},{1,0},{2,3},{3,2},{4,5},{5,4},{6,7},{7,6},{8,9},{9,8},{10,11... | collective-permute-start | bytes 1228808 | tf_op jit(solution)/shard_map/ppermute | solution.py:267
  52.2 9.2 %collective-permute-start.10 = (bf16[256,512]{1,0:T(8,128)(2,1)S(1)}, bf16[256,512]{1,0:T(8,128)(2,1)S(1)}, u32[]{:S(2)}, u32[]{:S(2)}) collective-permute-start(bf16[256,512]{1,0:T(8,128)(2,1)S(1)} %get-tuple-element.41.refs_0_), channel_id=1, source_target_pairs={{0,1},{1,0},{2,3},{3,2},{4,5},{5,4},{6,7},{7,6},{8,9},{9,8},{10,11... | collective-permute-start | bytes 786440 | tf_op jit(solution)/shard_map/ppermute | solution.py:267
  53.6 9.2 %collective-permute-start.12 = (bf16[256,512]{1,0:T(8,128)(2,1)S(1)}, bf16[256,512]{1,0:T(8,128)(2,1)S(1)}, u32[]{:S(2)}, u32[]{:S(2)}) collective-permute-start(bf16[256,512]{1,0:T(8,128)(2,1)S(1)} %get-tuple-element.42.refs_1_), channel_id=1, source_target_pairs={{0,2},{1,3},{2,0},{3,1},{4,6},{5,7},{6,4},{7,5},{8,10},{9,11},{10,... | collective-permute-start | bytes 786440 | tf_op jit(solution)/shard_map/ppermute | solution.py:267
  54.0 12.1 %collective-permute-start.14 = (bf16[256,512]{1,0:T(8,128)(2,1)S(1)}, bf16[256,512]{1,0:T(8,128)(2,1)S(1)}, u32[]{:S(2)}, u32[]{:S(2)}) collective-permute-start(bf16[256,512]{1,0:T(8,128)(2,1)S(1)} %get-tuple-element.41.refs_0_), channel_id=1, source_target_pairs={{0,2},{1,3},{2,0},{3,1},{4,6},{5,7},{6,4},{7,5},{8,10},{9,11},{10,... | collective-permute-start | bytes 786440 | tf_op jit(solution)/shard_map/ppermute | solution.py:267
  55.6 10.6 %collective-permute-start.15 = (bf16[256,512]{1,0:T(8,128)(2,1)S(1)}, bf16[256,512]{1,0:T(8,128)(2,1)S(1)}, u32[]{:S(2)}, u32[]{:S(2)}) collective-permute-start(bf16[256,512]{1,0:T(8,128)(2,1)S(1)} %get-tuple-element.42.refs_1_), channel_id=1, source_target_pairs={{0,1},{1,0},{2,3},{3,2},{4,5},{5,4},{6,7},{7,6},{8,9},{9,8},{10,11... | collective-permute-start | bytes 786440 | tf_op jit(solution)/shard_map/ppermute | solution.py:267
  61.4 7.6 %collective-permute-start.11 = (bf16[256,512]{1,0:T(8,128)(2,1)S(1)}, bf16[256,512]{1,0:T(8,128)(2,1)S(1)}, u32[]{:S(2)}, u32[]{:S(2)}) collective-permute-start(bf16[256,512]{1,0:T(8,128)(2,1)S(1)} %collective-permute-done.10.refs_0_), channel_id=1, source_target_pairs={{0,2},{1,3},{2,0},{3,1},{4,6},{5,7},{6,4},{7,5},{8,10},{9,11},{10,... | collective-permute-start | bytes 786440 | tf_op jit(solution)/shard_map/ppermute | solution.py:267
  62.8 6.4 %collective-permute-start.13 = (bf16[256,512]{1,0:T(8,128)(2,1)S(1)}, bf16[256,512]{1,0:T(8,128)(2,1)S(1)}, u32[]{:S(2)}, u32[]{:S(2)}) collective-permute-start(bf16[256,512]{1,0:T(8,128)(2,1)S(1)} %collective-permute-done.12.refs_1_), channel_id=1, source_target_pairs={{0,1},{1,0},{2,3},{3,2},{4,5},{5,4},{6,7},{7,6},{8,9},{9,8},{10,11... | collective-permute-start | bytes 786440 | tf_op jit(solution)/shard_map/ppermute | solution.py:267

commit v4 on v3

v4 whole, which is shorter than its diff:
```python
import functools

import jax
import jax.numpy as jnp
from jax import lax
from jax.experimental import pallas as pl
from jax.experimental.pallas import tpu as pltpu
from jax.sharding import PartitionSpec as P

EPS = 1e-05
LANES = 128
SQ = 16
bf16, f32 = jnp.bfloat16, jnp.float32
VMEM = pl.BlockSpec(memory_space=pltpu.VMEM)
HBM = pl.BlockSpec(memory_space=pltpu.HBM)

COST = pl.CostEstimate(flops=20 * 10**9, bytes_accessed=60 * 10**6, transcendentals=0)
FREE = pl.CostEstimate(flops=0, bytes_accessed=0, transcendentals=0)


def contract_last(left, right):
    return lax.dot_general(
        left, right, (((1,), (1,)), ((), ())), preferred_element_type=f32
    )


def mirror(mask, log):
    return sum(1 << (log - 1 - i) for i in range(log) if mask >> i & 1)


def call(body, outs, ins, in_specs=None, scratch=(), name=None, out_specs=None, after=None, cost=COST):
    in_specs = in_specs or [VMEM] * len(ins)
    ins = [
        pltpu.with_memory_space_constraint(a, pltpu.HBM) if spec is HBM else a
        for a, spec in zip(ins, in_specs)
    ]
    count = len(ins)
    kernel = body
    if after is not None:
        ins = ins + [after]
        in_specs = in_specs + [pl.BlockSpec(memory_space=pl.ANY)]

        def kernel(*refs):
            body(*refs[:count], *refs[count + 1 :])

    return pl.pallas_call(
        kernel,
        out_shape=[jax.ShapeDtypeStruct(s, d) for s, d in outs],
        in_specs=in_specs,
        out_specs=out_specs or [VMEM] * len(outs),
        scratch_shapes=list(scratch),
        compiler_params=pltpu.CompilerParams(vmem_limit_bytes=16 * 2**20),
        cost_estimate=cost,
        name=name,
    )(*ins)


def put_squares(out, at, squares):
    frames = squares.shape[1]
    high = squares.astype(bf16).astype(f32)
    both = jnp.concatenate([high, squares - high], axis=0).astype(bf16)
    out[at : at + SQ, :frames] = both
    if frames < out.shape[1]:
        out[at : at + SQ, frames:] = jnp.zeros((SQ, out.shape[1] - frames), bf16)


def get_squares(ref, at, frames):
    both = ref[at : at + SQ, :frames].astype(f32)
    return both[: SQ // 2] + both[SQ // 2 :]


def owner(mask):
    return lax.axis_index("mp") ^ mask


def span(start, size):
    return pl.ds(pl.multiple_of(start * size, size), size)


def cols_of(mask, side, half):
    return span(owner(mask) * 2 + side, half)


def put_block(log, share, out, product, up, adds, mask, side):
    frames, half = product.shape
    wide = up.shape[1] // 2
    for add in adds:
        product = product + add[:frames, :].astype(f32)
    out[:frames, :] = product.astype(bf16)
    for c in range(wide // half):
        col = side * wide + c * half
        part = up[span(owner(mask), share), col : col + half]
        rows = slice(frames + c * share, frames + (c + 1) * share)
        for add in adds:
            part = part + add[rows, :].astype(f32)
        out[rows, :] = part.astype(bf16)


def head_kernel(log, share, items, cot, w_depth, gain_hbm, context, w_out, *refs):
    outs, up = refs[: len(items)], refs[len(items)]
    cot_buf, depth_buf, gain_depth, context_buf, buf, sems = refs[len(items) + 1 :]
    half = buf.shape[2]
    pairs = [(cot, cot_buf), (w_depth, depth_buf), (gain_hbm, gain_depth)]
    pairs += [(context, context_buf)]
    for i, (mask, side) in enumerate(items):
        pairs.append((w_out.at[:, cols_of(mask, side, half)], buf.at[i]))
    copies = [pltpu.make_async_copy(a, b, sems.at[i]) for i, (a, b) in enumerate(pairs)]
    for copy in copies:
        copy.start()
    for copy in copies[:3]:
        copy.wait()
    up[...] = gain_depth[...] * contract_last(cot_buf[...], depth_buf[...])
    copies[3].wait()
    for i, (mask, side) in enumerate(items):
        copies[4 + i].wait()
        product = jnp.dot(context_buf[...], buf[i], preferred_element_type=f32)
        put_block(log, share, outs[i], product, up, [], mask, side)


def early_kernel(log, share, items, context, w_out, up, *refs):
    outs, (buf, sems) = refs[: len(items)], refs[len(items) :]
    half = buf.shape[2]
    copies = []
    for i, (mask, side) in enumerate(items):
        cols = cols_of(mask, side, half)
        copies.append(pltpu.make_async_copy(w_out.at[:, cols], buf.at[i], sems.at[i]))
        copies[-1].start()
    for i, (mask, side) in enumerate(items):
        copies[i].wait()
        product = jnp.dot(context[...], buf[i], preferred_element_type=f32)
        put_block(log, share, outs[i], product, up, [], mask, side)


def project_kernel(log, share, items, context, w_out, up, *refs):
    adds, outs = refs[: -len(items)], refs[-len(items) :]
    half = outs[0].shape[1]
    at = 0
    for (mask, side, count), out in zip(items, outs):
        product = jnp.dot(
            context[...], w_out[:, cols_of(mask, side, half)], preferred_element_type=f32
        )
        put_block(log, share, out, product, up, adds[at : at + count], mask, side)
        at += count


def keep_kernel(context, w_out, residual, out):
    out[...] = residual[...].astype(f32) + jnp.dot(
        context[...],
        w_out[:, span(lax.axis_index("mp"), out.shape[1])],
        preferred_element_type=f32,
    )


def state_kernel(log, share, gain, w_in, up, kept, *refs):
    adds, (state, raw, squares, *sends) = refs[: 2 * log], refs[2 * log :]
    frames, width = state.shape
    half = width // 2
    wide = raw.shape[1] // 2
    for side in range(2):
        cols = slice(side * half, (side + 1) * half)
        total = kept[:, cols]
        for add in adds[side * log : (side + 1) * log]:
            total = total + add[:frames, :].astype(f32)
        state[:, cols] = total
    value = state[...]
    gains = gain[:, span(lax.axis_index("mp"), width)]
    raw[...] = jnp.dot((value * gains).astype(bf16), w_in[...], preferred_element_type=f32)
    column = jnp.sum(value * value, axis=1, keepdims=True)
    row = jnp.transpose(jnp.broadcast_to(column, (frames, LANES)))[: SQ // 2]
    for side, send in enumerate(sends):
        squares[side] = row
        send[:frames, :] = raw[:, side * wide : (side + 1) * wide].astype(bf16)
        put_squares(send, frames, row)
        for c in range(wide // half):
            col = side * wide + c * half
            part = up[span(lax.axis_index("mp"), share), col : col + half]
            for add in adds[side * log : (side + 1) * log]:
                at = frames + c * share
                part = part + add[at : at + share, :].astype(f32)
            send[frames + SQ :, c * half : (c + 1) * half] = part.astype(bf16)


def reduce_kernel(raw, squares, *refs):
    sent, got, (raw_out, squares_out, *sends) = refs[:2], refs[2:4], refs[4:]
    frames, depth = raw.shape
    wide = depth // 2
    for side in range(2):
        cols = slice(side * wide, (side + 1) * wide)
        total = raw[:, cols] + got[side][:frames, :].astype(f32)
        raw_out[:, cols] = total
        sends[side][:frames, :] = total.astype(bf16)
        row = squares[side] + get_squares(got[side], frames, frames)
        squares_out[side] = row
        put_squares(sends[side], frames, row)
        first = frames + SQ
        held = sent[side].shape[0] - first
        sends[side][first : first + held, :] = sent[side][first:, :]
        sends[side][first + held :, :] = got[side][first:, :]


def depth_rows(raw, got, rows):
    wide = raw.shape[1] // 2
    return jnp.concatenate(
        [
            raw[rows, side * wide : (side + 1) * wide] + got[side][rows, :].astype(f32)
            for side in range(2)
        ],
        axis=1,
    )


def recip_of(squares, got, frames, features):
    row = squares[0] + get_squares(got[0], frames, frames)
    return jnp.transpose(
        jnp.broadcast_to(lax.rsqrt(row[:1] / features + EPS), (LANES, frames))
    )[:, :1]


def back_kernel(log, haves, share, features, gain, w_in, state, raw, squares, *refs):
    sent, got, (*grads, up, du) = refs[:2], refs[2:4], refs[4:]
    frames, width = state.shape
    half, wide = width // 2, raw.shape[1] // 2
    first = frames + SQ
    for side in range(2):
        held = sent[side].shape[0] - first
        for i, mask in enumerate(haves[side]):
            at = i * share
            ref, at = (sent[side], at) if at < held else (got[side], at - held)
            up[span(owner(mask), share), side * wide : (side + 1) * wide] = ref[
                first + at : first + at + share, :
            ]
    recip = recip_of(squares, got, frames, features)
    back = []
    step = 64 if frames % 64 == 0 else frames
    for at in range(0, frames, step):
        rows = slice(at, at + step)
        depth_in = depth_rows(raw, got, rows) * recip[rows]
        upstream = up[rows, :].astype(f32)
        urecip = lax.rsqrt(jnp.mean(depth_in * depth_in, axis=1, keepdims=True) + EPS)
        inner = jnp.mean(depth_in * upstream, axis=1, keepdims=True)
        part = urecip * upstream - depth_in * (urecip * urecip * urecip * inner)
        part = part.astype(bf16)
        du[rows, :] = part
        dot_du = jnp.sum(part.astype(f32) * depth_in, axis=1, keepdims=True) / recip[rows]
        back.append(recip[rows] * recip[rows] * recip[rows] * (dot_du / features))
    back = jnp.concatenate(back, axis=0)
    gains = gain[:, span(lax.axis_index("mp"), width)]
    for side, grad in enumerate(grads):
        cols = slice(side * half, (side + 1) * half)
        dnormed = contract_last(du[...], w_in[cols, :])
        grad[...] = (recip * (gains[:, cols] * dnormed) - state[:, cols] * back).astype(bf16)


def act_kernel(features, gain_depth, w_depth, raw, squares, *refs):
    got, grads, (out, grad_out, latent) = refs[:2], refs[2:4], refs[4:]
    frames = raw.shape[0]
    half = grads[0].shape[1]
    for side in range(2):
        grad_out[:, side * half : (side + 1) * half] = grads[side][...]
    recip = recip_of(squares, got, frames, features)
    step = 64 if frames % 64 == 0 else frames
    for at in range(0, frames, step):
        rows = slice(at, at + step)
        depth_in = depth_rows(raw, got, rows) * recip[rows]
        urecip = lax.rsqrt(jnp.mean(depth_in * depth_in, axis=1, keepdims=True) + EPS)
        latent[rows, :] = (depth_in * urecip * gain_depth[...]).astype(bf16)
    out[...] = jnp.dot(latent[...], w_depth[...], preferred_element_type=f32).astype(bf16)


def context_kernel(log, items, w_out, *refs):
    blocks, rest, out = refs[: len(items)], refs[len(items) : -1], refs[-1]
    total = rest[0][...]
    for (mask, side), block in zip(items, blocks):
        part = contract_last(block[...], w_out[:, cols_of(mask, side, block.shape[1])])
        total = total + part
    out[...] = total


def own_context_kernel(log, w_out, first, second, out, *copies):
    total = None
    for side, block in enumerate((first, second)):
        half = block.shape[1]
        part = contract_last(block[...], w_out[:, cols_of(0, side, half)])
        total = part if total is None else total + part
        copies[side][...] = block[...]
    out[...] = total


def last_kernel(log, items, w_out, *refs):
    blocks, (total, out, buf, sems) = refs[: len(items)], refs[len(items) :]
    step = total.shape[1] // 2
    copies = []
    for k in range(2):
        rows = slice(k * step, (k + 1) * step)
        value = total[:, rows]
        for (mask, side), block in zip(items, blocks):
            value = value + contract_last(
                block[...], w_out[rows, cols_of(mask, side, block.shape[1])]
            )
        buf[:, rows] = value.astype(bf16)
        copies.append(pltpu.make_async_copy(buf.at[:, rows], out.at[:, rows], sems.at[k]))
        copies[-1].start()
    for copy in copies:
        copy.wait()


def local(n, context, w_out, residual, gain_temporal, w_in, gain_depth, w_depth, cotangent):
    frames, width = residual.shape
    half = width // 2
    share = frames // n
    features = width * n
    heads = w_out.shape[0]
    depth, act = w_depth.shape[1:]
    wide = depth // 2
    log = n.bit_length() - 1
    bits = [1 << i for i in range(log)]
    orders = (bits, bits[::-1])
    gain = gain_temporal[None, :]
    block = ((frames + share * (wide // half), half), bf16)

    def swap(value, bit):
        return lax.ppermute(value, "mp", [(i, i ^ bit) for i in range(n)])

    def phase_of(mask, side):
        return min(i for i, bit in enumerate(orders[side]) if mask & bit)

    masks = sorted(range(1, n), key=lambda k: (-k.bit_count(), k))
    pairs = [((k, 0), (mirror(k, log), 1)) for k in masks]

    arrived = {}
    for pair in pairs:
        adds = [
            [arrived[mask ^ bit, side] for bit in orders[side][: phase_of(mask, side)]]
            for mask, side in pair
        ]
        if pair is pairs[0]:
            *values, up = call(
                functools.partial(head_kernel, log, share, pair),
                [block] * 2 + [((frames, depth), f32)],
                [cotangent[0], w_depth[0], gain_depth, context, w_out],
                [HBM] * 5,
                [
                    pltpu.VMEM((frames, act), bf16),
                    pltpu.VMEM((depth, act), bf16),
                    pltpu.VMEM((1, depth), f32),
                    pltpu.VMEM(context.shape, bf16),
                    pltpu.VMEM((2, heads, half), bf16),
                    pltpu.SemaphoreType.DMA((6,)),
                ],
                name="head",
            )
        elif not adds[0]:
            values = call(
                functools.partial(early_kernel, log, share, pair),
                [block] * 2,
                [context, w_out, up],
                [VMEM, HBM, VMEM],
                [pltpu.VMEM((2, heads, half), bf16), pltpu.SemaphoreType.DMA((2,))],
                name="early",
            )
        else:
            items = [(mask, side, len(a)) for (mask, side), a in zip(pair, adds)]
            values = call(
                functools.partial(project_kernel, log, share, items),
                [block] * 2,
                [context, w_out, up] + adds[0] + adds[1],
                name="project",
            )
        for (mask, side), value in zip(pair, values):
            arrived[mask, side] = swap(value, orders[side][phase_of(mask, side)])
    kept = call(
        keep_kernel,
        [((frames, width), f32)],
        [context, w_out, residual],
        name="keep",
        after=values[0],
    )[0]

    state, raw, squares, *sends = call(
        functools.partial(state_kernel, log, share),
        [((frames, width), f32), ((frames, depth), f32), ((2, SQ // 2, frames), f32)]
        + [((frames + SQ + share, wide), bf16)] * 2,
        [gain, w_in, up, kept] + [arrived[bit, side] for side in range(2) for bit in orders[side]],
        name="state",
    )
    haves = [[0], [0]]
    for i in range(log):
        got = [swap(sends[side], orders[side][i]) for side in range(2)]
        haves = [have + [k ^ orders[s][i] for k in have] for s, have in enumerate(haves)]
        if i < log - 1:
            raw, squares, *sends = call(
                reduce_kernel,
                [(raw.shape, f32), (squares.shape, f32)]
                + [((frames + SQ + share * len(haves[0]), wide), bf16)] * 2,
                [raw, squares] + list(sends) + got,
                name="reduce",
            )
    grads = call(
        functools.partial(back_kernel, log, haves, share, features),
        [((frames, half), bf16)] * 2,
        [gain, w_in, state, raw, squares] + list(sends) + got,
        scratch=[pltpu.VMEM((frames, depth), bf16)] * 2,
        name="back",
    )

    total, *again = call(
        functools.partial(own_context_kernel, log),
        [((frames, heads), f32)] + [((frames, half), bf16)] * 2,
        [w_out] + list(grads),
        name="grad_context",
    )
    blocks = {(0, side): grads[side] for side in range(2)}
    for i in range(log):
        for k in range(1 << i):
            for side, order in enumerate(orders):
                mask = haves[side][k]
                value = again[side] if i and not k else blocks[mask, side]
                blocks[mask ^ order[i], side] = swap(value, order[i])

    depth_act, grad_residual = call(
        functools.partial(act_kernel, features),
        [((frames, act), bf16), ((frames, width), bf16)],
        [gain_depth, w_depth[0], raw, squares] + got + list(grads),
        scratch=[pltpu.VMEM((frames, depth), bf16)],
        name="act",
    )
    keys = [((haves[0][k], 0), (haves[1][k], 1)) for k in range(n)]
    for pair in keys[1:-1]:
        total = call(
            functools.partial(context_kernel, log, pair),
            [((frames, heads), f32)],
            [w_out] + [blocks[key] for key in pair] + [total],
            name="grad_context",
        )[0]
    grad_context = call(
        functools.partial(last_kernel, log, keys[-1]),
        [((frames, heads), bf16)],
        [w_out] + [blocks[key] for key in keys[-1]] + [total],
        scratch=[pltpu.VMEM((frames, heads), bf16), pltpu.SemaphoreType.DMA((2,))],
        name="grad_context",
        out_specs=[HBM],
    )[0]
    return (depth_act[None], grad_residual, grad_context)


def solution(mesh):
    in_specs = (
        P("dp", "mp"),
        P("mp", None),
        P("dp", "mp"),
        P(),
        P("mp", None),
        P("mp", None),
        P("mp", None, None),
        P("mp", "dp", None),
    )
    out_specs = (P("mp", "dp", None), P("dp", "mp"), P("dp", "mp"))
    n = mesh.shape["mp"]

    def run(*args):
        return local(n, *args)

    return jax.shard_map(run, mesh=mesh, in_specs=in_specs, out_specs=out_specs, check_vma=False)
```

time: 70.9 us -> 69.9 us (0.986)
  transfers between devices with their start and end apart: 16 -> 16, of which waited for: 14 -> 15; matrix products, arithmetic and copies ran while one was open for 0% -> 0% of each run, Pallas kernels for 10% -> 11%
where the time goes in v4:
time: 69.9 us; the launch traced here: 69.8 us
  waiting for transfers between devices  36.6 us (52%)
  starting transfers between devices  18.3 us (26%)
  Pallas kernels  14 us (20%)
  between operations  0.74 us (1%)
    ppermute x16, waiting for transfers between devices, swap(): return lax.ppermute(value, 'mp', [(i, i ^ bit) for i in range(n)])  36.6 us
    ppermute x16, starting transfers between devices, swap(): return lax.ppermute(value, 'mp', [(i, i ^ bit) for i in range(n)])  18.3 us
    pallas_call x12, Pallas kernels, call(): pl.pallas_call(kernel, out_shape=[jax.ShapeDtypeStruct(s, d) for s, d in...  14 us
  transfers between devices with their start and end apart: 16, of which 15 were waited for; matrix products, arithmetic and copies ran while one was open for 0% of the time, Pallas kernels for 11%

profile of v4, /device:TPU:0, one launch (start us, length us, event | category | flops | bytes accessed | tf_op | source)
XLA Modules:
  0.0 69.8 jit_solution(11984196581921508500)
XLA Ops:
  0.6 0.0 copy-start.2
  0.6 0.0 slice-start
  0.7 2.9 %head.1 = (bf16[320,512]{1,0:T(8,128)(2,1)S(1)}, bf16[320,512]{1,0:T(8,128)(2,1)S(1)}, f32[256,1024]{1,0:T(8,128)S(1)}) custom-call(bf16[256,512]{1,0:T(8,128)(2,1)} %bitcast.10, bf16[1024,512]{1,0:T(8,128)(2,1)} %bitcast.6, f32[1,1024]{1,0:T(1,128)} %gain_depth.1, bf16[256,1024]{1,0:T(8,128)(2,1)} %context.5, bf16[1024,4096]{1,0:T(8,128)(2,1)} %w_out.13), custom_call_target="tpu_custom_call" | custom-call | flops 20000000000 | bytes 60000000 | tf_op jit(solution)/shard_map/head/pallas_call | solution.py:46
  3.5 3.0 %collective-permute-start = (bf16[320,512]{1,0:T(8,128)(2,1)S(1)}, bf16[320,512]{1,0:T(8,128)(2,1)S(1)}, u32[]{:S(2)}, u32[]{:S(2)}) collective-permute-start(bf16[320,512]{1,0:T(8,128)(2,1)S(1)} %get-tuple-element.27), channel_id=1, source_target_pairs={{0,1},{1,0},{2,3},{3,2},{4,5},{5,4},{6,7},{7,6},{8,9},{9,8},{10,11... | collective-permute-start | bytes 983048 | tf_op jit(solution)/shard_map/ppermute | solution.py:322
  6.5 1.5 %collective-permute-start.1 = (bf16[320,512]{1,0:T(8,128)(2,1)S(1)}, bf16[320,512]{1,0:T(8,128)(2,1)S(1)}, u32[]{:S(2)}, u32[]{:S(2)}) collective-permute-start(bf16[320,512]{1,0:T(8,128)(2,1)S(1)} %get-tuple-element.28), channel_id=1, source_target_pairs={{0,2},{1,3},{2,0},{3,1},{4,6},{5,7},{6,4},{7,5},{8,10},{9,11},{10,... | collective-permute-start | bytes 983048 | tf_op jit(solution)/shard_map/ppermute | solution.py:322
  8.1 2.1 %early.1 = (bf16[320,512]{1,0:T(8,128)(2,1)S(1)}, bf16[320,512]{1,0:T(8,128)(2,1)S(1)}) custom-call(bf16[256,1024]{1,0:T(8,128)(2,1)S(1)} %copy-done.2, bf16[1024,4096]{1,0:T(8,128)(2,1)} %w_out.13, f32[256,1024]{1,0:T(8,128)S(1)} %get-tuple-element.26.up), custom_call_target="tpu_custom_call" | custom-call | flops 20000000000 | bytes 60000000 | tf_op jit(solution)/shard_map/early/pallas_call | solution.py:46
  10.2 0.6 collective-permute-start.2
  10.8 0.3 collective-permute-start.4
  11.1 4.0 %collective-permute-done.refs_0_ = bf16[320,512]{1,0:T(8,128)(2,1)S(1)} collective-permute-done((bf16[320,512]{1,0:T(8,128)(2,1)S(1)}, bf16[320,512]{1,0:T(8,128)(2,1)S(1)}, u32[]{:S(2)}, u32[]{:S(2)}) %collective-permute-start) | collective-permute-done | bytes 327712 | tf_op jit(solution)/shard_map/ppermute | solution.py:322
  15.1 2.1 %collective-permute-done.1.refs_1_ = bf16[320,512]{1,0:T(8,128)(2,1)S(1)} collective-permute-done((bf16[320,512]{1,0:T(8,128)(2,1)S(1)}, bf16[320,512]{1,0:T(8,128)(2,1)S(1)}, u32[]{:S(2)}, u32[]{:S(2)}) %collective-permute-start.1) | collective-permute-done | bytes 327712 | tf_op jit(solution)/shard_map/ppermute | solution.py:322
  17.2 0.0 slice-done.1
  17.2 0.8 %project.1 = (bf16[320,512]{1,0:T(8,128)(2,1)S(1)}, bf16[320,512]{1,0:T(8,128)(2,1)S(1)}) custom-call(bf16[256,1024]{1,0:T(8,128)(2,1)S(1)} %copy-done.2, bf16[1024,4096]{1,0:T(8,128)(2,1)S(1)} %bitcast.5, f32[256,1024]{1,0:T(8,128)S(1)} %get-tuple-element.26.up, bf16[320,512]{1,0:T(8,128)(2,1)S(1)} %collective-permute-done.refs_0_, ...), custom_call_target="tpu_custom_call" | custom-call | flops 20000000000 | bytes 60000000 | tf_op jit(solution)/shard_map/project/pallas_call | solution.py:46
  18.0 0.1 collective-permute-start.5
  18.1 2.0 %collective-permute-start.3 = (bf16[320,512]{1,0:T(8,128)(2,1)S(1)}, bf16[320,512]{1,0:T(8,128)(2,1)S(1)}, u32[]{:S(2)}, u32[]{:S(2)}) collective-permute-start(bf16[320,512]{1,0:T(8,128)(2,1)S(1)} %get-tuple-element.29.refs_3_), channel_id=1, source_target_pairs={{0,2},{1,3},{2,0},{3,1},{4,6},{5,7},{6,4},{7,5},{8,10},{9,11},{10,... | collective-permute-start | bytes 983048 | tf_op jit(solution)/shard_map/ppermute | solution.py:322
  20.1 0.7 %keep.1.kept = f32[256,1024]{1,0:T(8,128)S(1)} custom-call(bf16[256,1024]{1,0:T(8,128)(2,1)S(1)} %copy-done.2, bf16[1024,4096]{1,0:T(8,128)(2,1)S(1)} %bitcast.5, bf16[256,1024]{1,0:T(8,128)(2,1)S(1)} %copy-done.3, bf16[320,512]{1,0:T(8,128)(2,1)S(1)} %get-tuple-element.29.refs_3_), custom_call_target="tpu_custom_call" | custom-call | flops 20000000000 | bytes 60000000 | tf_op jit(solution)/shard_map/keep/pallas_call | solution.py:46
  20.8 1.3 %collective-permute-done.2.refs_0_ = bf16[320,512]{1,0:T(8,128)(2,1)S(1)} collective-permute-done((bf16[320,512]{1,0:T(8,128)(2,1)S(1)}, bf16[320,512]{1,0:T(8,128)(2,1)S(1)}, u32[]{:S(2)}, u32[]{:S(2)}) %collective-permute-start.2) | collective-permute-done | bytes 327712 | tf_op jit(solution)/shard_map/ppermute | solution.py:322
  22.1 2.1 %collective-permute-done.4.refs_2_ = bf16[320,512]{1,0:T(8,128)(2,1)S(1)} collective-permute-done((bf16[320,512]{1,0:T(8,128)(2,1)S(1)}, bf16[320,512]{1,0:T(8,128)(2,1)S(1)}, u32[]{:S(2)}, u32[]{:S(2)}) %collective-permute-start.4) | collective-permute-done | bytes 327712 | tf_op jit(solution)/shard_map/ppermute | solution.py:322
  24.2 4.1 %collective-permute-done.5.refs_3_ = bf16[320,512]{1,0:T(8,128)(2,1)S(1)} collective-permute-done((bf16[320,512]{1,0:T(8,128)(2,1)S(1)}, bf16[320,512]{1,0:T(8,128)(2,1)S(1)}, u32[]{:S(2)}, u32[]{:S(2)}) %collective-permute-start.5) | collective-permute-done | bytes 327712 | tf_op jit(solution)/shard_map/ppermute | solution.py:322
  28.3 1.5 %collective-permute-done.3.refs_1_ = bf16[320,512]{1,0:T(8,128)(2,1)S(1)} collective-permute-done((bf16[320,512]{1,0:T(8,128)(2,1)S(1)}, bf16[320,512]{1,0:T(8,128)(2,1)S(1)}, u32[]{:S(2)}, u32[]{:S(2)}) %collective-permute-start.3) | collective-permute-done | bytes 327712 | tf_op jit(solution)/shard_map/ppermute | solution.py:322
  29.8 0.0 copy-done
  29.8 0.8 %state.1 = (f32[256,1024]{1,0:T(8,128)S(1)}, f32[256,1024]{1,0:T(8,128)S(1)}, f32[2,8,256]{2,1,0:T(8,128)S(1)}, bf16[336,512]{1,0:T(8,128)(2,1)S(1)}, bf16[336,512]{1,0:T(8,128)(2,1)S(1)}) custom-call(f32[1,4096]{1,0:T(1,128)S(1)} %bitcast.8, bf16[1024,1024]{1,0:T(8,128)(2,1)S(1)} %copy-done, f32[256,1024]{1,0:T(8,128)S(1)} %get-tuple-element.26.up, ...), custom_call_target="tpu_custom_call" | custom-call | flops 20000000000 | bytes 60000000 | tf_op jit(solution)/shard_map/state/pallas_call | solution.py:46
  30.6 0.5 collective-permute-start.6
  31.0 1.7 %collective-permute-start.7 = (bf16[336,512]{1,0:T(8,128)(2,1)S(1)}, bf16[336,512]{1,0:T(8,128)(2,1)S(1)}, u32[]{:S(2)}, u32[]{:S(2)}) collective-permute-start(bf16[336,512]{1,0:T(8,128)(2,1)S(1)} %get-tuple-element.36.refs_1_), channel_id=1, source_target_pairs={{0,2},{1,3},{2,0},{3,1},{4,6},{5,7},{6,4},{7,5},{8,10},{9,11},{10,... | collective-permute-start | bytes 1032200 | tf_op jit(solution)/shard_map/ppermute | solution.py:322
  32.7 6.6 %collective-permute-done.6.refs_2_ = bf16[336,512]{1,0:T(8,128)(2,1)S(1)} collective-permute-done((bf16[336,512]{1,0:T(8,128)(2,1)S(1)}, bf16[336,512]{1,0:T(8,128)(2,1)S(1)}, u32[]{:S(2)}, u32[]{:S(2)}) %collective-permute-start.6) | collective-permute-done | bytes 344096 | tf_op jit(solution)/shard_map/ppermute | solution.py:322
  39.2 0.4 collective-permute-done.7.refs_3_
  39.7 0.2 reduce.1
  39.8 1.5 %collective-permute-start.8 = (bf16[400,512]{1,0:T(8,128)(2,1)S(1)}, bf16[400,512]{1,0:T(8,128)(2,1)S(1)}, u32[]{:S(2)}, u32[]{:S(2)}) collective-permute-start(bf16[400,512]{1,0:T(8,128)(2,1)S(1)} %get-tuple-element.39.refs_0_), channel_id=1, source_target_pairs={{0,2},{1,3},{2,0},{3,1},{4,6},{5,7},{6,4},{7,5},{8,10},{9,11},{10,... | collective-permute-start | bytes 1228808 | tf_op jit(solution)/shard_map/ppermute | solution.py:322
  41.3 1.4 %collective-permute-start.9 = (bf16[400,512]{1,0:T(8,128)(2,1)S(1)}, bf16[400,512]{1,0:T(8,128)(2,1)S(1)}, u32[]{:S(2)}, u32[]{:S(2)}) collective-permute-start(bf16[400,512]{1,0:T(8,128)(2,1)S(1)} %get-tuple-element.40.refs_1_), channel_id=1, source_target_pairs={{0,1},{1,0},{2,3},{3,2},{4,5},{5,4},{6,7},{7,6},{8,9},{9,8},{10,11... | collective-permute-start | bytes 1228808 | tf_op jit(solution)/shard_map/ppermute | solution.py:322
  42.7 6.3 %collective-permute-done.8.refs_2_.refs_0_ = bf16[400,512]{1,0:T(8,128)(2,1)S(1)} collective-permute-done((bf16[400,512]{1,0:T(8,128)(2,1)S(1)}, bf16[400,512]{1,0:T(8,128)(2,1)S(1)}, u32[]{:S(2)}, u32[]{:S(2)}) %collective-permute-start.8) | collective-permute-done | bytes 409632 | tf_op jit(solution)/shard_map/ppermute | solution.py:322
  49.0 0.9 %collective-permute-done.9.refs_3_.refs_1_ = bf16[400,512]{1,0:T(8,128)(2,1)S(1)} collective-permute-done((bf16[400,512]{1,0:T(8,128)(2,1)S(1)}, bf16[400,512]{1,0:T(8,128)(2,1)S(1)}, u32[]{:S(2)}, u32[]{:S(2)}) %collective-permute-start.9) | collective-permute-done | bytes 409632 | tf_op jit(solution)/shard_map/ppermute | solution.py:322
  49.9 1.3 %back.1 = (bf16[256,512]{1,0:T(8,128)(2,1)S(1)}, bf16[256,512]{1,0:T(8,128)(2,1)S(1)}) custom-call(f32[1,4096]{1,0:T(1,128)S(1)} %bitcast.9, bf16[1024,1024]{1,0:T(8,128)(2,1)S(1)} %copy-done, f32[256,1024]{1,0:T(8,128)S(1)} %get-tuple-element.41.state, f32[256,1024]{1,0:T(8,128)S(1)} %get-tuple-element.37.raw, f32[2,8,256]{2,1,0:T(8,128)S(1)} %get-tuple-element.38.squares, ...), custom_call_target="tpu_custom_call" | custom-call | flops 20000000000 | bytes 60000000 | tf_op jit(solution)/shard_map/back/pallas_call | solution.py:46
  51.2 1.4 %collective-permute-start.10 = (bf16[256,512]{1,0:T(8,128)(2,1)S(1)}, bf16[256,512]{1,0:T(8,128)(2,1)S(1)}, u32[]{:S(2)}, u32[]{:S(2)}) collective-permute-start(bf16[256,512]{1,0:T(8,128)(2,1)S(1)} %get-tuple-element.42.refs_2_.first), channel_id=1, source_target_pairs={{0,1},{1,0},{2,3},{3,2},{4,5},{5,4},{6,7},{7,6},{8,9},{9,8},{10,11... | collective-permute-start | bytes 786440 | tf_op jit(solution)/shard_map/ppermute | solution.py:322
  52.7 0.5 collective-permute-start.12
  53.2 0.7 %grad_context.4 = (f32[256,1024]{1,0:T(8,128)S(1)}, bf16[256,512]{1,0:T(8,128)(2,1)S(1)}, bf16[256,512]{1,0:T(8,128)(2,1)S(1)}) custom-call(bf16[1024,4096]{1,0:T(8,128)(2,1)S(1)} %bitcast.5, bf16[256,512]{1,0:T(8,128)(2,1)S(1)} %get-tuple-element.42.refs_2_.first, bf16[256,512]{1,0:T(8,128)(2,1)S(1)} %get-tuple-element.43.refs_3_.second), custom_call_target="tpu_custom_call" | custom-call | flops 20000000000 | bytes 60000000 | tf_op jit(solution)/shard_map/grad_context/pallas_call | solution.py:46
  53.9 1.6 %collective-permute-start.14 = (bf16[256,512]{1,0:T(8,128)(2,1)S(1)}, bf16[256,512]{1,0:T(8,128)(2,1)S(1)}, u32[]{:S(2)}, u32[]{:S(2)}) collective-permute-start(bf16[256,512]{1,0:T(8,128)(2,1)S(1)} %get-tuple-element.46), channel_id=1, source_target_pairs={{0,2},{1,3},{2,0},{3,1},{4,6},{5,7},{6,4},{7,5},{8,10},{9,11},{10,... | collective-permute-start | bytes 786440 | tf_op jit(solution)/shard_map/ppermute | solution.py:322
  55.5 0.7 collective-permute-start.15
  56.2 1.6 %act.1 = (bf16[256,512]{1,0:T(8,128)(2,1)}, bf16[256,1024]{1,0:T(8,128)(2,1)}) custom-call(f32[1,1024]{1,0:T(1,128)S(1)} %copy-done.5, bf16[1024,512]{1,0:T(8,128)(2,1)S(1)} %bitcast.7, f32[256,1024]{1,0:T(8,128)S(1)} %get-tuple-element.37.raw, f32[2,8,256]{2,1,0:T(8,128)S(1)} %get-tuple-element.38.squares, ...), custom_call_target="tpu_custom_call" | custom-call | flops 20000000000 | bytes 60000000 | tf_op jit(solution)/shard_map/act/pallas_call | solution.py:46
  57.8 2.8 %collective-permute-done.10.refs_0_ = bf16[256,512]{1,0:T(8,128)(2,1)S(1)} collective-permute-done((bf16[256,512]{1,0:T(8,128)(2,1)S(1)}, bf16[256,512]{1,0:T(8,128)(2,1)S(1)}, u32[]{:S(2)}, u32[]{:S(2)}) %collective-permute-start.10) | collective-permute-done | bytes 262176 | tf_op jit(solution)/shard_map/ppermute | solution.py:322
  60.5 0.9 %collective-permute-start.11 = (bf16[256,512]{1,0:T(8,128)(2,1)S(1)}, bf16[256,512]{1,0:T(8,128)(2,1)S(1)}, u32[]{:S(2)}, u32[]{:S(2)}) collective-permute-start(bf16[256,512]{1,0:T(8,128)(2,1)S(1)} %collective-permute-done.10.refs_0_), channel_id=1, source_target_pairs={{0,2},{1,3},{2,0},{3,1},{4,6},{5,7},{6,4},{7,5},{8,10},{9,11},{10,... | collective-permute-start | bytes 786440 | tf_op jit(solution)/shard_map/ppermute | solution.py:322
  61.4 0.5 collective-permute-done.12.refs_1_
  61.9 0.7 collective-permute-start.13
  62.6 0.7 %grad_context.5.refs_2_ = f32[256,1024]{1,0:T(8,128)S(1)} custom-call(bf16[1024,4096]{1,0:T(8,128)(2,1)S(1)} %bitcast.5, bf16[256,512]{1,0:T(8,128)(2,1)S(1)} %collective-permute-done.10.refs_0_, bf16[256,512]{1,0:T(8,128)(2,1)S(1)} %collective-permute-done.12.refs_1_, f32[256,1024]{1,0:T(8,128)S(1)} %get-tuple-element.48.refs_2_), custom_call_target="tpu_custom_call" | custom-call | flops 20000000000 | bytes 60000000 | tf_op jit(solution)/shard_map/grad_context/pallas_call | solution.py:46
  63.3 1.9 %collective-permute-done.14.refs_0_ = bf16[256,512]{1,0:T(8,128)(2,1)S(1)} collective-permute-done((bf16[256,512]{1,0:T(8,128)(2,1)S(1)}, bf16[256,512]{1,0:T(8,128)(2,1)S(1)}, u32[]{:S(2)}, u32[]{:S(2)}) %collective-permute-start.14) | collective-permute-done | bytes 262176 | tf_op jit(solution)/shard_map/ppermute | solution.py:322
  65.2 0.0 collective-permute-done.15.refs_1_
  65.2 0.7 %grad_context.6.refs_2_ = f32[256,1024]{1,0:T(8,128)S(1)} custom-call(bf16[1024,4096]{1,0:T(8,128)(2,1)S(1)} %bitcast.5, bf16[256,512]{1,0:T(8,128)(2,1)S(1)} %collective-permute-done.14.refs_0_, bf16[256,512]{1,0:T(8,128)(2,1)S(1)} %collective-permute-done.15.refs_1_, f32[256,1024]{1,0:T(8,128)S(1)} %grad_context.5.refs_2_), custom_call_target="tpu_custom_call" | custom-call | flops 20000000000 | bytes 60000000 | tf_op jit(solution)/shard_map/grad_context/pallas_call | solution.py:46
  66.0 2.0 %collective-permute-done.11.refs_0_ = bf16[256,512]{1,0:T(8,128)(2,1)S(1)} collective-permute-done((bf16[256,512]{1,0:T(8,128)(2,1)S(1)}, bf16[256,512]{1,0:T(8,128)(2,1)S(1)}, u32[]{:S(2)}, u32[]{:S(2)}) %collective-permute-start.11) | collective-permute-done | bytes 262176 | tf_op jit(solution)/shard_map/ppermute | solution.py:322
  68.1 0.2 collective-permute-done.13.refs_1_
  68.3 1.5 %grad_context.7 = bf16[256,1024]{1,0:T(8,128)(2,1)} custom-call(bf16[1024,4096]{1,0:T(8,128)(2,1)S(1)} %bitcast.5, bf16[256,512]{1,0:T(8,128)(2,1)S(1)} %collective-permute-done.11.refs_0_, bf16[256,512]{1,0:T(8,128)(2,1)S(1)} %collective-permute-done.13.refs_1_, f32[256,1024]{1,0:T(8,128)S(1)} %grad_context.6.refs_2_), custom_call_target="tpu_custom_call" | custom-call | flops 20000000000 | bytes 60000000 | tf_op jit(solution)/shard_map/grad_context/pallas_call | solution.py:46
  (13 shorter events, 0.0 us)
Async XLA Ops:
  0.6 7.4 %copy-start.2 = (bf16[256,1024]{1,0:T(8,128)(2,1)S(1)}, bf16[256,1024]{1,0:T(8,128)(2,1)}, u32[]{:S(2)}) copy-start(bf16[256,1024]{1,0:T(8,128)(2,1)} %context.5) | copy-start | bytes 1572868
  0.6 16.5 %slice-start = ((s8[8388608]{0:T(1024)(128)(4,1)}), s8[4194304]{0:T(1024)(128)(4,1)S(1)}, s32[]{:S(2)}) async-start(s8[8388608]{0:T(1024)(128)(4,1)} %bitcast.4), calls=%async_computation | async-start | bytes 8388608
  3.5 11.5 %collective-permute-start = (bf16[320,512]{1,0:T(8,128)(2,1)S(1)}, bf16[320,512]{1,0:T(8,128)(2,1)S(1)}, u32[]{:S(2)}, u32[]{:S(2)}) collective-permute-start(bf16[320,512]{1,0:T(8,128)(2,1)S(1)} %get-tuple-element.27), channel_id=1, source_target_pairs={{0,1},{1,0},{2,3},{3,2},{4,5},{5,4},{6,7},{7,6},{8,9},{9,8},{10,11... | collective-permute-start | bytes 983048 | tf_op jit(solution)/shard_map/ppermute | solution.py:322
  6.5 10.6 %slice-start.1 = ((s8[8388608]{0:T(1024)(128)(4,1)}), s8[4194304]{0:T(1024)(128)(4,1)S(1)}, s32[]{:S(2)}) async-start(s8[8388608]{0:T(1024)(128)(4,1)} %bitcast.4), calls=%async_computation.1 | async-start | bytes 8388608
  6.5 10.6 %collective-permute-start.1 = (bf16[320,512]{1,0:T(8,128)(2,1)S(1)}, bf16[320,512]{1,0:T(8,128)(2,1)S(1)}, u32[]{:S(2)}, u32[]{:S(2)}) collective-permute-start(bf16[320,512]{1,0:T(8,128)(2,1)S(1)} %get-tuple-element.28), channel_id=1, source_target_pairs={{0,2},{1,3},{2,0},{3,1},{4,6},{5,7},{6,4},{7,5},{8,10},{9,11},{10,... | collective-permute-start | bytes 983048 | tf_op jit(solution)/shard_map/ppermute | solution.py:322
  10.2 11.9 %collective-permute-start.2 = (bf16[320,512]{1,0:T(8,128)(2,1)S(1)}, bf16[320,512]{1,0:T(8,128)(2,1)S(1)}, u32[]{:S(2)}, u32[]{:S(2)}) collective-permute-start(bf16[320,512]{1,0:T(8,128)(2,1)S(1)} %get-tuple-element.30), channel_id=1, source_target_pairs={{0,1},{1,0},{2,3},{3,2},{4,5},{5,4},{6,7},{7,6},{8,9},{9,8},{10,11... | collective-permute-start | bytes 983048 | tf_op jit(solution)/shard_map/ppermute | solution.py:322
  10.8 9.3 %copy-start.3 = (bf16[256,1024]{1,0:T(8,128)(2,1)S(1)}, bf16[256,1024]{1,0:T(8,128)(2,1)}, u32[]{:S(2)}) copy-start(bf16[256,1024]{1,0:T(8,128)(2,1)} %refs_2_.1) | copy-start | bytes 1572868
  10.8 13.4 %collective-permute-start.4 = (bf16[320,512]{1,0:T(8,128)(2,1)S(1)}, bf16[320,512]{1,0:T(8,128)(2,1)S(1)}, u32[]{:S(2)}, u32[]{:S(2)}) collective-permute-start(bf16[320,512]{1,0:T(8,128)(2,1)S(1)} %get-tuple-element.31), channel_id=1, source_target_pairs={{0,2},{1,3},{2,0},{3,1},{4,6},{5,7},{6,4},{7,5},{8,10},{9,11},{10,... | collective-permute-start | bytes 983048 | tf_op jit(solution)/shard_map/ppermute | solution.py:322
  18.0 10.3 %collective-permute-start.5 = (bf16[320,512]{1,0:T(8,128)(2,1)S(1)}, bf16[320,512]{1,0:T(8,128)(2,1)S(1)}, u32[]{:S(2)}, u32[]{:S(2)}) collective-permute-start(bf16[320,512]{1,0:T(8,128)(2,1)S(1)} %get-tuple-element.32), channel_id=1, source_target_pairs={{0,1},{1,0},{2,3},{3,2},{4,5},{5,4},{6,7},{7,6},{8,9},{9,8},{10,11... | collective-permute-start | bytes 983048 | tf_op jit(solution)/shard_map/ppermute | solution.py:322
  18.1 11.7 %copy-start = (bf16[1024,1024]{1,0:T(8,128)(2,1)S(1)}, bf16[1024,1024]{1,0:T(8,128)(2,1)}, u32[]{:S(2)}) copy-start(bf16[1024,1024]{1,0:T(8,128)(2,1)} %w_in.3) | copy-start | bytes 6291460
  18.1 11.7 %copy-start.4 = (f32[4096]{0:T(1024)S(1)}, f32[4096]{0:T(1024)}, u32[]{:S(2)}) copy-start(f32[4096]{0:T(1024)} %param.11) | copy-start | bytes 49156
  18.1 11.7 %collective-permute-start.3 = (bf16[320,512]{1,0:T(8,128)(2,1)S(1)}, bf16[320,512]{1,0:T(8,128)(2,1)S(1)}, u32[]{:S(2)}, u32[]{:S(2)}) collective-permute-start(bf16[320,512]{1,0:T(8,128)(2,1)S(1)} %get-tuple-element.29.refs_3_), channel_id=1, source_target_pairs={{0,2},{1,3},{2,0},{3,1},{4,6},{5,7},{6,4},{7,5},{8,10},{9,11},{10,... | collective-permute-start | bytes 983048 | tf_op jit(solution)/shard_map/ppermute | solution.py:322
  30.6 8.7 %collective-permute-start.6 = (bf16[336,512]{1,0:T(8,128)(2,1)S(1)}, bf16[336,512]{1,0:T(8,128)(2,1)S(1)}, u32[]{:S(2)}, u32[]{:S(2)}) collective-permute-start(bf16[336,512]{1,0:T(8,128)(2,1)S(1)} %get-tuple-element.35.refs_0_), channel_id=1, source_target_pairs={{0,1},{1,0},{2,3},{3,2},{4,5},{5,4},{6,7},{7,6},{8,9},{9,8},{10,11... | collective-permute-start | bytes 1032200 | tf_op jit(solution)/shard_map/ppermute | solution.py:322
  31.0 8.7 %collective-permute-start.7 = (bf16[336,512]{1,0:T(8,128)(2,1)S(1)}, bf16[336,512]{1,0:T(8,128)(2,1)S(1)}, u32[]{:S(2)}, u32[]{:S(2)}) collective-permute-start(bf16[336,512]{1,0:T(8,128)(2,1)S(1)} %get-tuple-element.36.refs_1_), channel_id=1, source_target_pairs={{0,2},{1,3},{2,0},{3,1},{4,6},{5,7},{6,4},{7,5},{8,10},{9,11},{10,... | collective-permute-start | bytes 1032200 | tf_op jit(solution)/shard_map/ppermute | solution.py:322
  39.8 9.2 %collective-permute-start.8 = (bf16[400,512]{1,0:T(8,128)(2,1)S(1)}, bf16[400,512]{1,0:T(8,128)(2,1)S(1)}, u32[]{:S(2)}, u32[]{:S(2)}) collective-permute-start(bf16[400,512]{1,0:T(8,128)(2,1)S(1)} %get-tuple-element.39.refs_0_), channel_id=1, source_target_pairs={{0,2},{1,3},{2,0},{3,1},{4,6},{5,7},{6,4},{7,5},{8,10},{9,11},{10,... | collective-permute-start | bytes 1228808 | tf_op jit(solution)/shard_map/ppermute | solution.py:322
  41.3 8.6 %collective-permute-start.9 = (bf16[400,512]{1,0:T(8,128)(2,1)S(1)}, bf16[400,512]{1,0:T(8,128)(2,1)S(1)}, u32[]{:S(2)}, u32[]{:S(2)}) collective-permute-start(bf16[400,512]{1,0:T(8,128)(2,1)S(1)} %get-tuple-element.40.refs_1_), channel_id=1, source_target_pairs={{0,1},{1,0},{2,3},{3,2},{4,5},{5,4},{6,7},{7,6},{8,9},{9,8},{10,11... | collective-permute-start | bytes 1228808 | tf_op jit(solution)/shard_map/ppermute | solution.py:322
  51.2 9.3 %collective-permute-start.10 = (bf16[256,512]{1,0:T(8,128)(2,1)S(1)}, bf16[256,512]{1,0:T(8,128)(2,1)S(1)}, u32[]{:S(2)}, u32[]{:S(2)}) collective-permute-start(bf16[256,512]{1,0:T(8,128)(2,1)S(1)} %get-tuple-element.42.refs_2_.first), channel_id=1, source_target_pairs={{0,1},{1,0},{2,3},{3,2},{4,5},{5,4},{6,7},{7,6},{8,9},{9,8},{10,11... | collective-permute-start | bytes 786440 | tf_op jit(solution)/shard_map/ppermute | solution.py:322
  52.7 3.5 %copy-start.1 = (bf16[1,1024,512]{2,1,0:T(8,128)(2,1)S(1)}, bf16[1,1024,512]{2,1,0:T(8,128)(2,1)}, u32[]{:S(2)}) copy-start(bf16[1,1024,512]{2,1,0:T(8,128)(2,1)} %param.14) | copy-start | bytes 3145732
  52.7 3.5 %copy-start.5 = (f32[1,1024]{1,0:T(1,128)S(1)}, f32[1,1024]{1,0:T(1,128)}, u32[]{:S(2)}) copy-start(f32[1,1024]{1,0:T(1,128)} %gain_depth.1) | copy-start | bytes 12292
  52.7 9.2 %collective-permute-start.12 = (bf16[256,512]{1,0:T(8,128)(2,1)S(1)}, bf16[256,512]{1,0:T(8,128)(2,1)S(1)}, u32[]{:S(2)}, u32[]{:S(2)}) collective-permute-start(bf16[256,512]{1,0:T(8,128)(2,1)S(1)} %get-tuple-element.43.refs_3_.second), channel_id=1, source_target_pairs={{0,2},{1,3},{2,0},{3,1},{4,6},{5,7},{6,4},{7,5},{8,10},{9,11},{10,... | collective-permute-start | bytes 786440 | tf_op jit(solution)/shard_map/ppermute | solution.py:322
  53.9 11.3 %collective-permute-start.14 = (bf16[256,512]{1,0:T(8,128)(2,1)S(1)}, bf16[256,512]{1,0:T(8,128)(2,1)S(1)}, u32[]{:S(2)}, u32[]{:S(2)}) collective-permute-start(bf16[256,512]{1,0:T(8,128)(2,1)S(1)} %get-tuple-element.46), channel_id=1, source_target_pairs={{0,2},{1,3},{2,0},{3,1},{4,6},{5,7},{6,4},{7,5},{8,10},{9,11},{10,... | collective-permute-start | bytes 786440 | tf_op jit(solution)/shard_map/ppermute | solution.py:322
  55.5 9.7 %collective-permute-start.15 = (bf16[256,512]{1,0:T(8,128)(2,1)S(1)}, bf16[256,512]{1,0:T(8,128)(2,1)S(1)}, u32[]{:S(2)}, u32[]{:S(2)}) collective-permute-start(bf16[256,512]{1,0:T(8,128)(2,1)S(1)} %get-tuple-element.47), channel_id=1, source_target_pairs={{0,1},{1,0},{2,3},{3,2},{4,5},{5,4},{6,7},{7,6},{8,9},{9,8},{10,11... | collective-permute-start | bytes 786440 | tf_op jit(solution)/shard_map/ppermute | solution.py:322
  60.5 7.5 %collective-permute-start.11 = (bf16[256,512]{1,0:T(8,128)(2,1)S(1)}, bf16[256,512]{1,0:T(8,128)(2,1)S(1)}, u32[]{:S(2)}, u32[]{:S(2)}) collective-permute-start(bf16[256,512]{1,0:T(8,128)(2,1)S(1)} %collective-permute-done.10.refs_0_), channel_id=1, source_target_pairs={{0,2},{1,3},{2,0},{3,1},{4,6},{5,7},{6,4},{7,5},{8,10},{9,11},{10,... | collective-permute-start | bytes 786440 | tf_op jit(solution)/shard_map/ppermute | solution.py:322
  61.9 6.4 %collective-permute-start.13 = (bf16[256,512]{1,0:T(8,128)(2,1)S(1)}, bf16[256,512]{1,0:T(8,128)(2,1)S(1)}, u32[]{:S(2)}, u32[]{:S(2)}) collective-permute-start(bf16[256,512]{1,0:T(8,128)(2,1)S(1)} %collective-permute-done.12.refs_1_), channel_id=1, source_target_pairs={{0,1},{1,0},{2,3},{3,2},{4,5},{5,4},{6,7},{7,6},{8,9},{9,8},{10,11... | collective-permute-start | bytes 786440 | tf_op jit(solution)/shard_map/ppermute | solution.py:322

commit v5 on v4

--- a/solution.py
+++ b/solution.py
@@ -81,66 +81,56 @@
     return span(owner(mask) * 2 + side, half)
 
 
-def put_block(log, share, out, product, up, adds, mask, side):
-    frames, half = product.shape
-    wide = up.shape[1] // 2
-    for add in adds:
-        product = product + add[:frames, :].astype(f32)
-    out[:frames, :] = product.astype(bf16)
-    for c in range(wide // half):
-        col = side * wide + c * half
-        part = up[span(owner(mask), share), col : col + half]
-        rows = slice(frames + c * share, frames + (c + 1) * share)
-        for add in adds:
-            part = part + add[rows, :].astype(f32)
-        out[rows, :] = part.astype(bf16)
-
-
-def head_kernel(log, share, items, cot, w_depth, gain_hbm, context, w_out, *refs):
-    outs, up = refs[: len(items)], refs[len(items)]
-    cot_buf, depth_buf, gain_depth, context_buf, buf, sems = refs[len(items) + 1 :]
-    half = buf.shape[2]
+def upstream_kernel(share, masks, cot, w_depth, gain_hbm, *refs):
+    *outs, up = refs[:-4]
+    cot_buf, depth_buf, gain_depth, sems = refs[-4:]
     pairs = [(cot, cot_buf), (w_depth, depth_buf), (gain_hbm, gain_depth)]
-    pairs += [(context, context_buf)]
-    for i, (mask, side) in enumerate(items):
-        pairs.append((w_out.at[:, cols_of(mask, side, half)], buf.at[i]))
     copies = [pltpu.make_async_copy(a, b, sems.at[i]) for i, (a, b) in enumerate(pairs)]
     for copy in copies:
         copy.start()
-    for copy in copies[:3]:
+    for copy in copies:
         copy.wait()
     up[...] = gain_depth[...] * contract_last(cot_buf[...], depth_buf[...])
-    copies[3].wait()
-    for i, (mask, side) in enumerate(items):
-        copies[4 + i].wait()
-        product = jnp.dot(context_buf[...], buf[i], preferred_element_type=f32)
-        put_block(log, share, outs[i], product, up, [], mask, side)
-
-
-def early_kernel(log, share, items, context, w_out, up, *refs):
-    outs, (buf, sems) = refs[: len(items)], refs[len(items) :]
-    half = buf.shape[2]
-    copies = []
-    for i, (mask, side) in enumerate(items):
-        cols = cols_of(mask, side, half)
-        copies.append(pltpu.make_async_copy(w_out.at[:, cols], buf.at[i], sems.at[i]))
-        copies[-1].start()
-    for i, (mask, side) in enumerate(items):
-        copies[i].wait()
-        product = jnp.dot(context[...], buf[i], preferred_element_type=f32)
-        put_block(log, share, outs[i], product, up, [], mask, side)
-
-
-def project_kernel(log, share, items, context, w_out, up, *refs):
-    adds, outs = refs[: -len(items)], refs[-len(items) :]
+    wide = up.shape[1] // 2
+    for side, out in enumerate(outs):
+        for i, mask in enumerate(masks[side]):
+            out[i * share : (i + 1) * share, :] = up[
+                span(owner(mask), share), side * wide : (side + 1) * wide
+            ].astype(bf16)
+
+
+def share_of(share, up, mask, side, got, place, adds, frames, half, c):
+    wide = up.shape[1] // 2
+    cols = slice(c * half, (c + 1) * half)
+    part = up[span(owner(mask), share), side * wide + c * half : side * wide + (c + 1) * half]
+    part = part + got[place * share : (place + 1) * share, cols].astype(f32)
+    for add in adds:
+        part = part + add[frames + c * share : frames + (c + 1) * share, :].astype(f32)
+    return part
+
+
+def project_kernel(share, items, context, w_out, *refs):
+    outs, refs = refs[-len(items) :], refs[: -len(items)]
     half = outs[0].shape[1]
-    at = 0
-    for (mask, side, count), out in zip(items, outs):
+    frames = context.shape[0]
+    at = 3
+    for (mask, side, count, place), out in zip(items, outs):
         product = jnp.dot(
             context[...], w_out[:, cols_of(mask, side, half)], preferred_element_type=f32
         )
-        put_block(log, share, out, product, up, adds[at : at + count], mask, side)
+        adds = refs[at : at + count]
         at += count
+        for add in adds:
+            product = product + add[:frames, :].astype(f32)
+        out[:frames, :] = product.astype(bf16)
+        if not count:
+            continue
+        up, got = refs[0], refs[1 + side]
+        for c in range(up.shape[1] // 2 // half):
+            rows = slice(frames + c * share, frames + (c + 1) * share)
+            out[rows, :] = share_of(
+                share, up, mask, side, got, place, adds[1:], frames, half, c
+            ).astype(bf16)
 
 
 def keep_kernel(context, w_out, residual, out):
@@ -151,8 +141,9 @@
     )
 
 
-def state_kernel(log, share, gain, w_in, up, kept, *refs):
-    adds, (state, raw, squares, *sends) = refs[: 2 * log], refs[2 * log :]
+def state_kernel(log, share, places, gain, w_in, up, kept, *refs):
+    got, adds = refs[:2], refs[2 : 2 + 2 * log]
+    state, raw, squares, *sends = refs[2 + 2 * log :]
     frames, width = state.shape
     half = width // 2
     wide = raw.shape[1] // 2
@@ -171,13 +162,11 @@
         squares[side] = row
         send[:frames, :] = raw[:, side * wide : (side + 1) * wide].astype(bf16)
         put_squares(send, frames, row)
+        late = adds[side * log + 1 : (side + 1) * log]
         for c in range(wide // half):
-            col = side * wide + c * half
-            part = up[span(lax.axis_index("mp"), share), col : col + half]
-            for add in adds[side * log : (side + 1) * log]:
-                at = frames + c * share
-                part = part + add[at : at + share, :].astype(f32)
-            send[frames + SQ :, c * half : (c + 1) * half] = part.astype(bf16)
+            send[frames + SQ :, c * half : (c + 1) * half] = share_of(
+                share, up, 0, side, got[side], places[side], late, frames, half, c
+            ).astype(bf16)
 
 
 def reduce_kernel(raw, squares, *refs):
@@ -286,18 +275,14 @@
     out[...] = total
 
 
-def last_kernel(log, items, w_out, *refs):
-    blocks, (total, out, buf, sems) = refs[: len(items)], refs[len(items) :]
-    step = total.shape[1] // 2
+def last_kernel(log, mask, side, w_out, block, total, out, buf, sems):
+    pieces = sems.shape[0]
+    step = total.shape[1] // pieces
     copies = []
-    for k in range(2):
+    for k in range(pieces):
         rows = slice(k * step, (k + 1) * step)
-        value = total[:, rows]
-        for (mask, side), block in zip(items, blocks):
-            value = value + contract_last(
-                block[...], w_out[rows, cols_of(mask, side, block.shape[1])]
-            )
-        buf[:, rows] = value.astype(bf16)
+        part = contract_last(block[...], w_out[rows, cols_of(mask, side, block.shape[1])])
+        buf[:, rows] = (total[:, rows] + part).astype(bf16)
         copies.append(pltpu.make_async_copy(buf.at[:, rows], out.at[:, rows], sems.at[k]))
         copies[-1].start()
     for copy in copies:
@@ -316,7 +301,7 @@
     bits = [1 << i for i in range(log)]
     orders = (bits, bits[::-1])
     gain = gain_temporal[None, :]
-    block = ((frames + share * (wide // half), half), bf16)
+    extra = share * (wide // half)
 
     def swap(value, bit):
         return lax.ppermute(value, "mp", [(i, i ^ bit) for i in range(n)])
@@ -327,45 +312,44 @@
     masks = sorted(range(1, n), key=lambda k: (-k.bit_count(), k))
     pairs = [((k, 0), (mirror(k, log), 1)) for k in masks]
 
+    first = [[mask for mask in range(1, n) if phase_of(mask, side) == 0] for side in range(2)]
+    *values, up = call(
+        functools.partial(upstream_kernel, share, first),
+        [((share * n // 2, wide), bf16)] * 2 + [((frames, depth), f32)],
+        [cotangent[0], w_depth[0], gain_depth],
+        [HBM] * 3,
+        [
+            pltpu.VMEM((frames, act), bf16),
+            pltpu.VMEM((depth, act), bf16),
+            pltpu.VMEM((1, depth), f32),
+            pltpu.SemaphoreType.DMA((3,)),
+        ],
+        name="upstream",
+    )
+    got_up = [swap(values[side], orders[side][0]) for side in range(2)]
+
+    def place(mask, side):
+        return first[side].index(mask ^ orders[side][0])
+
     arrived = {}
+    token = up
     for pair in pairs:
-        adds = [
-            [arrived[mask ^ bit, side] for bit in orders[side][: phase_of(mask, side)]]
-            for mask, side in pair
-        ]
-        if pair is pairs[0]:
-            *values, up = call(
-                functools.partial(head_kernel, log, share, pair),
-                [block] * 2 + [((frames, depth), f32)],
-                [cotangent[0], w_depth[0], gain_depth, context, w_out],
-                [HBM] * 5,
-                [
-                    pltpu.VMEM((frames, act), bf16),
-                    pltpu.VMEM((depth, act), bf16),
-                    pltpu.VMEM((1, depth), f32),
-                    pltpu.VMEM(context.shape, bf16),
-                    pltpu.VMEM((2, heads, half), bf16),
-                    pltpu.SemaphoreType.DMA((6,)),
-                ],
-                name="head",
-            )
-        elif not adds[0]:
-            values = call(
-                functools.partial(early_kernel, log, share, pair),
-                [block] * 2,
-                [context, w_out, up],
-                [VMEM, HBM, VMEM],
-                [pltpu.VMEM((2, heads, half), bf16), pltpu.SemaphoreType.DMA((2,))],
-                name="early",
-            )
-        else:
-            items = [(mask, side, len(a)) for (mask, side), a in zip(pair, adds)]
-            values = call(
-                functools.partial(project_kernel, log, share, items),
-                [block] * 2,
-                [context, w_out, up] + adds[0] + adds[1],
-                name="project",
-            )
+        items, listed = [], []
+        for mask, side in pair:
+            phase = phase_of(mask, side)
+            listed += [arrived[mask ^ bit, side] for bit in orders[side][:phase]]
+            items.append((mask, side, phase, place(mask, side) if phase else 0))
+        shape = ((frames + (extra if phase else 0), half), bf16)
+        values = call(
+            functools.partial(project_kernel, share, items),
+            [shape] * 2,
+            [context, w_out, up] + got_up + listed
+            if listed
+            else [context, w_out, up, gain, gain],
+            name="project",
+            after=token,
+        )
+        token = values[0]
         for (mask, side), value in zip(pair, values):
             arrived[mask, side] = swap(value, orders[side][phase_of(mask, side)])
     kept = call(
@@ -377,10 +361,12 @@
     )[0]
 
     state, raw, squares, *sends = call(
-        functools.partial(state_kernel, log, share),
+        functools.partial(state_kernel, log, share, [place(0, side) for side in range(2)]),
         [((frames, width), f32), ((frames, depth), f32), ((2, SQ // 2, frames), f32)]
         + [((frames + SQ + share, wide), bf16)] * 2,
-        [gain, w_in, up, kept] + [arrived[bit, side] for side in range(2) for bit in orders[side]],
+        [gain, w_in, up, kept]
+        + got_up
+        + [arrived[bit, side] for side in range(2) for bit in orders[side]],
         name="state",
     )
     haves = [[0], [0]]
@@ -425,7 +411,8 @@
         name="act",
     )
     keys = [((haves[0][k], 0), (haves[1][k], 1)) for k in range(n)]
-    for pair in keys[1:-1]:
+    final = keys[-1][1]
+    for pair in keys[1:-1] + [keys[-1][:1]]:
         total = call(
             functools.partial(context_kernel, log, pair),
             [((frames, heads), f32)],
@@ -433,9 +420,9 @@
             name="grad_context",
         )[0]
     grad_context = call(
-        functools.partial(last_kernel, log, keys[-1]),
+        functools.partial(last_kernel, log, *final),
         [((frames, heads), bf16)],
-        [w_out] + [blocks[key] for key in keys[-1]] + [total],
+        [w_out, blocks[final], total],
         scratch=[pltpu.VMEM((frames, heads), bf16), pltpu.SemaphoreType.DMA((2,))],
         name="grad_context",
         out_specs=[HBM],

time: 69.9 us -> 69 us (0.987)
  starting transfers between devices: 18.3 us -> 21.3 us
  waiting for transfers between devices: 36.6 us -> 34.2 us
  Pallas kernels: 14 us -> 12.6 us
    ppermute x16 -> x18, starting transfers between devices: 18.3 us -> 21.3 us  [swap(): return lax.ppermute(value, 'mp', [(i, i ^ bit) for i in range(n)])]
    ppermute x16 -> x18, waiting for transfers between devices: 36.6 us -> 34.2 us  [swap(): return lax.ppermute(value, 'mp', [(i, i ^ bit) for i in range(n)])]
    pallas_call x12 -> x14, Pallas kernels: 14 us -> 12.6 us  [call(): pl.pallas_call(kernel, out_shape=[jax.ShapeDtypeStruct(s, d) for s, d in...]
  transfers between devices with their start and end apart: 16 -> 18, of which waited for: 15 -> 14; matrix products, arithmetic and copies ran while one was open for 0% -> 0% of each run, Pallas kernels for 11% -> 10%
where the time goes in v5:
time: 69 us; the launch traced here: 68.9 us
  waiting for transfers between devices  34.2 us (50%)
  starting transfers between devices  21.3 us (31%)
  Pallas kernels  12.6 us (18%)
  between operations  0.77 us (1%)
    ppermute x18, waiting for transfers between devices, swap(): return lax.ppermute(value, 'mp', [(i, i ^ bit) for i in range(n)])  34.2 us
    ppermute x18, starting transfers between devices, swap(): return lax.ppermute(value, 'mp', [(i, i ^ bit) for i in range(n)])  21.3 us
    pallas_call x14, Pallas kernels, call(): pl.pallas_call(kernel, out_shape=[jax.ShapeDtypeStruct(s, d) for s, d in...  12.6 us
  transfers between devices with their start and end apart: 18, of which 14 were waited for; matrix products, arithmetic and copies ran while one was open for 0% of the time, Pallas kernels for 10%

profile of v5, /device:TPU:0, one launch (start us, length us, event | category | flops | bytes accessed | tf_op | source)
XLA Modules:
  0.0 68.9 jit_solution(11238228117104029179)
XLA Ops:
  0.7 2.0 %upstream.1 = (bf16[128,512]{1,0:T(8,128)(2,1)S(1)}, bf16[128,512]{1,0:T(8,128)(2,1)S(1)}, f32[256,1024]{1,0:T(8,128)S(1)}) custom-call(bf16[256,512]{1,0:T(8,128)(2,1)} %bitcast.12, bf16[1024,512]{1,0:T(8,128)(2,1)} %bitcast.4, f32[1,1024]{1,0:T(1,128)} %gain_depth.1), custom_call_target="tpu_custom_call" | custom-call | flops 20000000000 | bytes 60000000 | tf_op jit(solution)/shard_map/upstream/pallas_call | solution.py:46
  2.6 3.0 %collective-permute-start = (bf16[128,512]{1,0:T(8,128)(2,1)S(1)}, bf16[128,512]{1,0:T(8,128)(2,1)S(1)}, u32[]{:S(2)}, u32[]{:S(2)}) collective-permute-start(bf16[128,512]{1,0:T(8,128)(2,1)S(1)} %get-tuple-element.29), channel_id=1, source_target_pairs={{0,1},{1,0},{2,3},{3,2},{4,5},{5,4},{6,7},{7,6},{8,9},{9,8},{10,11... | collective-permute-start | bytes 393224 | tf_op jit(solution)/shard_map/ppermute | solution.py:307
  5.7 1.5 %collective-permute-start.1 = (bf16[128,512]{1,0:T(8,128)(2,1)S(1)}, bf16[128,512]{1,0:T(8,128)(2,1)S(1)}, u32[]{:S(2)}, u32[]{:S(2)}) collective-permute-start(bf16[128,512]{1,0:T(8,128)(2,1)S(1)} %get-tuple-element.30), channel_id=1, source_target_pairs={{0,2},{1,3},{2,0},{3,1},{4,6},{5,7},{6,4},{7,5},{8,10},{9,11},{10,... | collective-permute-start | bytes 393224 | tf_op jit(solution)/shard_map/ppermute | solution.py:307
  7.2 0.7 %project.3 = (bf16[256,512]{1,0:T(8,128)(2,1)S(1)}, bf16[256,512]{1,0:T(8,128)(2,1)S(1)}) custom-call(bf16[256,1024]{1,0:T(8,128)(2,1)S(1)} %copy-done.3, bf16[1024,4096]{1,0:T(8,128)(2,1)S(1)} %copy-done, f32[256,1024]{1,0:T(8,128)S(1)} %get-tuple-element.28.refs_2_.refs_5_.up, f32[1,4096]{1,0:T(1,128)S(1)} %bitcast.6, f32[1,4096]{1,0:T(1,128)S(1)} %bitcast.7, ...), custom_call_target="tpu_custom_call" | custom-call | flops 20000000000 | bytes 60000000 | tf_op jit(solution)/shard_map/project/pallas_call | solution.py:46
  7.9 0.6 collective-permute-start.3
  8.5 1.2 %collective-permute-start.2 = (bf16[256,512]{1,0:T(8,128)(2,1)S(1)}, bf16[256,512]{1,0:T(8,128)(2,1)S(1)}, u32[]{:S(2)}, u32[]{:S(2)}) collective-permute-start(bf16[256,512]{1,0:T(8,128)(2,1)S(1)} %get-tuple-element.31.refs_5_), channel_id=1, source_target_pairs={{0,1},{1,0},{2,3},{3,2},{4,5},{5,4},{6,7},{7,6},{8,9},{9,8},{10,11... | collective-permute-start | bytes 786440 | tf_op jit(solution)/shard_map/ppermute | solution.py:307
  9.7 0.7 %project.4 = (bf16[256,512]{1,0:T(8,128)(2,1)S(1)}, bf16[256,512]{1,0:T(8,128)(2,1)S(1)}) custom-call(bf16[256,1024]{1,0:T(8,128)(2,1)S(1)} %copy-done.3, bf16[1024,4096]{1,0:T(8,128)(2,1)S(1)} %copy-done, f32[256,1024]{1,0:T(8,128)S(1)} %get-tuple-element.28.refs_2_.refs_5_.up, f32[1,4096]{1,0:T(1,128)S(1)} %bitcast.8, f32[1,4096]{1,0:T(1,128)S(1)} %bitcast.9, ...), custom_call_target="tpu_custom_call" | custom-call | flops 20000000000 | bytes 60000000 | tf_op jit(solution)/shard_map/project/pallas_call | solution.py:46
  10.4 0.9 %collective-permute-start.6 = (bf16[256,512]{1,0:T(8,128)(2,1)S(1)}, bf16[256,512]{1,0:T(8,128)(2,1)S(1)}, u32[]{:S(2)}, u32[]{:S(2)}) collective-permute-start(bf16[256,512]{1,0:T(8,128)(2,1)S(1)} %get-tuple-element.35), channel_id=1, source_target_pairs={{0,2},{1,3},{2,0},{3,1},{4,6},{5,7},{6,4},{7,5},{8,10},{9,11},{10,... | collective-permute-start | bytes 786440 | tf_op jit(solution)/shard_map/ppermute | solution.py:307
  11.3 0.0 collective-permute-done.refs_3_.refs_0_
  11.3 1.5 %collective-permute-start.4 = (bf16[256,512]{1,0:T(8,128)(2,1)S(1)}, bf16[256,512]{1,0:T(8,128)(2,1)S(1)}, u32[]{:S(2)}, u32[]{:S(2)}) collective-permute-start(bf16[256,512]{1,0:T(8,128)(2,1)S(1)} %get-tuple-element.33.refs_7_), channel_id=1, source_target_pairs={{0,1},{1,0},{2,3},{3,2},{4,5},{5,4},{6,7},{7,6},{8,9},{9,8},{10,11... | collective-permute-start | bytes 786440 | tf_op jit(solution)/shard_map/ppermute | solution.py:307
  12.8 4.4 %collective-permute-done.3.refs_6_ = bf16[256,512]{1,0:T(8,128)(2,1)S(1)} collective-permute-done((bf16[256,512]{1,0:T(8,128)(2,1)S(1)}, bf16[256,512]{1,0:T(8,128)(2,1)S(1)}, u32[]{:S(2)}, u32[]{:S(2)}) %collective-permute-start.3) | collective-permute-done | bytes 262176 | tf_op jit(solution)/shard_map/ppermute | solution.py:307
  17.2 0.5 collective-permute-done.2.refs_5_
  17.7 0.7 %project.5 = (bf16[320,512]{1,0:T(8,128)(2,1)S(1)}, bf16[320,512]{1,0:T(8,128)(2,1)S(1)}) custom-call(bf16[256,1024]{1,0:T(8,128)(2,1)S(1)} %copy-done.3, bf16[1024,4096]{1,0:T(8,128)(2,1)S(1)} %copy-done, f32[256,1024]{1,0:T(8,128)S(1)} %get-tuple-element.28.refs_2_.refs_5_.up, bf16[128,512]{1,0:T(8,128)(2,1)S(1)} %collective-permute-done.refs_3_.refs_0_, ...), custom_call_target="tpu_custom_call" | custom-call | flops 20000000000 | bytes 60000000 | tf_op jit(solution)/shard_map/project/pallas_call | solution.py:46
  18.5 1.3 %collective-permute-start.7 = (bf16[320,512]{1,0:T(8,128)(2,1)S(1)}, bf16[320,512]{1,0:T(8,128)(2,1)S(1)}, u32[]{:S(2)}, u32[]{:S(2)}) collective-permute-start(bf16[320,512]{1,0:T(8,128)(2,1)S(1)} %get-tuple-element.36), channel_id=1, source_target_pairs={{0,1},{1,0},{2,3},{3,2},{4,5},{5,4},{6,7},{7,6},{8,9},{9,8},{10,11... | collective-permute-start | bytes 983048 | tf_op jit(solution)/shard_map/ppermute | solution.py:307
  19.8 0.8 %collective-permute-start.5 = (bf16[320,512]{1,0:T(8,128)(2,1)S(1)}, bf16[320,512]{1,0:T(8,128)(2,1)S(1)}, u32[]{:S(2)}, u32[]{:S(2)}) collective-permute-start(bf16[320,512]{1,0:T(8,128)(2,1)S(1)} %get-tuple-element.34.refs_3_), channel_id=1, source_target_pairs={{0,2},{1,3},{2,0},{3,1},{4,6},{5,7},{6,4},{7,5},{8,10},{9,11},{10,... | collective-permute-start | bytes 983048 | tf_op jit(solution)/shard_map/ppermute | solution.py:307
  20.6 0.7 %keep.1.kept = f32[256,1024]{1,0:T(8,128)S(1)} custom-call(bf16[256,1024]{1,0:T(8,128)(2,1)S(1)} %copy-done.3, bf16[1024,4096]{1,0:T(8,128)(2,1)S(1)} %copy-done, bf16[256,1024]{1,0:T(8,128)(2,1)S(1)} %copy-done.4, bf16[320,512]{1,0:T(8,128)(2,1)S(1)} %get-tuple-element.34.refs_3_), custom_call_target="tpu_custom_call" | custom-call | flops 20000000000 | bytes 60000000 | tf_op jit(solution)/shard_map/keep/pallas_call | solution.py:46
  21.3 1.5 %collective-permute-done.6.refs_4_ = bf16[256,512]{1,0:T(8,128)(2,1)S(1)} collective-permute-done((bf16[256,512]{1,0:T(8,128)(2,1)S(1)}, bf16[256,512]{1,0:T(8,128)(2,1)S(1)}, u32[]{:S(2)}, u32[]{:S(2)}) %collective-permute-start.6) | collective-permute-done | bytes 262176 | tf_op jit(solution)/shard_map/ppermute | solution.py:307
  22.8 0.5 collective-permute-done.4.refs_2_
  23.3 5.3 %collective-permute-done.7.refs_5_ = bf16[320,512]{1,0:T(8,128)(2,1)S(1)} collective-permute-done((bf16[320,512]{1,0:T(8,128)(2,1)S(1)}, bf16[320,512]{1,0:T(8,128)(2,1)S(1)}, u32[]{:S(2)}, u32[]{:S(2)}) %collective-permute-start.7) | collective-permute-done | bytes 327712 | tf_op jit(solution)/shard_map/ppermute | solution.py:307
  28.6 0.2 collective-permute-done.5.refs_3_
  28.9 0.8 %state.1 = (f32[256,1024]{1,0:T(8,128)S(1)}, f32[256,1024]{1,0:T(8,128)S(1)}, f32[2,8,256]{2,1,0:T(8,128)S(1)}, bf16[336,512]{1,0:T(8,128)(2,1)S(1)}, bf16[336,512]{1,0:T(8,128)(2,1)S(1)}) custom-call(f32[1,4096]{1,0:T(1,128)S(1)} %bitcast.10, bf16[1024,1024]{1,0:T(8,128)(2,1)S(1)} %copy-done.1, f32[256,1024]{1,0:T(8,128)S(1)} %get-tuple-element.28.refs_2_.refs_5_.up, ...), custom_call_target="tpu_custom_call" | custom-call | flops 20000000000 | bytes 60000000 | tf_op jit(solution)/shard_map/state/pallas_call | solution.py:46
  29.7 1.3 %collective-permute-start.8 = (bf16[336,512]{1,0:T(8,128)(2,1)S(1)}, bf16[336,512]{1,0:T(8,128)(2,1)S(1)}, u32[]{:S(2)}, u32[]{:S(2)}) collective-permute-start(bf16[336,512]{1,0:T(8,128)(2,1)S(1)} %get-tuple-element.39.refs_0_), channel_id=1, source_target_pairs={{0,1},{1,0},{2,3},{3,2},{4,5},{5,4},{6,7},{7,6},{8,9},{9,8},{10,11... | collective-permute-start | bytes 1032200 | tf_op jit(solution)/shard_map/ppermute | solution.py:307
  31.0 0.8 %collective-permute-start.9 = (bf16[336,512]{1,0:T(8,128)(2,1)S(1)}, bf16[336,512]{1,0:T(8,128)(2,1)S(1)}, u32[]{:S(2)}, u32[]{:S(2)}) collective-permute-start(bf16[336,512]{1,0:T(8,128)(2,1)S(1)} %get-tuple-element.40.refs_1_), channel_id=1, source_target_pairs={{0,2},{1,3},{2,0},{3,1},{4,6},{5,7},{6,4},{7,5},{8,10},{9,11},{10,... | collective-permute-start | bytes 1032200 | tf_op jit(solution)/shard_map/ppermute | solution.py:307
  31.8 6.5 %collective-permute-done.8.refs_2_ = bf16[336,512]{1,0:T(8,128)(2,1)S(1)} collective-permute-done((bf16[336,512]{1,0:T(8,128)(2,1)S(1)}, bf16[336,512]{1,0:T(8,128)(2,1)S(1)}, u32[]{:S(2)}, u32[]{:S(2)}) %collective-permute-start.8) | collective-permute-done | bytes 344096 | tf_op jit(solution)/shard_map/ppermute | solution.py:307
  38.3 1.1 %collective-permute-done.9.refs_3_ = bf16[336,512]{1,0:T(8,128)(2,1)S(1)} collective-permute-done((bf16[336,512]{1,0:T(8,128)(2,1)S(1)}, bf16[336,512]{1,0:T(8,128)(2,1)S(1)}, u32[]{:S(2)}, u32[]{:S(2)}) %collective-permute-start.9) | collective-permute-done | bytes 344096 | tf_op jit(solution)/shard_map/ppermute | solution.py:307
  39.3 0.2 reduce.1
  39.5 0.7 collective-permute-start.10
  40.2 1.7 %collective-permute-start.11 = (bf16[400,512]{1,0:T(8,128)(2,1)S(1)}, bf16[400,512]{1,0:T(8,128)(2,1)S(1)}, u32[]{:S(2)}, u32[]{:S(2)}) collective-permute-start(bf16[400,512]{1,0:T(8,128)(2,1)S(1)} %get-tuple-element.44.refs_1_), channel_id=1, source_target_pairs={{0,1},{1,0},{2,3},{3,2},{4,5},{5,4},{6,7},{7,6},{8,9},{9,8},{10,11... | collective-permute-start | bytes 1228808 | tf_op jit(solution)/shard_map/ppermute | solution.py:307
  41.8 6.5 %collective-permute-done.10.refs_2_.refs_0_ = bf16[400,512]{1,0:T(8,128)(2,1)S(1)} collective-permute-done((bf16[400,512]{1,0:T(8,128)(2,1)S(1)}, bf16[400,512]{1,0:T(8,128)(2,1)S(1)}, u32[]{:S(2)}, u32[]{:S(2)}) %collective-permute-start.10) | collective-permute-done | bytes 409632 | tf_op jit(solution)/shard_map/ppermute | solution.py:307
  48.4 0.5 collective-permute-done.11.refs_3_.refs_1_
  48.9 1.3 %back.1 = (bf16[256,512]{1,0:T(8,128)(2,1)S(1)}, bf16[256,512]{1,0:T(8,128)(2,1)S(1)}) custom-call(f32[1,4096]{1,0:T(1,128)S(1)} %bitcast.11, bf16[1024,1024]{1,0:T(8,128)(2,1)S(1)} %copy-done.1, f32[256,1024]{1,0:T(8,128)S(1)} %get-tuple-element.45.state, f32[256,1024]{1,0:T(8,128)S(1)} %get-tuple-element.41.raw, ...), custom_call_target="tpu_custom_call" | custom-call | flops 20000000000 | bytes 60000000 | tf_op jit(solution)/shard_map/back/pallas_call | solution.py:46
  50.2 1.5 %collective-permute-start.14 = (bf16[256,512]{1,0:T(8,128)(2,1)S(1)}, bf16[256,512]{1,0:T(8,128)(2,1)S(1)}, u32[]{:S(2)}, u32[]{:S(2)}) collective-permute-start(bf16[256,512]{1,0:T(8,128)(2,1)S(1)} %get-tuple-element.46.refs_2_.first), channel_id=1, source_target_pairs={{0,1},{1,0},{2,3},{3,2},{4,5},{5,4},{6,7},{7,6},{8,9},{9,8},{10,11... | collective-permute-start | bytes 786440 | tf_op jit(solution)/shard_map/ppermute | solution.py:307
  51.8 0.4 collective-permute-start.12
  52.1 0.7 %grad_context.5 = (f32[256,1024]{1,0:T(8,128)S(1)}, bf16[256,512]{1,0:T(8,128)(2,1)S(1)}, bf16[256,512]{1,0:T(8,128)(2,1)S(1)}) custom-call(bf16[1024,4096]{1,0:T(8,128)(2,1)S(1)} %copy-done, bf16[256,512]{1,0:T(8,128)(2,1)S(1)} %get-tuple-element.46.refs_2_.first, bf16[256,512]{1,0:T(8,128)(2,1)S(1)} %get-tuple-element.47.refs_3_.second), custom_call_target="tpu_custom_call" | custom-call | flops 20000000000 | bytes 60000000 | tf_op jit(solution)/shard_map/grad_context/pallas_call | solution.py:46
  52.9 1.7 %collective-permute-start.16 = (bf16[256,512]{1,0:T(8,128)(2,1)S(1)}, bf16[256,512]{1,0:T(8,128)(2,1)S(1)}, u32[]{:S(2)}, u32[]{:S(2)}) collective-permute-start(bf16[256,512]{1,0:T(8,128)(2,1)S(1)} %get-tuple-element.50), channel_id=1, source_target_pairs={{0,2},{1,3},{2,0},{3,1},{4,6},{5,7},{6,4},{7,5},{8,10},{9,11},{10,... | collective-permute-start | bytes 786440 | tf_op jit(solution)/shard_map/ppermute | solution.py:307
  54.6 0.6 collective-permute-start.17
  55.2 1.6 %act.1 = (bf16[256,512]{1,0:T(8,128)(2,1)}, bf16[256,1024]{1,0:T(8,128)(2,1)}) custom-call(f32[1,1024]{1,0:T(1,128)S(1)} %copy-done.6, bf16[1024,512]{1,0:T(8,128)(2,1)S(1)} %bitcast.5, f32[256,1024]{1,0:T(8,128)S(1)} %get-tuple-element.41.raw, f32[2,8,256]{2,1,0:T(8,128)S(1)} %get-tuple-element.42.squares, ...), custom_call_target="tpu_custom_call" | custom-call | flops 20000000000 | bytes 60000000 | tf_op jit(solution)/shard_map/act/pallas_call | solution.py:46
  56.8 2.8 %collective-permute-done.14.refs_0_ = bf16[256,512]{1,0:T(8,128)(2,1)S(1)} collective-permute-done((bf16[256,512]{1,0:T(8,128)(2,1)S(1)}, bf16[256,512]{1,0:T(8,128)(2,1)S(1)}, u32[]{:S(2)}, u32[]{:S(2)}) %collective-permute-start.14) | collective-permute-done | bytes 262176 | tf_op jit(solution)/shard_map/ppermute | solution.py:307
  59.5 1.2 %collective-permute-start.15 = (bf16[256,512]{1,0:T(8,128)(2,1)S(1)}, bf16[256,512]{1,0:T(8,128)(2,1)S(1)}, u32[]{:S(2)}, u32[]{:S(2)}) collective-permute-start(bf16[256,512]{1,0:T(8,128)(2,1)S(1)} %collective-permute-done.14.refs_0_), channel_id=1, source_target_pairs={{0,2},{1,3},{2,0},{3,1},{4,6},{5,7},{6,4},{7,5},{8,10},{9,11},{10,... | collective-permute-start | bytes 786440 | tf_op jit(solution)/shard_map/ppermute | solution.py:307
  60.8 0.3 collective-permute-done.12.refs_1_
  61.0 0.6 collective-permute-start.13
  61.6 0.8 %grad_context.6.refs_2_ = f32[256,1024]{1,0:T(8,128)S(1)} custom-call(bf16[1024,4096]{1,0:T(8,128)(2,1)S(1)} %copy-done, bf16[256,512]{1,0:T(8,128)(2,1)S(1)} %collective-permute-done.14.refs_0_, bf16[256,512]{1,0:T(8,128)(2,1)S(1)} %collective-permute-done.12.refs_1_, f32[256,1024]{1,0:T(8,128)S(1)} %get-tuple-element.52.refs_2_), custom_call_target="tpu_custom_call" | custom-call | flops 20000000000 | bytes 60000000 | tf_op jit(solution)/shard_map/grad_context/pallas_call | solution.py:46
  62.3 2.0 %collective-permute-done.16.refs_0_ = bf16[256,512]{1,0:T(8,128)(2,1)S(1)} collective-permute-done((bf16[256,512]{1,0:T(8,128)(2,1)S(1)}, bf16[256,512]{1,0:T(8,128)(2,1)S(1)}, u32[]{:S(2)}, u32[]{:S(2)}) %collective-permute-start.16) | collective-permute-done | bytes 262176 | tf_op jit(solution)/shard_map/ppermute | solution.py:307
  64.4 0.7 %grad_context.7.refs_1_ = f32[256,1024]{1,0:T(8,128)S(1)} custom-call(bf16[1024,4096]{1,0:T(8,128)(2,1)S(1)} %copy-done, bf16[256,512]{1,0:T(8,128)(2,1)S(1)} %collective-permute-done.16.refs_0_, bf16[256,512]{1,0:T(8,128)(2,1)S(1)} %collective-permute-done.17.refs_1_, f32[256,1024]{1,0:T(8,128)S(1)} %grad_context.6.refs_2_), custom_call_target="tpu_custom_call" | custom-call | flops 20000000000 | bytes 60000000 | tf_op jit(solution)/shard_map/grad_context/pallas_call | solution.py:46
  65.1 2.1 %collective-permute-done.15.refs_0_ = bf16[256,512]{1,0:T(8,128)(2,1)S(1)} collective-permute-done((bf16[256,512]{1,0:T(8,128)(2,1)S(1)}, bf16[256,512]{1,0:T(8,128)(2,1)S(1)}, u32[]{:S(2)}, u32[]{:S(2)}) %collective-permute-start.15) | collective-permute-done | bytes 262176 | tf_op jit(solution)/shard_map/ppermute | solution.py:307
  67.2 0.5 grad_context.8.total
  67.7 0.0 collective-permute-done.13.block
  67.7 1.2 %grad_context.9 = bf16[256,1024]{1,0:T(8,128)(2,1)} custom-call(bf16[1024,4096]{1,0:T(8,128)(2,1)S(1)} %copy-done, bf16[256,512]{1,0:T(8,128)(2,1)S(1)} %collective-permute-done.13.block, f32[256,1024]{1,0:T(8,128)S(1)} %grad_context.8.total), custom_call_target="tpu_custom_call" | custom-call | flops 20000000000 | bytes 60000000 | tf_op jit(solution)/shard_map/grad_context/pallas_call | solution.py:46
  (16 shorter events, 0.0 us)
Async XLA Ops:
  0.6 6.5 %copy-start = (bf16[1024,4096]{1,0:T(8,128)(2,1)S(1)}, bf16[1024,4096]{1,0:T(8,128)(2,1)}, u32[]{:S(2)}) copy-start(bf16[1024,4096]{1,0:T(8,128)(2,1)} %w_out.9) | copy-start | bytes 25165828
  0.6 6.5 %copy-start.3 = (bf16[256,1024]{1,0:T(8,128)(2,1)S(1)}, bf16[256,1024]{1,0:T(8,128)(2,1)}, u32[]{:S(2)}) copy-start(bf16[256,1024]{1,0:T(8,128)(2,1)} %refs_0_.7) | copy-start | bytes 1572868
  0.7 6.5 %copy-start.5 = (f32[4096]{0:T(1024)S(1)}, f32[4096]{0:T(1024)}, u32[]{:S(2)}) copy-start(f32[4096]{0:T(1024)} %param.11) | copy-start | bytes 49156
  2.6 8.7 %collective-permute-start = (bf16[128,512]{1,0:T(8,128)(2,1)S(1)}, bf16[128,512]{1,0:T(8,128)(2,1)S(1)}, u32[]{:S(2)}, u32[]{:S(2)}) collective-permute-start(bf16[128,512]{1,0:T(8,128)(2,1)S(1)} %get-tuple-element.29), channel_id=1, source_target_pairs={{0,1},{1,0},{2,3},{3,2},{4,5},{5,4},{6,7},{7,6},{8,9},{9,8},{10,11... | collective-permute-start | bytes 393224 | tf_op jit(solution)/shard_map/ppermute | solution.py:307
  5.7 7.2 %collective-permute-start.1 = (bf16[128,512]{1,0:T(8,128)(2,1)S(1)}, bf16[128,512]{1,0:T(8,128)(2,1)S(1)}, u32[]{:S(2)}, u32[]{:S(2)}) collective-permute-start(bf16[128,512]{1,0:T(8,128)(2,1)S(1)} %get-tuple-element.30), channel_id=1, source_target_pairs={{0,2},{1,3},{2,0},{3,1},{4,6},{5,7},{6,4},{7,5},{8,10},{9,11},{10,... | collective-permute-start | bytes 393224 | tf_op jit(solution)/shard_map/ppermute | solution.py:307
  7.9 9.3 %collective-permute-start.3 = (bf16[256,512]{1,0:T(8,128)(2,1)S(1)}, bf16[256,512]{1,0:T(8,128)(2,1)S(1)}, u32[]{:S(2)}, u32[]{:S(2)}) collective-permute-start(bf16[256,512]{1,0:T(8,128)(2,1)S(1)} %get-tuple-element.32), channel_id=1, source_target_pairs={{0,2},{1,3},{2,0},{3,1},{4,6},{5,7},{6,4},{7,5},{8,10},{9,11},{10,... | collective-permute-start | bytes 786440 | tf_op jit(solution)/shard_map/ppermute | solution.py:307
  8.5 9.2 %collective-permute-start.2 = (bf16[256,512]{1,0:T(8,128)(2,1)S(1)}, bf16[256,512]{1,0:T(8,128)(2,1)S(1)}, u32[]{:S(2)}, u32[]{:S(2)}) collective-permute-start(bf16[256,512]{1,0:T(8,128)(2,1)S(1)} %get-tuple-element.31.refs_5_), channel_id=1, source_target_pairs={{0,1},{1,0},{2,3},{3,2},{4,5},{5,4},{6,7},{7,6},{8,9},{9,8},{10,11... | collective-permute-start | bytes 786440 | tf_op jit(solution)/shard_map/ppermute | solution.py:307
  10.4 12.4 %collective-permute-start.6 = (bf16[256,512]{1,0:T(8,128)(2,1)S(1)}, bf16[256,512]{1,0:T(8,128)(2,1)S(1)}, u32[]{:S(2)}, u32[]{:S(2)}) collective-permute-start(bf16[256,512]{1,0:T(8,128)(2,1)S(1)} %get-tuple-element.35), channel_id=1, source_target_pairs={{0,2},{1,3},{2,0},{3,1},{4,6},{5,7},{6,4},{7,5},{8,10},{9,11},{10,... | collective-permute-start | bytes 786440 | tf_op jit(solution)/shard_map/ppermute | solution.py:307
  11.3 9.3 %copy-start.4 = (bf16[256,1024]{1,0:T(8,128)(2,1)S(1)}, bf16[256,1024]{1,0:T(8,128)(2,1)}, u32[]{:S(2)}) copy-start(bf16[256,1024]{1,0:T(8,128)(2,1)} %refs_2_.1) | copy-start | bytes 1572868
  11.3 12.0 %collective-permute-start.4 = (bf16[256,512]{1,0:T(8,128)(2,1)S(1)}, bf16[256,512]{1,0:T(8,128)(2,1)S(1)}, u32[]{:S(2)}, u32[]{:S(2)}) collective-permute-start(bf16[256,512]{1,0:T(8,128)(2,1)S(1)} %get-tuple-element.33.refs_7_), channel_id=1, source_target_pairs={{0,1},{1,0},{2,3},{3,2},{4,5},{5,4},{6,7},{7,6},{8,9},{9,8},{10,11... | collective-permute-start | bytes 786440 | tf_op jit(solution)/shard_map/ppermute | solution.py:307
  18.5 10.2 %collective-permute-start.7 = (bf16[320,512]{1,0:T(8,128)(2,1)S(1)}, bf16[320,512]{1,0:T(8,128)(2,1)S(1)}, u32[]{:S(2)}, u32[]{:S(2)}) collective-permute-start(bf16[320,512]{1,0:T(8,128)(2,1)S(1)} %get-tuple-element.36), channel_id=1, source_target_pairs={{0,1},{1,0},{2,3},{3,2},{4,5},{5,4},{6,7},{7,6},{8,9},{9,8},{10,11... | collective-permute-start | bytes 983048 | tf_op jit(solution)/shard_map/ppermute | solution.py:307
  19.8 9.1 %copy-start.1 = (bf16[1024,1024]{1,0:T(8,128)(2,1)S(1)}, bf16[1024,1024]{1,0:T(8,128)(2,1)}, u32[]{:S(2)}) copy-start(bf16[1024,1024]{1,0:T(8,128)(2,1)} %w_in.3) | copy-start | bytes 6291460
  19.8 9.1 %collective-permute-start.5 = (bf16[320,512]{1,0:T(8,128)(2,1)S(1)}, bf16[320,512]{1,0:T(8,128)(2,1)S(1)}, u32[]{:S(2)}, u32[]{:S(2)}) collective-permute-start(bf16[320,512]{1,0:T(8,128)(2,1)S(1)} %get-tuple-element.34.refs_3_), channel_id=1, source_target_pairs={{0,2},{1,3},{2,0},{3,1},{4,6},{5,7},{6,4},{7,5},{8,10},{9,11},{10,... | collective-permute-start | bytes 983048 | tf_op jit(solution)/shard_map/ppermute | solution.py:307
  29.7 8.6 %collective-permute-start.8 = (bf16[336,512]{1,0:T(8,128)(2,1)S(1)}, bf16[336,512]{1,0:T(8,128)(2,1)S(1)}, u32[]{:S(2)}, u32[]{:S(2)}) collective-permute-start(bf16[336,512]{1,0:T(8,128)(2,1)S(1)} %get-tuple-element.39.refs_0_), channel_id=1, source_target_pairs={{0,1},{1,0},{2,3},{3,2},{4,5},{5,4},{6,7},{7,6},{8,9},{9,8},{10,11... | collective-permute-start | bytes 1032200 | tf_op jit(solution)/shard_map/ppermute | solution.py:307
  31.0 8.3 %collective-permute-start.9 = (bf16[336,512]{1,0:T(8,128)(2,1)S(1)}, bf16[336,512]{1,0:T(8,128)(2,1)S(1)}, u32[]{:S(2)}, u32[]{:S(2)}) collective-permute-start(bf16[336,512]{1,0:T(8,128)(2,1)S(1)} %get-tuple-element.40.refs_1_), channel_id=1, source_target_pairs={{0,2},{1,3},{2,0},{3,1},{4,6},{5,7},{6,4},{7,5},{8,10},{9,11},{10,... | collective-permute-start | bytes 1032200 | tf_op jit(solution)/shard_map/ppermute | solution.py:307
  39.5 8.9 %collective-permute-start.10 = (bf16[400,512]{1,0:T(8,128)(2,1)S(1)}, bf16[400,512]{1,0:T(8,128)(2,1)S(1)}, u32[]{:S(2)}, u32[]{:S(2)}) collective-permute-start(bf16[400,512]{1,0:T(8,128)(2,1)S(1)} %get-tuple-element.43.refs_0_), channel_id=1, source_target_pairs={{0,2},{1,3},{2,0},{3,1},{4,6},{5,7},{6,4},{7,5},{8,10},{9,11},{10,... | collective-permute-start | bytes 1228808 | tf_op jit(solution)/shard_map/ppermute | solution.py:307
  40.2 8.7 %collective-permute-start.11 = (bf16[400,512]{1,0:T(8,128)(2,1)S(1)}, bf16[400,512]{1,0:T(8,128)(2,1)S(1)}, u32[]{:S(2)}, u32[]{:S(2)}) collective-permute-start(bf16[400,512]{1,0:T(8,128)(2,1)S(1)} %get-tuple-element.44.refs_1_), channel_id=1, source_target_pairs={{0,1},{1,0},{2,3},{3,2},{4,5},{5,4},{6,7},{7,6},{8,9},{9,8},{10,11... | collective-permute-start | bytes 1228808 | tf_op jit(solution)/shard_map/ppermute | solution.py:307
  50.2 9.3 %collective-permute-start.14 = (bf16[256,512]{1,0:T(8,128)(2,1)S(1)}, bf16[256,512]{1,0:T(8,128)(2,1)S(1)}, u32[]{:S(2)}, u32[]{:S(2)}) collective-permute-start(bf16[256,512]{1,0:T(8,128)(2,1)S(1)} %get-tuple-element.46.refs_2_.first), channel_id=1, source_target_pairs={{0,1},{1,0},{2,3},{3,2},{4,5},{5,4},{6,7},{7,6},{8,9},{9,8},{10,11... | collective-permute-start | bytes 786440 | tf_op jit(solution)/shard_map/ppermute | solution.py:307
  51.8 3.4 %copy-start.2 = (bf16[1,1024,512]{2,1,0:T(8,128)(2,1)S(1)}, bf16[1,1024,512]{2,1,0:T(8,128)(2,1)}, u32[]{:S(2)}) copy-start(bf16[1,1024,512]{2,1,0:T(8,128)(2,1)} %param.14) | copy-start | bytes 3145732
  51.8 3.4 %copy-start.6 = (f32[1,1024]{1,0:T(1,128)S(1)}, f32[1,1024]{1,0:T(1,128)}, u32[]{:S(2)}) copy-start(f32[1,1024]{1,0:T(1,128)} %gain_depth.1) | copy-start | bytes 12292
  51.8 9.2 %collective-permute-start.12 = (bf16[256,512]{1,0:T(8,128)(2,1)S(1)}, bf16[256,512]{1,0:T(8,128)(2,1)S(1)}, u32[]{:S(2)}, u32[]{:S(2)}) collective-permute-start(bf16[256,512]{1,0:T(8,128)(2,1)S(1)} %get-tuple-element.47.refs_3_.second), channel_id=1, source_target_pairs={{0,2},{1,3},{2,0},{3,1},{4,6},{5,7},{6,4},{7,5},{8,10},{9,11},{10,... | collective-permute-start | bytes 786440 | tf_op jit(solution)/shard_map/ppermute | solution.py:307
  52.9 11.5 %collective-permute-start.16 = (bf16[256,512]{1,0:T(8,128)(2,1)S(1)}, bf16[256,512]{1,0:T(8,128)(2,1)S(1)}, u32[]{:S(2)}, u32[]{:S(2)}) collective-permute-start(bf16[256,512]{1,0:T(8,128)(2,1)S(1)} %get-tuple-element.50), channel_id=1, source_target_pairs={{0,2},{1,3},{2,0},{3,1},{4,6},{5,7},{6,4},{7,5},{8,10},{9,11},{10,... | collective-permute-start | bytes 786440 | tf_op jit(solution)/shard_map/ppermute | solution.py:307
  54.6 9.8 %collective-permute-start.17 = (bf16[256,512]{1,0:T(8,128)(2,1)S(1)}, bf16[256,512]{1,0:T(8,128)(2,1)S(1)}, u32[]{:S(2)}, u32[]{:S(2)}) collective-permute-start(bf16[256,512]{1,0:T(8,128)(2,1)S(1)} %get-tuple-element.51), channel_id=1, source_target_pairs={{0,1},{1,0},{2,3},{3,2},{4,5},{5,4},{6,7},{7,6},{8,9},{9,8},{10,11... | collective-permute-start | bytes 786440 | tf_op jit(solution)/shard_map/ppermute | solution.py:307
  59.5 7.7 %collective-permute-start.15 = (bf16[256,512]{1,0:T(8,128)(2,1)S(1)}, bf16[256,512]{1,0:T(8,128)(2,1)S(1)}, u32[]{:S(2)}, u32[]{:S(2)}) collective-permute-start(bf16[256,512]{1,0:T(8,128)(2,1)S(1)} %collective-permute-done.14.refs_0_), channel_id=1, source_target_pairs={{0,2},{1,3},{2,0},{3,1},{4,6},{5,7},{6,4},{7,5},{8,10},{9,11},{10,... | collective-permute-start | bytes 786440 | tf_op jit(solution)/shard_map/ppermute | solution.py:307
  61.0 6.6 %collective-permute-start.13 = (bf16[256,512]{1,0:T(8,128)(2,1)S(1)}, bf16[256,512]{1,0:T(8,128)(2,1)S(1)}, u32[]{:S(2)}, u32[]{:S(2)}) collective-permute-start(bf16[256,512]{1,0:T(8,128)(2,1)S(1)} %collective-permute-done.12.refs_1_), channel_id=1, source_target_pairs={{0,1},{1,0},{2,3},{3,2},{4,5},{5,4},{6,7},{7,6},{8,9},{9,8},{10,11... | collective-permute-start | bytes 786440 | tf_op jit(solution)/shard_map/ppermute | solution.py:307

commit v6 on v5

--- a/solution.py
+++ b/solution.py
@@ -10,6 +10,7 @@
 EPS = 1e-05
 LANES = 128
 SQ = 16
+OUT_PIECES = 4
 bf16, f32 = jnp.bfloat16, jnp.float32
 VMEM = pl.BlockSpec(memory_space=pltpu.VMEM)
 HBM = pl.BlockSpec(memory_space=pltpu.HBM)
@@ -84,13 +85,21 @@
 def upstream_kernel(share, masks, cot, w_depth, gain_hbm, *refs):
     *outs, up = refs[:-4]
     cot_buf, depth_buf, gain_depth, sems = refs[-4:]
-    pairs = [(cot, cot_buf), (w_depth, depth_buf), (gain_hbm, gain_depth)]
+    pieces = sems.shape[0] - 2
+    step = depth_buf.shape[0] // pieces
+    pairs = [(cot, cot_buf), (gain_hbm, gain_depth)]
+    for k in range(pieces):
+        rows = pl.ds(k * step, step)
+        pairs.append((w_depth.at[rows, :], depth_buf.at[rows, :]))
     copies = [pltpu.make_async_copy(a, b, sems.at[i]) for i, (a, b) in enumerate(pairs)]
     for copy in copies:
         copy.start()
-    for copy in copies:
-        copy.wait()
-    up[...] = gain_depth[...] * contract_last(cot_buf[...], depth_buf[...])
+    copies[0].wait()
+    copies[1].wait()
+    for k in range(pieces):
+        copies[2 + k].wait()
+        cols = slice(k * step, (k + 1) * step)
+        up[:, cols] = gain_depth[:, cols] * contract_last(cot_buf[...], depth_buf[cols, :])
     wide = up.shape[1] // 2
     for side, out in enumerate(outs):
         for i, mask in enumerate(masks[side]):
@@ -99,38 +108,42 @@
             ].astype(bf16)
 
 
-def share_of(share, up, mask, side, got, place, adds, frames, half, c):
+def put_shares(share, items, up, gots, outs, first):
     wide = up.shape[1] // 2
-    cols = slice(c * half, (c + 1) * half)
-    part = up[span(owner(mask), share), side * wide + c * half : side * wide + (c + 1) * half]
-    part = part + got[place * share : (place + 1) * share, cols].astype(f32)
-    for add in adds:
-        part = part + add[frames + c * share : frames + (c + 1) * share, :].astype(f32)
-    return part
-
-
-def project_kernel(share, items, context, w_out, *refs):
-    outs, refs = refs[-len(items) :], refs[: -len(items)]
+    for side, (rows, out) in enumerate(zip(items, outs)):
+        for i, (mask, places) in enumerate(rows):
+            part = up[span(owner(mask), share), side * wide : (side + 1) * wide]
+            for phase, at in enumerate(places):
+                part = part + gots[2 * phase + side][at : at + share, :].astype(f32)
+            out[first + i * share : first + (i + 1) * share, :] = part.astype(bf16)
+
+
+def shares_kernel(share, items, up, *refs):
+    put_shares(share, items, up, refs[:-2], refs[-2:], 0)
+
+
+def join_kernel(*refs):
+    for side in range(2):
+        first, second, out = refs[side], refs[2 + side], refs[4 + side]
+        out[: first.shape[0], :] = first[...]
+        out[first.shape[0] :, :] = second[...]
+
+
+def project_kernel(share, items, riders, context, w_out, *refs):
+    adds, outs = refs[: -len(items)], refs[-len(items) :]
     half = outs[0].shape[1]
     frames = context.shape[0]
-    at = 3
-    for (mask, side, count, place), out in zip(items, outs):
+    at = 0
+    for (mask, side, count), out in zip(items, outs):
         product = jnp.dot(
             context[...], w_out[:, cols_of(mask, side, half)], preferred_element_type=f32
         )
-        adds = refs[at : at + count]
-        at += count
-        for add in adds:
+        for add in adds[at : at + count]:
             product = product + add[:frames, :].astype(f32)
         out[:frames, :] = product.astype(bf16)
-        if not count:
-            continue
-        up, got = refs[0], refs[1 + side]
-        for c in range(up.shape[1] // 2 // half):
-            rows = slice(frames + c * share, frames + (c + 1) * share)
-            out[rows, :] = share_of(
-                share, up, mask, side, got, place, adds[1:], frames, half, c
-            ).astype(bf16)
+        at += count
+    if riders:
+        put_shares(share, riders, adds[at], adds[at + 1 :], outs[::-1], frames)
 
 
 def keep_kernel(context, w_out, residual, out):
@@ -141,9 +154,8 @@
     )
 
 
-def state_kernel(log, share, places, gain, w_in, up, kept, *refs):
-    got, adds = refs[:2], refs[2 : 2 + 2 * log]
-    state, raw, squares, *sends = refs[2 + 2 * log :]
+def state_kernel(log, gain, w_in, kept, *refs):
+    adds, (state, raw, squares, *sends) = refs[: 2 * log], refs[2 * log :]
     frames, width = state.shape
     half = width // 2
     wide = raw.shape[1] // 2
@@ -159,18 +171,13 @@
     column = jnp.sum(value * value, axis=1, keepdims=True)
     row = jnp.transpose(jnp.broadcast_to(column, (frames, LANES)))[: SQ // 2]
     for side, send in enumerate(sends):
-        squares[side] = row
         send[:frames, :] = raw[:, side * wide : (side + 1) * wide].astype(bf16)
-        put_squares(send, frames, row)
-        late = adds[side * log + 1 : (side + 1) * log]
-        for c in range(wide // half):
-            send[frames + SQ :, c * half : (c + 1) * half] = share_of(
-                share, up, 0, side, got[side], places[side], late, frames, half, c
-            ).astype(bf16)
+    squares[...] = row
+    put_squares(sends[0], frames, row)
 
 
 def reduce_kernel(raw, squares, *refs):
-    sent, got, (raw_out, squares_out, *sends) = refs[:2], refs[2:4], refs[4:]
+    got, (raw_out, squares_out, *sends) = refs[:2], refs[2:]
     frames, depth = raw.shape
     wide = depth // 2
     for side in range(2):
@@ -178,13 +185,9 @@
         total = raw[:, cols] + got[side][:frames, :].astype(f32)
         raw_out[:, cols] = total
         sends[side][:frames, :] = total.astype(bf16)
-        row = squares[side] + get_squares(got[side], frames, frames)
-        squares_out[side] = row
-        put_squares(sends[side], frames, row)
-        first = frames + SQ
-        held = sent[side].shape[0] - first
-        sends[side][first : first + held, :] = sent[side][first:, :]
-        sends[side][first + held :, :] = got[side][first:, :]
+    row = squares[...] + get_squares(got[0], frames, frames)
+    squares_out[...] = row
+    put_squares(sends[0], frames, row)
 
 
 def depth_rows(raw, got, rows):
@@ -199,25 +202,29 @@
 
 
 def recip_of(squares, got, frames, features):
-    row = squares[0] + get_squares(got[0], frames, frames)
+    row = squares[...] + get_squares(got[0], frames, frames)
     return jnp.transpose(
         jnp.broadcast_to(lax.rsqrt(row[:1] / features + EPS), (LANES, frames))
     )[:, :1]
 
 
-def back_kernel(log, haves, share, features, gain, w_in, state, raw, squares, *refs):
-    sent, got, (*grads, up, du) = refs[:2], refs[2:4], refs[4:]
-    frames, width = state.shape
-    half, wide = width // 2, raw.shape[1] // 2
-    first = frames + SQ
+def assemble_kernel(haves, share, *refs):
+    sent, rest, up = refs[:2], refs[2:4], refs[4]
+    wide = up.shape[1] // 2
     for side in range(2):
-        held = sent[side].shape[0] - first
+        held = sent[side].shape[0]
         for i, mask in enumerate(haves[side]):
             at = i * share
-            ref, at = (sent[side], at) if at < held else (got[side], at - held)
+            ref, at = (sent[side], at) if at < held else (rest[side], at - held)
             up[span(owner(mask), share), side * wide : (side + 1) * wide] = ref[
-                first + at : first + at + share, :
+                at : at + share, :
             ]
+
+
+def back_kernel(features, gain, w_in, up, state, raw, squares, *refs):
+    got, (*grads, du) = refs[:2], refs[2:]
+    frames, width = state.shape
+    half = width // 2
     recip = recip_of(squares, got, frames, features)
     back = []
     step = 64 if frames % 64 == 0 else frames
@@ -275,14 +282,19 @@
     out[...] = total
 
 
-def last_kernel(log, mask, side, w_out, block, total, out, buf, sems):
+def last_kernel(items, w_out, *refs):
+    blocks, (total, out, buf, sems) = refs[: len(items)], refs[len(items) :]
     pieces = sems.shape[0]
     step = total.shape[1] // pieces
     copies = []
     for k in range(pieces):
         rows = slice(k * step, (k + 1) * step)
-        part = contract_last(block[...], w_out[rows, cols_of(mask, side, block.shape[1])])
-        buf[:, rows] = (total[:, rows] + part).astype(bf16)
+        value = total[:, rows]
+        for (mask, side), block in zip(items, blocks):
+            value = value + contract_last(
+                block[...], w_out[rows, cols_of(mask, side, block.shape[1])]
+            )
+        buf[:, rows] = value.astype(bf16)
         copies.append(pltpu.make_async_copy(buf.at[:, rows], out.at[:, rows], sems.at[k]))
         copies[-1].start()
     for copy in copies:
@@ -301,7 +313,6 @@
     bits = [1 << i for i in range(log)]
     orders = (bits, bits[::-1])
     gain = gain_temporal[None, :]
-    extra = share * (wide // half)
 
     def swap(value, bit):
         return lax.ppermute(value, "mp", [(i, i ^ bit) for i in range(n)])
@@ -312,9 +323,47 @@
     masks = sorted(range(1, n), key=lambda k: (-k.bit_count(), k))
     pairs = [((k, 0), (mirror(k, log), 1)) for k in masks]
 
-    first = [[mask for mask in range(1, n) if phase_of(mask, side) == 0] for side in range(2)]
+    lists = [
+        [[k for k in range(1, n) if phase_of(k, side) == i] for i in range(log)]
+        for side in range(2)
+    ]
+
+    def share_items(phase, gots):
+        items = []
+        for side, order in enumerate(orders):
+            masks = lists[side][phase] if phase < log else [0]
+            items.append(
+                [
+                    (
+                        k,
+                        [
+                            gots[j][1] + lists[side][j].index(k ^ order[j]) * share
+                            for j in range(phase)
+                        ],
+                    )
+                    for k in masks
+                ]
+            )
+        return items, [value for values, _ in gots for value in values]
+
+    def shares(phase, gots, after):
+        items, listed = share_items(phase, gots)
+        return list(
+            call(
+                functools.partial(shares_kernel, share, items),
+                [((share * len(items[0]), wide), bf16)] * 2,
+                [up] + listed,
+                name="shares",
+                after=after,
+                cost=FREE,
+            )
+        )
+
+    def both(values, i):
+        return [swap(values[side], orders[side][i]) for side in range(2)]
+
     *values, up = call(
-        functools.partial(upstream_kernel, share, first),
+        functools.partial(upstream_kernel, share, [lists[side][0] for side in range(2)]),
         [((share * n // 2, wide), bf16)] * 2 + [((frames, depth), f32)],
         [cotangent[0], w_depth[0], gain_depth],
         [HBM] * 3,
@@ -326,66 +375,91 @@
         ],
         name="upstream",
     )
-    got_up = [swap(values[side], orders[side][0]) for side in range(2)]
-
-    def place(mask, side):
-        return first[side].index(mask ^ orders[side][0])
+    share_gots = [(both(values, 0), 0)]
 
     arrived = {}
     token = up
     for pair in pairs:
-        items, listed = [], []
+        items, listed, riders, extra = [], [], None, 0
         for mask, side in pair:
             phase = phase_of(mask, side)
             listed += [arrived[mask ^ bit, side] for bit in orders[side][:phase]]
-            items.append((mask, side, phase, place(mask, side) if phase else 0))
-        shape = ((frames + (extra if phase else 0), half), bf16)
+            items.append((mask, side, phase))
+        if log == 2 and wide == half and pair is pairs[-2]:
+            riders, more = share_items(1, share_gots)
+            listed += [up] + more
+            extra = share * len(riders[0])
+        elif log != 2 and pair is pairs[-1]:
+            for i in range(1, log):
+                values = shares(i, share_gots, token)
+                token = values[0]
+                share_gots.append((both(values, i), 0))
         values = call(
-            functools.partial(project_kernel, share, items),
-            [shape] * 2,
-            [context, w_out, up] + got_up + listed
-            if listed
-            else [context, w_out, up, gain, gain],
+            functools.partial(project_kernel, share, items, riders),
+            [((frames + extra, half), bf16)] * 2,
+            [context, w_out] + listed,
             name="project",
             after=token,
         )
         token = values[0]
         for (mask, side), value in zip(pair, values):
             arrived[mask, side] = swap(value, orders[side][phase_of(mask, side)])
+        if riders:
+            share_gots.append(([arrived[key] for key in pair[::-1]], frames))
     kept = call(
         keep_kernel,
         [((frames, width), f32)],
         [context, w_out, residual],
         name="keep",
-        after=values[0],
+        after=token,
     )[0]
+    own_share = shares(log, share_gots, kept)
+    share_got = both(own_share, 0)
 
     state, raw, squares, *sends = call(
-        functools.partial(state_kernel, log, share, [place(0, side) for side in range(2)]),
-        [((frames, width), f32), ((frames, depth), f32), ((2, SQ // 2, frames), f32)]
-        + [((frames + SQ + share, wide), bf16)] * 2,
-        [gain, w_in, up, kept]
-        + got_up
-        + [arrived[bit, side] for side in range(2) for bit in orders[side]],
+        functools.partial(state_kernel, log),
+        [((frames, width), f32), ((frames, depth), f32), ((SQ // 2, frames), f32)]
+        + [((frames + SQ, wide), bf16), ((frames, wide), bf16)],
+        [gain, w_in, kept] + [arrived[bit, side] for side in range(2) for bit in orders[side]],
         name="state",
+        after=own_share[0],
     )
     haves = [[0], [0]]
+    token = squares
     for i in range(log):
-        got = [swap(sends[side], orders[side][i]) for side in range(2)]
+        got = both(sends, i)
         haves = [have + [k ^ orders[s][i] for k in have] for s, have in enumerate(haves)]
         if i < log - 1:
+            own_share = list(
+                call(
+                    join_kernel,
+                    [((2 * own_share[0].shape[0], wide), bf16)] * 2,
+                    own_share + share_got,
+                    name="join",
+                    after=token,
+                )
+            )
+            share_got = both(own_share, i + 1)
             raw, squares, *sends = call(
                 reduce_kernel,
-                [(raw.shape, f32), (squares.shape, f32)]
-                + [((frames + SQ + share * len(haves[0]), wide), bf16)] * 2,
-                [raw, squares] + list(sends) + got,
+                [(raw.shape, f32), (squares.shape, f32)] + [((frames + SQ, wide), bf16), ((frames, wide), bf16)],
+                [raw, squares] + got,
                 name="reduce",
+                after=own_share[0],
             )
+            token = squares
+    up_all = call(
+        functools.partial(assemble_kernel, haves, share),
+        [((frames, depth), bf16)],
+        own_share + share_got,
+        name="assemble",
+        after=token,
+    )[0]
     grads = call(
-        functools.partial(back_kernel, log, haves, share, features),
+        functools.partial(back_kernel, features),
         [((frames, half), bf16)] * 2,
-        [gain, w_in, state, raw, squares] + list(sends) + got,
-        scratch=[pltpu.VMEM((frames, depth), bf16)] * 2,
+        [gain, w_in, up_all, state, raw, squares] + got,
+        scratch=[pltpu.VMEM((frames, depth), bf16)],
         name="back",
     )
 
@@ -411,8 +485,7 @@
         name="act",
     )
     keys = [((haves[0][k], 0), (haves[1][k], 1)) for k in range(n)]
-    final = keys[-1][1]
-    for pair in keys[1:-1] + [keys[-1][:1]]:
+    for pair in keys[1:-1]:
         total = call(
             functools.partial(context_kernel, log, pair),
             [((frames, heads), f32)],
@@ -420,10 +493,13 @@
             name="grad_context",
         )[0]
     grad_context = call(
-        functools.partial(last_kernel, log, *final),
+        functools.partial(last_kernel, keys[-1]),
         [((frames, heads), bf16)],
-        [w_out, blocks[final], total],
-        scratch=[pltpu.VMEM((frames, heads), bf16), pltpu.SemaphoreType.DMA((2,))],
+        [w_out] + [blocks[key] for key in keys[-1]] + [total],
+        scratch=[
+            pltpu.VMEM((frames, heads), bf16),
+            pltpu.SemaphoreType.DMA((min(OUT_PIECES, heads // LANES),)),
+        ],
         name="grad_context",
         out_specs=[HBM],
     )[0]

time: 69 us -> 67.1 us (0.972)
  waiting for transfers between devices: 34.2 us -> 27.8 us
  starting transfers between devices: 21.3 us -> 25.7 us
    ppermute x18 -> x22, waiting for transfers between devices: 34.2 us -> 27.8 us  [swap(): return lax.ppermute(value, 'mp', [(i, i ^ bit) for i in range(n)])]
    ppermute x18 -> x22, starting transfers between devices: 21.3 us -> 25.7 us  [swap(): return lax.ppermute(value, 'mp', [(i, i ^ bit) for i in range(n)])]
    pallas_call x14 -> x16, Pallas kernels: 12.6 us -> 12.6 us  [call(): pl.pallas_call(kernel, out_shape=[jax.ShapeDtypeStruct(s, d) for s, d in...]
  transfers between devices with their start and end apart: 18 -> 22, of which waited for: 14 -> 12; matrix products, arithmetic and copies ran while one was open for 0% -> 0% of each run, Pallas kernels for 10% -> 12%
where the time goes in v6:
time: 67.1 us; the launch traced here: 67 us
  waiting for transfers between devices  27.8 us (41%)
  starting transfers between devices  25.7 us (38%)
  Pallas kernels  12.6 us (19%)
  between operations  0.78 us (1%)
    ppermute x22, waiting for transfers between devices, swap(): return lax.ppermute(value, 'mp', [(i, i ^ bit) for i in range(n)])  27.8 us
    ppermute x22, starting transfers between devices, swap(): return lax.ppermute(value, 'mp', [(i, i ^ bit) for i in range(n)])  25.7 us
    pallas_call x16, Pallas kernels, call(): pl.pallas_call(kernel, out_shape=[jax.ShapeDtypeStruct(s, d) for s, d in...  12.6 us
  transfers between devices with their start and end apart: 22, of which 12 were waited for; matrix products, arithmetic and copies ran while one was open for 0% of the time, Pallas kernels for 12%

profile of v6, /device:TPU:0, one launch (start us, length us, event | category | flops | bytes accessed | tf_op | source)
XLA Modules:
  0.0 67.0 jit_solution(9488173630299361302)
XLA Ops:
  0.7 2.0 %upstream.1 = (bf16[128,512]{1,0:T(8,128)(2,1)S(1)}, bf16[128,512]{1,0:T(8,128)(2,1)S(1)}, f32[256,1024]{1,0:T(8,128)S(1)}) custom-call(bf16[256,512]{1,0:T(8,128)(2,1)} %bitcast.8, bf16[1024,512]{1,0:T(8,128)(2,1)} %bitcast.4, f32[1,1024]{1,0:T(1,128)} %gain_depth.1), custom_call_target="tpu_custom_call" | custom-call | flops 20000000000 | bytes 60000000 | tf_op jit(solution)/shard_map/upstream/pallas_call | solution.py:47
  2.7 3.0 %collective-permute-start.2 = (bf16[128,512]{1,0:T(8,128)(2,1)S(1)}, bf16[128,512]{1,0:T(8,128)(2,1)S(1)}, u32[]{:S(2)}, u32[]{:S(2)}) collective-permute-start(bf16[128,512]{1,0:T(8,128)(2,1)S(1)} %get-tuple-element.35), channel_id=1, source_target_pairs={{0,1},{1,0},{2,3},{3,2},{4,5},{5,4},{6,7},{7,6},{8,9},{9,8},{10,11... | collective-permute-start | bytes 393224 | tf_op jit(solution)/shard_map/ppermute | solution.py:318
  5.7 1.5 %collective-permute-start.3 = (bf16[128,512]{1,0:T(8,128)(2,1)S(1)}, bf16[128,512]{1,0:T(8,128)(2,1)S(1)}, u32[]{:S(2)}, u32[]{:S(2)}) collective-permute-start(bf16[128,512]{1,0:T(8,128)(2,1)S(1)} %get-tuple-element.36), channel_id=1, source_target_pairs={{0,2},{1,3},{2,0},{3,1},{4,6},{5,7},{6,4},{7,5},{8,10},{9,11},{10,... | collective-permute-start | bytes 393224 | tf_op jit(solution)/shard_map/ppermute | solution.py:318
  7.2 0.7 %project.3 = (bf16[256,512]{1,0:T(8,128)(2,1)S(1)}, bf16[256,512]{1,0:T(8,128)(2,1)S(1)}) custom-call(bf16[256,1024]{1,0:T(8,128)(2,1)S(1)} %copy-done.3, bf16[1024,4096]{1,0:T(8,128)(2,1)S(1)} %copy-done, f32[256,1024]{1,0:T(8,128)S(1)} %get-tuple-element.32.refs_2_.refs_0_), custom_call_target="tpu_custom_call" | custom-call | flops 20000000000 | bytes 60000000 | tf_op jit(solution)/shard_map/project/pallas_call | solution.py:47
  7.9 0.6 collective-permute-start
  8.5 1.2 %collective-permute-start.1 = (bf16[256,512]{1,0:T(8,128)(2,1)S(1)}, bf16[256,512]{1,0:T(8,128)(2,1)S(1)}, u32[]{:S(2)}, u32[]{:S(2)}) collective-permute-start(bf16[256,512]{1,0:T(8,128)(2,1)S(1)} %get-tuple-element.34), channel_id=1, source_target_pairs={{0,2},{1,3},{2,0},{3,1},{4,6},{5,7},{6,4},{7,5},{8,10},{9,11},{10,... | collective-permute-start | bytes 786440 | tf_op jit(solution)/shard_map/ppermute | solution.py:318
  9.7 0.0 collective-permute-done.2.refs_3_.refs_1_
  9.7 1.2 %collective-permute-done.3.refs_4_.refs_2_ = bf16[128,512]{1,0:T(8,128)(2,1)S(1)} collective-permute-done((bf16[128,512]{1,0:T(8,128)(2,1)S(1)}, bf16[128,512]{1,0:T(8,128)(2,1)S(1)}, u32[]{:S(2)}, u32[]{:S(2)}) %collective-permute-start.3) | collective-permute-done | bytes 131104 | tf_op jit(solution)/shard_map/ppermute | solution.py:318
  10.9 0.7 %project.4 = (bf16[320,512]{1,0:T(8,128)(2,1)S(1)}, bf16[320,512]{1,0:T(8,128)(2,1)S(1)}) custom-call(bf16[256,1024]{1,0:T(8,128)(2,1)S(1)} %copy-done.3, bf16[1024,4096]{1,0:T(8,128)(2,1)S(1)} %copy-done, f32[256,1024]{1,0:T(8,128)S(1)} %get-tuple-element.32.refs_2_.refs_0_, bf16[128,512]{1,0:T(8,128)(2,1)S(1)} %collective-permute-done.2.refs_3_.refs_1_, ...), custom_call_target="tpu_custom_call" | custom-call | flops 20000000000 | bytes 60000000 | tf_op jit(solution)/shard_map/project/pallas_call | solution.py:47
  11.6 0.3 collective-permute-start.4
  11.9 1.8 %collective-permute-start.6 = (bf16[320,512]{1,0:T(8,128)(2,1)S(1)}, bf16[320,512]{1,0:T(8,128)(2,1)S(1)}, u32[]{:S(2)}, u32[]{:S(2)}) collective-permute-start(bf16[320,512]{1,0:T(8,128)(2,1)S(1)} %get-tuple-element.39), channel_id=1, source_target_pairs={{0,2},{1,3},{2,0},{3,1},{4,6},{5,7},{6,4},{7,5},{8,10},{9,11},{10,... | collective-permute-start | bytes 983048 | tf_op jit(solution)/shard_map/ppermute | solution.py:318
  13.8 3.5 %collective-permute-done.refs_2_ = bf16[256,512]{1,0:T(8,128)(2,1)S(1)} collective-permute-done((bf16[256,512]{1,0:T(8,128)(2,1)S(1)}, bf16[256,512]{1,0:T(8,128)(2,1)S(1)}, u32[]{:S(2)}, u32[]{:S(2)}) %collective-permute-start) | collective-permute-done | bytes 262176 | tf_op jit(solution)/shard_map/ppermute | solution.py:318
  17.2 0.5 collective-permute-done.1.refs_3_
  17.8 0.7 %project.5 = (bf16[256,512]{1,0:T(8,128)(2,1)S(1)}, bf16[256,512]{1,0:T(8,128)(2,1)S(1)}) custom-call(bf16[256,1024]{1,0:T(8,128)(2,1)S(1)} %copy-done.3, bf16[1024,4096]{1,0:T(8,128)(2,1)S(1)} %copy-done, bf16[256,512]{1,0:T(8,128)(2,1)S(1)} %collective-permute-done.refs_2_, bf16[256,512]{1,0:T(8,128)(2,1)S(1)} %collective-permute-done.1.refs_3_, ...), custom_call_target="tpu_custom_call" | custom-call | flops 20000000000 | bytes 60000000 | tf_op jit(solution)/shard_map/project/pallas_call | solution.py:47
  18.5 1.3 %collective-permute-start.5 = (bf16[256,512]{1,0:T(8,128)(2,1)S(1)}, bf16[256,512]{1,0:T(8,128)(2,1)S(1)}, u32[]{:S(2)}, u32[]{:S(2)}) collective-permute-start(bf16[256,512]{1,0:T(8,128)(2,1)S(1)} %get-tuple-element.38.refs_3_), channel_id=1, source_target_pairs={{0,2},{1,3},{2,0},{3,1},{4,6},{5,7},{6,4},{7,5},{8,10},{9,11},{10,... | collective-permute-start | bytes 786440 | tf_op jit(solution)/shard_map/ppermute | solution.py:318
  19.7 0.8 %collective-permute-start.7 = (bf16[256,512]{1,0:T(8,128)(2,1)S(1)}, bf16[256,512]{1,0:T(8,128)(2,1)S(1)}, u32[]{:S(2)}, u32[]{:S(2)}) collective-permute-start(bf16[256,512]{1,0:T(8,128)(2,1)S(1)} %get-tuple-element.40), channel_id=1, source_target_pairs={{0,1},{1,0},{2,3},{3,2},{4,5},{5,4},{6,7},{7,6},{8,9},{9,8},{10,11... | collective-permute-start | bytes 786440 | tf_op jit(solution)/shard_map/ppermute | solution.py:318
  20.6 0.7 %keep.1.refs_5_.refs_2_ = f32[256,1024]{1,0:T(8,128)S(1)} custom-call(bf16[256,1024]{1,0:T(8,128)(2,1)S(1)} %copy-done.3, bf16[1024,4096]{1,0:T(8,128)(2,1)S(1)} %copy-done, bf16[256,1024]{1,0:T(8,128)(2,1)S(1)} %copy-done.4, bf16[256,512]{1,0:T(8,128)(2,1)S(1)} %get-tuple-element.38.refs_3_), custom_call_target="tpu_custom_call" | custom-call | flops 20000000000 | bytes 60000000 | tf_op jit(solution)/shard_map/keep/pallas_call | solution.py:47
  21.3 3.0 %collective-permute-done.4.refs_4_.refs_3_ = bf16[320,512]{1,0:T(8,128)(2,1)S(1)} collective-permute-done((bf16[320,512]{1,0:T(8,128)(2,1)S(1)}, bf16[320,512]{1,0:T(8,128)(2,1)S(1)}, u32[]{:S(2)}, u32[]{:S(2)}) %collective-permute-start.4) | collective-permute-done | bytes 327712 | tf_op jit(solution)/shard_map/ppermute | solution.py:318
  24.2 0.5 collective-permute-done.6.refs_3_.refs_5_
  24.8 1.6 %collective-permute-start.10 = (bf16[64,512]{1,0:T(8,128)(2,1)S(1)}, bf16[64,512]{1,0:T(8,128)(2,1)S(1)}, u32[]{:S(2)}, u32[]{:S(2)}) collective-permute-start(bf16[64,512]{1,0:T(8,128)(2,1)S(1)} %get-tuple-element.41.refs_7_.refs_0_), channel_id=1, source_target_pairs={{0,1},{1,0},{2,3},{3,2},{4,5},{5,4},{6,7},{7,6},{8,9},{9,8},{10,11... | collective-permute-start | bytes 196616 | tf_op jit(solution)/shard_map/ppermute | solution.py:318
  26.4 0.5 collective-permute-start.11
  26.9 2.7 %collective-permute-done.5.refs_4_ = bf16[256,512]{1,0:T(8,128)(2,1)S(1)} collective-permute-done((bf16[256,512]{1,0:T(8,128)(2,1)S(1)}, bf16[256,512]{1,0:T(8,128)(2,1)S(1)}, u32[]{:S(2)}, u32[]{:S(2)}) %collective-permute-start.5) | collective-permute-done | bytes 262176 | tf_op jit(solution)/shard_map/ppermute | solution.py:318
  29.6 0.0 collective-permute-done.7.refs_6_
  29.6 0.8 %state.1 = (f32[256,1024]{1,0:T(8,128)S(1)}, f32[256,1024]{1,0:T(8,128)S(1)}, f32[8,256]{1,0:T(8,128)S(1)}, bf16[272,512]{1,0:T(8,128)(2,1)S(1)}, bf16[256,512]{1,0:T(8,128)(2,1)S(1)}) custom-call(f32[1,4096]{1,0:T(1,128)S(1)} %bitcast.6, bf16[1024,1024]{1,0:T(8,128)(2,1)S(1)} %copy-done.1, f32[256,1024]{1,0:T(8,128)S(1)} %keep.1.refs_5_.refs_2_, ...), custom_call_target="tpu_custom_call" | custom-call | flops 20000000000 | bytes 60000000 | tf_op jit(solution)/shard_map/state/pallas_call | solution.py:47
  30.4 1.0 %collective-permute-start.8 = (bf16[272,512]{1,0:T(8,128)(2,1)S(1)}, bf16[272,512]{1,0:T(8,128)(2,1)S(1)}, u32[]{:S(2)}, u32[]{:S(2)}) collective-permute-start(bf16[272,512]{1,0:T(8,128)(2,1)S(1)} %get-tuple-element.44), channel_id=1, source_target_pairs={{0,1},{1,0},{2,3},{3,2},{4,5},{5,4},{6,7},{7,6},{8,9},{9,8},{10,11... | collective-permute-start | bytes 835592 | tf_op jit(solution)/shard_map/ppermute | solution.py:318
  31.4 1.1 %collective-permute-start.9 = (bf16[256,512]{1,0:T(8,128)(2,1)S(1)}, bf16[256,512]{1,0:T(8,128)(2,1)S(1)}, u32[]{:S(2)}, u32[]{:S(2)}) collective-permute-start(bf16[256,512]{1,0:T(8,128)(2,1)S(1)} %get-tuple-element.45), channel_id=1, source_target_pairs={{0,2},{1,3},{2,0},{3,1},{4,6},{5,7},{6,4},{7,5},{8,10},{9,11},{10,... | collective-permute-start | bytes 786440 | tf_op jit(solution)/shard_map/ppermute | solution.py:318
  32.5 1.0 %collective-permute-start.14 = (bf16[128,512]{1,0:T(8,128)(2,1)S(1)}, bf16[128,512]{1,0:T(8,128)(2,1)S(1)}, u32[]{:S(2)}, u32[]{:S(2)}) collective-permute-start(bf16[128,512]{1,0:T(8,128)(2,1)S(1)} %get-tuple-element.47.refs_4_.refs_0_), channel_id=1, source_target_pairs={{0,2},{1,3},{2,0},{3,1},{4,6},{5,7},{6,4},{7,5},{8,10},{9,11},{10,... | collective-permute-start | bytes 393224 | tf_op jit(solution)/shard_map/ppermute | solution.py:318
  33.5 1.1 %collective-permute-start.15 = (bf16[128,512]{1,0:T(8,128)(2,1)S(1)}, bf16[128,512]{1,0:T(8,128)(2,1)S(1)}, u32[]{:S(2)}, u32[]{:S(2)}) collective-permute-start(bf16[128,512]{1,0:T(8,128)(2,1)S(1)} %get-tuple-element.52.refs_1_), channel_id=1, source_target_pairs={{0,1},{1,0},{2,3},{3,2},{4,5},{5,4},{6,7},{7,6},{8,9},{9,8},{10,11... | collective-permute-start | bytes 393224 | tf_op jit(solution)/shard_map/ppermute | solution.py:318
  34.6 4.9 %collective-permute-done.9.refs_3_ = bf16[256,512]{1,0:T(8,128)(2,1)S(1)} collective-permute-done((bf16[256,512]{1,0:T(8,128)(2,1)S(1)}, bf16[256,512]{1,0:T(8,128)(2,1)S(1)}, u32[]{:S(2)}, u32[]{:S(2)}) %collective-permute-start.9) | collective-permute-done | bytes 262176 | tf_op jit(solution)/shard_map/ppermute | solution.py:318
  39.5 0.2 reduce.1
  39.6 1.9 %collective-permute-start.12 = (bf16[272,512]{1,0:T(8,128)(2,1)S(1)}, bf16[272,512]{1,0:T(8,128)(2,1)S(1)}, u32[]{:S(2)}, u32[]{:S(2)}) collective-permute-start(bf16[272,512]{1,0:T(8,128)(2,1)S(1)} %get-tuple-element.50), channel_id=1, source_target_pairs={{0,2},{1,3},{2,0},{3,1},{4,6},{5,7},{6,4},{7,5},{8,10},{9,11},{10,... | collective-permute-start | bytes 835592 | tf_op jit(solution)/shard_map/ppermute | solution.py:318
  41.5 1.5 %collective-permute-start.13 = (bf16[256,512]{1,0:T(8,128)(2,1)S(1)}, bf16[256,512]{1,0:T(8,128)(2,1)S(1)}, u32[]{:S(2)}, u32[]{:S(2)}) collective-permute-start(bf16[256,512]{1,0:T(8,128)(2,1)S(1)} %get-tuple-element.51), channel_id=1, source_target_pairs={{0,1},{1,0},{2,3},{3,2},{4,5},{5,4},{6,7},{7,6},{8,9},{9,8},{10,11... | collective-permute-start | bytes 786440 | tf_op jit(solution)/shard_map/ppermute | solution.py:318
  43.0 6.1 %collective-permute-done.13.refs_1_ = bf16[256,512]{1,0:T(8,128)(2,1)S(1)} collective-permute-done((bf16[256,512]{1,0:T(8,128)(2,1)S(1)}, bf16[256,512]{1,0:T(8,128)(2,1)S(1)}, u32[]{:S(2)}, u32[]{:S(2)}) %collective-permute-start.13) | collective-permute-done | bytes 262176 | tf_op jit(solution)/shard_map/ppermute | solution.py:318
  49.1 1.4 %back.1 = (bf16[256,512]{1,0:T(8,128)(2,1)S(1)}, bf16[256,512]{1,0:T(8,128)(2,1)S(1)}) custom-call(f32[1,4096]{1,0:T(1,128)S(1)} %bitcast.7, bf16[1024,1024]{1,0:T(8,128)(2,1)S(1)} %copy-done.1, bf16[256,1024]{1,0:T(8,128)(2,1)S(1)} %assemble.1.up, f32[256,1024]{1,0:T(8,128)S(1)} %get-tuple-element.53.state, f32[256,1024]{1,0:T(8,128)S(1)} %get-tuple-element.48.raw, ...), custom_call_target="tpu_custom_call" | custom-call | flops 20000000000 | bytes 60000000 | tf_op jit(solution)/shard_map/back/pallas_call | solution.py:47
  50.5 1.6 %collective-permute-start.16 = (bf16[256,512]{1,0:T(8,128)(2,1)S(1)}, bf16[256,512]{1,0:T(8,128)(2,1)S(1)}, u32[]{:S(2)}, u32[]{:S(2)}) collective-permute-start(bf16[256,512]{1,0:T(8,128)(2,1)S(1)} %get-tuple-element.54.refs_2_.first), channel_id=1, source_target_pairs={{0,1},{1,0},{2,3},{3,2},{4,5},{5,4},{6,7},{7,6},{8,9},{9,8},{10,11... | collective-permute-start | bytes 786440 | tf_op jit(solution)/shard_map/ppermute | solution.py:318
  52.0 0.7 %grad_context.4 = (f32[256,1024]{1,0:T(8,128)S(1)}, bf16[256,512]{1,0:T(8,128)(2,1)S(1)}, bf16[256,512]{1,0:T(8,128)(2,1)S(1)}) custom-call(bf16[1024,4096]{1,0:T(8,128)(2,1)S(1)} %copy-done, bf16[256,512]{1,0:T(8,128)(2,1)S(1)} %get-tuple-element.54.refs_2_.first, bf16[256,512]{1,0:T(8,128)(2,1)S(1)} %get-tuple-element.55.refs_3_.second), custom_call_target="tpu_custom_call" | custom-call | flops 20000000000 | bytes 60000000 | tf_op jit(solution)/shard_map/grad_context/pallas_call | solution.py:47
  52.8 2.1 %collective-permute-start.20 = (bf16[256,512]{1,0:T(8,128)(2,1)S(1)}, bf16[256,512]{1,0:T(8,128)(2,1)S(1)}, u32[]{:S(2)}, u32[]{:S(2)}) collective-permute-start(bf16[256,512]{1,0:T(8,128)(2,1)S(1)} %get-tuple-element.58), channel_id=1, source_target_pairs={{0,2},{1,3},{2,0},{3,1},{4,6},{5,7},{6,4},{7,5},{8,10},{9,11},{10,... | collective-permute-start | bytes 786440 | tf_op jit(solution)/shard_map/ppermute | solution.py:318
  54.9 0.5 collective-permute-start.21
  55.4 1.6 %act.1 = (bf16[256,512]{1,0:T(8,128)(2,1)}, bf16[256,1024]{1,0:T(8,128)(2,1)}) custom-call(f32[1,1024]{1,0:T(1,128)S(1)} %copy-done.6, bf16[1024,512]{1,0:T(8,128)(2,1)S(1)} %bitcast.5, f32[256,1024]{1,0:T(8,128)S(1)} %get-tuple-element.48.raw, f32[8,256]{1,0:T(8,128)S(1)} %get-tuple-element.49.refs_4_.squares, ...), custom_call_target="tpu_custom_call" | custom-call | flops 20000000000 | bytes 60000000 | tf_op jit(solution)/shard_map/act/pallas_call | solution.py:47
  57.0 2.1 %collective-permute-done.16.refs_0_ = bf16[256,512]{1,0:T(8,128)(2,1)S(1)} collective-permute-done((bf16[256,512]{1,0:T(8,128)(2,1)S(1)}, bf16[256,512]{1,0:T(8,128)(2,1)S(1)}, u32[]{:S(2)}, u32[]{:S(2)}) %collective-permute-start.16) | collective-permute-done | bytes 262176 | tf_op jit(solution)/shard_map/ppermute | solution.py:318
  59.1 1.5 %collective-permute-start.19 = (bf16[256,512]{1,0:T(8,128)(2,1)S(1)}, bf16[256,512]{1,0:T(8,128)(2,1)S(1)}, u32[]{:S(2)}, u32[]{:S(2)}) collective-permute-start(bf16[256,512]{1,0:T(8,128)(2,1)S(1)} %collective-permute-done.18.refs_1_), channel_id=1, source_target_pairs={{0,1},{1,0},{2,3},{3,2},{4,5},{5,4},{6,7},{7,6},{8,9},{9,8},{10,11... | collective-permute-start | bytes 786440 | tf_op jit(solution)/shard_map/ppermute | solution.py:318
  60.6 0.7 %grad_context.5.refs_2_ = f32[256,1024]{1,0:T(8,128)S(1)} custom-call(bf16[1024,4096]{1,0:T(8,128)(2,1)S(1)} %copy-done, bf16[256,512]{1,0:T(8,128)(2,1)S(1)} %collective-permute-done.16.refs_0_, bf16[256,512]{1,0:T(8,128)(2,1)S(1)} %collective-permute-done.18.refs_1_, f32[256,1024]{1,0:T(8,128)S(1)} %get-tuple-element.60.refs_2_), custom_call_target="tpu_custom_call" | custom-call | flops 20000000000 | bytes 60000000 | tf_op jit(solution)/shard_map/grad_context/pallas_call | solution.py:47
  61.3 0.5 collective-permute-done.20.refs_0_
  61.8 0.1 collective-permute-done.21.refs_1_
  61.9 0.7 %grad_context.6.refs_2_ = f32[256,1024]{1,0:T(8,128)S(1)} custom-call(bf16[1024,4096]{1,0:T(8,128)(2,1)S(1)} %copy-done, bf16[256,512]{1,0:T(8,128)(2,1)S(1)} %collective-permute-done.20.refs_0_, bf16[256,512]{1,0:T(8,128)(2,1)S(1)} %collective-permute-done.21.refs_1_, f32[256,1024]{1,0:T(8,128)S(1)} %grad_context.5.refs_2_), custom_call_target="tpu_custom_call" | custom-call | flops 20000000000 | bytes 60000000 | tf_op jit(solution)/shard_map/grad_context/pallas_call | solution.py:47
  62.7 2.8 %collective-permute-done.17.refs_0_ = bf16[256,512]{1,0:T(8,128)(2,1)S(1)} collective-permute-done((bf16[256,512]{1,0:T(8,128)(2,1)S(1)}, bf16[256,512]{1,0:T(8,128)(2,1)S(1)}, u32[]{:S(2)}, u32[]{:S(2)}) %collective-permute-start.17) | collective-permute-done | bytes 262176 | tf_op jit(solution)/shard_map/ppermute | solution.py:318
  65.5 0.0 collective-permute-done.19.refs_1_
  65.5 1.5 %grad_context.7 = bf16[256,1024]{1,0:T(8,128)(2,1)} custom-call(bf16[1024,4096]{1,0:T(8,128)(2,1)S(1)} %copy-done, bf16[256,512]{1,0:T(8,128)(2,1)S(1)} %collective-permute-done.17.refs_0_, bf16[256,512]{1,0:T(8,128)(2,1)S(1)} %collective-permute-done.19.refs_1_, f32[256,1024]{1,0:T(8,128)S(1)} %grad_context.6.refs_2_), custom_call_target="tpu_custom_call" | custom-call | flops 20000000000 | bytes 60000000 | tf_op jit(solution)/shard_map/grad_context/pallas_call | solution.py:47
  (26 shorter events, 0.2 us)
Async XLA Ops:
  0.6 6.5 %copy-start = (bf16[1024,4096]{1,0:T(8,128)(2,1)S(1)}, bf16[1024,4096]{1,0:T(8,128)(2,1)}, u32[]{:S(2)}) copy-start(bf16[1024,4096]{1,0:T(8,128)(2,1)} %w_out.7) | copy-start | bytes 25165828
  0.6 6.5 %copy-start.3 = (bf16[256,1024]{1,0:T(8,128)(2,1)S(1)}, bf16[256,1024]{1,0:T(8,128)(2,1)}, u32[]{:S(2)}) copy-start(bf16[256,1024]{1,0:T(8,128)(2,1)} %refs_0_.7) | copy-start | bytes 1572868
  2.7 7.1 %collective-permute-start.2 = (bf16[128,512]{1,0:T(8,128)(2,1)S(1)}, bf16[128,512]{1,0:T(8,128)(2,1)S(1)}, u32[]{:S(2)}, u32[]{:S(2)}) collective-permute-start(bf16[128,512]{1,0:T(8,128)(2,1)S(1)} %get-tuple-element.35), channel_id=1, source_target_pairs={{0,1},{1,0},{2,3},{3,2},{4,5},{5,4},{6,7},{7,6},{8,9},{9,8},{10,11... | collective-permute-start | bytes 393224 | tf_op jit(solution)/shard_map/ppermute | solution.py:318
  5.7 5.2 %collective-permute-start.3 = (bf16[128,512]{1,0:T(8,128)(2,1)S(1)}, bf16[128,512]{1,0:T(8,128)(2,1)S(1)}, u32[]{:S(2)}, u32[]{:S(2)}) collective-permute-start(bf16[128,512]{1,0:T(8,128)(2,1)S(1)} %get-tuple-element.36), channel_id=1, source_target_pairs={{0,2},{1,3},{2,0},{3,1},{4,6},{5,7},{6,4},{7,5},{8,10},{9,11},{10,... | collective-permute-start | bytes 393224 | tf_op jit(solution)/shard_map/ppermute | solution.py:318
  7.9 9.3 %collective-permute-start = (bf16[256,512]{1,0:T(8,128)(2,1)S(1)}, bf16[256,512]{1,0:T(8,128)(2,1)S(1)}, u32[]{:S(2)}, u32[]{:S(2)}) collective-permute-start(bf16[256,512]{1,0:T(8,128)(2,1)S(1)} %get-tuple-element.33.refs_5_), channel_id=1, source_target_pairs={{0,1},{1,0},{2,3},{3,2},{4,5},{5,4},{6,7},{7,6},{8,9},{9,8},{10,11... | collective-permute-start | bytes 786440 | tf_op jit(solution)/shard_map/ppermute | solution.py:318
  8.5 9.2 %collective-permute-start.1 = (bf16[256,512]{1,0:T(8,128)(2,1)S(1)}, bf16[256,512]{1,0:T(8,128)(2,1)S(1)}, u32[]{:S(2)}, u32[]{:S(2)}) collective-permute-start(bf16[256,512]{1,0:T(8,128)(2,1)S(1)} %get-tuple-element.34), channel_id=1, source_target_pairs={{0,2},{1,3},{2,0},{3,1},{4,6},{5,7},{6,4},{7,5},{8,10},{9,11},{10,... | collective-permute-start | bytes 786440 | tf_op jit(solution)/shard_map/ppermute | solution.py:318
  11.6 12.6 %collective-permute-start.4 = (bf16[320,512]{1,0:T(8,128)(2,1)S(1)}, bf16[320,512]{1,0:T(8,128)(2,1)S(1)}, u32[]{:S(2)}, u32[]{:S(2)}) collective-permute-start(bf16[320,512]{1,0:T(8,128)(2,1)S(1)} %get-tuple-element.37.refs_4_), channel_id=1, source_target_pairs={{0,1},{1,0},{2,3},{3,2},{4,5},{5,4},{6,7},{7,6},{8,9},{9,8},{10,11... | collective-permute-start | bytes 983048 | tf_op jit(solution)/shard_map/ppermute | solution.py:318
  11.9 8.6 %copy-start.4 = (bf16[256,1024]{1,0:T(8,128)(2,1)S(1)}, bf16[256,1024]{1,0:T(8,128)(2,1)}, u32[]{:S(2)}) copy-start(bf16[256,1024]{1,0:T(8,128)(2,1)} %refs_2_.1) | copy-start | bytes 1572868
  11.9 12.9 %collective-permute-start.6 = (bf16[320,512]{1,0:T(8,128)(2,1)S(1)}, bf16[320,512]{1,0:T(8,128)(2,1)S(1)}, u32[]{:S(2)}, u32[]{:S(2)}) collective-permute-start(bf16[320,512]{1,0:T(8,128)(2,1)S(1)} %get-tuple-element.39), channel_id=1, source_target_pairs={{0,2},{1,3},{2,0},{3,1},{4,6},{5,7},{6,4},{7,5},{8,10},{9,11},{10,... | collective-permute-start | bytes 983048 | tf_op jit(solution)/shard_map/ppermute | solution.py:318
  18.5 11.1 %collective-permute-start.5 = (bf16[256,512]{1,0:T(8,128)(2,1)S(1)}, bf16[256,512]{1,0:T(8,128)(2,1)S(1)}, u32[]{:S(2)}, u32[]{:S(2)}) collective-permute-start(bf16[256,512]{1,0:T(8,128)(2,1)S(1)} %get-tuple-element.38.refs_3_), channel_id=1, source_target_pairs={{0,2},{1,3},{2,0},{3,1},{4,6},{5,7},{6,4},{7,5},{8,10},{9,11},{10,... | collective-permute-start | bytes 786440 | tf_op jit(solution)/shard_map/ppermute | solution.py:318
  19.7 9.8 %copy-start.1 = (bf16[1024,1024]{1,0:T(8,128)(2,1)S(1)}, bf16[1024,1024]{1,0:T(8,128)(2,1)}, u32[]{:S(2)}) copy-start(bf16[1024,1024]{1,0:T(8,128)(2,1)} %w_in.1) | copy-start | bytes 6291460
  19.7 9.8 %copy-start.5 = (f32[4096]{0:T(1024)S(1)}, f32[4096]{0:T(1024)}, u32[]{:S(2)}) copy-start(f32[4096]{0:T(1024)} %param.11) | copy-start | bytes 49156
  19.7 9.8 %collective-permute-start.7 = (bf16[256,512]{1,0:T(8,128)(2,1)S(1)}, bf16[256,512]{1,0:T(8,128)(2,1)S(1)}, u32[]{:S(2)}, u32[]{:S(2)}) collective-permute-start(bf16[256,512]{1,0:T(8,128)(2,1)S(1)} %get-tuple-element.40), channel_id=1, source_target_pairs={{0,1},{1,0},{2,3},{3,2},{4,5},{5,4},{6,7},{7,6},{8,9},{9,8},{10,11... | collective-permute-start | bytes 786440 | tf_op jit(solution)/shard_map/ppermute | solution.py:318
  24.8 7.7 %collective-permute-start.10 = (bf16[64,512]{1,0:T(8,128)(2,1)S(1)}, bf16[64,512]{1,0:T(8,128)(2,1)S(1)}, u32[]{:S(2)}, u32[]{:S(2)}) collective-permute-start(bf16[64,512]{1,0:T(8,128)(2,1)S(1)} %get-tuple-element.41.refs_7_.refs_0_), channel_id=1, source_target_pairs={{0,1},{1,0},{2,3},{3,2},{4,5},{5,4},{6,7},{7,6},{8,9},{9,8},{10,11... | collective-permute-start | bytes 196616 | tf_op jit(solution)/shard_map/ppermute | solution.py:318
  26.4 6.1 %collective-permute-start.11 = (bf16[64,512]{1,0:T(8,128)(2,1)S(1)}, bf16[64,512]{1,0:T(8,128)(2,1)S(1)}, u32[]{:S(2)}, u32[]{:S(2)}) collective-permute-start(bf16[64,512]{1,0:T(8,128)(2,1)S(1)} %get-tuple-element.46.refs_1_), channel_id=1, source_target_pairs={{0,2},{1,3},{2,0},{3,1},{4,6},{5,7},{6,4},{7,5},{8,10},{9,11},{10,... | collective-permute-start | bytes 196616 | tf_op jit(solution)/shard_map/ppermute | solution.py:318
  30.4 9.1 %collective-permute-start.8 = (bf16[272,512]{1,0:T(8,128)(2,1)S(1)}, bf16[272,512]{1,0:T(8,128)(2,1)S(1)}, u32[]{:S(2)}, u32[]{:S(2)}) collective-permute-start(bf16[272,512]{1,0:T(8,128)(2,1)S(1)} %get-tuple-element.44), channel_id=1, source_target_pairs={{0,1},{1,0},{2,3},{3,2},{4,5},{5,4},{6,7},{7,6},{8,9},{9,8},{10,11... | collective-permute-start | bytes 835592 | tf_op jit(solution)/shard_map/ppermute | solution.py:318
  31.4 8.1 %collective-permute-start.9 = (bf16[256,512]{1,0:T(8,128)(2,1)S(1)}, bf16[256,512]{1,0:T(8,128)(2,1)S(1)}, u32[]{:S(2)}, u32[]{:S(2)}) collective-permute-start(bf16[256,512]{1,0:T(8,128)(2,1)S(1)} %get-tuple-element.45), channel_id=1, source_target_pairs={{0,2},{1,3},{2,0},{3,1},{4,6},{5,7},{6,4},{7,5},{8,10},{9,11},{10,... | collective-permute-start | bytes 786440 | tf_op jit(solution)/shard_map/ppermute | solution.py:318
  32.5 10.5 %collective-permute-start.14 = (bf16[128,512]{1,0:T(8,128)(2,1)S(1)}, bf16[128,512]{1,0:T(8,128)(2,1)S(1)}, u32[]{:S(2)}, u32[]{:S(2)}) collective-permute-start(bf16[128,512]{1,0:T(8,128)(2,1)S(1)} %get-tuple-element.47.refs_4_.refs_0_), channel_id=1, source_target_pairs={{0,2},{1,3},{2,0},{3,1},{4,6},{5,7},{6,4},{7,5},{8,10},{9,11},{10,... | collective-permute-start | bytes 393224 | tf_op jit(solution)/shard_map/ppermute | solution.py:318
  33.5 9.5 %collective-permute-start.15 = (bf16[128,512]{1,0:T(8,128)(2,1)S(1)}, bf16[128,512]{1,0:T(8,128)(2,1)S(1)}, u32[]{:S(2)}, u32[]{:S(2)}) collective-permute-start(bf16[128,512]{1,0:T(8,128)(2,1)S(1)} %get-tuple-element.52.refs_1_), channel_id=1, source_target_pairs={{0,1},{1,0},{2,3},{3,2},{4,5},{5,4},{6,7},{7,6},{8,9},{9,8},{10,11... | collective-permute-start | bytes 393224 | tf_op jit(solution)/shard_map/ppermute | solution.py:318
  39.6 9.4 %collective-permute-start.12 = (bf16[272,512]{1,0:T(8,128)(2,1)S(1)}, bf16[272,512]{1,0:T(8,128)(2,1)S(1)}, u32[]{:S(2)}, u32[]{:S(2)}) collective-permute-start(bf16[272,512]{1,0:T(8,128)(2,1)S(1)} %get-tuple-element.50), channel_id=1, source_target_pairs={{0,2},{1,3},{2,0},{3,1},{4,6},{5,7},{6,4},{7,5},{8,10},{9,11},{10,... | collective-permute-start | bytes 835592 | tf_op jit(solution)/shard_map/ppermute | solution.py:318
  41.5 7.6 %collective-permute-start.13 = (bf16[256,512]{1,0:T(8,128)(2,1)S(1)}, bf16[256,512]{1,0:T(8,128)(2,1)S(1)}, u32[]{:S(2)}, u32[]{:S(2)}) collective-permute-start(bf16[256,512]{1,0:T(8,128)(2,1)S(1)} %get-tuple-element.51), channel_id=1, source_target_pairs={{0,1},{1,0},{2,3},{3,2},{4,5},{5,4},{6,7},{7,6},{8,9},{9,8},{10,11... | collective-permute-start | bytes 786440 | tf_op jit(solution)/shard_map/ppermute | solution.py:318
  50.5 8.6 %collective-permute-start.16 = (bf16[256,512]{1,0:T(8,128)(2,1)S(1)}, bf16[256,512]{1,0:T(8,128)(2,1)S(1)}, u32[]{:S(2)}, u32[]{:S(2)}) collective-permute-start(bf16[256,512]{1,0:T(8,128)(2,1)S(1)} %get-tuple-element.54.refs_2_.first), channel_id=1, source_target_pairs={{0,1},{1,0},{2,3},{3,2},{4,5},{5,4},{6,7},{7,6},{8,9},{9,8},{10,11... | collective-permute-start | bytes 786440 | tf_op jit(solution)/shard_map/ppermute | solution.py:318
  52.0 3.4 %copy-start.2 = (bf16[1,1024,512]{2,1,0:T(8,128)(2,1)S(1)}, bf16[1,1024,512]{2,1,0:T(8,128)(2,1)}, u32[]{:S(2)}) copy-start(bf16[1,1024,512]{2,1,0:T(8,128)(2,1)} %param.14) | copy-start | bytes 3145732
  52.0 3.4 %copy-start.6 = (f32[1,1024]{1,0:T(1,128)S(1)}, f32[1,1024]{1,0:T(1,128)}, u32[]{:S(2)}) copy-start(f32[1,1024]{1,0:T(1,128)} %gain_depth.1) | copy-start | bytes 12292
  52.0 7.1 %collective-permute-start.18 = (bf16[256,512]{1,0:T(8,128)(2,1)S(1)}, bf16[256,512]{1,0:T(8,128)(2,1)S(1)}, u32[]{:S(2)}, u32[]{:S(2)}) collective-permute-start(bf16[256,512]{1,0:T(8,128)(2,1)S(1)} %get-tuple-element.55.refs_3_.second), channel_id=1, source_target_pairs={{0,2},{1,3},{2,0},{3,1},{4,6},{5,7},{6,4},{7,5},{8,10},{9,11},{10,... | collective-permute-start | bytes 786440 | tf_op jit(solution)/shard_map/ppermute | solution.py:318
  52.8 9.0 %collective-permute-start.20 = (bf16[256,512]{1,0:T(8,128)(2,1)S(1)}, bf16[256,512]{1,0:T(8,128)(2,1)S(1)}, u32[]{:S(2)}, u32[]{:S(2)}) collective-permute-start(bf16[256,512]{1,0:T(8,128)(2,1)S(1)} %get-tuple-element.58), channel_id=1, source_target_pairs={{0,2},{1,3},{2,0},{3,1},{4,6},{5,7},{6,4},{7,5},{8,10},{9,11},{10,... | collective-permute-start | bytes 786440 | tf_op jit(solution)/shard_map/ppermute | solution.py:318
  54.9 7.0 %collective-permute-start.21 = (bf16[256,512]{1,0:T(8,128)(2,1)S(1)}, bf16[256,512]{1,0:T(8,128)(2,1)S(1)}, u32[]{:S(2)}, u32[]{:S(2)}) collective-permute-start(bf16[256,512]{1,0:T(8,128)(2,1)S(1)} %get-tuple-element.59), channel_id=1, source_target_pairs={{0,1},{1,0},{2,3},{3,2},{4,5},{5,4},{6,7},{7,6},{8,9},{9,8},{10,11... | collective-permute-start | bytes 786440 | tf_op jit(solution)/shard_map/ppermute | solution.py:318
  59.1 6.4 %collective-permute-start.17 = (bf16[256,512]{1,0:T(8,128)(2,1)S(1)}, bf16[256,512]{1,0:T(8,128)(2,1)S(1)}, u32[]{:S(2)}, u32[]{:S(2)}) collective-permute-start(bf16[256,512]{1,0:T(8,128)(2,1)S(1)} %collective-permute-done.16.refs_0_), channel_id=1, source_target_pairs={{0,2},{1,3},{2,0},{3,1},{4,6},{5,7},{6,4},{7,5},{8,10},{9,11},{10,... | collective-permute-start | bytes 786440 | tf_op jit(solution)/shard_map/ppermute | solution.py:318
  59.1 6.4 %collective-permute-start.19 = (bf16[256,512]{1,0:T(8,128)(2,1)S(1)}, bf16[256,512]{1,0:T(8,128)(2,1)S(1)}, u32[]{:S(2)}, u32[]{:S(2)}) collective-permute-start(bf16[256,512]{1,0:T(8,128)(2,1)S(1)} %collective-permute-done.18.refs_1_), channel_id=1, source_target_pairs={{0,1},{1,0},{2,3},{3,2},{4,5},{5,4},{6,7},{7,6},{8,9},{9,8},{10,11... | collective-permute-start | bytes 786440 | tf_op jit(solution)/shard_map/ppermute | solution.py:318

commit v7 on v6

--- a/solution.py
+++ b/solution.py
@@ -146,6 +146,26 @@
         put_shares(share, riders, adds[at], adds[at + 1 :], outs[::-1], frames)
 
 
+def product_kernel(items, context, w_out, *outs):
+    for (mask, side), out in zip(items, outs):
+        out[...] = jnp.dot(
+            context[...],
+            w_out[:, cols_of(mask, side, out.shape[1])],
+            preferred_element_type=f32,
+        )
+
+
+def add_kernel(counts, *refs):
+    products, adds, outs = refs[:2], refs[2:-2], refs[-2:]
+    at = 0
+    for product, count, out in zip(products, counts, outs):
+        total = product[...]
+        for add in adds[at : at + count]:
+            total = total + add[: total.shape[0], :].astype(f32)
+        out[...] = total.astype(bf16)
+        at += count
+
+
 def keep_kernel(context, w_out, residual, out):
     out[...] = residual[...].astype(f32) + jnp.dot(
         context[...],
@@ -394,13 +414,30 @@
                 values = shares(i, share_gots, token)
                 token = values[0]
                 share_gots.append((both(values, i), 0))
-        values = call(
-            functools.partial(project_kernel, share, items, riders),
-            [((frames + extra, half), bf16)] * 2,
-            [context, w_out] + listed,
-            name="project",
-            after=token,
-        )
+        if pair is pairs[-1]:
+            products = call(
+                functools.partial(product_kernel, pair),
+                [((frames, half), f32)] * 2,
+                [context, w_out],
+                name="product",
+                after=token,
+            )
+            values = call(
+                functools.partial(add_kernel, [count for _, _, count in items]),
+                [((frames, half), bf16)] * 2,
+                list(products) + listed,
+                name="add",
+                cost=FREE,
+                after=token,
+            )
+        else:
+            values = call(
+                functools.partial(project_kernel, share, items, riders),
+                [((frames + extra, half), bf16)] * 2,
+                [context, w_out] + listed,
+                name="project",
+                after=token,
+            )
         token = values[0]
         for (mask, side), value in zip(pair, values):
             arrived[mask, side] = swap(value, orders[side][phase_of(mask, side)])
@@ -411,6 +448,7 @@
         [((frames, width), f32)],
         [context, w_out, residual],
         name="keep",
+        cost=FREE,
         after=token,
     )[0]
     own_share = shares(log, share_gots, kept)

time: 67.1 us -> 67.2 us (level)
    pallas_call x16 -> x17, Pallas kernels: 12.6 us -> 12.7 us  [call(): pl.pallas_call(kernel, out_shape=[jax.ShapeDtypeStruct(s, d) for s, d in...]
where the time goes in v7:
time: 67.2 us; the launch traced here: 67 us
  waiting for transfers between devices  27.7 us (41%)
  starting transfers between devices  25.8 us (38%)
  Pallas kernels  12.7 us (19%)
  between operations  0.79 us (1%)
    ppermute x22, waiting for transfers between devices, swap(): return lax.ppermute(value, 'mp', [(i, i ^ bit) for i in range(n)])  27.7 us
    ppermute x22, starting transfers between devices, swap(): return lax.ppermute(value, 'mp', [(i, i ^ bit) for i in range(n)])  25.8 us
    pallas_call x17, Pallas kernels, call(): pl.pallas_call(kernel, out_shape=[jax.ShapeDtypeStruct(s, d) for s, d in...  12.7 us
  transfers between devices with their start and end apart: 22, of which 12 were waited for; matrix products, arithmetic and copies ran while one was open for 0% of the time, Pallas kernels for 12%

profile of v7, /device:TPU:0, one launch (start us, length us, event | category | flops | bytes accessed | tf_op | source)
XLA Modules:
  0.0 67.0 jit_solution(1900798276131798072)
XLA Ops:
  0.7 2.0 %upstream.1 = (bf16[128,512]{1,0:T(8,128)(2,1)S(1)}, bf16[128,512]{1,0:T(8,128)(2,1)S(1)}, f32[256,1024]{1,0:T(8,128)S(1)}) custom-call(bf16[256,512]{1,0:T(8,128)(2,1)} %bitcast.8, bf16[1024,512]{1,0:T(8,128)(2,1)} %bitcast.4, f32[1,1024]{1,0:T(1,128)} %gain_depth.1), custom_call_target="tpu_custom_call" | custom-call | flops 20000000000 | bytes 60000000 | tf_op jit(solution)/shard_map/upstream/pallas_call | solution.py:47
  2.7 3.0 %collective-permute-start = (bf16[128,512]{1,0:T(8,128)(2,1)S(1)}, bf16[128,512]{1,0:T(8,128)(2,1)S(1)}, u32[]{:S(2)}, u32[]{:S(2)}) collective-permute-start(bf16[128,512]{1,0:T(8,128)(2,1)S(1)} %get-tuple-element.35), channel_id=1, source_target_pairs={{0,1},{1,0},{2,3},{3,2},{4,5},{5,4},{6,7},{7,6},{8,9},{9,8},{10,11... | collective-permute-start | bytes 393224 | tf_op jit(solution)/shard_map/ppermute | solution.py:338
  5.7 1.5 %collective-permute-start.1 = (bf16[128,512]{1,0:T(8,128)(2,1)S(1)}, bf16[128,512]{1,0:T(8,128)(2,1)S(1)}, u32[]{:S(2)}, u32[]{:S(2)}) collective-permute-start(bf16[128,512]{1,0:T(8,128)(2,1)S(1)} %get-tuple-element.36), channel_id=1, source_target_pairs={{0,2},{1,3},{2,0},{3,1},{4,6},{5,7},{6,4},{7,5},{8,10},{9,11},{10,... | collective-permute-start | bytes 393224 | tf_op jit(solution)/shard_map/ppermute | solution.py:338
  7.2 0.7 %project.2 = (bf16[256,512]{1,0:T(8,128)(2,1)S(1)}, bf16[256,512]{1,0:T(8,128)(2,1)S(1)}) custom-call(bf16[256,1024]{1,0:T(8,128)(2,1)S(1)} %copy-done.1, bf16[1024,4096]{1,0:T(8,128)(2,1)S(1)} %copy-done, f32[256,1024]{1,0:T(8,128)S(1)} %get-tuple-element.34.refs_2_.refs_0_), custom_call_target="tpu_custom_call" | custom-call | flops 20000000000 | bytes 60000000 | tf_op jit(solution)/shard_map/project/pallas_call | solution.py:47
  7.9 0.6 collective-permute-start.2
  8.5 1.2 %collective-permute-start.3 = (bf16[256,512]{1,0:T(8,128)(2,1)S(1)}, bf16[256,512]{1,0:T(8,128)(2,1)S(1)}, u32[]{:S(2)}, u32[]{:S(2)}) collective-permute-start(bf16[256,512]{1,0:T(8,128)(2,1)S(1)} %get-tuple-element.41), channel_id=1, source_target_pairs={{0,2},{1,3},{2,0},{3,1},{4,6},{5,7},{6,4},{7,5},{8,10},{9,11},{10,... | collective-permute-start | bytes 786440 | tf_op jit(solution)/shard_map/ppermute | solution.py:338
  9.7 1.2 %collective-permute-done.1.refs_4_.refs_2_ = bf16[128,512]{1,0:T(8,128)(2,1)S(1)} collective-permute-done((bf16[128,512]{1,0:T(8,128)(2,1)S(1)}, bf16[128,512]{1,0:T(8,128)(2,1)S(1)}, u32[]{:S(2)}, u32[]{:S(2)}) %collective-permute-start.1) | collective-permute-done | bytes 131104 | tf_op jit(solution)/shard_map/ppermute | solution.py:338
  10.9 0.7 %project.3 = (bf16[320,512]{1,0:T(8,128)(2,1)S(1)}, bf16[320,512]{1,0:T(8,128)(2,1)S(1)}) custom-call(bf16[256,1024]{1,0:T(8,128)(2,1)S(1)} %copy-done.1, bf16[1024,4096]{1,0:T(8,128)(2,1)S(1)} %copy-done, f32[256,1024]{1,0:T(8,128)S(1)} %get-tuple-element.34.refs_2_.refs_0_, bf16[128,512]{1,0:T(8,128)(2,1)S(1)} %collective-permute-done.refs_3_.refs_1_, ...), custom_call_target="tpu_custom_call" | custom-call | flops 20000000000 | bytes 60000000 | tf_op jit(solution)/shard_map/project/pallas_call | solution.py:47
  11.6 0.3 collective-permute-start.4
  11.9 1.8 %collective-permute-start.6 = (bf16[320,512]{1,0:T(8,128)(2,1)S(1)}, bf16[320,512]{1,0:T(8,128)(2,1)S(1)}, u32[]{:S(2)}, u32[]{:S(2)}) collective-permute-start(bf16[320,512]{1,0:T(8,128)(2,1)S(1)} %get-tuple-element.43), channel_id=1, source_target_pairs={{0,2},{1,3},{2,0},{3,1},{4,6},{5,7},{6,4},{7,5},{8,10},{9,11},{10,... | collective-permute-start | bytes 983048 | tf_op jit(solution)/shard_map/ppermute | solution.py:338
  13.8 0.7 %product.1 = (f32[256,512]{1,0:T(8,128)S(1)}, f32[256,512]{1,0:T(8,128)S(1)}) custom-call(bf16[256,1024]{1,0:T(8,128)(2,1)S(1)} %copy-done.1, bf16[1024,4096]{1,0:T(8,128)(2,1)S(1)} %copy-done, bf16[320,512]{1,0:T(8,128)(2,1)S(1)} %get-tuple-element.38.refs_2_.refs_4_), custom_call_target="tpu_custom_call" | custom-call | flops 20000000000 | bytes 60000000 | tf_op jit(solution)/shard_map/product/pallas_call | solution.py:47
  14.5 0.0 copy-start.3
  14.5 2.7 %collective-permute-done.2.refs_2_ = bf16[256,512]{1,0:T(8,128)(2,1)S(1)} collective-permute-done((bf16[256,512]{1,0:T(8,128)(2,1)S(1)}, bf16[256,512]{1,0:T(8,128)(2,1)S(1)}, u32[]{:S(2)}, u32[]{:S(2)}) %collective-permute-start.2) | collective-permute-done | bytes 262176 | tf_op jit(solution)/shard_map/ppermute | solution.py:338
  17.2 0.5 collective-permute-done.3.refs_3_
  17.8 0.1 add.1
  17.8 1.3 %collective-permute-start.5 = (bf16[256,512]{1,0:T(8,128)(2,1)S(1)}, bf16[256,512]{1,0:T(8,128)(2,1)S(1)}, u32[]{:S(2)}, u32[]{:S(2)}) collective-permute-start(bf16[256,512]{1,0:T(8,128)(2,1)S(1)} %get-tuple-element.42.refs_3_), channel_id=1, source_target_pairs={{0,2},{1,3},{2,0},{3,1},{4,6},{5,7},{6,4},{7,5},{8,10},{9,11},{10,... | collective-permute-start | bytes 786440 | tf_op jit(solution)/shard_map/ppermute | solution.py:338
  19.1 0.8 %collective-permute-start.7 = (bf16[256,512]{1,0:T(8,128)(2,1)S(1)}, bf16[256,512]{1,0:T(8,128)(2,1)S(1)}, u32[]{:S(2)}, u32[]{:S(2)}) collective-permute-start(bf16[256,512]{1,0:T(8,128)(2,1)S(1)} %get-tuple-element.44), channel_id=1, source_target_pairs={{0,1},{1,0},{2,3},{3,2},{4,5},{5,4},{6,7},{7,6},{8,9},{9,8},{10,11... | collective-permute-start | bytes 786440 | tf_op jit(solution)/shard_map/ppermute | solution.py:338
  19.9 0.7 %keep.1.refs_5_.refs_2_ = f32[256,1024]{1,0:T(8,128)S(1)} custom-call(bf16[256,1024]{1,0:T(8,128)(2,1)S(1)} %copy-done.1, bf16[1024,4096]{1,0:T(8,128)(2,1)S(1)} %copy-done, bf16[256,1024]{1,0:T(8,128)(2,1)S(1)} %copy-done.2, bf16[256,512]{1,0:T(8,128)(2,1)S(1)} %get-tuple-element.42.refs_3_), custom_call_target="tpu_custom_call" | custom-call | tf_op jit(solution)/shard_map/keep/pallas_call | solution.py:47
  20.6 3.6 %collective-permute-done.4.refs_4_.refs_3_ = bf16[320,512]{1,0:T(8,128)(2,1)S(1)} collective-permute-done((bf16[320,512]{1,0:T(8,128)(2,1)S(1)}, bf16[320,512]{1,0:T(8,128)(2,1)S(1)}, u32[]{:S(2)}, u32[]{:S(2)}) %collective-permute-start.4) | collective-permute-done | bytes 327712 | tf_op jit(solution)/shard_map/ppermute | solution.py:338
  24.2 0.5 collective-permute-done.6.refs_3_.refs_5_
  24.8 1.6 %collective-permute-start.10 = (bf16[64,512]{1,0:T(8,128)(2,1)S(1)}, bf16[64,512]{1,0:T(8,128)(2,1)S(1)}, u32[]{:S(2)}, u32[]{:S(2)}) collective-permute-start(bf16[64,512]{1,0:T(8,128)(2,1)S(1)} %get-tuple-element.45.refs_7_.refs_0_), channel_id=1, source_target_pairs={{0,1},{1,0},{2,3},{3,2},{4,5},{5,4},{6,7},{7,6},{8,9},{9,8},{10,11... | collective-permute-start | bytes 196616 | tf_op jit(solution)/shard_map/ppermute | solution.py:338
  26.4 0.5 collective-permute-start.11
  26.9 2.7 %collective-permute-done.5.refs_4_ = bf16[256,512]{1,0:T(8,128)(2,1)S(1)} collective-permute-done((bf16[256,512]{1,0:T(8,128)(2,1)S(1)}, bf16[256,512]{1,0:T(8,128)(2,1)S(1)}, u32[]{:S(2)}, u32[]{:S(2)}) %collective-permute-start.5) | collective-permute-done | bytes 262176 | tf_op jit(solution)/shard_map/ppermute | solution.py:338
  29.6 0.8 %state.1 = (f32[256,1024]{1,0:T(8,128)S(1)}, f32[256,1024]{1,0:T(8,128)S(1)}, f32[8,256]{1,0:T(8,128)S(1)}, bf16[272,512]{1,0:T(8,128)(2,1)S(1)}, bf16[256,512]{1,0:T(8,128)(2,1)S(1)}) custom-call(f32[1,4096]{1,0:T(1,128)S(1)} %bitcast.6, bf16[1024,1024]{1,0:T(8,128)(2,1)S(1)} %copy-done.3, f32[256,1024]{1,0:T(8,128)S(1)} %keep.1.refs_5_.refs_2_, ...), custom_call_target="tpu_custom_call" | custom-call | flops 20000000000 | bytes 60000000 | tf_op jit(solution)/shard_map/state/pallas_call | solution.py:47
  30.4 1.0 %collective-permute-start.8 = (bf16[272,512]{1,0:T(8,128)(2,1)S(1)}, bf16[272,512]{1,0:T(8,128)(2,1)S(1)}, u32[]{:S(2)}, u32[]{:S(2)}) collective-permute-start(bf16[272,512]{1,0:T(8,128)(2,1)S(1)} %get-tuple-element.48), channel_id=1, source_target_pairs={{0,1},{1,0},{2,3},{3,2},{4,5},{5,4},{6,7},{7,6},{8,9},{9,8},{10,11... | collective-permute-start | bytes 835592 | tf_op jit(solution)/shard_map/ppermute | solution.py:338
  31.4 1.1 %collective-permute-start.9 = (bf16[256,512]{1,0:T(8,128)(2,1)S(1)}, bf16[256,512]{1,0:T(8,128)(2,1)S(1)}, u32[]{:S(2)}, u32[]{:S(2)}) collective-permute-start(bf16[256,512]{1,0:T(8,128)(2,1)S(1)} %get-tuple-element.49), channel_id=1, source_target_pairs={{0,2},{1,3},{2,0},{3,1},{4,6},{5,7},{6,4},{7,5},{8,10},{9,11},{10,... | collective-permute-start | bytes 786440 | tf_op jit(solution)/shard_map/ppermute | solution.py:338
  32.5 1.0 %collective-permute-start.14 = (bf16[128,512]{1,0:T(8,128)(2,1)S(1)}, bf16[128,512]{1,0:T(8,128)(2,1)S(1)}, u32[]{:S(2)}, u32[]{:S(2)}) collective-permute-start(bf16[128,512]{1,0:T(8,128)(2,1)S(1)} %get-tuple-element.51.refs_4_.refs_0_), channel_id=1, source_target_pairs={{0,2},{1,3},{2,0},{3,1},{4,6},{5,7},{6,4},{7,5},{8,10},{9,11},{10,... | collective-permute-start | bytes 393224 | tf_op jit(solution)/shard_map/ppermute | solution.py:338
  33.5 1.1 %collective-permute-start.15 = (bf16[128,512]{1,0:T(8,128)(2,1)S(1)}, bf16[128,512]{1,0:T(8,128)(2,1)S(1)}, u32[]{:S(2)}, u32[]{:S(2)}) collective-permute-start(bf16[128,512]{1,0:T(8,128)(2,1)S(1)} %get-tuple-element.56.refs_1_), channel_id=1, source_target_pairs={{0,1},{1,0},{2,3},{3,2},{4,5},{5,4},{6,7},{7,6},{8,9},{9,8},{10,11... | collective-permute-start | bytes 393224 | tf_op jit(solution)/shard_map/ppermute | solution.py:338
  34.6 4.9 %collective-permute-done.9.refs_3_ = bf16[256,512]{1,0:T(8,128)(2,1)S(1)} collective-permute-done((bf16[256,512]{1,0:T(8,128)(2,1)S(1)}, bf16[256,512]{1,0:T(8,128)(2,1)S(1)}, u32[]{:S(2)}, u32[]{:S(2)}) %collective-permute-start.9) | collective-permute-done | bytes 262176 | tf_op jit(solution)/shard_map/ppermute | solution.py:338
  39.5 0.2 reduce.1
  39.7 1.9 %collective-permute-start.12 = (bf16[272,512]{1,0:T(8,128)(2,1)S(1)}, bf16[272,512]{1,0:T(8,128)(2,1)S(1)}, u32[]{:S(2)}, u32[]{:S(2)}) collective-permute-start(bf16[272,512]{1,0:T(8,128)(2,1)S(1)} %get-tuple-element.54), channel_id=1, source_target_pairs={{0,2},{1,3},{2,0},{3,1},{4,6},{5,7},{6,4},{7,5},{8,10},{9,11},{10,... | collective-permute-start | bytes 835592 | tf_op jit(solution)/shard_map/ppermute | solution.py:338
  41.5 1.5 %collective-permute-start.13 = (bf16[256,512]{1,0:T(8,128)(2,1)S(1)}, bf16[256,512]{1,0:T(8,128)(2,1)S(1)}, u32[]{:S(2)}, u32[]{:S(2)}) collective-permute-start(bf16[256,512]{1,0:T(8,128)(2,1)S(1)} %get-tuple-element.55), channel_id=1, source_target_pairs={{0,1},{1,0},{2,3},{3,2},{4,5},{5,4},{6,7},{7,6},{8,9},{9,8},{10,11... | collective-permute-start | bytes 786440 | tf_op jit(solution)/shard_map/ppermute | solution.py:338
  43.1 6.0 %collective-permute-done.13.refs_1_ = bf16[256,512]{1,0:T(8,128)(2,1)S(1)} collective-permute-done((bf16[256,512]{1,0:T(8,128)(2,1)S(1)}, bf16[256,512]{1,0:T(8,128)(2,1)S(1)}, u32[]{:S(2)}, u32[]{:S(2)}) %collective-permute-start.13) | collective-permute-done | bytes 262176 | tf_op jit(solution)/shard_map/ppermute | solution.py:338
  49.1 1.4 %back.1 = (bf16[256,512]{1,0:T(8,128)(2,1)S(1)}, bf16[256,512]{1,0:T(8,128)(2,1)S(1)}) custom-call(f32[1,4096]{1,0:T(1,128)S(1)} %bitcast.7, bf16[1024,1024]{1,0:T(8,128)(2,1)S(1)} %copy-done.3, bf16[256,1024]{1,0:T(8,128)(2,1)S(1)} %assemble.1.up, f32[256,1024]{1,0:T(8,128)S(1)} %get-tuple-element.57.state, f32[256,1024]{1,0:T(8,128)S(1)} %get-tuple-element.52.raw, ...), custom_call_target="tpu_custom_call" | custom-call | flops 20000000000 | bytes 60000000 | tf_op jit(solution)/shard_map/back/pallas_call | solution.py:47
  50.5 1.6 %collective-permute-start.16 = (bf16[256,512]{1,0:T(8,128)(2,1)S(1)}, bf16[256,512]{1,0:T(8,128)(2,1)S(1)}, u32[]{:S(2)}, u32[]{:S(2)}) collective-permute-start(bf16[256,512]{1,0:T(8,128)(2,1)S(1)} %get-tuple-element.58.refs_2_.first), channel_id=1, source_target_pairs={{0,1},{1,0},{2,3},{3,2},{4,5},{5,4},{6,7},{7,6},{8,9},{9,8},{10,11... | collective-permute-start | bytes 786440 | tf_op jit(solution)/shard_map/ppermute | solution.py:338
  52.1 0.7 %grad_context.4 = (f32[256,1024]{1,0:T(8,128)S(1)}, bf16[256,512]{1,0:T(8,128)(2,1)S(1)}, bf16[256,512]{1,0:T(8,128)(2,1)S(1)}) custom-call(bf16[1024,4096]{1,0:T(8,128)(2,1)S(1)} %copy-done, bf16[256,512]{1,0:T(8,128)(2,1)S(1)} %get-tuple-element.58.refs_2_.first, bf16[256,512]{1,0:T(8,128)(2,1)S(1)} %get-tuple-element.59.refs_3_.second), custom_call_target="tpu_custom_call" | custom-call | flops 20000000000 | bytes 60000000 | tf_op jit(solution)/shard_map/grad_context/pallas_call | solution.py:47
  52.8 2.1 %collective-permute-start.20 = (bf16[256,512]{1,0:T(8,128)(2,1)S(1)}, bf16[256,512]{1,0:T(8,128)(2,1)S(1)}, u32[]{:S(2)}, u32[]{:S(2)}) collective-permute-start(bf16[256,512]{1,0:T(8,128)(2,1)S(1)} %get-tuple-element.62), channel_id=1, source_target_pairs={{0,2},{1,3},{2,0},{3,1},{4,6},{5,7},{6,4},{7,5},{8,10},{9,11},{10,... | collective-permute-start | bytes 786440 | tf_op jit(solution)/shard_map/ppermute | solution.py:338
  54.9 0.5 collective-permute-start.21
  55.4 1.6 %act.1 = (bf16[256,512]{1,0:T(8,128)(2,1)}, bf16[256,1024]{1,0:T(8,128)(2,1)}) custom-call(f32[1,1024]{1,0:T(1,128)S(1)} %copy-done.6, bf16[1024,512]{1,0:T(8,128)(2,1)S(1)} %bitcast.5, f32[256,1024]{1,0:T(8,128)S(1)} %get-tuple-element.52.raw, f32[8,256]{1,0:T(8,128)S(1)} %get-tuple-element.53.refs_4_.squares, ...), custom_call_target="tpu_custom_call" | custom-call | flops 20000000000 | bytes 60000000 | tf_op jit(solution)/shard_map/act/pallas_call | solution.py:47
  57.0 2.1 %collective-permute-done.16.refs_0_ = bf16[256,512]{1,0:T(8,128)(2,1)S(1)} collective-permute-done((bf16[256,512]{1,0:T(8,128)(2,1)S(1)}, bf16[256,512]{1,0:T(8,128)(2,1)S(1)}, u32[]{:S(2)}, u32[]{:S(2)}) %collective-permute-start.16) | collective-permute-done | bytes 262176 | tf_op jit(solution)/shard_map/ppermute | solution.py:338
  59.1 1.5 %collective-permute-start.19 = (bf16[256,512]{1,0:T(8,128)(2,1)S(1)}, bf16[256,512]{1,0:T(8,128)(2,1)S(1)}, u32[]{:S(2)}, u32[]{:S(2)}) collective-permute-start(bf16[256,512]{1,0:T(8,128)(2,1)S(1)} %collective-permute-done.18.refs_1_), channel_id=1, source_target_pairs={{0,1},{1,0},{2,3},{3,2},{4,5},{5,4},{6,7},{7,6},{8,9},{9,8},{10,11... | collective-permute-start | bytes 786440 | tf_op jit(solution)/shard_map/ppermute | solution.py:338
  60.6 0.7 %grad_context.5.refs_2_ = f32[256,1024]{1,0:T(8,128)S(1)} custom-call(bf16[1024,4096]{1,0:T(8,128)(2,1)S(1)} %copy-done, bf16[256,512]{1,0:T(8,128)(2,1)S(1)} %collective-permute-done.16.refs_0_, bf16[256,512]{1,0:T(8,128)(2,1)S(1)} %collective-permute-done.18.refs_1_, f32[256,1024]{1,0:T(8,128)S(1)} %get-tuple-element.64.refs_2_), custom_call_target="tpu_custom_call" | custom-call | flops 20000000000 | bytes 60000000 | tf_op jit(solution)/shard_map/grad_context/pallas_call | solution.py:47
  61.4 0.5 collective-permute-done.20.refs_0_
  61.9 0.1 collective-permute-done.21.refs_1_
  61.9 0.7 %grad_context.6.refs_2_ = f32[256,1024]{1,0:T(8,128)S(1)} custom-call(bf16[1024,4096]{1,0:T(8,128)(2,1)S(1)} %copy-done, bf16[256,512]{1,0:T(8,128)(2,1)S(1)} %collective-permute-done.20.refs_0_, bf16[256,512]{1,0:T(8,128)(2,1)S(1)} %collective-permute-done.21.refs_1_, f32[256,1024]{1,0:T(8,128)S(1)} %grad_context.5.refs_2_), custom_call_target="tpu_custom_call" | custom-call | flops 20000000000 | bytes 60000000 | tf_op jit(solution)/shard_map/grad_context/pallas_call | solution.py:47
  62.7 2.8 %collective-permute-done.17.refs_0_ = bf16[256,512]{1,0:T(8,128)(2,1)S(1)} collective-permute-done((bf16[256,512]{1,0:T(8,128)(2,1)S(1)}, bf16[256,512]{1,0:T(8,128)(2,1)S(1)}, u32[]{:S(2)}, u32[]{:S(2)}) %collective-permute-start.17) | collective-permute-done | bytes 262176 | tf_op jit(solution)/shard_map/ppermute | solution.py:338
  65.5 0.0 collective-permute-done.19.refs_1_
  65.5 1.5 %grad_context.7 = bf16[256,1024]{1,0:T(8,128)(2,1)} custom-call(bf16[1024,4096]{1,0:T(8,128)(2,1)S(1)} %copy-done, bf16[256,512]{1,0:T(8,128)(2,1)S(1)} %collective-permute-done.17.refs_0_, bf16[256,512]{1,0:T(8,128)(2,1)S(1)} %collective-permute-done.19.refs_1_, f32[256,1024]{1,0:T(8,128)S(1)} %grad_context.6.refs_2_), custom_call_target="tpu_custom_call" | custom-call | flops 20000000000 | bytes 60000000 | tf_op jit(solution)/shard_map/grad_context/pallas_call | solution.py:47
  (27 shorter events, 0.2 us)
Async XLA Ops:
  0.6 6.5 %copy-start = (bf16[1024,4096]{1,0:T(8,128)(2,1)S(1)}, bf16[1024,4096]{1,0:T(8,128)(2,1)}, u32[]{:S(2)}) copy-start(bf16[1024,4096]{1,0:T(8,128)(2,1)} %w_out.7) | copy-start | bytes 25165828
  0.6 6.5 %copy-start.1 = (bf16[256,1024]{1,0:T(8,128)(2,1)S(1)}, bf16[256,1024]{1,0:T(8,128)(2,1)}, u32[]{:S(2)}) copy-start(bf16[256,1024]{1,0:T(8,128)(2,1)} %refs_0_.7) | copy-start | bytes 1572868
  2.7 7.1 %collective-permute-start = (bf16[128,512]{1,0:T(8,128)(2,1)S(1)}, bf16[128,512]{1,0:T(8,128)(2,1)S(1)}, u32[]{:S(2)}, u32[]{:S(2)}) collective-permute-start(bf16[128,512]{1,0:T(8,128)(2,1)S(1)} %get-tuple-element.35), channel_id=1, source_target_pairs={{0,1},{1,0},{2,3},{3,2},{4,5},{5,4},{6,7},{7,6},{8,9},{9,8},{10,11... | collective-permute-start | bytes 393224 | tf_op jit(solution)/shard_map/ppermute | solution.py:338
  5.7 5.2 %collective-permute-start.1 = (bf16[128,512]{1,0:T(8,128)(2,1)S(1)}, bf16[128,512]{1,0:T(8,128)(2,1)S(1)}, u32[]{:S(2)}, u32[]{:S(2)}) collective-permute-start(bf16[128,512]{1,0:T(8,128)(2,1)S(1)} %get-tuple-element.36), channel_id=1, source_target_pairs={{0,2},{1,3},{2,0},{3,1},{4,6},{5,7},{6,4},{7,5},{8,10},{9,11},{10,... | collective-permute-start | bytes 393224 | tf_op jit(solution)/shard_map/ppermute | solution.py:338
  7.9 9.3 %collective-permute-start.2 = (bf16[256,512]{1,0:T(8,128)(2,1)S(1)}, bf16[256,512]{1,0:T(8,128)(2,1)S(1)}, u32[]{:S(2)}, u32[]{:S(2)}) collective-permute-start(bf16[256,512]{1,0:T(8,128)(2,1)S(1)} %get-tuple-element.37.refs_5_), channel_id=1, source_target_pairs={{0,1},{1,0},{2,3},{3,2},{4,5},{5,4},{6,7},{7,6},{8,9},{9,8},{10,11... | collective-permute-start | bytes 786440 | tf_op jit(solution)/shard_map/ppermute | solution.py:338
  8.5 9.2 %collective-permute-start.3 = (bf16[256,512]{1,0:T(8,128)(2,1)S(1)}, bf16[256,512]{1,0:T(8,128)(2,1)S(1)}, u32[]{:S(2)}, u32[]{:S(2)}) collective-permute-start(bf16[256,512]{1,0:T(8,128)(2,1)S(1)} %get-tuple-element.41), channel_id=1, source_target_pairs={{0,2},{1,3},{2,0},{3,1},{4,6},{5,7},{6,4},{7,5},{8,10},{9,11},{10,... | collective-permute-start | bytes 786440 | tf_op jit(solution)/shard_map/ppermute | solution.py:338
  11.6 12.6 %collective-permute-start.4 = (bf16[320,512]{1,0:T(8,128)(2,1)S(1)}, bf16[320,512]{1,0:T(8,128)(2,1)S(1)}, u32[]{:S(2)}, u32[]{:S(2)}) collective-permute-start(bf16[320,512]{1,0:T(8,128)(2,1)S(1)} %get-tuple-element.38.refs_2_.refs_4_), channel_id=1, source_target_pairs={{0,1},{1,0},{2,3},{3,2},{4,5},{5,4},{6,7},{7,6},{8,9},{9,8},{10,11... | collective-permute-start | bytes 983048 | tf_op jit(solution)/shard_map/ppermute | solution.py:338
  11.9 8.0 %copy-start.2 = (bf16[256,1024]{1,0:T(8,128)(2,1)S(1)}, bf16[256,1024]{1,0:T(8,128)(2,1)}, u32[]{:S(2)}) copy-start(bf16[256,1024]{1,0:T(8,128)(2,1)} %refs_2_.1) | copy-start | bytes 1572868
  11.9 12.9 %collective-permute-start.6 = (bf16[320,512]{1,0:T(8,128)(2,1)S(1)}, bf16[320,512]{1,0:T(8,128)(2,1)S(1)}, u32[]{:S(2)}, u32[]{:S(2)}) collective-permute-start(bf16[320,512]{1,0:T(8,128)(2,1)S(1)} %get-tuple-element.43), channel_id=1, source_target_pairs={{0,2},{1,3},{2,0},{3,1},{4,6},{5,7},{6,4},{7,5},{8,10},{9,11},{10,... | collective-permute-start | bytes 983048 | tf_op jit(solution)/shard_map/ppermute | solution.py:338
  14.5 15.1 %copy-start.3 = (bf16[1024,1024]{1,0:T(8,128)(2,1)S(1)}, bf16[1024,1024]{1,0:T(8,128)(2,1)}, u32[]{:S(2)}) copy-start(bf16[1024,1024]{1,0:T(8,128)(2,1)} %w_in.1) | copy-start | bytes 6291460
  14.5 15.1 %copy-start.5 = (f32[4096]{0:T(1024)S(1)}, f32[4096]{0:T(1024)}, u32[]{:S(2)}) copy-start(f32[4096]{0:T(1024)} %param.11) | copy-start | bytes 49156
  17.8 11.7 %collective-permute-start.5 = (bf16[256,512]{1,0:T(8,128)(2,1)S(1)}, bf16[256,512]{1,0:T(8,128)(2,1)S(1)}, u32[]{:S(2)}, u32[]{:S(2)}) collective-permute-start(bf16[256,512]{1,0:T(8,128)(2,1)S(1)} %get-tuple-element.42.refs_3_), channel_id=1, source_target_pairs={{0,2},{1,3},{2,0},{3,1},{4,6},{5,7},{6,4},{7,5},{8,10},{9,11},{10,... | collective-permute-start | bytes 786440 | tf_op jit(solution)/shard_map/ppermute | solution.py:338
  19.1 10.5 %collective-permute-start.7 = (bf16[256,512]{1,0:T(8,128)(2,1)S(1)}, bf16[256,512]{1,0:T(8,128)(2,1)S(1)}, u32[]{:S(2)}, u32[]{:S(2)}) collective-permute-start(bf16[256,512]{1,0:T(8,128)(2,1)S(1)} %get-tuple-element.44), channel_id=1, source_target_pairs={{0,1},{1,0},{2,3},{3,2},{4,5},{5,4},{6,7},{7,6},{8,9},{9,8},{10,11... | collective-permute-start | bytes 786440 | tf_op jit(solution)/shard_map/ppermute | solution.py:338
  24.8 7.7 %collective-permute-start.10 = (bf16[64,512]{1,0:T(8,128)(2,1)S(1)}, bf16[64,512]{1,0:T(8,128)(2,1)S(1)}, u32[]{:S(2)}, u32[]{:S(2)}) collective-permute-start(bf16[64,512]{1,0:T(8,128)(2,1)S(1)} %get-tuple-element.45.refs_7_.refs_0_), channel_id=1, source_target_pairs={{0,1},{1,0},{2,3},{3,2},{4,5},{5,4},{6,7},{7,6},{8,9},{9,8},{10,11... | collective-permute-start | bytes 196616 | tf_op jit(solution)/shard_map/ppermute | solution.py:338
  26.4 6.1 %collective-permute-start.11 = (bf16[64,512]{1,0:T(8,128)(2,1)S(1)}, bf16[64,512]{1,0:T(8,128)(2,1)S(1)}, u32[]{:S(2)}, u32[]{:S(2)}) collective-permute-start(bf16[64,512]{1,0:T(8,128)(2,1)S(1)} %get-tuple-element.50.refs_1_), channel_id=1, source_target_pairs={{0,2},{1,3},{2,0},{3,1},{4,6},{5,7},{6,4},{7,5},{8,10},{9,11},{10,... | collective-permute-start | bytes 196616 | tf_op jit(solution)/shard_map/ppermute | solution.py:338
  30.4 9.1 %collective-permute-start.8 = (bf16[272,512]{1,0:T(8,128)(2,1)S(1)}, bf16[272,512]{1,0:T(8,128)(2,1)S(1)}, u32[]{:S(2)}, u32[]{:S(2)}) collective-permute-start(bf16[272,512]{1,0:T(8,128)(2,1)S(1)} %get-tuple-element.48), channel_id=1, source_target_pairs={{0,1},{1,0},{2,3},{3,2},{4,5},{5,4},{6,7},{7,6},{8,9},{9,8},{10,11... | collective-permute-start | bytes 835592 | tf_op jit(solution)/shard_map/ppermute | solution.py:338
  31.4 8.1 %collective-permute-start.9 = (bf16[256,512]{1,0:T(8,128)(2,1)S(1)}, bf16[256,512]{1,0:T(8,128)(2,1)S(1)}, u32[]{:S(2)}, u32[]{:S(2)}) collective-permute-start(bf16[256,512]{1,0:T(8,128)(2,1)S(1)} %get-tuple-element.49), channel_id=1, source_target_pairs={{0,2},{1,3},{2,0},{3,1},{4,6},{5,7},{6,4},{7,5},{8,10},{9,11},{10,... | collective-permute-start | bytes 786440 | tf_op jit(solution)/shard_map/ppermute | solution.py:338
  32.5 10.5 %collective-permute-start.14 = (bf16[128,512]{1,0:T(8,128)(2,1)S(1)}, bf16[128,512]{1,0:T(8,128)(2,1)S(1)}, u32[]{:S(2)}, u32[]{:S(2)}) collective-permute-start(bf16[128,512]{1,0:T(8,128)(2,1)S(1)} %get-tuple-element.51.refs_4_.refs_0_), channel_id=1, source_target_pairs={{0,2},{1,3},{2,0},{3,1},{4,6},{5,7},{6,4},{7,5},{8,10},{9,11},{10,... | collective-permute-start | bytes 393224 | tf_op jit(solution)/shard_map/ppermute | solution.py:338
  33.5 9.5 %collective-permute-start.15 = (bf16[128,512]{1,0:T(8,128)(2,1)S(1)}, bf16[128,512]{1,0:T(8,128)(2,1)S(1)}, u32[]{:S(2)}, u32[]{:S(2)}) collective-permute-start(bf16[128,512]{1,0:T(8,128)(2,1)S(1)} %get-tuple-element.56.refs_1_), channel_id=1, source_target_pairs={{0,1},{1,0},{2,3},{3,2},{4,5},{5,4},{6,7},{7,6},{8,9},{9,8},{10,11... | collective-permute-start | bytes 393224 | tf_op jit(solution)/shard_map/ppermute | solution.py:338
  39.7 9.4 %collective-permute-start.12 = (bf16[272,512]{1,0:T(8,128)(2,1)S(1)}, bf16[272,512]{1,0:T(8,128)(2,1)S(1)}, u32[]{:S(2)}, u32[]{:S(2)}) collective-permute-start(bf16[272,512]{1,0:T(8,128)(2,1)S(1)} %get-tuple-element.54), channel_id=1, source_target_pairs={{0,2},{1,3},{2,0},{3,1},{4,6},{5,7},{6,4},{7,5},{8,10},{9,11},{10,... | collective-permute-start | bytes 835592 | tf_op jit(solution)/shard_map/ppermute | solution.py:338
  41.5 7.6 %collective-permute-start.13 = (bf16[256,512]{1,0:T(8,128)(2,1)S(1)}, bf16[256,512]{1,0:T(8,128)(2,1)S(1)}, u32[]{:S(2)}, u32[]{:S(2)}) collective-permute-start(bf16[256,512]{1,0:T(8,128)(2,1)S(1)} %get-tuple-element.55), channel_id=1, source_target_pairs={{0,1},{1,0},{2,3},{3,2},{4,5},{5,4},{6,7},{7,6},{8,9},{9,8},{10,11... | collective-permute-start | bytes 786440 | tf_op jit(solution)/shard_map/ppermute | solution.py:338
  50.5 8.6 %collective-permute-start.16 = (bf16[256,512]{1,0:T(8,128)(2,1)S(1)}, bf16[256,512]{1,0:T(8,128)(2,1)S(1)}, u32[]{:S(2)}, u32[]{:S(2)}) collective-permute-start(bf16[256,512]{1,0:T(8,128)(2,1)S(1)} %get-tuple-element.58.refs_2_.first), channel_id=1, source_target_pairs={{0,1},{1,0},{2,3},{3,2},{4,5},{5,4},{6,7},{7,6},{8,9},{9,8},{10,11... | collective-permute-start | bytes 786440 | tf_op jit(solution)/shard_map/ppermute | solution.py:338
  52.1 3.4 %copy-start.4 = (bf16[1,1024,512]{2,1,0:T(8,128)(2,1)S(1)}, bf16[1,1024,512]{2,1,0:T(8,128)(2,1)}, u32[]{:S(2)}) copy-start(bf16[1,1024,512]{2,1,0:T(8,128)(2,1)} %param.14) | copy-start | bytes 3145732
  52.1 3.4 %copy-start.6 = (f32[1,1024]{1,0:T(1,128)S(1)}, f32[1,1024]{1,0:T(1,128)}, u32[]{:S(2)}) copy-start(f32[1,1024]{1,0:T(1,128)} %gain_depth.1) | copy-start | bytes 12292
  52.1 7.1 %collective-permute-start.18 = (bf16[256,512]{1,0:T(8,128)(2,1)S(1)}, bf16[256,512]{1,0:T(8,128)(2,1)S(1)}, u32[]{:S(2)}, u32[]{:S(2)}) collective-permute-start(bf16[256,512]{1,0:T(8,128)(2,1)S(1)} %get-tuple-element.59.refs_3_.second), channel_id=1, source_target_pairs={{0,2},{1,3},{2,0},{3,1},{4,6},{5,7},{6,4},{7,5},{8,10},{9,11},{10,... | collective-permute-start | bytes 786440 | tf_op jit(solution)/shard_map/ppermute | solution.py:338
  52.8 9.1 %collective-permute-start.20 = (bf16[256,512]{1,0:T(8,128)(2,1)S(1)}, bf16[256,512]{1,0:T(8,128)(2,1)S(1)}, u32[]{:S(2)}, u32[]{:S(2)}) collective-permute-start(bf16[256,512]{1,0:T(8,128)(2,1)S(1)} %get-tuple-element.62), channel_id=1, source_target_pairs={{0,2},{1,3},{2,0},{3,1},{4,6},{5,7},{6,4},{7,5},{8,10},{9,11},{10,... | collective-permute-start | bytes 786440 | tf_op jit(solution)/shard_map/ppermute | solution.py:338
  54.9 7.0 %collective-permute-start.21 = (bf16[256,512]{1,0:T(8,128)(2,1)S(1)}, bf16[256,512]{1,0:T(8,128)(2,1)S(1)}, u32[]{:S(2)}, u32[]{:S(2)}) collective-permute-start(bf16[256,512]{1,0:T(8,128)(2,1)S(1)} %get-tuple-element.63), channel_id=1, source_target_pairs={{0,1},{1,0},{2,3},{3,2},{4,5},{5,4},{6,7},{7,6},{8,9},{9,8},{10,11... | collective-permute-start | bytes 786440 | tf_op jit(solution)/shard_map/ppermute | solution.py:338
  59.1 6.4 %collective-permute-start.17 = (bf16[256,512]{1,0:T(8,128)(2,1)S(1)}, bf16[256,512]{1,0:T(8,128)(2,1)S(1)}, u32[]{:S(2)}, u32[]{:S(2)}) collective-permute-start(bf16[256,512]{1,0:T(8,128)(2,1)S(1)} %collective-permute-done.16.refs_0_), channel_id=1, source_target_pairs={{0,2},{1,3},{2,0},{3,1},{4,6},{5,7},{6,4},{7,5},{8,10},{9,11},{10,... | collective-permute-start | bytes 786440 | tf_op jit(solution)/shard_map/ppermute | solution.py:338
  59.1 6.4 %collective-permute-start.19 = (bf16[256,512]{1,0:T(8,128)(2,1)S(1)}, bf16[256,512]{1,0:T(8,128)(2,1)S(1)}, u32[]{:S(2)}, u32[]{:S(2)}) collective-permute-start(bf16[256,512]{1,0:T(8,128)(2,1)S(1)} %collective-permute-done.18.refs_1_), channel_id=1, source_target_pairs={{0,1},{1,0},{2,3},{3,2},{4,5},{5,4},{6,7},{7,6},{8,9},{9,8},{10,11... | collective-permute-start | bytes 786440 | tf_op jit(solution)/shard_map/ppermute | solution.py:338

commit v8 on v6

--- a/solution.py
+++ b/solution.py
@@ -237,8 +237,8 @@
         part = urecip * upstream - depth_in * (urecip * urecip * urecip * inner)
         part = part.astype(bf16)
         du[rows, :] = part
-        dot_du = jnp.sum(part.astype(f32) * depth_in, axis=1, keepdims=True) / recip[rows]
-        back.append(recip[rows] * recip[rows] * recip[rows] * (dot_du / features))
+        dot_du = jnp.sum(part.astype(f32) * depth_in, axis=1, keepdims=True)
+        back.append(recip[rows] * recip[rows] * (dot_du * (1.0 / features)))
     back = jnp.concatenate(back, axis=0)
     gains = gain[:, span(lax.axis_index("mp"), width)]
     for side, grad in enumerate(grads):

time: 67.1 us -> 67.1 us (level)
  no operation moved by 1% of the time
where the time goes in v8:
time: 67.1 us; the launch traced here: 67 us
  waiting for transfers between devices  27.8 us (41%)
  starting transfers between devices  25.8 us (38%)
  Pallas kernels  12.6 us (19%)
  between operations  0.78 us (1%)
    ppermute x22, waiting for transfers between devices, swap(): return lax.ppermute(value, 'mp', [(i, i ^ bit) for i in range(n)])  27.8 us
    ppermute x22, starting transfers between devices, swap(): return lax.ppermute(value, 'mp', [(i, i ^ bit) for i in range(n)])  25.8 us
    pallas_call x16, Pallas kernels, call(): pl.pallas_call(kernel, out_shape=[jax.ShapeDtypeStruct(s, d) for s, d in...  12.6 us
  transfers between devices with their start and end apart: 22, of which 12 were waited for; matrix products, arithmetic and copies ran while one was open for 0% of the time, Pallas kernels for 12%

profile of v8, /device:TPU:0, one launch (start us, length us, event | category | flops | bytes accessed | tf_op | source)
XLA Modules:
  0.0 67.0 jit_solution(115352954320172073)
XLA Ops:
  0.7 2.0 %upstream.1 = (bf16[128,512]{1,0:T(8,128)(2,1)S(1)}, bf16[128,512]{1,0:T(8,128)(2,1)S(1)}, f32[256,1024]{1,0:T(8,128)S(1)}) custom-call(bf16[256,512]{1,0:T(8,128)(2,1)} %bitcast.8, bf16[1024,512]{1,0:T(8,128)(2,1)} %bitcast.4, f32[1,1024]{1,0:T(1,128)} %gain_depth.1), custom_call_target="tpu_custom_call" | custom-call | flops 20000000000 | bytes 60000000 | tf_op jit(solution)/shard_map/upstream/pallas_call | solution.py:47
  2.7 3.0 %collective-permute-start.2 = (bf16[128,512]{1,0:T(8,128)(2,1)S(1)}, bf16[128,512]{1,0:T(8,128)(2,1)S(1)}, u32[]{:S(2)}, u32[]{:S(2)}) collective-permute-start(bf16[128,512]{1,0:T(8,128)(2,1)S(1)} %get-tuple-element.35), channel_id=1, source_target_pairs={{0,1},{1,0},{2,3},{3,2},{4,5},{5,4},{6,7},{7,6},{8,9},{9,8},{10,11... | collective-permute-start | bytes 393224 | tf_op jit(solution)/shard_map/ppermute | solution.py:318
  5.7 1.5 %collective-permute-start.3 = (bf16[128,512]{1,0:T(8,128)(2,1)S(1)}, bf16[128,512]{1,0:T(8,128)(2,1)S(1)}, u32[]{:S(2)}, u32[]{:S(2)}) collective-permute-start(bf16[128,512]{1,0:T(8,128)(2,1)S(1)} %get-tuple-element.36), channel_id=1, source_target_pairs={{0,2},{1,3},{2,0},{3,1},{4,6},{5,7},{6,4},{7,5},{8,10},{9,11},{10,... | collective-permute-start | bytes 393224 | tf_op jit(solution)/shard_map/ppermute | solution.py:318
  7.2 0.7 %project.3 = (bf16[256,512]{1,0:T(8,128)(2,1)S(1)}, bf16[256,512]{1,0:T(8,128)(2,1)S(1)}) custom-call(bf16[256,1024]{1,0:T(8,128)(2,1)S(1)} %copy-done.3, bf16[1024,4096]{1,0:T(8,128)(2,1)S(1)} %copy-done, f32[256,1024]{1,0:T(8,128)S(1)} %get-tuple-element.32.refs_2_.refs_0_), custom_call_target="tpu_custom_call" | custom-call | flops 20000000000 | bytes 60000000 | tf_op jit(solution)/shard_map/project/pallas_call | solution.py:47
  7.9 0.6 collective-permute-start
  8.5 1.2 %collective-permute-start.1 = (bf16[256,512]{1,0:T(8,128)(2,1)S(1)}, bf16[256,512]{1,0:T(8,128)(2,1)S(1)}, u32[]{:S(2)}, u32[]{:S(2)}) collective-permute-start(bf16[256,512]{1,0:T(8,128)(2,1)S(1)} %get-tuple-element.34), channel_id=1, source_target_pairs={{0,2},{1,3},{2,0},{3,1},{4,6},{5,7},{6,4},{7,5},{8,10},{9,11},{10,... | collective-permute-start | bytes 786440 | tf_op jit(solution)/shard_map/ppermute | solution.py:318
  9.7 0.0 collective-permute-done.2.refs_3_.refs_1_
  9.7 1.2 %collective-permute-done.3.refs_4_.refs_2_ = bf16[128,512]{1,0:T(8,128)(2,1)S(1)} collective-permute-done((bf16[128,512]{1,0:T(8,128)(2,1)S(1)}, bf16[128,512]{1,0:T(8,128)(2,1)S(1)}, u32[]{:S(2)}, u32[]{:S(2)}) %collective-permute-start.3) | collective-permute-done | bytes 131104 | tf_op jit(solution)/shard_map/ppermute | solution.py:318
  10.9 0.7 %project.4 = (bf16[320,512]{1,0:T(8,128)(2,1)S(1)}, bf16[320,512]{1,0:T(8,128)(2,1)S(1)}) custom-call(bf16[256,1024]{1,0:T(8,128)(2,1)S(1)} %copy-done.3, bf16[1024,4096]{1,0:T(8,128)(2,1)S(1)} %copy-done, f32[256,1024]{1,0:T(8,128)S(1)} %get-tuple-element.32.refs_2_.refs_0_, bf16[128,512]{1,0:T(8,128)(2,1)S(1)} %collective-permute-done.2.refs_3_.refs_1_, ...), custom_call_target="tpu_custom_call" | custom-call | flops 20000000000 | bytes 60000000 | tf_op jit(solution)/shard_map/project/pallas_call | solution.py:47
  11.6 0.3 collective-permute-start.4
  11.9 1.8 %collective-permute-start.6 = (bf16[320,512]{1,0:T(8,128)(2,1)S(1)}, bf16[320,512]{1,0:T(8,128)(2,1)S(1)}, u32[]{:S(2)}, u32[]{:S(2)}) collective-permute-start(bf16[320,512]{1,0:T(8,128)(2,1)S(1)} %get-tuple-element.39), channel_id=1, source_target_pairs={{0,2},{1,3},{2,0},{3,1},{4,6},{5,7},{6,4},{7,5},{8,10},{9,11},{10,... | collective-permute-start | bytes 983048 | tf_op jit(solution)/shard_map/ppermute | solution.py:318
  13.8 3.5 %collective-permute-done.refs_2_ = bf16[256,512]{1,0:T(8,128)(2,1)S(1)} collective-permute-done((bf16[256,512]{1,0:T(8,128)(2,1)S(1)}, bf16[256,512]{1,0:T(8,128)(2,1)S(1)}, u32[]{:S(2)}, u32[]{:S(2)}) %collective-permute-start) | collective-permute-done | bytes 262176 | tf_op jit(solution)/shard_map/ppermute | solution.py:318
  17.2 0.5 collective-permute-done.1.refs_3_
  17.8 0.7 %project.5 = (bf16[256,512]{1,0:T(8,128)(2,1)S(1)}, bf16[256,512]{1,0:T(8,128)(2,1)S(1)}) custom-call(bf16[256,1024]{1,0:T(8,128)(2,1)S(1)} %copy-done.3, bf16[1024,4096]{1,0:T(8,128)(2,1)S(1)} %copy-done, bf16[256,512]{1,0:T(8,128)(2,1)S(1)} %collective-permute-done.refs_2_, bf16[256,512]{1,0:T(8,128)(2,1)S(1)} %collective-permute-done.1.refs_3_, ...), custom_call_target="tpu_custom_call" | custom-call | flops 20000000000 | bytes 60000000 | tf_op jit(solution)/shard_map/project/pallas_call | solution.py:47
  18.5 1.3 %collective-permute-start.5 = (bf16[256,512]{1,0:T(8,128)(2,1)S(1)}, bf16[256,512]{1,0:T(8,128)(2,1)S(1)}, u32[]{:S(2)}, u32[]{:S(2)}) collective-permute-start(bf16[256,512]{1,0:T(8,128)(2,1)S(1)} %get-tuple-element.38.refs_3_), channel_id=1, source_target_pairs={{0,2},{1,3},{2,0},{3,1},{4,6},{5,7},{6,4},{7,5},{8,10},{9,11},{10,... | collective-permute-start | bytes 786440 | tf_op jit(solution)/shard_map/ppermute | solution.py:318
  19.7 0.8 %collective-permute-start.7 = (bf16[256,512]{1,0:T(8,128)(2,1)S(1)}, bf16[256,512]{1,0:T(8,128)(2,1)S(1)}, u32[]{:S(2)}, u32[]{:S(2)}) collective-permute-start(bf16[256,512]{1,0:T(8,128)(2,1)S(1)} %get-tuple-element.40), channel_id=1, source_target_pairs={{0,1},{1,0},{2,3},{3,2},{4,5},{5,4},{6,7},{7,6},{8,9},{9,8},{10,11... | collective-permute-start | bytes 786440 | tf_op jit(solution)/shard_map/ppermute | solution.py:318
  20.6 0.7 %keep.1.refs_5_.refs_2_ = f32[256,1024]{1,0:T(8,128)S(1)} custom-call(bf16[256,1024]{1,0:T(8,128)(2,1)S(1)} %copy-done.3, bf16[1024,4096]{1,0:T(8,128)(2,1)S(1)} %copy-done, bf16[256,1024]{1,0:T(8,128)(2,1)S(1)} %copy-done.4, bf16[256,512]{1,0:T(8,128)(2,1)S(1)} %get-tuple-element.38.refs_3_), custom_call_target="tpu_custom_call" | custom-call | flops 20000000000 | bytes 60000000 | tf_op jit(solution)/shard_map/keep/pallas_call | solution.py:47
  21.3 3.0 %collective-permute-done.4.refs_4_.refs_3_ = bf16[320,512]{1,0:T(8,128)(2,1)S(1)} collective-permute-done((bf16[320,512]{1,0:T(8,128)(2,1)S(1)}, bf16[320,512]{1,0:T(8,128)(2,1)S(1)}, u32[]{:S(2)}, u32[]{:S(2)}) %collective-permute-start.4) | collective-permute-done | bytes 327712 | tf_op jit(solution)/shard_map/ppermute | solution.py:318
  24.2 0.5 collective-permute-done.6.refs_3_.refs_5_
  24.8 1.6 %collective-permute-start.10 = (bf16[64,512]{1,0:T(8,128)(2,1)S(1)}, bf16[64,512]{1,0:T(8,128)(2,1)S(1)}, u32[]{:S(2)}, u32[]{:S(2)}) collective-permute-start(bf16[64,512]{1,0:T(8,128)(2,1)S(1)} %get-tuple-element.41.refs_7_.refs_0_), channel_id=1, source_target_pairs={{0,1},{1,0},{2,3},{3,2},{4,5},{5,4},{6,7},{7,6},{8,9},{9,8},{10,11... | collective-permute-start | bytes 196616 | tf_op jit(solution)/shard_map/ppermute | solution.py:318
  26.4 0.5 collective-permute-start.11
  26.9 2.7 %collective-permute-done.5.refs_4_ = bf16[256,512]{1,0:T(8,128)(2,1)S(1)} collective-permute-done((bf16[256,512]{1,0:T(8,128)(2,1)S(1)}, bf16[256,512]{1,0:T(8,128)(2,1)S(1)}, u32[]{:S(2)}, u32[]{:S(2)}) %collective-permute-start.5) | collective-permute-done | bytes 262176 | tf_op jit(solution)/shard_map/ppermute | solution.py:318
  29.6 0.0 collective-permute-done.7.refs_6_
  29.6 0.8 %state.1 = (f32[256,1024]{1,0:T(8,128)S(1)}, f32[256,1024]{1,0:T(8,128)S(1)}, f32[8,256]{1,0:T(8,128)S(1)}, bf16[272,512]{1,0:T(8,128)(2,1)S(1)}, bf16[256,512]{1,0:T(8,128)(2,1)S(1)}) custom-call(f32[1,4096]{1,0:T(1,128)S(1)} %bitcast.6, bf16[1024,1024]{1,0:T(8,128)(2,1)S(1)} %copy-done.1, f32[256,1024]{1,0:T(8,128)S(1)} %keep.1.refs_5_.refs_2_, ...), custom_call_target="tpu_custom_call" | custom-call | flops 20000000000 | bytes 60000000 | tf_op jit(solution)/shard_map/state/pallas_call | solution.py:47
  30.4 1.0 %collective-permute-start.8 = (bf16[272,512]{1,0:T(8,128)(2,1)S(1)}, bf16[272,512]{1,0:T(8,128)(2,1)S(1)}, u32[]{:S(2)}, u32[]{:S(2)}) collective-permute-start(bf16[272,512]{1,0:T(8,128)(2,1)S(1)} %get-tuple-element.44), channel_id=1, source_target_pairs={{0,1},{1,0},{2,3},{3,2},{4,5},{5,4},{6,7},{7,6},{8,9},{9,8},{10,11... | collective-permute-start | bytes 835592 | tf_op jit(solution)/shard_map/ppermute | solution.py:318
  31.4 1.1 %collective-permute-start.9 = (bf16[256,512]{1,0:T(8,128)(2,1)S(1)}, bf16[256,512]{1,0:T(8,128)(2,1)S(1)}, u32[]{:S(2)}, u32[]{:S(2)}) collective-permute-start(bf16[256,512]{1,0:T(8,128)(2,1)S(1)} %get-tuple-element.45), channel_id=1, source_target_pairs={{0,2},{1,3},{2,0},{3,1},{4,6},{5,7},{6,4},{7,5},{8,10},{9,11},{10,... | collective-permute-start | bytes 786440 | tf_op jit(solution)/shard_map/ppermute | solution.py:318
  32.5 1.0 %collective-permute-start.14 = (bf16[128,512]{1,0:T(8,128)(2,1)S(1)}, bf16[128,512]{1,0:T(8,128)(2,1)S(1)}, u32[]{:S(2)}, u32[]{:S(2)}) collective-permute-start(bf16[128,512]{1,0:T(8,128)(2,1)S(1)} %get-tuple-element.47.refs_4_.refs_0_), channel_id=1, source_target_pairs={{0,2},{1,3},{2,0},{3,1},{4,6},{5,7},{6,4},{7,5},{8,10},{9,11},{10,... | collective-permute-start | bytes 393224 | tf_op jit(solution)/shard_map/ppermute | solution.py:318
  33.5 1.1 %collective-permute-start.15 = (bf16[128,512]{1,0:T(8,128)(2,1)S(1)}, bf16[128,512]{1,0:T(8,128)(2,1)S(1)}, u32[]{:S(2)}, u32[]{:S(2)}) collective-permute-start(bf16[128,512]{1,0:T(8,128)(2,1)S(1)} %get-tuple-element.52.refs_1_), channel_id=1, source_target_pairs={{0,1},{1,0},{2,3},{3,2},{4,5},{5,4},{6,7},{7,6},{8,9},{9,8},{10,11... | collective-permute-start | bytes 393224 | tf_op jit(solution)/shard_map/ppermute | solution.py:318
  34.6 4.9 %collective-permute-done.9.refs_3_ = bf16[256,512]{1,0:T(8,128)(2,1)S(1)} collective-permute-done((bf16[256,512]{1,0:T(8,128)(2,1)S(1)}, bf16[256,512]{1,0:T(8,128)(2,1)S(1)}, u32[]{:S(2)}, u32[]{:S(2)}) %collective-permute-start.9) | collective-permute-done | bytes 262176 | tf_op jit(solution)/shard_map/ppermute | solution.py:318
  39.5 0.2 reduce.1
  39.6 1.9 %collective-permute-start.12 = (bf16[272,512]{1,0:T(8,128)(2,1)S(1)}, bf16[272,512]{1,0:T(8,128)(2,1)S(1)}, u32[]{:S(2)}, u32[]{:S(2)}) collective-permute-start(bf16[272,512]{1,0:T(8,128)(2,1)S(1)} %get-tuple-element.50), channel_id=1, source_target_pairs={{0,2},{1,3},{2,0},{3,1},{4,6},{5,7},{6,4},{7,5},{8,10},{9,11},{10,... | collective-permute-start | bytes 835592 | tf_op jit(solution)/shard_map/ppermute | solution.py:318
  41.5 1.5 %collective-permute-start.13 = (bf16[256,512]{1,0:T(8,128)(2,1)S(1)}, bf16[256,512]{1,0:T(8,128)(2,1)S(1)}, u32[]{:S(2)}, u32[]{:S(2)}) collective-permute-start(bf16[256,512]{1,0:T(8,128)(2,1)S(1)} %get-tuple-element.51), channel_id=1, source_target_pairs={{0,1},{1,0},{2,3},{3,2},{4,5},{5,4},{6,7},{7,6},{8,9},{9,8},{10,11... | collective-permute-start | bytes 786440 | tf_op jit(solution)/shard_map/ppermute | solution.py:318
  43.0 6.1 %collective-permute-done.13.refs_1_ = bf16[256,512]{1,0:T(8,128)(2,1)S(1)} collective-permute-done((bf16[256,512]{1,0:T(8,128)(2,1)S(1)}, bf16[256,512]{1,0:T(8,128)(2,1)S(1)}, u32[]{:S(2)}, u32[]{:S(2)}) %collective-permute-start.13) | collective-permute-done | bytes 262176 | tf_op jit(solution)/shard_map/ppermute | solution.py:318
  49.1 1.4 %back.1 = (bf16[256,512]{1,0:T(8,128)(2,1)S(1)}, bf16[256,512]{1,0:T(8,128)(2,1)S(1)}) custom-call(f32[1,4096]{1,0:T(1,128)S(1)} %bitcast.7, bf16[1024,1024]{1,0:T(8,128)(2,1)S(1)} %copy-done.1, bf16[256,1024]{1,0:T(8,128)(2,1)S(1)} %assemble.1.up, f32[256,1024]{1,0:T(8,128)S(1)} %get-tuple-element.53.state, f32[256,1024]{1,0:T(8,128)S(1)} %get-tuple-element.48.raw, ...), custom_call_target="tpu_custom_call" | custom-call | flops 20000000000 | bytes 60000000 | tf_op jit(solution)/shard_map/back/pallas_call | solution.py:47
  50.5 1.6 %collective-permute-start.16 = (bf16[256,512]{1,0:T(8,128)(2,1)S(1)}, bf16[256,512]{1,0:T(8,128)(2,1)S(1)}, u32[]{:S(2)}, u32[]{:S(2)}) collective-permute-start(bf16[256,512]{1,0:T(8,128)(2,1)S(1)} %get-tuple-element.54.refs_2_.first), channel_id=1, source_target_pairs={{0,1},{1,0},{2,3},{3,2},{4,5},{5,4},{6,7},{7,6},{8,9},{9,8},{10,11... | collective-permute-start | bytes 786440 | tf_op jit(solution)/shard_map/ppermute | solution.py:318
  52.0 0.7 %grad_context.4 = (f32[256,1024]{1,0:T(8,128)S(1)}, bf16[256,512]{1,0:T(8,128)(2,1)S(1)}, bf16[256,512]{1,0:T(8,128)(2,1)S(1)}) custom-call(bf16[1024,4096]{1,0:T(8,128)(2,1)S(1)} %copy-done, bf16[256,512]{1,0:T(8,128)(2,1)S(1)} %get-tuple-element.54.refs_2_.first, bf16[256,512]{1,0:T(8,128)(2,1)S(1)} %get-tuple-element.55.refs_3_.second), custom_call_target="tpu_custom_call" | custom-call | flops 20000000000 | bytes 60000000 | tf_op jit(solution)/shard_map/grad_context/pallas_call | solution.py:47
  52.8 2.1 %collective-permute-start.20 = (bf16[256,512]{1,0:T(8,128)(2,1)S(1)}, bf16[256,512]{1,0:T(8,128)(2,1)S(1)}, u32[]{:S(2)}, u32[]{:S(2)}) collective-permute-start(bf16[256,512]{1,0:T(8,128)(2,1)S(1)} %get-tuple-element.58), channel_id=1, source_target_pairs={{0,2},{1,3},{2,0},{3,1},{4,6},{5,7},{6,4},{7,5},{8,10},{9,11},{10,... | collective-permute-start | bytes 786440 | tf_op jit(solution)/shard_map/ppermute | solution.py:318
  54.9 0.5 collective-permute-start.21
  55.4 1.6 %act.1 = (bf16[256,512]{1,0:T(8,128)(2,1)}, bf16[256,1024]{1,0:T(8,128)(2,1)}) custom-call(f32[1,1024]{1,0:T(1,128)S(1)} %copy-done.6, bf16[1024,512]{1,0:T(8,128)(2,1)S(1)} %bitcast.5, f32[256,1024]{1,0:T(8,128)S(1)} %get-tuple-element.48.raw, f32[8,256]{1,0:T(8,128)S(1)} %get-tuple-element.49.refs_4_.squares, ...), custom_call_target="tpu_custom_call" | custom-call | flops 20000000000 | bytes 60000000 | tf_op jit(solution)/shard_map/act/pallas_call | solution.py:47
  57.0 2.1 %collective-permute-done.16.refs_0_ = bf16[256,512]{1,0:T(8,128)(2,1)S(1)} collective-permute-done((bf16[256,512]{1,0:T(8,128)(2,1)S(1)}, bf16[256,512]{1,0:T(8,128)(2,1)S(1)}, u32[]{:S(2)}, u32[]{:S(2)}) %collective-permute-start.16) | collective-permute-done | bytes 262176 | tf_op jit(solution)/shard_map/ppermute | solution.py:318
  59.1 1.5 %collective-permute-start.19 = (bf16[256,512]{1,0:T(8,128)(2,1)S(1)}, bf16[256,512]{1,0:T(8,128)(2,1)S(1)}, u32[]{:S(2)}, u32[]{:S(2)}) collective-permute-start(bf16[256,512]{1,0:T(8,128)(2,1)S(1)} %collective-permute-done.18.refs_1_), channel_id=1, source_target_pairs={{0,1},{1,0},{2,3},{3,2},{4,5},{5,4},{6,7},{7,6},{8,9},{9,8},{10,11... | collective-permute-start | bytes 786440 | tf_op jit(solution)/shard_map/ppermute | solution.py:318
  60.6 0.7 %grad_context.5.refs_2_ = f32[256,1024]{1,0:T(8,128)S(1)} custom-call(bf16[1024,4096]{1,0:T(8,128)(2,1)S(1)} %copy-done, bf16[256,512]{1,0:T(8,128)(2,1)S(1)} %collective-permute-done.16.refs_0_, bf16[256,512]{1,0:T(8,128)(2,1)S(1)} %collective-permute-done.18.refs_1_, f32[256,1024]{1,0:T(8,128)S(1)} %get-tuple-element.60.refs_2_), custom_call_target="tpu_custom_call" | custom-call | flops 20000000000 | bytes 60000000 | tf_op jit(solution)/shard_map/grad_context/pallas_call | solution.py:47
  61.3 0.5 collective-permute-done.20.refs_0_
  61.8 0.1 collective-permute-done.21.refs_1_
  61.9 0.7 %grad_context.6.refs_2_ = f32[256,1024]{1,0:T(8,128)S(1)} custom-call(bf16[1024,4096]{1,0:T(8,128)(2,1)S(1)} %copy-done, bf16[256,512]{1,0:T(8,128)(2,1)S(1)} %collective-permute-done.20.refs_0_, bf16[256,512]{1,0:T(8,128)(2,1)S(1)} %collective-permute-done.21.refs_1_, f32[256,1024]{1,0:T(8,128)S(1)} %grad_context.5.refs_2_), custom_call_target="tpu_custom_call" | custom-call | flops 20000000000 | bytes 60000000 | tf_op jit(solution)/shard_map/grad_context/pallas_call | solution.py:47
  62.7 2.8 %collective-permute-done.17.refs_0_ = bf16[256,512]{1,0:T(8,128)(2,1)S(1)} collective-permute-done((bf16[256,512]{1,0:T(8,128)(2,1)S(1)}, bf16[256,512]{1,0:T(8,128)(2,1)S(1)}, u32[]{:S(2)}, u32[]{:S(2)}) %collective-permute-start.17) | collective-permute-done | bytes 262176 | tf_op jit(solution)/shard_map/ppermute | solution.py:318
  65.5 0.0 collective-permute-done.19.refs_1_
  65.5 1.5 %grad_context.7 = bf16[256,1024]{1,0:T(8,128)(2,1)} custom-call(bf16[1024,4096]{1,0:T(8,128)(2,1)S(1)} %copy-done, bf16[256,512]{1,0:T(8,128)(2,1)S(1)} %collective-permute-done.17.refs_0_, bf16[256,512]{1,0:T(8,128)(2,1)S(1)} %collective-permute-done.19.refs_1_, f32[256,1024]{1,0:T(8,128)S(1)} %grad_context.6.refs_2_), custom_call_target="tpu_custom_call" | custom-call | flops 20000000000 | bytes 60000000 | tf_op jit(solution)/shard_map/grad_context/pallas_call | solution.py:47
  (26 shorter events, 0.2 us)
Async XLA Ops:
  0.6 6.5 %copy-start = (bf16[1024,4096]{1,0:T(8,128)(2,1)S(1)}, bf16[1024,4096]{1,0:T(8,128)(2,1)}, u32[]{:S(2)}) copy-start(bf16[1024,4096]{1,0:T(8,128)(2,1)} %w_out.7) | copy-start | bytes 25165828
  0.6 6.5 %copy-start.3 = (bf16[256,1024]{1,0:T(8,128)(2,1)S(1)}, bf16[256,1024]{1,0:T(8,128)(2,1)}, u32[]{:S(2)}) copy-start(bf16[256,1024]{1,0:T(8,128)(2,1)} %refs_0_.7) | copy-start | bytes 1572868
  2.7 7.1 %collective-permute-start.2 = (bf16[128,512]{1,0:T(8,128)(2,1)S(1)}, bf16[128,512]{1,0:T(8,128)(2,1)S(1)}, u32[]{:S(2)}, u32[]{:S(2)}) collective-permute-start(bf16[128,512]{1,0:T(8,128)(2,1)S(1)} %get-tuple-element.35), channel_id=1, source_target_pairs={{0,1},{1,0},{2,3},{3,2},{4,5},{5,4},{6,7},{7,6},{8,9},{9,8},{10,11... | collective-permute-start | bytes 393224 | tf_op jit(solution)/shard_map/ppermute | solution.py:318
  5.7 5.2 %collective-permute-start.3 = (bf16[128,512]{1,0:T(8,128)(2,1)S(1)}, bf16[128,512]{1,0:T(8,128)(2,1)S(1)}, u32[]{:S(2)}, u32[]{:S(2)}) collective-permute-start(bf16[128,512]{1,0:T(8,128)(2,1)S(1)} %get-tuple-element.36), channel_id=1, source_target_pairs={{0,2},{1,3},{2,0},{3,1},{4,6},{5,7},{6,4},{7,5},{8,10},{9,11},{10,... | collective-permute-start | bytes 393224 | tf_op jit(solution)/shard_map/ppermute | solution.py:318
  7.9 9.3 %collective-permute-start = (bf16[256,512]{1,0:T(8,128)(2,1)S(1)}, bf16[256,512]{1,0:T(8,128)(2,1)S(1)}, u32[]{:S(2)}, u32[]{:S(2)}) collective-permute-start(bf16[256,512]{1,0:T(8,128)(2,1)S(1)} %get-tuple-element.33.refs_5_), channel_id=1, source_target_pairs={{0,1},{1,0},{2,3},{3,2},{4,5},{5,4},{6,7},{7,6},{8,9},{9,8},{10,11... | collective-permute-start | bytes 786440 | tf_op jit(solution)/shard_map/ppermute | solution.py:318
  8.5 9.2 %collective-permute-start.1 = (bf16[256,512]{1,0:T(8,128)(2,1)S(1)}, bf16[256,512]{1,0:T(8,128)(2,1)S(1)}, u32[]{:S(2)}, u32[]{:S(2)}) collective-permute-start(bf16[256,512]{1,0:T(8,128)(2,1)S(1)} %get-tuple-element.34), channel_id=1, source_target_pairs={{0,2},{1,3},{2,0},{3,1},{4,6},{5,7},{6,4},{7,5},{8,10},{9,11},{10,... | collective-permute-start | bytes 786440 | tf_op jit(solution)/shard_map/ppermute | solution.py:318
  11.6 12.6 %collective-permute-start.4 = (bf16[320,512]{1,0:T(8,128)(2,1)S(1)}, bf16[320,512]{1,0:T(8,128)(2,1)S(1)}, u32[]{:S(2)}, u32[]{:S(2)}) collective-permute-start(bf16[320,512]{1,0:T(8,128)(2,1)S(1)} %get-tuple-element.37.refs_4_), channel_id=1, source_target_pairs={{0,1},{1,0},{2,3},{3,2},{4,5},{5,4},{6,7},{7,6},{8,9},{9,8},{10,11... | collective-permute-start | bytes 983048 | tf_op jit(solution)/shard_map/ppermute | solution.py:318
  11.9 8.6 %copy-start.4 = (bf16[256,1024]{1,0:T(8,128)(2,1)S(1)}, bf16[256,1024]{1,0:T(8,128)(2,1)}, u32[]{:S(2)}) copy-start(bf16[256,1024]{1,0:T(8,128)(2,1)} %refs_2_.1) | copy-start | bytes 1572868
  11.9 12.9 %collective-permute-start.6 = (bf16[320,512]{1,0:T(8,128)(2,1)S(1)}, bf16[320,512]{1,0:T(8,128)(2,1)S(1)}, u32[]{:S(2)}, u32[]{:S(2)}) collective-permute-start(bf16[320,512]{1,0:T(8,128)(2,1)S(1)} %get-tuple-element.39), channel_id=1, source_target_pairs={{0,2},{1,3},{2,0},{3,1},{4,6},{5,7},{6,4},{7,5},{8,10},{9,11},{10,... | collective-permute-start | bytes 983048 | tf_op jit(solution)/shard_map/ppermute | solution.py:318
  18.5 11.1 %collective-permute-start.5 = (bf16[256,512]{1,0:T(8,128)(2,1)S(1)}, bf16[256,512]{1,0:T(8,128)(2,1)S(1)}, u32[]{:S(2)}, u32[]{:S(2)}) collective-permute-start(bf16[256,512]{1,0:T(8,128)(2,1)S(1)} %get-tuple-element.38.refs_3_), channel_id=1, source_target_pairs={{0,2},{1,3},{2,0},{3,1},{4,6},{5,7},{6,4},{7,5},{8,10},{9,11},{10,... | collective-permute-start | bytes 786440 | tf_op jit(solution)/shard_map/ppermute | solution.py:318
  19.7 9.8 %copy-start.1 = (bf16[1024,1024]{1,0:T(8,128)(2,1)S(1)}, bf16[1024,1024]{1,0:T(8,128)(2,1)}, u32[]{:S(2)}) copy-start(bf16[1024,1024]{1,0:T(8,128)(2,1)} %w_in.1) | copy-start | bytes 6291460
  19.7 9.8 %copy-start.5 = (f32[4096]{0:T(1024)S(1)}, f32[4096]{0:T(1024)}, u32[]{:S(2)}) copy-start(f32[4096]{0:T(1024)} %param.11) | copy-start | bytes 49156
  19.7 9.8 %collective-permute-start.7 = (bf16[256,512]{1,0:T(8,128)(2,1)S(1)}, bf16[256,512]{1,0:T(8,128)(2,1)S(1)}, u32[]{:S(2)}, u32[]{:S(2)}) collective-permute-start(bf16[256,512]{1,0:T(8,128)(2,1)S(1)} %get-tuple-element.40), channel_id=1, source_target_pairs={{0,1},{1,0},{2,3},{3,2},{4,5},{5,4},{6,7},{7,6},{8,9},{9,8},{10,11... | collective-permute-start | bytes 786440 | tf_op jit(solution)/shard_map/ppermute | solution.py:318
  24.8 7.7 %collective-permute-start.10 = (bf16[64,512]{1,0:T(8,128)(2,1)S(1)}, bf16[64,512]{1,0:T(8,128)(2,1)S(1)}, u32[]{:S(2)}, u32[]{:S(2)}) collective-permute-start(bf16[64,512]{1,0:T(8,128)(2,1)S(1)} %get-tuple-element.41.refs_7_.refs_0_), channel_id=1, source_target_pairs={{0,1},{1,0},{2,3},{3,2},{4,5},{5,4},{6,7},{7,6},{8,9},{9,8},{10,11... | collective-permute-start | bytes 196616 | tf_op jit(solution)/shard_map/ppermute | solution.py:318
  26.4 6.1 %collective-permute-start.11 = (bf16[64,512]{1,0:T(8,128)(2,1)S(1)}, bf16[64,512]{1,0:T(8,128)(2,1)S(1)}, u32[]{:S(2)}, u32[]{:S(2)}) collective-permute-start(bf16[64,512]{1,0:T(8,128)(2,1)S(1)} %get-tuple-element.46.refs_1_), channel_id=1, source_target_pairs={{0,2},{1,3},{2,0},{3,1},{4,6},{5,7},{6,4},{7,5},{8,10},{9,11},{10,... | collective-permute-start | bytes 196616 | tf_op jit(solution)/shard_map/ppermute | solution.py:318
  30.4 9.1 %collective-permute-start.8 = (bf16[272,512]{1,0:T(8,128)(2,1)S(1)}, bf16[272,512]{1,0:T(8,128)(2,1)S(1)}, u32[]{:S(2)}, u32[]{:S(2)}) collective-permute-start(bf16[272,512]{1,0:T(8,128)(2,1)S(1)} %get-tuple-element.44), channel_id=1, source_target_pairs={{0,1},{1,0},{2,3},{3,2},{4,5},{5,4},{6,7},{7,6},{8,9},{9,8},{10,11... | collective-permute-start | bytes 835592 | tf_op jit(solution)/shard_map/ppermute | solution.py:318
  31.4 8.1 %collective-permute-start.9 = (bf16[256,512]{1,0:T(8,128)(2,1)S(1)}, bf16[256,512]{1,0:T(8,128)(2,1)S(1)}, u32[]{:S(2)}, u32[]{:S(2)}) collective-permute-start(bf16[256,512]{1,0:T(8,128)(2,1)S(1)} %get-tuple-element.45), channel_id=1, source_target_pairs={{0,2},{1,3},{2,0},{3,1},{4,6},{5,7},{6,4},{7,5},{8,10},{9,11},{10,... | collective-permute-start | bytes 786440 | tf_op jit(solution)/shard_map/ppermute | solution.py:318
  32.5 10.5 %collective-permute-start.14 = (bf16[128,512]{1,0:T(8,128)(2,1)S(1)}, bf16[128,512]{1,0:T(8,128)(2,1)S(1)}, u32[]{:S(2)}, u32[]{:S(2)}) collective-permute-start(bf16[128,512]{1,0:T(8,128)(2,1)S(1)} %get-tuple-element.47.refs_4_.refs_0_), channel_id=1, source_target_pairs={{0,2},{1,3},{2,0},{3,1},{4,6},{5,7},{6,4},{7,5},{8,10},{9,11},{10,... | collective-permute-start | bytes 393224 | tf_op jit(solution)/shard_map/ppermute | solution.py:318
  33.5 9.5 %collective-permute-start.15 = (bf16[128,512]{1,0:T(8,128)(2,1)S(1)}, bf16[128,512]{1,0:T(8,128)(2,1)S(1)}, u32[]{:S(2)}, u32[]{:S(2)}) collective-permute-start(bf16[128,512]{1,0:T(8,128)(2,1)S(1)} %get-tuple-element.52.refs_1_), channel_id=1, source_target_pairs={{0,1},{1,0},{2,3},{3,2},{4,5},{5,4},{6,7},{7,6},{8,9},{9,8},{10,11... | collective-permute-start | bytes 393224 | tf_op jit(solution)/shard_map/ppermute | solution.py:318
  39.6 9.4 %collective-permute-start.12 = (bf16[272,512]{1,0:T(8,128)(2,1)S(1)}, bf16[272,512]{1,0:T(8,128)(2,1)S(1)}, u32[]{:S(2)}, u32[]{:S(2)}) collective-permute-start(bf16[272,512]{1,0:T(8,128)(2,1)S(1)} %get-tuple-element.50), channel_id=1, source_target_pairs={{0,2},{1,3},{2,0},{3,1},{4,6},{5,7},{6,4},{7,5},{8,10},{9,11},{10,... | collective-permute-start | bytes 835592 | tf_op jit(solution)/shard_map/ppermute | solution.py:318
  41.5 7.6 %collective-permute-start.13 = (bf16[256,512]{1,0:T(8,128)(2,1)S(1)}, bf16[256,512]{1,0:T(8,128)(2,1)S(1)}, u32[]{:S(2)}, u32[]{:S(2)}) collective-permute-start(bf16[256,512]{1,0:T(8,128)(2,1)S(1)} %get-tuple-element.51), channel_id=1, source_target_pairs={{0,1},{1,0},{2,3},{3,2},{4,5},{5,4},{6,7},{7,6},{8,9},{9,8},{10,11... | collective-permute-start | bytes 786440 | tf_op jit(solution)/shard_map/ppermute | solution.py:318
  50.5 8.6 %collective-permute-start.16 = (bf16[256,512]{1,0:T(8,128)(2,1)S(1)}, bf16[256,512]{1,0:T(8,128)(2,1)S(1)}, u32[]{:S(2)}, u32[]{:S(2)}) collective-permute-start(bf16[256,512]{1,0:T(8,128)(2,1)S(1)} %get-tuple-element.54.refs_2_.first), channel_id=1, source_target_pairs={{0,1},{1,0},{2,3},{3,2},{4,5},{5,4},{6,7},{7,6},{8,9},{9,8},{10,11... | collective-permute-start | bytes 786440 | tf_op jit(solution)/shard_map/ppermute | solution.py:318
  52.0 3.4 %copy-start.2 = (bf16[1,1024,512]{2,1,0:T(8,128)(2,1)S(1)}, bf16[1,1024,512]{2,1,0:T(8,128)(2,1)}, u32[]{:S(2)}) copy-start(bf16[1,1024,512]{2,1,0:T(8,128)(2,1)} %param.14) | copy-start | bytes 3145732
  52.0 3.4 %copy-start.6 = (f32[1,1024]{1,0:T(1,128)S(1)}, f32[1,1024]{1,0:T(1,128)}, u32[]{:S(2)}) copy-start(f32[1,1024]{1,0:T(1,128)} %gain_depth.1) | copy-start | bytes 12292
  52.0 7.1 %collective-permute-start.18 = (bf16[256,512]{1,0:T(8,128)(2,1)S(1)}, bf16[256,512]{1,0:T(8,128)(2,1)S(1)}, u32[]{:S(2)}, u32[]{:S(2)}) collective-permute-start(bf16[256,512]{1,0:T(8,128)(2,1)S(1)} %get-tuple-element.55.refs_3_.second), channel_id=1, source_target_pairs={{0,2},{1,3},{2,0},{3,1},{4,6},{5,7},{6,4},{7,5},{8,10},{9,11},{10,... | collective-permute-start | bytes 786440 | tf_op jit(solution)/shard_map/ppermute | solution.py:318
  52.8 9.0 %collective-permute-start.20 = (bf16[256,512]{1,0:T(8,128)(2,1)S(1)}, bf16[256,512]{1,0:T(8,128)(2,1)S(1)}, u32[]{:S(2)}, u32[]{:S(2)}) collective-permute-start(bf16[256,512]{1,0:T(8,128)(2,1)S(1)} %get-tuple-element.58), channel_id=1, source_target_pairs={{0,2},{1,3},{2,0},{3,1},{4,6},{5,7},{6,4},{7,5},{8,10},{9,11},{10,... | collective-permute-start | bytes 786440 | tf_op jit(solution)/shard_map/ppermute | solution.py:318
  54.9 7.0 %collective-permute-start.21 = (bf16[256,512]{1,0:T(8,128)(2,1)S(1)}, bf16[256,512]{1,0:T(8,128)(2,1)S(1)}, u32[]{:S(2)}, u32[]{:S(2)}) collective-permute-start(bf16[256,512]{1,0:T(8,128)(2,1)S(1)} %get-tuple-element.59), channel_id=1, source_target_pairs={{0,1},{1,0},{2,3},{3,2},{4,5},{5,4},{6,7},{7,6},{8,9},{9,8},{10,11... | collective-permute-start | bytes 786440 | tf_op jit(solution)/shard_map/ppermute | solution.py:318
  59.1 6.4 %collective-permute-start.17 = (bf16[256,512]{1,0:T(8,128)(2,1)S(1)}, bf16[256,512]{1,0:T(8,128)(2,1)S(1)}, u32[]{:S(2)}, u32[]{:S(2)}) collective-permute-start(bf16[256,512]{1,0:T(8,128)(2,1)S(1)} %collective-permute-done.16.refs_0_), channel_id=1, source_target_pairs={{0,2},{1,3},{2,0},{3,1},{4,6},{5,7},{6,4},{7,5},{8,10},{9,11},{10,... | collective-permute-start | bytes 786440 | tf_op jit(solution)/shard_map/ppermute | solution.py:318
  59.1 6.4 %collective-permute-start.19 = (bf16[256,512]{1,0:T(8,128)(2,1)S(1)}, bf16[256,512]{1,0:T(8,128)(2,1)S(1)}, u32[]{:S(2)}, u32[]{:S(2)}) collective-permute-start(bf16[256,512]{1,0:T(8,128)(2,1)S(1)} %collective-permute-done.18.refs_1_), channel_id=1, source_target_pairs={{0,1},{1,0},{2,3},{3,2},{4,5},{5,4},{6,7},{7,6},{8,9},{9,8},{10,11... | collective-permute-start | bytes 786440 | tf_op jit(solution)/shard_map/ppermute | solution.py:318

commit v9 on v6

--- a/solution.py
+++ b/solution.py
@@ -176,8 +176,8 @@
     put_squares(sends[0], frames, row)
 
 
-def reduce_kernel(raw, squares, *refs):
-    got, (raw_out, squares_out, *sends) = refs[:2], refs[2:]
+def reduce_kernel(starts, held, raw, squares, *refs):
+    got, own, more, (raw_out, squares_out, *sends) = refs[:2], refs[2:4], refs[4:6], refs[6:]
     frames, depth = raw.shape
     wide = depth // 2
     for side in range(2):
@@ -185,9 +185,11 @@
         total = raw[:, cols] + got[side][:frames, :].astype(f32)
         raw_out[:, cols] = total
         sends[side][:frames, :] = total.astype(bf16)
-    row = squares[...] + get_squares(got[0], frames, frames)
+        sends[side][frames : frames + held, :] = own[side][starts[0] : starts[0] + held, :]
+        sends[side][frames + held : frames + 2 * held, :] = more[side][starts[1] : starts[1] + held, :]
+    row = squares[...] + get_squares(got[0], got[0].shape[0] - SQ, frames)
     squares_out[...] = row
-    put_squares(sends[0], frames, row)
+    put_squares(sends[0], frames + 2 * held, row)
 
 
 def depth_rows(raw, got, rows):
@@ -202,29 +204,24 @@
 
 
 def recip_of(squares, got, frames, features):
-    row = squares[...] + get_squares(got[0], frames, frames)
+    row = squares[...] + get_squares(got[0], got[0].shape[0] - SQ, frames)
     return jnp.transpose(
         jnp.broadcast_to(lax.rsqrt(row[:1] / features + EPS), (LANES, frames))
     )[:, :1]
 
 
-def assemble_kernel(haves, share, *refs):
-    sent, rest, up = refs[:2], refs[2:4], refs[4]
-    wide = up.shape[1] // 2
+def back_kernel(haves, share, features, gain, w_in, state, raw, squares, *refs):
+    sent, got, (*grads, up, du) = refs[:2], refs[2:4], refs[4:]
+    frames, width = state.shape
+    half, wide = width // 2, raw.shape[1] // 2
+    held = sent[1].shape[0] - frames
     for side in range(2):
-        held = sent[side].shape[0]
         for i, mask in enumerate(haves[side]):
             at = i * share
-            ref, at = (sent[side], at) if at < held else (rest[side], at - held)
+            ref, at = (sent[side], at) if at < held else (got[side], at - held)
             up[span(owner(mask), share), side * wide : (side + 1) * wide] = ref[
-                at : at + share, :
+                frames + at : frames + at + share, :
             ]
-
-
-def back_kernel(features, gain, w_in, up, state, raw, squares, *refs):
-    got, (*grads, du) = refs[:2], refs[2:]
-    frames, width = state.shape
-    half = width // 2
     recip = recip_of(squares, got, frames, features)
     back = []
     step = 64 if frames % 64 == 0 else frames
@@ -425,41 +422,36 @@
         after=own_share[0],
     )
     haves = [[0], [0]]
-    token = squares
     for i in range(log):
         got = both(sends, i)
         haves = [have + [k ^ orders[s][i] for k in have] for s, have in enumerate(haves)]
         if i < log - 1:
-            own_share = list(
-                call(
-                    join_kernel,
-                    [((2 * own_share[0].shape[0], wide), bf16)] * 2,
-                    own_share + share_got,
-                    name="join",
-                    after=token,
+            held = share << i
+            rows = frames + 2 * held
+            starts, own, more = (frames, frames), list(sends), got
+            if i == 0:
+                starts = (0, held)
+                own = more = list(
+                    call(
+                        join_kernel,
+                        [((2 * held, wide), bf16)] * 2,
+                        own_share + share_got,
+                        name="join",
+                        after=squares,
+                    )
                 )
+            raw, squares, *sends = call(
+                functools.partial(reduce_kernel, starts, held),
+                [(raw.shape, f32), (squares.shape, f32)]
+                + [((rows + SQ, wide), bf16), ((rows, wide), bf16)],
+                [raw, squares] + got + own + more,
+                name="reduce",
             )
-            share_got = both(own_share, i + 1)
-            raw, squares, *sends = call(
-                reduce_kernel,
-                [(raw.shape, f32), (squares.shape, f32)] + [((frames + SQ, wide), bf16), ((frames, wide), bf16)],
-                [raw, squares] + got,
-                name="reduce",
-                after=own_share[0],
-            )
-            token = squares
-    up_all = call(
-        functools.partial(assemble_kernel, haves, share),
-        [((frames, depth), bf16)],
-        own_share + share_got,
-        name="assemble",
-        after=token,
-    )[0]
     grads = call(
-        functools.partial(back_kernel, features),
+        functools.partial(back_kernel, haves, share, features),
         [((frames, half), bf16)] * 2,
-        [gain, w_in, up_all, state, raw, squares] + got,
-        scratch=[pltpu.VMEM((frames, depth), bf16)],
+        [gain, w_in, state, raw, squares] + list(sends) + got,
+        scratch=[pltpu.VMEM((frames, depth), bf16)] * 2,
         name="back",
     )
 

time: 67.1 us -> 67.5 us (level)
  waiting for transfers between devices: 27.8 us -> 30.9 us
  starting transfers between devices: 25.7 us -> 23.1 us
    ppermute x22 -> x20, waiting for transfers between devices: 27.8 us -> 30.9 us  [swap(): return lax.ppermute(value, 'mp', [(i, i ^ bit) for i in range(n)])]
    ppermute x22 -> x20, starting transfers between devices: 25.7 us -> 23.1 us  [swap(): return lax.ppermute(value, 'mp', [(i, i ^ bit) for i in range(n)])]
    pallas_call x16 -> x15, Pallas kernels: 12.6 us -> 12.6 us  [call(): pl.pallas_call(kernel, out_shape=[jax.ShapeDtypeStruct(s, d) for s, d in...]
  transfers between devices with their start and end apart: 22 -> 20, of which waited for: 12 -> 12; matrix products, arithmetic and copies ran while one was open for 0% -> 0% of each run, Pallas kernels for 12% -> 11%
where the time goes in v9:
time: 67.5 us; the launch traced here: 67.4 us
  waiting for transfers between devices  30.9 us (46%)
  starting transfers between devices  23.1 us (34%)
  Pallas kernels  12.6 us (19%)
  between operations  0.77 us (1%)
    ppermute x20, waiting for transfers between devices, swap(): return lax.ppermute(value, 'mp', [(i, i ^ bit) for i in range(n)])  30.9 us
    ppermute x20, starting transfers between devices, swap(): return lax.ppermute(value, 'mp', [(i, i ^ bit) for i in range(n)])  23.1 us
    pallas_call x15, Pallas kernels, call(): pl.pallas_call(kernel, out_shape=[jax.ShapeDtypeStruct(s, d) for s, d in...  12.6 us
  transfers between devices with their start and end apart: 20, of which 12 were waited for; matrix products, arithmetic and copies ran while one was open for 0% of the time, Pallas kernels for 11%

profile of v9, /device:TPU:0, one launch (start us, length us, event | category | flops | bytes accessed | tf_op | source)
XLA Modules:
  0.0 67.4 jit_solution(10939466091903983150)
XLA Ops:
  0.7 2.0 %upstream.1 = (bf16[128,512]{1,0:T(8,128)(2,1)S(1)}, bf16[128,512]{1,0:T(8,128)(2,1)S(1)}, f32[256,1024]{1,0:T(8,128)S(1)}) custom-call(bf16[256,512]{1,0:T(8,128)(2,1)} %bitcast.8, bf16[1024,512]{1,0:T(8,128)(2,1)} %bitcast.4, f32[1,1024]{1,0:T(1,128)} %gain_depth.1), custom_call_target="tpu_custom_call" | custom-call | flops 20000000000 | bytes 60000000 | tf_op jit(solution)/shard_map/upstream/pallas_call | solution.py:47
  2.7 3.0 %collective-permute-start.2 = (bf16[128,512]{1,0:T(8,128)(2,1)S(1)}, bf16[128,512]{1,0:T(8,128)(2,1)S(1)}, u32[]{:S(2)}, u32[]{:S(2)}) collective-permute-start(bf16[128,512]{1,0:T(8,128)(2,1)S(1)} %get-tuple-element.35), channel_id=1, source_target_pairs={{0,1},{1,0},{2,3},{3,2},{4,5},{5,4},{6,7},{7,6},{8,9},{9,8},{10,11... | collective-permute-start | bytes 393224 | tf_op jit(solution)/shard_map/ppermute | solution.py:315
  5.7 1.5 %collective-permute-start.3 = (bf16[128,512]{1,0:T(8,128)(2,1)S(1)}, bf16[128,512]{1,0:T(8,128)(2,1)S(1)}, u32[]{:S(2)}, u32[]{:S(2)}) collective-permute-start(bf16[128,512]{1,0:T(8,128)(2,1)S(1)} %get-tuple-element.36), channel_id=1, source_target_pairs={{0,2},{1,3},{2,0},{3,1},{4,6},{5,7},{6,4},{7,5},{8,10},{9,11},{10,... | collective-permute-start | bytes 393224 | tf_op jit(solution)/shard_map/ppermute | solution.py:315
  7.2 0.7 %project.3 = (bf16[256,512]{1,0:T(8,128)(2,1)S(1)}, bf16[256,512]{1,0:T(8,128)(2,1)S(1)}) custom-call(bf16[256,1024]{1,0:T(8,128)(2,1)S(1)} %copy-done.3, bf16[1024,4096]{1,0:T(8,128)(2,1)S(1)} %copy-done, f32[256,1024]{1,0:T(8,128)S(1)} %get-tuple-element.32.refs_2_.refs_0_), custom_call_target="tpu_custom_call" | custom-call | flops 20000000000 | bytes 60000000 | tf_op jit(solution)/shard_map/project/pallas_call | solution.py:47
  7.9 0.6 collective-permute-start
  8.5 1.2 %collective-permute-start.1 = (bf16[256,512]{1,0:T(8,128)(2,1)S(1)}, bf16[256,512]{1,0:T(8,128)(2,1)S(1)}, u32[]{:S(2)}, u32[]{:S(2)}) collective-permute-start(bf16[256,512]{1,0:T(8,128)(2,1)S(1)} %get-tuple-element.34), channel_id=1, source_target_pairs={{0,2},{1,3},{2,0},{3,1},{4,6},{5,7},{6,4},{7,5},{8,10},{9,11},{10,... | collective-permute-start | bytes 786440 | tf_op jit(solution)/shard_map/ppermute | solution.py:315
  9.7 1.2 %collective-permute-done.3.refs_4_.refs_2_ = bf16[128,512]{1,0:T(8,128)(2,1)S(1)} collective-permute-done((bf16[128,512]{1,0:T(8,128)(2,1)S(1)}, bf16[128,512]{1,0:T(8,128)(2,1)S(1)}, u32[]{:S(2)}, u32[]{:S(2)}) %collective-permute-start.3) | collective-permute-done | bytes 131104 | tf_op jit(solution)/shard_map/ppermute | solution.py:315
  10.9 0.7 %project.4 = (bf16[320,512]{1,0:T(8,128)(2,1)S(1)}, bf16[320,512]{1,0:T(8,128)(2,1)S(1)}) custom-call(bf16[256,1024]{1,0:T(8,128)(2,1)S(1)} %copy-done.3, bf16[1024,4096]{1,0:T(8,128)(2,1)S(1)} %copy-done, f32[256,1024]{1,0:T(8,128)S(1)} %get-tuple-element.32.refs_2_.refs_0_, bf16[128,512]{1,0:T(8,128)(2,1)S(1)} %collective-permute-done.2.refs_3_.refs_1_, ...), custom_call_target="tpu_custom_call" | custom-call | flops 20000000000 | bytes 60000000 | tf_op jit(solution)/shard_map/project/pallas_call | solution.py:47
  11.6 0.3 collective-permute-start.4
  11.9 1.8 %collective-permute-start.6 = (bf16[320,512]{1,0:T(8,128)(2,1)S(1)}, bf16[320,512]{1,0:T(8,128)(2,1)S(1)}, u32[]{:S(2)}, u32[]{:S(2)}) collective-permute-start(bf16[320,512]{1,0:T(8,128)(2,1)S(1)} %get-tuple-element.39), channel_id=1, source_target_pairs={{0,2},{1,3},{2,0},{3,1},{4,6},{5,7},{6,4},{7,5},{8,10},{9,11},{10,... | collective-permute-start | bytes 983048 | tf_op jit(solution)/shard_map/ppermute | solution.py:315
  13.8 3.5 %collective-permute-done.refs_2_ = bf16[256,512]{1,0:T(8,128)(2,1)S(1)} collective-permute-done((bf16[256,512]{1,0:T(8,128)(2,1)S(1)}, bf16[256,512]{1,0:T(8,128)(2,1)S(1)}, u32[]{:S(2)}, u32[]{:S(2)}) %collective-permute-start) | collective-permute-done | bytes 262176 | tf_op jit(solution)/shard_map/ppermute | solution.py:315
  17.2 0.5 collective-permute-done.1.refs_3_
  17.8 0.7 %project.5 = (bf16[256,512]{1,0:T(8,128)(2,1)S(1)}, bf16[256,512]{1,0:T(8,128)(2,1)S(1)}) custom-call(bf16[256,1024]{1,0:T(8,128)(2,1)S(1)} %copy-done.3, bf16[1024,4096]{1,0:T(8,128)(2,1)S(1)} %copy-done, bf16[256,512]{1,0:T(8,128)(2,1)S(1)} %collective-permute-done.refs_2_, bf16[256,512]{1,0:T(8,128)(2,1)S(1)} %collective-permute-done.1.refs_3_, ...), custom_call_target="tpu_custom_call" | custom-call | flops 20000000000 | bytes 60000000 | tf_op jit(solution)/shard_map/project/pallas_call | solution.py:47
  18.5 1.3 %collective-permute-start.5 = (bf16[256,512]{1,0:T(8,128)(2,1)S(1)}, bf16[256,512]{1,0:T(8,128)(2,1)S(1)}, u32[]{:S(2)}, u32[]{:S(2)}) collective-permute-start(bf16[256,512]{1,0:T(8,128)(2,1)S(1)} %get-tuple-element.38.refs_3_), channel_id=1, source_target_pairs={{0,2},{1,3},{2,0},{3,1},{4,6},{5,7},{6,4},{7,5},{8,10},{9,11},{10,... | collective-permute-start | bytes 786440 | tf_op jit(solution)/shard_map/ppermute | solution.py:315
  19.7 0.8 %collective-permute-start.7 = (bf16[256,512]{1,0:T(8,128)(2,1)S(1)}, bf16[256,512]{1,0:T(8,128)(2,1)S(1)}, u32[]{:S(2)}, u32[]{:S(2)}) collective-permute-start(bf16[256,512]{1,0:T(8,128)(2,1)S(1)} %get-tuple-element.40), channel_id=1, source_target_pairs={{0,1},{1,0},{2,3},{3,2},{4,5},{5,4},{6,7},{7,6},{8,9},{9,8},{10,11... | collective-permute-start | bytes 786440 | tf_op jit(solution)/shard_map/ppermute | solution.py:315
  20.6 0.7 %keep.1.refs_5_.refs_2_ = f32[256,1024]{1,0:T(8,128)S(1)} custom-call(bf16[256,1024]{1,0:T(8,128)(2,1)S(1)} %copy-done.3, bf16[1024,4096]{1,0:T(8,128)(2,1)S(1)} %copy-done, bf16[256,1024]{1,0:T(8,128)(2,1)S(1)} %copy-done.4, bf16[256,512]{1,0:T(8,128)(2,1)S(1)} %get-tuple-element.38.refs_3_), custom_call_target="tpu_custom_call" | custom-call | flops 20000000000 | bytes 60000000 | tf_op jit(solution)/shard_map/keep/pallas_call | solution.py:47
  21.3 3.0 %collective-permute-done.4.refs_4_.refs_3_ = bf16[320,512]{1,0:T(8,128)(2,1)S(1)} collective-permute-done((bf16[320,512]{1,0:T(8,128)(2,1)S(1)}, bf16[320,512]{1,0:T(8,128)(2,1)S(1)}, u32[]{:S(2)}, u32[]{:S(2)}) %collective-permute-start.4) | collective-permute-done | bytes 327712 | tf_op jit(solution)/shard_map/ppermute | solution.py:315
  24.2 0.5 collective-permute-done.6.refs_3_.refs_5_
  24.8 1.6 %collective-permute-start.10 = (bf16[64,512]{1,0:T(8,128)(2,1)S(1)}, bf16[64,512]{1,0:T(8,128)(2,1)S(1)}, u32[]{:S(2)}, u32[]{:S(2)}) collective-permute-start(bf16[64,512]{1,0:T(8,128)(2,1)S(1)} %get-tuple-element.41.refs_7_.refs_0_), channel_id=1, source_target_pairs={{0,1},{1,0},{2,3},{3,2},{4,5},{5,4},{6,7},{7,6},{8,9},{9,8},{10,11... | collective-permute-start | bytes 196616 | tf_op jit(solution)/shard_map/ppermute | solution.py:315
  26.4 0.5 collective-permute-start.11
  26.9 2.7 %collective-permute-done.5.refs_4_ = bf16[256,512]{1,0:T(8,128)(2,1)S(1)} collective-permute-done((bf16[256,512]{1,0:T(8,128)(2,1)S(1)}, bf16[256,512]{1,0:T(8,128)(2,1)S(1)}, u32[]{:S(2)}, u32[]{:S(2)}) %collective-permute-start.5) | collective-permute-done | bytes 262176 | tf_op jit(solution)/shard_map/ppermute | solution.py:315
  29.6 0.8 %state.1 = (f32[256,1024]{1,0:T(8,128)S(1)}, f32[256,1024]{1,0:T(8,128)S(1)}, f32[8,256]{1,0:T(8,128)S(1)}, bf16[272,512]{1,0:T(8,128)(2,1)S(1)}, bf16[256,512]{1,0:T(8,128)(2,1)S(1)}) custom-call(f32[1,4096]{1,0:T(1,128)S(1)} %bitcast.6, bf16[1024,1024]{1,0:T(8,128)(2,1)S(1)} %copy-done.1, f32[256,1024]{1,0:T(8,128)S(1)} %keep.1.refs_5_.refs_2_, ...), custom_call_target="tpu_custom_call" | custom-call | flops 20000000000 | bytes 60000000 | tf_op jit(solution)/shard_map/state/pallas_call | solution.py:47
  30.4 1.0 %collective-permute-start.8 = (bf16[272,512]{1,0:T(8,128)(2,1)S(1)}, bf16[272,512]{1,0:T(8,128)(2,1)S(1)}, u32[]{:S(2)}, u32[]{:S(2)}) collective-permute-start(bf16[272,512]{1,0:T(8,128)(2,1)S(1)} %get-tuple-element.44), channel_id=1, source_target_pairs={{0,1},{1,0},{2,3},{3,2},{4,5},{5,4},{6,7},{7,6},{8,9},{9,8},{10,11... | collective-permute-start | bytes 835592 | tf_op jit(solution)/shard_map/ppermute | solution.py:315
  31.4 1.1 %collective-permute-start.9 = (bf16[256,512]{1,0:T(8,128)(2,1)S(1)}, bf16[256,512]{1,0:T(8,128)(2,1)S(1)}, u32[]{:S(2)}, u32[]{:S(2)}) collective-permute-start(bf16[256,512]{1,0:T(8,128)(2,1)S(1)} %get-tuple-element.45), channel_id=1, source_target_pairs={{0,2},{1,3},{2,0},{3,1},{4,6},{5,7},{6,4},{7,5},{8,10},{9,11},{10,... | collective-permute-start | bytes 786440 | tf_op jit(solution)/shard_map/ppermute | solution.py:315
  32.5 0.0 collective-permute-done.10.refs_2_
  32.5 0.0 collective-permute-done.11.refs_3_
  32.5 5.8 %collective-permute-done.9.refs_1_ = bf16[256,512]{1,0:T(8,128)(2,1)S(1)} collective-permute-done((bf16[256,512]{1,0:T(8,128)(2,1)S(1)}, bf16[256,512]{1,0:T(8,128)(2,1)S(1)}, u32[]{:S(2)}, u32[]{:S(2)}) %collective-permute-start.9) | collective-permute-done | bytes 262176 | tf_op jit(solution)/shard_map/ppermute | solution.py:315
  38.3 0.0 collective-permute-done.8.refs_0_
  38.3 0.2 reduce.1
  38.5 0.6 collective-permute-start.12
  39.1 1.5 %collective-permute-start.13 = (bf16[384,512]{1,0:T(8,128)(2,1)S(1)}, bf16[384,512]{1,0:T(8,128)(2,1)S(1)}, u32[]{:S(2)}, u32[]{:S(2)}) collective-permute-start(bf16[384,512]{1,0:T(8,128)(2,1)S(1)} %get-tuple-element.52.refs_1_), channel_id=1, source_target_pairs={{0,1},{1,0},{2,3},{3,2},{4,5},{5,4},{6,7},{7,6},{8,9},{9,8},{10,11... | collective-permute-start | bytes 1179656 | tf_op jit(solution)/shard_map/ppermute | solution.py:315
  40.6 6.4 %collective-permute-done.13.refs_3_.refs_1_ = bf16[384,512]{1,0:T(8,128)(2,1)S(1)} collective-permute-done((bf16[384,512]{1,0:T(8,128)(2,1)S(1)}, bf16[384,512]{1,0:T(8,128)(2,1)S(1)}, u32[]{:S(2)}, u32[]{:S(2)}) %collective-permute-start.13) | collective-permute-done | bytes 393248 | tf_op jit(solution)/shard_map/ppermute | solution.py:315
  47.0 1.3 %back.1 = (bf16[256,512]{1,0:T(8,128)(2,1)S(1)}, bf16[256,512]{1,0:T(8,128)(2,1)S(1)}) custom-call(f32[1,4096]{1,0:T(1,128)S(1)} %bitcast.7, bf16[1024,1024]{1,0:T(8,128)(2,1)S(1)} %copy-done.1, f32[256,1024]{1,0:T(8,128)S(1)} %get-tuple-element.53.state, f32[256,1024]{1,0:T(8,128)S(1)} %get-tuple-element.49.raw, f32[8,256]{1,0:T(8,128)S(1)} %get-tuple-element.50.squares, ...), custom_call_target="tpu_custom_call" | custom-call | flops 20000000000 | bytes 60000000 | tf_op jit(solution)/shard_map/back/pallas_call | solution.py:47
  48.4 1.5 %collective-permute-start.14 = (bf16[256,512]{1,0:T(8,128)(2,1)S(1)}, bf16[256,512]{1,0:T(8,128)(2,1)S(1)}, u32[]{:S(2)}, u32[]{:S(2)}) collective-permute-start(bf16[256,512]{1,0:T(8,128)(2,1)S(1)} %get-tuple-element.54.refs_2_.first), channel_id=1, source_target_pairs={{0,1},{1,0},{2,3},{3,2},{4,5},{5,4},{6,7},{7,6},{8,9},{9,8},{10,11... | collective-permute-start | bytes 786440 | tf_op jit(solution)/shard_map/ppermute | solution.py:315
  49.9 0.7 %collective-permute-start.16 = (bf16[256,512]{1,0:T(8,128)(2,1)S(1)}, bf16[256,512]{1,0:T(8,128)(2,1)S(1)}, u32[]{:S(2)}, u32[]{:S(2)}) collective-permute-start(bf16[256,512]{1,0:T(8,128)(2,1)S(1)} %get-tuple-element.55.refs_3_.second), channel_id=1, source_target_pairs={{0,2},{1,3},{2,0},{3,1},{4,6},{5,7},{6,4},{7,5},{8,10},{9,11},{10,... | collective-permute-start | bytes 786440 | tf_op jit(solution)/shard_map/ppermute | solution.py:315
  50.5 0.7 %grad_context.4 = (f32[256,1024]{1,0:T(8,128)S(1)}, bf16[256,512]{1,0:T(8,128)(2,1)S(1)}, bf16[256,512]{1,0:T(8,128)(2,1)S(1)}) custom-call(bf16[1024,4096]{1,0:T(8,128)(2,1)S(1)} %copy-done, bf16[256,512]{1,0:T(8,128)(2,1)S(1)} %get-tuple-element.54.refs_2_.first, bf16[256,512]{1,0:T(8,128)(2,1)S(1)} %get-tuple-element.55.refs_3_.second), custom_call_target="tpu_custom_call" | custom-call | flops 20000000000 | bytes 60000000 | tf_op jit(solution)/shard_map/grad_context/pallas_call | solution.py:47
  51.3 1.4 %collective-permute-start.18 = (bf16[256,512]{1,0:T(8,128)(2,1)S(1)}, bf16[256,512]{1,0:T(8,128)(2,1)S(1)}, u32[]{:S(2)}, u32[]{:S(2)}) collective-permute-start(bf16[256,512]{1,0:T(8,128)(2,1)S(1)} %get-tuple-element.58), channel_id=1, source_target_pairs={{0,2},{1,3},{2,0},{3,1},{4,6},{5,7},{6,4},{7,5},{8,10},{9,11},{10,... | collective-permute-start | bytes 786440 | tf_op jit(solution)/shard_map/ppermute | solution.py:315
  52.7 0.6 collective-permute-start.19
  53.3 1.6 %act.1 = (bf16[256,512]{1,0:T(8,128)(2,1)}, bf16[256,1024]{1,0:T(8,128)(2,1)}) custom-call(f32[1,1024]{1,0:T(1,128)S(1)} %copy-done.6, bf16[1024,512]{1,0:T(8,128)(2,1)S(1)} %bitcast.5, f32[256,1024]{1,0:T(8,128)S(1)} %get-tuple-element.49.raw, f32[8,256]{1,0:T(8,128)S(1)} %get-tuple-element.50.squares, ...), custom_call_target="tpu_custom_call" | custom-call | flops 20000000000 | bytes 60000000 | tf_op jit(solution)/shard_map/act/pallas_call | solution.py:47
  54.9 2.8 %collective-permute-done.14.refs_0_ = bf16[256,512]{1,0:T(8,128)(2,1)S(1)} collective-permute-done((bf16[256,512]{1,0:T(8,128)(2,1)S(1)}, bf16[256,512]{1,0:T(8,128)(2,1)S(1)}, u32[]{:S(2)}, u32[]{:S(2)}) %collective-permute-start.14) | collective-permute-done | bytes 262176 | tf_op jit(solution)/shard_map/ppermute | solution.py:315
  57.7 1.8 %collective-permute-start.15 = (bf16[256,512]{1,0:T(8,128)(2,1)S(1)}, bf16[256,512]{1,0:T(8,128)(2,1)S(1)}, u32[]{:S(2)}, u32[]{:S(2)}) collective-permute-start(bf16[256,512]{1,0:T(8,128)(2,1)S(1)} %collective-permute-done.14.refs_0_), channel_id=1, source_target_pairs={{0,2},{1,3},{2,0},{3,1},{4,6},{5,7},{6,4},{7,5},{8,10},{9,11},{10,... | collective-permute-start | bytes 786440 | tf_op jit(solution)/shard_map/ppermute | solution.py:315
  59.5 0.3 collective-permute-start.17
  59.8 0.8 %grad_context.5.refs_2_ = f32[256,1024]{1,0:T(8,128)S(1)} custom-call(bf16[1024,4096]{1,0:T(8,128)(2,1)S(1)} %copy-done, bf16[256,512]{1,0:T(8,128)(2,1)S(1)} %collective-permute-done.14.refs_0_, bf16[256,512]{1,0:T(8,128)(2,1)S(1)} %collective-permute-done.16.refs_1_, f32[256,1024]{1,0:T(8,128)S(1)} %get-tuple-element.60.refs_2_), custom_call_target="tpu_custom_call" | custom-call | flops 20000000000 | bytes 60000000 | tf_op jit(solution)/shard_map/grad_context/pallas_call | solution.py:47
  60.5 1.6 %collective-permute-done.18.refs_0_ = bf16[256,512]{1,0:T(8,128)(2,1)S(1)} collective-permute-done((bf16[256,512]{1,0:T(8,128)(2,1)S(1)}, bf16[256,512]{1,0:T(8,128)(2,1)S(1)}, u32[]{:S(2)}, u32[]{:S(2)}) %collective-permute-start.18) | collective-permute-done | bytes 262176 | tf_op jit(solution)/shard_map/ppermute | solution.py:315
  62.1 0.7 %grad_context.6.refs_2_ = f32[256,1024]{1,0:T(8,128)S(1)} custom-call(bf16[1024,4096]{1,0:T(8,128)(2,1)S(1)} %copy-done, bf16[256,512]{1,0:T(8,128)(2,1)S(1)} %collective-permute-done.18.refs_0_, bf16[256,512]{1,0:T(8,128)(2,1)S(1)} %collective-permute-done.19.refs_1_, f32[256,1024]{1,0:T(8,128)S(1)} %grad_context.5.refs_2_), custom_call_target="tpu_custom_call" | custom-call | flops 20000000000 | bytes 60000000 | tf_op jit(solution)/shard_map/grad_context/pallas_call | solution.py:47
  62.9 2.1 %collective-permute-done.15.refs_0_ = bf16[256,512]{1,0:T(8,128)(2,1)S(1)} collective-permute-done((bf16[256,512]{1,0:T(8,128)(2,1)S(1)}, bf16[256,512]{1,0:T(8,128)(2,1)S(1)}, u32[]{:S(2)}, u32[]{:S(2)}) %collective-permute-start.15) | collective-permute-done | bytes 262176 | tf_op jit(solution)/shard_map/ppermute | solution.py:315
  64.9 0.9 %collective-permute-done.17.refs_1_ = bf16[256,512]{1,0:T(8,128)(2,1)S(1)} collective-permute-done((bf16[256,512]{1,0:T(8,128)(2,1)S(1)}, bf16[256,512]{1,0:T(8,128)(2,1)S(1)}, u32[]{:S(2)}, u32[]{:S(2)}) %collective-permute-start.17) | collective-permute-done | bytes 262176 | tf_op jit(solution)/shard_map/ppermute | solution.py:315
  65.8 1.5 %grad_context.7 = bf16[256,1024]{1,0:T(8,128)(2,1)} custom-call(bf16[1024,4096]{1,0:T(8,128)(2,1)S(1)} %copy-done, bf16[256,512]{1,0:T(8,128)(2,1)S(1)} %collective-permute-done.15.refs_0_, bf16[256,512]{1,0:T(8,128)(2,1)S(1)} %collective-permute-done.17.refs_1_, f32[256,1024]{1,0:T(8,128)S(1)} %grad_context.6.refs_2_), custom_call_target="tpu_custom_call" | custom-call | flops 20000000000 | bytes 60000000 | tf_op jit(solution)/shard_map/grad_context/pallas_call | solution.py:47
  (21 shorter events, 0.1 us)
Async XLA Ops:
  0.6 6.5 %copy-start = (bf16[1024,4096]{1,0:T(8,128)(2,1)S(1)}, bf16[1024,4096]{1,0:T(8,128)(2,1)}, u32[]{:S(2)}) copy-start(bf16[1024,4096]{1,0:T(8,128)(2,1)} %w_out.7) | copy-start | bytes 25165828
  0.6 6.5 %copy-start.3 = (bf16[256,1024]{1,0:T(8,128)(2,1)S(1)}, bf16[256,1024]{1,0:T(8,128)(2,1)}, u32[]{:S(2)}) copy-start(bf16[256,1024]{1,0:T(8,128)(2,1)} %refs_0_.7) | copy-start | bytes 1572868
  2.7 7.1 %collective-permute-start.2 = (bf16[128,512]{1,0:T(8,128)(2,1)S(1)}, bf16[128,512]{1,0:T(8,128)(2,1)S(1)}, u32[]{:S(2)}, u32[]{:S(2)}) collective-permute-start(bf16[128,512]{1,0:T(8,128)(2,1)S(1)} %get-tuple-element.35), channel_id=1, source_target_pairs={{0,1},{1,0},{2,3},{3,2},{4,5},{5,4},{6,7},{7,6},{8,9},{9,8},{10,11... | collective-permute-start | bytes 393224 | tf_op jit(solution)/shard_map/ppermute | solution.py:315
  5.7 5.2 %collective-permute-start.3 = (bf16[128,512]{1,0:T(8,128)(2,1)S(1)}, bf16[128,512]{1,0:T(8,128)(2,1)S(1)}, u32[]{:S(2)}, u32[]{:S(2)}) collective-permute-start(bf16[128,512]{1,0:T(8,128)(2,1)S(1)} %get-tuple-element.36), channel_id=1, source_target_pairs={{0,2},{1,3},{2,0},{3,1},{4,6},{5,7},{6,4},{7,5},{8,10},{9,11},{10,... | collective-permute-start | bytes 393224 | tf_op jit(solution)/shard_map/ppermute | solution.py:315
  7.9 9.3 %collective-permute-start = (bf16[256,512]{1,0:T(8,128)(2,1)S(1)}, bf16[256,512]{1,0:T(8,128)(2,1)S(1)}, u32[]{:S(2)}, u32[]{:S(2)}) collective-permute-start(bf16[256,512]{1,0:T(8,128)(2,1)S(1)} %get-tuple-element.33.refs_5_), channel_id=1, source_target_pairs={{0,1},{1,0},{2,3},{3,2},{4,5},{5,4},{6,7},{7,6},{8,9},{9,8},{10,11... | collective-permute-start | bytes 786440 | tf_op jit(solution)/shard_map/ppermute | solution.py:315
  8.5 9.2 %collective-permute-start.1 = (bf16[256,512]{1,0:T(8,128)(2,1)S(1)}, bf16[256,512]{1,0:T(8,128)(2,1)S(1)}, u32[]{:S(2)}, u32[]{:S(2)}) collective-permute-start(bf16[256,512]{1,0:T(8,128)(2,1)S(1)} %get-tuple-element.34), channel_id=1, source_target_pairs={{0,2},{1,3},{2,0},{3,1},{4,6},{5,7},{6,4},{7,5},{8,10},{9,11},{10,... | collective-permute-start | bytes 786440 | tf_op jit(solution)/shard_map/ppermute | solution.py:315
  11.6 12.6 %collective-permute-start.4 = (bf16[320,512]{1,0:T(8,128)(2,1)S(1)}, bf16[320,512]{1,0:T(8,128)(2,1)S(1)}, u32[]{:S(2)}, u32[]{:S(2)}) collective-permute-start(bf16[320,512]{1,0:T(8,128)(2,1)S(1)} %get-tuple-element.37.refs_4_), channel_id=1, source_target_pairs={{0,1},{1,0},{2,3},{3,2},{4,5},{5,4},{6,7},{7,6},{8,9},{9,8},{10,11... | collective-permute-start | bytes 983048 | tf_op jit(solution)/shard_map/ppermute | solution.py:315
  11.9 8.6 %copy-start.4 = (bf16[256,1024]{1,0:T(8,128)(2,1)S(1)}, bf16[256,1024]{1,0:T(8,128)(2,1)}, u32[]{:S(2)}) copy-start(bf16[256,1024]{1,0:T(8,128)(2,1)} %refs_2_.1) | copy-start | bytes 1572868
  11.9 12.9 %collective-permute-start.6 = (bf16[320,512]{1,0:T(8,128)(2,1)S(1)}, bf16[320,512]{1,0:T(8,128)(2,1)S(1)}, u32[]{:S(2)}, u32[]{:S(2)}) collective-permute-start(bf16[320,512]{1,0:T(8,128)(2,1)S(1)} %get-tuple-element.39), channel_id=1, source_target_pairs={{0,2},{1,3},{2,0},{3,1},{4,6},{5,7},{6,4},{7,5},{8,10},{9,11},{10,... | collective-permute-start | bytes 983048 | tf_op jit(solution)/shard_map/ppermute | solution.py:315
  18.5 11.1 %collective-permute-start.5 = (bf16[256,512]{1,0:T(8,128)(2,1)S(1)}, bf16[256,512]{1,0:T(8,128)(2,1)S(1)}, u32[]{:S(2)}, u32[]{:S(2)}) collective-permute-start(bf16[256,512]{1,0:T(8,128)(2,1)S(1)} %get-tuple-element.38.refs_3_), channel_id=1, source_target_pairs={{0,2},{1,3},{2,0},{3,1},{4,6},{5,7},{6,4},{7,5},{8,10},{9,11},{10,... | collective-permute-start | bytes 786440 | tf_op jit(solution)/shard_map/ppermute | solution.py:315
  19.7 9.8 %copy-start.1 = (bf16[1024,1024]{1,0:T(8,128)(2,1)S(1)}, bf16[1024,1024]{1,0:T(8,128)(2,1)}, u32[]{:S(2)}) copy-start(bf16[1024,1024]{1,0:T(8,128)(2,1)} %w_in.1) | copy-start | bytes 6291460
  19.7 9.8 %copy-start.5 = (f32[4096]{0:T(1024)S(1)}, f32[4096]{0:T(1024)}, u32[]{:S(2)}) copy-start(f32[4096]{0:T(1024)} %param.11) | copy-start | bytes 49156
  19.7 9.8 %collective-permute-start.7 = (bf16[256,512]{1,0:T(8,128)(2,1)S(1)}, bf16[256,512]{1,0:T(8,128)(2,1)S(1)}, u32[]{:S(2)}, u32[]{:S(2)}) collective-permute-start(bf16[256,512]{1,0:T(8,128)(2,1)S(1)} %get-tuple-element.40), channel_id=1, source_target_pairs={{0,1},{1,0},{2,3},{3,2},{4,5},{5,4},{6,7},{7,6},{8,9},{9,8},{10,11... | collective-permute-start | bytes 786440 | tf_op jit(solution)/shard_map/ppermute | solution.py:315
  24.8 7.7 %collective-permute-start.10 = (bf16[64,512]{1,0:T(8,128)(2,1)S(1)}, bf16[64,512]{1,0:T(8,128)(2,1)S(1)}, u32[]{:S(2)}, u32[]{:S(2)}) collective-permute-start(bf16[64,512]{1,0:T(8,128)(2,1)S(1)} %get-tuple-element.41.refs_7_.refs_0_), channel_id=1, source_target_pairs={{0,1},{1,0},{2,3},{3,2},{4,5},{5,4},{6,7},{7,6},{8,9},{9,8},{10,11... | collective-permute-start | bytes 196616 | tf_op jit(solution)/shard_map/ppermute | solution.py:315
  26.4 6.1 %collective-permute-start.11 = (bf16[64,512]{1,0:T(8,128)(2,1)S(1)}, bf16[64,512]{1,0:T(8,128)(2,1)S(1)}, u32[]{:S(2)}, u32[]{:S(2)}) collective-permute-start(bf16[64,512]{1,0:T(8,128)(2,1)S(1)} %get-tuple-element.46.refs_1_), channel_id=1, source_target_pairs={{0,2},{1,3},{2,0},{3,1},{4,6},{5,7},{6,4},{7,5},{8,10},{9,11},{10,... | collective-permute-start | bytes 196616 | tf_op jit(solution)/shard_map/ppermute | solution.py:315
  30.4 8.0 %collective-permute-start.8 = (bf16[272,512]{1,0:T(8,128)(2,1)S(1)}, bf16[272,512]{1,0:T(8,128)(2,1)S(1)}, u32[]{:S(2)}, u32[]{:S(2)}) collective-permute-start(bf16[272,512]{1,0:T(8,128)(2,1)S(1)} %get-tuple-element.44), channel_id=1, source_target_pairs={{0,1},{1,0},{2,3},{3,2},{4,5},{5,4},{6,7},{7,6},{8,9},{9,8},{10,11... | collective-permute-start | bytes 835592 | tf_op jit(solution)/shard_map/ppermute | solution.py:315
  31.4 6.9 %collective-permute-start.9 = (bf16[256,512]{1,0:T(8,128)(2,1)S(1)}, bf16[256,512]{1,0:T(8,128)(2,1)S(1)}, u32[]{:S(2)}, u32[]{:S(2)}) collective-permute-start(bf16[256,512]{1,0:T(8,128)(2,1)S(1)} %get-tuple-element.45), channel_id=1, source_target_pairs={{0,2},{1,3},{2,0},{3,1},{4,6},{5,7},{6,4},{7,5},{8,10},{9,11},{10,... | collective-permute-start | bytes 786440 | tf_op jit(solution)/shard_map/ppermute | solution.py:315
  38.5 8.5 %collective-permute-start.12 = (bf16[400,512]{1,0:T(8,128)(2,1)S(1)}, bf16[400,512]{1,0:T(8,128)(2,1)S(1)}, u32[]{:S(2)}, u32[]{:S(2)}) collective-permute-start(bf16[400,512]{1,0:T(8,128)(2,1)S(1)} %get-tuple-element.51.refs_0_), channel_id=1, source_target_pairs={{0,2},{1,3},{2,0},{3,1},{4,6},{5,7},{6,4},{7,5},{8,10},{9,11},{10,... | collective-permute-start | bytes 1228808 | tf_op jit(solution)/shard_map/ppermute | solution.py:315
  39.1 7.9 %collective-permute-start.13 = (bf16[384,512]{1,0:T(8,128)(2,1)S(1)}, bf16[384,512]{1,0:T(8,128)(2,1)S(1)}, u32[]{:S(2)}, u32[]{:S(2)}) collective-permute-start(bf16[384,512]{1,0:T(8,128)(2,1)S(1)} %get-tuple-element.52.refs_1_), channel_id=1, source_target_pairs={{0,1},{1,0},{2,3},{3,2},{4,5},{5,4},{6,7},{7,6},{8,9},{9,8},{10,11... | collective-permute-start | bytes 1179656 | tf_op jit(solution)/shard_map/ppermute | solution.py:315
  48.4 9.3 %collective-permute-start.14 = (bf16[256,512]{1,0:T(8,128)(2,1)S(1)}, bf16[256,512]{1,0:T(8,128)(2,1)S(1)}, u32[]{:S(2)}, u32[]{:S(2)}) collective-permute-start(bf16[256,512]{1,0:T(8,128)(2,1)S(1)} %get-tuple-element.54.refs_2_.first), channel_id=1, source_target_pairs={{0,1},{1,0},{2,3},{3,2},{4,5},{5,4},{6,7},{7,6},{8,9},{9,8},{10,11... | collective-permute-start | bytes 786440 | tf_op jit(solution)/shard_map/ppermute | solution.py:315
  49.8 3.5 %copy-start.2 = (bf16[1,1024,512]{2,1,0:T(8,128)(2,1)S(1)}, bf16[1,1024,512]{2,1,0:T(8,128)(2,1)}, u32[]{:S(2)}) copy-start(bf16[1,1024,512]{2,1,0:T(8,128)(2,1)} %param.14) | copy-start | bytes 3145732
  49.8 3.5 %copy-start.6 = (f32[1,1024]{1,0:T(1,128)S(1)}, f32[1,1024]{1,0:T(1,128)}, u32[]{:S(2)}) copy-start(f32[1,1024]{1,0:T(1,128)} %gain_depth.1) | copy-start | bytes 12292
  49.9 9.6 %collective-permute-start.16 = (bf16[256,512]{1,0:T(8,128)(2,1)S(1)}, bf16[256,512]{1,0:T(8,128)(2,1)S(1)}, u32[]{:S(2)}, u32[]{:S(2)}) collective-permute-start(bf16[256,512]{1,0:T(8,128)(2,1)S(1)} %get-tuple-element.55.refs_3_.second), channel_id=1, source_target_pairs={{0,2},{1,3},{2,0},{3,1},{4,6},{5,7},{6,4},{7,5},{8,10},{9,11},{10,... | collective-permute-start | bytes 786440 | tf_op jit(solution)/shard_map/ppermute | solution.py:315
  51.3 10.8 %collective-permute-start.18 = (bf16[256,512]{1,0:T(8,128)(2,1)S(1)}, bf16[256,512]{1,0:T(8,128)(2,1)S(1)}, u32[]{:S(2)}, u32[]{:S(2)}) collective-permute-start(bf16[256,512]{1,0:T(8,128)(2,1)S(1)} %get-tuple-element.58), channel_id=1, source_target_pairs={{0,2},{1,3},{2,0},{3,1},{4,6},{5,7},{6,4},{7,5},{8,10},{9,11},{10,... | collective-permute-start | bytes 786440 | tf_op jit(solution)/shard_map/ppermute | solution.py:315
  52.7 9.4 %collective-permute-start.19 = (bf16[256,512]{1,0:T(8,128)(2,1)S(1)}, bf16[256,512]{1,0:T(8,128)(2,1)S(1)}, u32[]{:S(2)}, u32[]{:S(2)}) collective-permute-start(bf16[256,512]{1,0:T(8,128)(2,1)S(1)} %get-tuple-element.59), channel_id=1, source_target_pairs={{0,1},{1,0},{2,3},{3,2},{4,5},{5,4},{6,7},{7,6},{8,9},{9,8},{10,11... | collective-permute-start | bytes 786440 | tf_op jit(solution)/shard_map/ppermute | solution.py:315
  57.7 7.2 %collective-permute-start.15 = (bf16[256,512]{1,0:T(8,128)(2,1)S(1)}, bf16[256,512]{1,0:T(8,128)(2,1)S(1)}, u32[]{:S(2)}, u32[]{:S(2)}) collective-permute-start(bf16[256,512]{1,0:T(8,128)(2,1)S(1)} %collective-permute-done.14.refs_0_), channel_id=1, source_target_pairs={{0,2},{1,3},{2,0},{3,1},{4,6},{5,7},{6,4},{7,5},{8,10},{9,11},{10,... | collective-permute-start | bytes 786440 | tf_op jit(solution)/shard_map/ppermute | solution.py:315
  59.5 6.4 %collective-permute-start.17 = (bf16[256,512]{1,0:T(8,128)(2,1)S(1)}, bf16[256,512]{1,0:T(8,128)(2,1)S(1)}, u32[]{:S(2)}, u32[]{:S(2)}) collective-permute-start(bf16[256,512]{1,0:T(8,128)(2,1)S(1)} %collective-permute-done.16.refs_1_), channel_id=1, source_target_pairs={{0,1},{1,0},{2,3},{3,2},{4,5},{5,4},{6,7},{7,6},{8,9},{9,8},{10,11... | collective-permute-start | bytes 786440 | tf_op jit(solution)/shard_map/ppermute | solution.py:315
